TPU v7x, 32 devices: a whole 2x2x4 slice. The times are simulated.
32 devices in a mesh: rep: 2 (over x), shard: 16 (over z, y, core).
Axes of the slice: x: 2, y: 2, z: 4, core: 2. Of those that a mesh axis runs over, the one named last changes fastest.
Arguments:
- hidden_in: bfloat16 [2, 2048, 2048], P('rep', 'shard'), may hold values from -6 to 6
- segments: int32 [2, 2048], P('rep'), may hold values from 0 to 7, never falling along the last dimension, each value on 1 to 1024 neighbouring positions
- cotangent: bfloat16 [2, 2048, 2048], P('rep', 'shard'), may hold values from -6 to 6
- qkv_weight: bfloat16 [2048, 2560], P('shard'), may hold values from -0.125 to 0.125
- out_weight: bfloat16 [2048, 2048], P('shard'), may hold values from -0.5 to 0.5
- gate_up_weight: bfloat16 [2048, 11264], P('shard'), may hold values from -0.125 to 0.125
- down_weight: bfloat16 [5632, 2048], P('shard'), may hold values from -0.078125 to 0.078125
- attn_gain: bfloat16 [2048], P('shard'), may hold values from 0.099609375 to 1.8984375
- ffn_gain: bfloat16 [2048], P('shard'), may hold values from 0.099609375 to 1.8984375
Outputs:
- hidden_out: bfloat16 [2, 2048, 2048], P('rep', 'shard')
- grad_hidden: bfloat16 [2, 2048, 2048], P('rep', 'shard')
- grad_qkv_weight: float32 [2048, 2560], P('shard')
- grad_out_weight: float32 [2048, 2048], P('shard')
- grad_gate_up_weight: float32 [2048, 11264], P('shard')
- grad_down_weight: float32 [5632, 2048], P('shard')
- grad_attn_gain: float32 [2048], P('shard')
- grad_ffn_gain: float32 [2048], P('shard')
Inputs may be any that keep to these rules, and one draw needn't show every extreme that they name: `segments`: segment numbers never fall along a sequence; a document holds at most 1024 tokens, and some document holds exactly that many.
All inputs are finite; a program needn't handle non-finite values.
Results may differ from a plain program's by a relative error of at most 0.014.
Values may be sent and summed in bfloat16 or wider, within the bound.
No kernel may reach another device: no remote copies, remote signals or barrier semaphores. Data moves between devices by JAX's collectives and lax.ppermute only.
A program may use at most 448 MiB of HBM per device.

v0:
```python
import math

import jax
import jax.numpy as jnp
from jax import lax
from jax.sharding import PartitionSpec as P

HEADS = 32
KV_HEADS = 4
HEAD_DIM = 64
FF = 5632


EPS = 1e-05


def rms_forward(values, gain):
    factor = lax.rsqrt(jnp.mean(values * values, -1, keepdims=True) + EPS)
    normed = values * factor
    return (factor, normed, (normed * gain).astype(jnp.bfloat16))


def rms_backward(grad_normed, factor, normed, gain):
    gain_grad = jnp.sum(grad_normed * normed, 0)
    scaled = grad_normed * gain
    return (gain_grad, factor * (scaled - normed * jnp.mean(scaled * normed, -1, keepdims=True)))


def rope_tables(positions):
    freqs = jnp.exp(
        jnp.arange(HEAD_DIM // 2, dtype=jnp.float32) * (-2.0 * math.log(10000.0) / HEAD_DIM)
    )
    angles = positions.astype(jnp.float32)[:, None] * freqs[None, :]
    return (jnp.cos(angles)[:, None, :], jnp.sin(angles)[:, None, :])


def rope_apply(values, cosine, sine):
    half = values.shape[-1] // 2
    first = values[..., :half]
    second = values[..., half:]
    return jnp.concatenate([first * cosine - second * sine, second * cosine + first * sine], -1)


def rope_revert(values, cosine, sine):
    half = values.shape[-1] // 2
    first = values[..., :half]
    second = values[..., half:]
    return jnp.concatenate([first * cosine + second * sine, second * cosine - first * sine], -1)


def pair_scores(pair_queries, key_head, allowed):
    scores = jnp.dot(pair_queries, key_head.T, preferred_element_type=jnp.float32) * HEAD_DIM ** (
        -0.5
    )
    return jnp.where(allowed, scores, -jnp.inf)


def pair_forward(pair_queries, key_head, value_head, allowed):
    scores = pair_scores(pair_queries, key_head, allowed)
    top = jnp.max(scores, -1, keepdims=True)
    expon = jnp.exp(scores - top)
    total = jnp.sum(expon, -1, keepdims=True)
    weights_half = (expon / total).astype(jnp.bfloat16)
    attended = jnp.dot(weights_half, value_head, preferred_element_type=jnp.float32).astype(
        jnp.bfloat16
    )
    return (attended, (top + jnp.log(total))[:, 0])


def pair_backward(pair_queries, key_head, value_head, allowed, logsum, attended, grad_att):
    scores = pair_scores(pair_queries, key_head, allowed)
    probs = jnp.where(allowed, jnp.exp(scores - logsum[:, None]), 0.0)
    delta = jnp.sum(grad_att.astype(jnp.float32) * attended.astype(jnp.float32), -1, keepdims=True)
    grad_probs = jnp.dot(grad_att, value_head.T, preferred_element_type=jnp.float32)
    grad_scores = (probs * (grad_probs - delta) * HEAD_DIM ** (-0.5)).astype(jnp.bfloat16)
    grad_query = jnp.dot(grad_scores, key_head, preferred_element_type=jnp.float32)
    grad_key = jnp.dot(grad_scores.T, pair_queries, preferred_element_type=jnp.float32)
    grad_value = jnp.dot(probs.astype(jnp.bfloat16).T, grad_att, preferred_element_type=jnp.float32)
    return (grad_query, grad_key, grad_value)


def on_device(
    hidden_in,
    segments,
    cotangent,
    qkv_weight,
    out_weight,
    gate_up_weight,
    down_weight,
    attn_gain,
    ffn_gain,
):
    tok_rows = hidden_in.shape[1]
    seg_row = segments[0]
    qsize = HEADS * HEAD_DIM
    ksize = KV_HEADS * HEAD_DIM
    pairs = HEADS // 2
    per_group = HEADS // KV_HEADS // 2
    gathered = (
        lax.all_gather(qkv_weight, "shard", axis=0, tiled=True),
        lax.all_gather(out_weight, "shard", axis=0, tiled=True),
        lax.all_gather(gate_up_weight, "shard", axis=0, tiled=True),
        lax.all_gather(down_weight, "shard", axis=0, tiled=True),
        lax.all_gather(attn_gain, "shard", axis=0, tiled=True),
        lax.all_gather(ffn_gain, "shard", axis=0, tiled=True),
    )
    full_qkv, full_out, full_gate_up, full_down = (
        gathered[0],
        gathered[1],
        gathered[2],
        gathered[3],
    )
    gain_one = gathered[4].astype(jnp.float32)
    gain_two = gathered[5].astype(jnp.float32)
    offset = lax.axis_index("shard") * tok_rows
    local_seg = lax.dynamic_slice_in_dim(seg_row, offset, tok_rows)
    starts = jnp.sum((seg_row[None, :] < local_seg[:, None]).astype(jnp.int32), 1)
    query_index = offset + jnp.arange(tok_rows, dtype=jnp.int32)
    cosine, sine = rope_tables(query_index - starts)
    hidden32 = hidden_in[0].astype(jnp.float32)
    factor_one, normed_one, input_one = rms_forward(hidden32, gain_one)
    projections = jnp.dot(input_one, full_qkv, preferred_element_type=jnp.float32)
    queries = rope_apply(
        projections[:, :qsize].reshape(tok_rows, HEADS, HEAD_DIM), cosine, sine
    ).astype(jnp.bfloat16)
    keys = rope_apply(
        projections[:, qsize : qsize + ksize].reshape(tok_rows, KV_HEADS, HEAD_DIM), cosine, sine
    ).astype(jnp.bfloat16)
    values = projections[:, qsize + ksize :].astype(jnp.bfloat16)
    keys_all, values_all = (
        lax.all_gather(keys.reshape(tok_rows, ksize), "shard", axis=0, tiled=True),
        lax.all_gather(values, "shard", axis=0, tiled=True),
    )
    length = keys_all.shape[0]
    key_heads = keys_all.reshape(length, KV_HEADS, HEAD_DIM).transpose(1, 0, 2)
    value_heads = values_all.reshape(length, KV_HEADS, HEAD_DIM).transpose(1, 0, 2)
    key_index = jnp.arange(length, dtype=jnp.int32)
    pair_index_rows = jnp.concatenate([query_index, query_index])
    pair_seg_rows = jnp.concatenate([local_seg, local_seg])
    allowed = (key_index[None, :] <= pair_index_rows[:, None]) & (
        seg_row[None, :] == pair_seg_rows[:, None]
    )
    query_pairs = (
        queries.reshape(tok_rows, pairs, 2, HEAD_DIM)
        .transpose(1, 2, 0, 3)
        .reshape(pairs, 2 * tok_rows, HEAD_DIM)
    )
    pair_ids = jnp.arange(pairs, dtype=jnp.int32)

    def forward_pair(carry, item):
        pair_queries, pair_number = item
        group = pair_number // per_group
        out, logsum = pair_forward(pair_queries, key_heads[group], value_heads[group], allowed)
        return (carry, (out, logsum))

    _, (pair_out, pair_logsum) = lax.scan(forward_pair, None, (query_pairs, pair_ids))
    attended = (
        pair_out.reshape(pairs, 2, tok_rows, HEAD_DIM)
        .transpose(2, 0, 1, 3)
        .reshape(tok_rows, qsize)
    )
    residual = hidden32 + jnp.dot(attended, full_out, preferred_element_type=jnp.float32)
    factor_two, normed_two, input_two = rms_forward(residual, gain_two)
    gate_up = jnp.dot(input_two, full_gate_up, preferred_element_type=jnp.float32)
    gate = gate_up[:, :FF]
    upward = gate_up[:, FF:]
    sigma = jax.nn.sigmoid(gate)
    activation = (gate * sigma * upward).astype(jnp.bfloat16)
    hidden_out = (
        residual + jnp.dot(activation, full_down, preferred_element_type=jnp.float32)
    ).astype(jnp.bfloat16)
    back_qkv, back_out, back_gate_up, back_down = (
        lax.all_gather(qkv_weight, "shard", axis=0, tiled=True),
        lax.all_gather(out_weight, "shard", axis=0, tiled=True),
        lax.all_gather(gate_up_weight, "shard", axis=0, tiled=True),
        lax.all_gather(down_weight, "shard", axis=0, tiled=True),
    )
    cot_half = cotangent[0]
    grad_activation = jnp.dot(cot_half, back_down.T, preferred_element_type=jnp.float32)
    grad_gate = grad_activation * upward * (sigma * (1.0 + gate * (1.0 - sigma)))
    grad_up = grad_activation * gate * sigma
    grad_gate_up = jnp.concatenate([grad_gate, grad_up], -1).astype(jnp.bfloat16)
    gate_up_term = jnp.dot(input_two.T, grad_gate_up, preferred_element_type=jnp.float32)
    grad_input_two = jnp.dot(grad_gate_up, back_gate_up.T, preferred_element_type=jnp.float32)
    gain_two_term, grad_back_two = rms_backward(grad_input_two, factor_two, normed_two, gain_two)
    grad_residual = cot_half.astype(jnp.float32) + grad_back_two
    down_term = jnp.dot(activation.T, cot_half, preferred_element_type=jnp.float32)
    ffn_parts = (
        lax.psum_scatter(gate_up_term, "shard", scatter_dimension=0, tiled=True),
        lax.psum_scatter(down_term, "shard", scatter_dimension=0, tiled=True),
        lax.psum_scatter(gain_two_term, "shard", scatter_dimension=0, tiled=True),
    )
    ffn_parts = lax.psum((ffn_parts[0], ffn_parts[1], ffn_parts[2]), "rep")
    residual_half = grad_residual.astype(jnp.bfloat16)
    out_term = jnp.dot(attended.T, residual_half, preferred_element_type=jnp.float32)
    grad_attended = jnp.dot(residual_half, back_out.T, preferred_element_type=jnp.float32).astype(
        jnp.bfloat16
    )
    grad_pairs = (
        grad_attended.reshape(tok_rows, pairs, 2, HEAD_DIM)
        .transpose(1, 2, 0, 3)
        .reshape(pairs, 2 * tok_rows, HEAD_DIM)
    )

    def backward_pair(carry, item):
        pair_queries, pair_grad, pair_att, pair_log, pair_number = item
        group = pair_number // per_group
        grad_query, grad_key, grad_value = pair_backward(
            pair_queries,
            key_heads[group],
            value_heads[group],
            allowed,
            pair_log,
            pair_att,
            pair_grad,
        )
        key_acc = carry[0].at[:, group].add(grad_key)
        value_acc = carry[1].at[:, group].add(grad_value)
        return ((key_acc, value_acc), grad_query)

    zero_acc = jnp.zeros((length, KV_HEADS, HEAD_DIM), jnp.float32)
    (key_sums, value_sums), query_grads = lax.scan(
        backward_pair,
        (zero_acc, zero_acc),
        (query_pairs, grad_pairs, pair_out, pair_logsum, pair_ids),
    )
    key_local, value_local = (
        lax.psum_scatter(key_sums.reshape(length, ksize), "shard", scatter_dimension=0, tiled=True),
        lax.psum_scatter(
            value_sums.reshape(length, ksize), "shard", scatter_dimension=0, tiled=True
        ),
    )
    grad_queries = (
        query_grads.reshape(pairs, 2, tok_rows, HEAD_DIM)
        .transpose(2, 0, 1, 3)
        .reshape(tok_rows, HEADS, HEAD_DIM)
    )
    grad_queries = rope_revert(grad_queries, cosine, sine).reshape(tok_rows, qsize)
    grad_keys = rope_revert(key_local.reshape(tok_rows, KV_HEADS, HEAD_DIM), cosine, sine).reshape(
        tok_rows, ksize
    )
    grad_projections = jnp.concatenate([grad_queries, grad_keys, value_local], -1).astype(
        jnp.bfloat16
    )
    qkv_term = jnp.dot(input_one.T, grad_projections, preferred_element_type=jnp.float32)
    grad_input_one = jnp.dot(grad_projections, back_qkv.T, preferred_element_type=jnp.float32)
    gain_one_term, grad_back_one = rms_backward(grad_input_one, factor_one, normed_one, gain_one)
    grad_hidden = (grad_residual + grad_back_one).astype(jnp.bfloat16)
    attn_parts = (
        lax.psum_scatter(qkv_term, "shard", scatter_dimension=0, tiled=True),
        lax.psum_scatter(out_term, "shard", scatter_dimension=0, tiled=True),
        lax.psum_scatter(gain_one_term, "shard", scatter_dimension=0, tiled=True),
    )
    attn_parts = lax.psum((attn_parts[0], attn_parts[1], attn_parts[2]), "rep")
    return (
        hidden_out[None],
        grad_hidden[None],
        attn_parts[0],
        attn_parts[1],
        ffn_parts[0],
        ffn_parts[1],
        attn_parts[2],
        ffn_parts[2],
    )


def solution(mesh):
    return jax.shard_map(
        on_device,
        mesh=mesh,
        in_specs=(
            P("rep", "shard", None),
            P("rep", None),
            P("rep", "shard", None),
            P("shard", None),
            P("shard", None),
            P("shard", None),
            P("shard", None),
            P("shard"),
            P("shard"),
        ),
        out_specs=(
            P("rep", "shard", None),
            P("rep", "shard", None),
            P("shard", None),
            P("shard", None),
            P("shard", None),
            P("shard", None),
            P("shard"),
            P("shard"),
        ),
        check_vma=False,
    )
```

profile of v0, /device:TPU:0, one launch (start us, length us, event | category | flops | bytes accessed | tf_op | source)
XLA Modules:
  0.0 3018.2 jit_solution(15382327820212648054)
XLA Ops:
  8.0 23.3 all-gather
  34.3 66.6 %all-gather.9.cloned.1.call-done = bf16[2048,2560]{1,0:T(8,128)(2,1)} async-done(((bf16[128,2560]{1,0:T(8,128)(2,1)}), bf16[2048,2560]{1,0:T(8,128)(2,1)}) %all-gather.9.cloned.1.call-update) | async-done | bytes 10485776 | tf_op jit(solution)/shard_map/all_gather | solution.py:100
  100.9 5.7 fusion.80
  110.0 19.1 all-gather.1
  131.1 11.5 all-gather.11.cloned.1.call-done
  145.3 37.5 %all-gather.13.cloned.1.call-done = bf16[2048,256]{1,0:T(8,128)(2,1)} async-done(((bf16[128,256]{1,0:T(8,128)(2,1)}), bf16[2048,256]{1,0:T(8,128)(2,1)}) %all-gather.13.cloned.1.call-update) | async-done | bytes 1048592 | tf_op jit(solution)/shard_map/all_gather | solution.py:132
  186.1 135.7 %while.34 = (s32[]{:T(128)}, bf16[16,256,64]{1,2,0:T(8,128)(2,1)S(1)}, f32[16,256]{1,0:T(8,128)}, bf16[16,256,64]{2,1,0:T(8,128)(2,1)}, s32[16]{0:T(128)S(1)}, /...) while((s32[]{:T(128)}, ...), condition=%wide.region_5.6_spmd.clone, body=%wide.region_2.5_spmd.clone.sunk | while | flops 140001040 | bytes 7459189 | solution.py:156
  323.3 4.9 multiply_reduce_fusion.2
  328.2 157.6 %all-gather.17.cloned.1.call-done = bf16[2048,11264]{1,0:T(8,128)(2,1)} async-done(((bf16[128,11264]{1,0:T(8,128)(2,1)}), bf16[2048,11264]{1,0:T(8,128)(2,1)}) %all-gather.17.cloned.1.call-update) | async-done | bytes 46137360 | tf_op jit(solution)/shard_map/all_gather | solution.py:102
  485.8 21.1 fusion.86
  506.9 99.0 %all-gather.19.cloned.1.call-done = bf16[5632,2048]{1,0:T(8,128)(2,1)} async-done(((bf16[352,2048]{1,0:T(8,128)(2,1)}), bf16[5632,2048]{1,0:T(8,128)(2,1)}) %all-gather.19.cloned.1.call-update) | async-done | bytes 23068688 | tf_op jit(solution)/shard_map/all_gather | solution.py:103
  606.0 14.6 multiply_convert_fusion.1
  620.6 22.3 multiply_reduce_fusion
  645.9 6.3 convolution_convert_fusion.1
  657.0 286.7 %while.35 = (s32[]{:T(128)}, f32[2048,4,64]{0,2,1:T(8,128)}, f32[2048,4,64]{0,2,1:T(8,128)}, f32[16,256,64]{1,2,0:T(8,128)}, s32[16]{0:T(128)S(1)}, /*index=5*/b...) while((s32[]{:T(128)}, f32[2048,4,64]{0,2,1:T(8,128)}, ...), condition=%wide.region_11.12_spmd.clone, body=%wide.region_8.11_spmd.clone.sunk | while | flops 342425376 | bytes 13650886 | solution.py:222
  667.0 2.9 fusion.140
  669.9 2.9 fusion.141
  687.9 2.9 fusion.141
  705.8 2.9 fusion.141
  720.8 2.9 fusion.140
  723.7 2.9 fusion.141
  756.6 2.9 fusion.140
  813.2 2.9 fusion.141
  828.2 2.9 fusion.140
  831.1 2.9 fusion.141
  846.1 2.9 fusion.140
  849.0 2.9 fusion.141
  866.9 2.9 fusion.141
  884.8 2.9 fusion.141
  902.8 2.9 fusion.141
  920.7 2.9 fusion.141
  938.6 2.9 fusion.141
  945.0 8.3 fusion.76
  955.0 50.4 %reduce-scatter.9.cloned.1.call-done = f32[128,256]{0,1:T(8,128)} async-done(((f32[2048,256]{0,1:T(8,128)}), f32[128,256]{0,1:T(8,128)}) %reduce-scatter.9.cloned.1.call-update) | async-done | bytes 131088 | tf_op jit(solution)/shard_map/reduce_scatter | solution.py:229
  1006.3 64.4 %reduce-scatter.7.cloned.1.call-done = f32[128,256]{0,1:T(8,128)} async-done(((f32[2048,256]{0,1:T(8,128)}), f32[128,256]{0,1:T(8,128)}) %reduce-scatter.7.cloned.1.call-update) | async-done | bytes 131088 | tf_op jit(solution)/shard_map/reduce_scatter | solution.py:228
  1071.7 11.2 fusion.74
  1084.0 23.9 fusion.70
  1108.6 34.3 %fusion.55 = f32[2048,11264]{1,0:T(8,128)} fusion(bf16[128,5632]{1,0:T(8,128)(2,1)} %get-tuple-element.523, bf16[128,5632]{1,0:T(8,128)(2,1)} %copy-done.6, f32[128,2048]{1,0:T(8,128)S(1)} %get-tuple-element.536, f32[2048]{0:T(1024)S(1)} %bitcast.204, f32[128]{0:T(128)S(1)} %copy-done.20), kind=kOutput, calls=%fused_computation.77 | convolution fusion | flops 5912133632 | bytes 96215552 | tf_op jit(solution)/shard_map/dot_general | solution.py:183
  1143.3 109.2 %reduce-scatter.13.cloned.1.call-done = f32[128,2048]{1,0:T(8,128)} async-done(((f32[2048,2048]{1,0:T(8,128)}), f32[128,2048]{1,0:T(8,128)}) %reduce-scatter.13.cloned.1.call-update) | async-done | bytes 1048592 | tf_op jit(solution)/shard_map/reduce_scatter | solution.py:251
  1252.4 213.9 %reduce-scatter.11.cloned.1.call-done = f32[128,2560]{1,0:T(8,128)} async-done(((f32[2048,2560]{1,0:T(8,128)}), f32[128,2560]{1,0:T(8,128)}) %reduce-scatter.11.cloned.1.call-update) | async-done | bytes 1310736 | tf_op jit(solution)/shard_map/reduce_scatter | solution.py:250
  1466.3 435.9 %reduce-scatter.17.cloned.1.call-done = f32[352,2048]{1,0:T(8,128)} async-done(((f32[5632,2048]{1,0:T(8,128)}), f32[352,2048]{1,0:T(8,128)}) %reduce-scatter.17.cloned.1.call-update) | async-done | bytes 2883600 | tf_op jit(solution)/shard_map/reduce_scatter | solution.py:190
  1902.2 840.0 %reduce-scatter.15.cloned.1.call-done = f32[128,11264]{1,0:T(8,128)} async-done(((f32[2048,11264]{1,0:T(8,128)}), f32[128,11264]{1,0:T(8,128)}) %reduce-scatter.15.cloned.1.call-update) | async-done | bytes 5767184 | tf_op jit(solution)/shard_map/reduce_scatter | solution.py:189
  2744.1 13.2 fusion.54
  2757.3 7.7 fusion.67
  2765.0 58.5 %all-reduce.2 = (f32[2048]{0:T(1024)S(1)}, f32[2048]{0:T(1024)S(1)}) all-reduce(f32[2048]{0:T(1024)S(1)} %get-tuple-element.462, f32[2048]{0:T(1024)S(1)} %copy-done.21), channel_id=8, replica_groups=mesh['rep'=2,'shard'=16] {'shard'}, use_global_device_ids=true, to_apply=%region_24.25.clone | all-reduce | flops 4096 | bytes 32768
  2823.7 5.5 all-reduce.3
  2830.4 170.0 %all-reduce.7.cloned.1.call-done = (f32[128,2560]{1,0:T(8,128)}, f32[128,2048]{1,0:T(8,128)}, f32[128,11264]{1,0:T(8,128)}, f32[352,2048]{1,0:T(8,128)}) async-done(((f32[128,2560]{1,0:T(8,128)}, f32[128,2048]{1,0:T(8,128)}, f32[128,11264]{1,0:T(8,128)}, f32[352,2048]{1,0:T(8,128)}), (f32[128,2560]{1,0:T(8,128)}, f32[128,2048]{1,0:T(8,128)}, f32[128,11264]{1,0:T(8,128)}, ...) | async-done | bytes 11010064 | tf_op jit(solution)/shard_map/psum | solution.py:254
  3003.9 5.9 copy.117
  (400 shorter events, 327.4 us)
Async XLA Ops:
  7.2 93.7 %all-gather.9.cloned.1.call-start = ((), (), s32[]{:S(2)}) async-start(), calls=%async_computation.6 | async-start | bytes 11141120 | tf_op jit(solution)/shard_map/all_gather | solution.py:100
  7.9 134.7 %all-gather.11.cloned.1.call-start = ((), (), s32[]{:S(2)}) async-start(), calls=%async_computation.7 | async-start | bytes 1114112 | tf_op jit(solution)/shard_map/all_gather | solution.py:131
  34.1 72.5 %copy-start.23 = (f32[128]{0:T(128)}, f32[128]{0:T(128)S(1)}, u32[]{:S(2)}) copy-start(f32[128]{0:T(128)S(1)} %add_rsqrt_fusion.1) | copy-start | bytes 1540
  34.3 95.3 %copy-start.15 = (f32[128,32]{0,1:T(8,128)}, f32[128,32]{0,1:T(8,128)S(1)}, u32[]{:S(2)}) copy-start(f32[128,32]{0,1:T(8,128)S(1)} %get-tuple-element.533) | copy-start | bytes 49156
  34.3 95.3 %copy-start.17 = (f32[128,32]{0,1:T(8,128)}, f32[128,32]{0,1:T(8,128)S(1)}, u32[]{:S(2)}) copy-start(f32[128,32]{0,1:T(8,128)S(1)} %get-tuple-element.534) | copy-start | bytes 49156
  107.5 75.3 %all-gather.13.cloned.1.call-start = ((), (), s32[]{:S(2)}) async-start(), calls=%async_computation.8 | async-start | bytes 1114112 | tf_op jit(solution)/shard_map/all_gather | solution.py:132
  108.2 213.9 %all-gather.15.cloned.1.call-start = ((), (), s32[]{:S(2)}) async-start(), calls=%async_computation.9 | async-start | bytes 8912896 | tf_op jit(solution)/shard_map/all_gather | solution.py:101
  108.8 1.3 copy-start.31
  108.8 377.0 %all-gather.17.cloned.1.call-start = ((), (), s32[]{:S(2)}) async-start(), calls=%async_computation.10 | async-start | bytes 49020928 | tf_op jit(solution)/shard_map/all_gather | solution.py:102
  109.4 496.6 %all-gather.19.cloned.1.call-start = ((), (), s32[]{:S(2)}) async-start(), calls=%async_computation.11 | async-start | bytes 24510464 | tf_op jit(solution)/shard_map/all_gather | solution.py:103
  110.0 895.4 %reduce-scatter.9.cloned.1.call-start = ((), (), s32[]{:S(2)}) async-start(), calls=%async_computation.13 | async-start | bytes 2228224 | tf_op jit(solution)/shard_map/reduce_scatter | solution.py:229
  184.3 1.8 copy-start.25
  321.8 6.3 copy-start.14
  321.8 6.4 copy-start.27
  321.8 6.4 copy-start.29
  321.8 1.5 copy-start.2
  322.1 6.1 copy-start.4
  328.2 178.7 %copy-start.19 = (f32[128]{0:T(128)}, f32[128]{0:T(128)S(1)}, u32[]{:S(2)}) copy-start(f32[128]{0:T(128)S(1)} %add_rsqrt_fusion) | copy-start | bytes 1540
  485.8 120.2 %copy-start.8 = (bf16[1,128,2048]{2,1,0:T(8,128)(2,1)S(1)}, bf16[1,128,2048]{2,1,0:T(8,128)(2,1)}, u32[]{:S(2)}) copy-start(bf16[1,128,2048]{2,1,0:T(8,128)(2,1)} %param.19) | copy-start | bytes 1572868
  620.6 22.3 copy-start.6
  644.9 1.0 copy-start
  653.8 3.2 copy-start.22
  653.8 3.2 copy-start.26
  653.8 3.2 copy-start.28
  653.9 3.2 copy-start.30
  943.7 1.2 copy-start.1
  943.7 1.4 copy-start.5
  943.7 127.0 %reduce-scatter.7.cloned.1.call-start = ((), (), s32[]{:S(2)}) async-start(), calls=%async_computation.12 | async-start | bytes 2228224 | tf_op jit(solution)/shard_map/reduce_scatter | solution.py:228
  944.5 308.0 %reduce-scatter.13.cloned.1.call-start = ((), (), s32[]{:S(2)}) async-start(), calls=%async_computation.15 | async-start | bytes 17825792 | tf_op jit(solution)/shard_map/reduce_scatter | solution.py:251
  953.3 1.3 copy-start.12
  953.4 1.4 copy-start.16
  953.4 1.4 copy-start.18
  953.4 512.9 %reduce-scatter.11.cloned.1.call-start = ((), (), s32[]{:S(2)}) async-start(), calls=%async_computation.14 | async-start | bytes 22282240 | tf_op jit(solution)/shard_map/reduce_scatter | solution.py:250
  954.7 116.9 %copy-start.3 = (bf16[1,128,2048]{2,1,0:T(8,128)(2,1)S(1)}, bf16[1,128,2048]{2,1,0:T(8,128)(2,1)}, u32[]{:S(2)}) copy-start(bf16[1,128,2048]{2,1,0:T(8,128)(2,1)} %param.17) | copy-start | bytes 1572868
  955.0 127.9 %copy-start.10 = (bf16[128,32,64]{0,2,1:T(8,128)(2,1)}, bf16[128,32,64]{0,2,1:T(8,128)(2,1)S(1)}, u32[]{:S(2)}) copy-start(bf16[128,32,64]{0,2,1:T(8,128)(2,1)S(1)} %pad_maximum_fusion.4) | copy-start | bytes 1572868
  1082.8 1.2 copy-start.9
  1082.9 819.4 %reduce-scatter.17.cloned.1.call-start = ((), (), s32[]{:S(2)}) async-start(), calls=%async_computation.17 | async-start | bytes 49020928 | tf_op jit(solution)/shard_map/reduce_scatter | solution.py:190
  1108.0 0.7 copy-start.20
  1108.0 1634.2 %reduce-scatter.15.cloned.1.call-start = ((), (), s32[]{:S(2)}) async-start(), calls=%async_computation.16 | async-start | bytes 98041856 | tf_op jit(solution)/shard_map/reduce_scatter | solution.py:189
  1143.0 1857.4 %all-reduce.7.cloned.1.call-start = ((), (), s32[]{:S(2)}) async-start(), calls=%async_computation.18 | async-start | bytes 22020096 | tf_op jit(solution)/shard_map/psum | solution.py:254
  2742.2 0.7 copy-start.32
  2744.1 13.2 copy-start.11
  2744.1 13.2 copy-start.24
  2757.3 7.7 copy-start.21
  3000.4 2.6 copy-start.13
  3003.9 5.9 copy-start.7
Sparse Core Ops, SparseCore 0:
  10.3 90.5 all-gather.8
  107.6 34.9 all-gather.10
  145.3 37.4 all-gather.12
  184.8 73.8 all-gather.14
  260.1 225.6 all-gather.16
  487.2 118.6 all-gather.18
  943.8 61.5 reduce-scatter.8
  1010.2 60.5 reduce-scatter.6
  1074.9 177.5 reduce-scatter.12
  1256.4 209.8 reduce-scatter.10
  1470.6 431.6 reduce-scatter.16
  1906.3 835.8 reduce-scatter.14
  2745.0 255.3 all-reduce.6
where the time goes:
time: 3030 us; the launch traced here: 3020 us
  waiting for transfers between devices  2260 us (75%)
  matrix products  412 us (14%)
  blocking collectives  106 us (3%)
  local copies, waits for them, and re-layouts  97.3 us (3%)
  loops' own time  84.2 us (3%)
  other arithmetic  43.3 us (1%)
    reduce_scatter x1, waiting for transfers between devices, on_device(): lax.psum_scatter(gate_up_term, 'shard', scatter_dimension=0, tiled=True)  840 us
    reduce_scatter x1, waiting for transfers between devices, on_device(): lax.psum_scatter(down_term, 'shard', scatter_dimension=0, tiled=True)  436 us
    reduce_scatter x1, waiting for transfers between devices, on_device(): lax.psum_scatter(qkv_term, 'shard', scatter_dimension=0, tiled=True)  214 us
    psum x1, waiting for transfers between devices, on_device(): attn_parts = lax.psum((attn_parts[0], attn_parts[1], attn_parts[2]), 'rep')  170 us
    all_gather x1, waiting for transfers between devices, on_device(): lax.all_gather(gate_up_weight, 'shard', axis=0, tiled=True)  158 us
    reduce_scatter x1, waiting for transfers between devices, on_device(): lax.psum_scatter(out_term, 'shard', scatter_dimension=0, tiled=True)  109 us
    all_gather x1, waiting for transfers between devices, on_device(): lax.all_gather(down_weight, 'shard', axis=0, tiled=True)  99 us
    all_gather x1, waiting for transfers between devices, on_device(): lax.all_gather(qkv_weight, 'shard', axis=0, tiled=True)  66.6 us
  transfers between devices with their start and end apart: 13, of which 12 were waited for; matrix products, arithmetic and copies ran while one was open for 8% of the time, Pallas kernels for 0%

commit v1 on v0

v1 whole, which is shorter than its diff:
```python
import math

import jax
import jax.numpy as jnp
from jax import lax
from jax.experimental import pallas as pl
from jax.experimental.pallas import tpu as pltpu
from jax.sharding import PartitionSpec as P

HEADS = 32
KV_HEADS = 4
HEAD_DIM = 64
REACH = 1024
EPS = 1e-05
F32 = jnp.float32
BF16 = jnp.bfloat16
LANES = 128
SCALE = HEAD_DIM**-0.5


def dot(a, b, dims=((1,), (0,))):
    return lax.dot_general(a, b, (dims, ((), ())), preferred_element_type=F32)


def after(value, *others):
    return lax.optimization_barrier((value, *others))[0]


def pick(flag, one, other):
    return jnp.where(flag == 0, one, other)


class Ring:
    def __init__(self, size):
        self.size = size
        self.chips = size // 2
        rows = self.chips // 2
        self.order = [2 * i for i in range(rows)] + [2 * i + 1 for i in reversed(range(rows))]
        self.place = {chip: at for at, chip in enumerate(self.order)}
        self.half = self.chips // 2

        def turned(step):
            return [
                (s, self.order[(self.place[s // 2] + step) % self.chips] * 2 + s % 2)
                for s in range(size)
            ]

        self.ahead = turned(1)
        self.back = turned(-1)
        self.sibling = [(s, s ^ 1) for s in range(size)]
        self.core_groups = [list(range(core, size, 2)) for core in range(2)]
        self.index = lax.axis_index("shard")
        self.core = self.index % 2
        self.at = jnp.asarray([self.place[i] for i in range(self.chips)], jnp.int32)[
            self.index // 2
        ]

    def swap(self, value):
        return lax.ppermute(value, "shard", self.sibling)

    def gather(self, block):
        n, h = self.chips, block.shape[0] // 2
        found = [None] * n
        found[0] = cw = ccw = block
        for k in range(1, self.half):
            cw = lax.ppermute(cw, "shard", self.ahead)
            found[n - k] = cw
            ccw = lax.ppermute(ccw, "shard", self.back)
            found[k] = ccw
        top = lax.ppermute(cw[:h], "shard", self.ahead)
        low = lax.ppermute(ccw[h:], "shard", self.back)
        found[self.half] = jnp.concatenate([top, low], 0)
        return found

    def gather_both(self, block):
        own = self.gather(block)
        return own, [self.swap(b) for b in own]

    def scatter(self, parts):
        n, m = self.chips, self.half
        h = parts[0].shape[0] // 2
        cw = lax.ppermute(parts[m][:h].astype(BF16), "shard", self.ahead).astype(F32)
        ccw = lax.ppermute(parts[m][h:].astype(BF16), "shard", self.back).astype(F32)
        for k in range(m - 1, 0, -1):
            ahead, back = parts[k].astype(F32), parts[n - k].astype(F32)
            if k == m - 1:
                ahead = jnp.concatenate([ahead[:h] + cw, ahead[h:]], 0)
                back = jnp.concatenate([back[:h], back[h:] + ccw], 0)
            else:
                ahead, back = ahead + cw, back + ccw
            cw = lax.ppermute(ahead.astype(BF16), "shard", self.ahead).astype(F32)
            ccw = lax.ppermute(back.astype(BF16), "shard", self.back).astype(F32)
        return parts[0].astype(F32) + cw + ccw

    def split_cores(self, value, axis):
        shape = value.shape
        width = shape[axis] // self.size
        cut = value.reshape(shape[:axis] + (self.chips, 2, width) + shape[axis + 1 :])
        zero = lax.index_in_dim(cut, 0, axis + 1, False)
        one = lax.index_in_dim(cut, 1, axis + 1, False)
        flat = shape[:axis] + (self.chips * width,) + shape[axis + 1 :]
        return (
            pick(self.core, zero, one).reshape(flat),
            pick(self.core, one, zero).reshape(flat),
        )

    def join_cores(self, own, other, axis):
        shape = own.shape
        width = shape[axis] // self.chips
        cut = shape[:axis] + (self.chips, width) + shape[axis + 1 :]
        own, other = own.reshape(cut), other.reshape(cut)
        joined = jnp.stack([pick(self.core, own, other), pick(self.core, other, own)], axis + 1)
        return joined.reshape(shape[:axis] + (2 * shape[axis],) + shape[axis + 1 :])

    def to_ring(self, value, axis):
        width = value.shape[axis] // self.chips
        pieces = [
            lax.slice_in_dim(value, i * width, (i + 1) * width, axis=axis) for i in self.order
        ]
        double = jnp.concatenate(pieces + pieces[:-1], axis)
        return lax.dynamic_slice_in_dim(double, self.at * width, self.chips * width, axis)

    def from_ring(self, value, axis):
        width = value.shape[axis] // self.chips
        double = jnp.concatenate([value, value], axis)
        start = (self.chips - self.at) * width
        turned = lax.dynamic_slice_in_dim(double, start, self.chips * width, axis)
        pieces = [
            lax.slice_in_dim(turned, self.place[i] * width, (self.place[i] + 1) * width, axis=axis)
            for i in range(self.chips)
        ]
        return jnp.concatenate(pieces, axis)


def lane_low(shape):
    return lax.broadcasted_iota(jnp.int32, shape, len(shape) - 1) % LANES < HEAD_DIM


def rotated(values):
    quarter = HEAD_DIM // 2
    first = lax.broadcasted_iota(jnp.int32, values.shape, 1) % HEAD_DIM < quarter
    return jnp.where(
        first, -pltpu.roll(values, LANES - quarter, 1), pltpu.roll(values, quarter, 1)
    )


def kv_prepare_kernel(proj_ref, cos_ref, sin_ref, out_ref):
    for pair in range(KV_HEADS // 2):
        keys = proj_ref[:, pair * LANES : (pair + 1) * LANES]
        keys = keys * cos_ref[...] + rotated(keys) * sin_ref[...]
        at = KV_HEADS // 2 + pair
        values = proj_ref[:, at * LANES : (at + 1) * LANES]
        low = lane_low(keys.shape)
        one = jnp.where(low, keys, pltpu.roll(values, HEAD_DIM, 1))
        two = jnp.where(low, pltpu.roll(keys, HEAD_DIM, 1), values)
        out_ref[:, 2 * pair * LANES : (2 * pair + 1) * LANES] = one.astype(BF16)
        out_ref[:, (2 * pair + 1) * LANES : (2 * pair + 2) * LANES] = two.astype(BF16)


def kv_finish_kernel(grad_ref, cos_ref, sin_ref, out_ref):
    for pair in range(KV_HEADS // 2):
        one = grad_ref[:, 2 * pair * LANES : (2 * pair + 1) * LANES]
        two = grad_ref[:, (2 * pair + 1) * LANES : (2 * pair + 2) * LANES]
        low = lane_low(one.shape)
        keys = jnp.where(low, one, pltpu.roll(two, HEAD_DIM, 1))
        values = jnp.where(low, pltpu.roll(one, HEAD_DIM, 1), two)
        keys = keys * cos_ref[...] - rotated(keys) * sin_ref[...]
        at = KV_HEADS // 2 + pair
        out_ref[:, pair * LANES : (pair + 1) * LANES] = keys.astype(BF16)
        out_ref[:, at * LANES : (at + 1) * LANES] = values.astype(BF16)


def load_window(places_ref, kv_ref, window, rows):
    for b in range(window.shape[0] // rows):
        window[b * rows : (b + 1) * rows, :] = kv_ref[places_ref[b]]


def allowed_pairs(first_ref, reach, keys, rows):
    key = lax.broadcasted_iota(jnp.int32, (keys, rows), 0)
    token = lax.broadcasted_iota(jnp.int32, (keys, rows), 1)
    allowed = (key >= first_ref[...]) & (key <= token + reach)
    return jnp.concatenate([allowed, allowed], 1)


def stacked(block, low_side):
    turned = pltpu.roll(block, HEAD_DIM, 1)
    low = lane_low(block.shape)
    if low_side:
        one, two = jnp.where(low, block, 0.0), jnp.where(low, turned, 0.0)
    else:
        one, two = jnp.where(low, 0.0, turned), jnp.where(low, 0.0, block)
    return jnp.concatenate([one, two], 0).astype(BF16)


def attend_kernel(
    places_ref, proj_ref, kv_ref, first_ref, cos_ref, sin_ref, q_ref, out_ref, log_ref, window
):
    rows = proj_ref.shape[0]
    keys = window.shape[0]

    @pl.when(pl.program_id(1) == 0)
    def _():
        load_window(places_ref, kv_ref, window, rows)

    block = proj_ref[...]
    block = block * cos_ref[...] + rotated(block) * sin_ref[...]
    q_ref[...] = block.astype(BF16)
    queries = stacked(block, True)
    score = dot(window[...], queries, ((1,), (1,))) * SCALE
    allowed = allowed_pairs(first_ref, keys - rows, keys, rows)
    score = jnp.where(allowed, score, -jnp.inf)
    top = jnp.max(score, 0, keepdims=True)
    expon = jnp.exp(score - top)
    total = jnp.sum(expon, 0, keepdims=True)
    log_ref[0] = top + jnp.log(total)
    probs = (expon * (1.0 / total)).astype(BF16)
    out = dot(probs, window[...], ((0,), (0,)))
    one, two = out[:rows], out[rows:]
    out_ref[...] = jnp.where(lane_low(one.shape), pltpu.roll(one, HEAD_DIM, 1), two).astype(BF16)


def attend_back_kernel(
    places_ref,
    q_ref,
    grad_ref,
    att_ref,
    log_ref,
    kv_ref,
    first_ref,
    cos_ref,
    sin_ref,
    gq_ref,
    gkv_ref,
    window,
    total,
):
    rows = q_ref.shape[0]
    keys = window.shape[0]
    step = pl.program_id(1)

    @pl.when(step == 0)
    def _():
        load_window(places_ref, kv_ref, window, rows)
        total[...] = jnp.zeros_like(total)

    grad = grad_ref[...].astype(F32)
    queries = stacked(q_ref[...].astype(F32), True)
    grads = stacked(grad, False)
    product = jnp.transpose(grad * att_ref[...].astype(F32))
    delta = jnp.concatenate(
        [
            jnp.sum(product[:HEAD_DIM], 0, keepdims=True),
            jnp.sum(product[HEAD_DIM:], 0, keepdims=True),
        ],
        1,
    )
    score = dot(window[...], queries, ((1,), (1,))) * SCALE
    allowed = allowed_pairs(first_ref, keys - rows, keys, rows)
    probs = jnp.where(allowed, jnp.exp(score - log_ref[0]), 0.0)
    grad_probs = dot(window[...], grads, ((1,), (1,)))
    grad_scores = (probs * (grad_probs - delta) * SCALE).astype(BF16)
    total[...] += dot(grad_scores, queries) + dot(probs.astype(BF16), grads)
    grad_queries = dot(grad_scores, window[...], ((0,), (0,)))
    one, two = grad_queries[:rows], grad_queries[rows:]
    block = jnp.where(lane_low(one.shape), one, pltpu.roll(two, HEAD_DIM, 1))
    gq_ref[...] = (block * cos_ref[...] - rotated(block) * sin_ref[...]).astype(BF16)

    @pl.when(step == pl.num_programs(1) - 1)
    def _():
        gkv_ref[...] = jnp.zeros_like(gkv_ref)
        for b in range(keys // rows):
            gkv_ref[places_ref[b]] = total[b * rows : (b + 1) * rows, :]


def whole(shape):
    return pl.BlockSpec(shape, lambda *_: (0,) * len(shape))


def small_kernel(kernel, width, dtype, *args):
    rows = args[0].shape[0]
    return pl.pallas_call(kernel, out_shape=jax.ShapeDtypeStruct((rows, width), dtype))(*args)


def attend(places, proj, kv, first, cosine, sine):
    rows = proj.shape[0]
    keys = places.shape[0] * rows
    inner = HEADS // KV_HEADS // 2
    pairs = HEADS // 2
    pair_spec = pl.BlockSpec((rows, LANES), lambda g, i, _: (0, g * inner + i))
    return pl.pallas_call(
        attend_kernel,
        grid_spec=pltpu.PrefetchScalarGridSpec(
            num_scalar_prefetch=1,
            grid=(KV_HEADS, inner),
            in_specs=[
                pair_spec,
                pl.BlockSpec((kv.shape[0], rows, LANES), lambda g, i, _: (0, 0, g)),
                whole((1, rows)),
                whole((rows, LANES)),
                whole((rows, LANES)),
            ],
            out_specs=[
                pair_spec,
                pair_spec,
                pl.BlockSpec((1, 1, 2 * rows), lambda g, i, _: (g * inner + i, 0, 0)),
            ],
            scratch_shapes=[pltpu.VMEM((keys, LANES), BF16)],
        ),
        out_shape=[
            jax.ShapeDtypeStruct((rows, pairs * LANES), BF16),
            jax.ShapeDtypeStruct((rows, pairs * LANES), BF16),
            jax.ShapeDtypeStruct((pairs, 1, 2 * rows), F32),
        ],
        compiler_params=pltpu.CompilerParams(vmem_limit_bytes=32 * 1024 * 1024),
    )(places, proj, kv, first, cosine, sine)


def attend_back(places, queries, grad, attended, logs, kv, first, cosine, sine):
    rows = queries.shape[0]
    keys = places.shape[0] * rows
    inner = HEADS // KV_HEADS // 2
    pair_spec = pl.BlockSpec((rows, LANES), lambda g, i, _: (0, g * inner + i))
    kv_spec = pl.BlockSpec((kv.shape[0], rows, LANES), lambda g, i, _: (0, 0, g))
    return pl.pallas_call(
        attend_back_kernel,
        grid_spec=pltpu.PrefetchScalarGridSpec(
            num_scalar_prefetch=1,
            grid=(KV_HEADS, inner),
            in_specs=[
                pair_spec,
                pair_spec,
                pair_spec,
                pl.BlockSpec((1, 1, 2 * rows), lambda g, i, _: (g * inner + i, 0, 0)),
                kv_spec,
                whole((1, rows)),
                whole((rows, LANES)),
                whole((rows, LANES)),
            ],
            out_specs=[pair_spec, kv_spec],
            scratch_shapes=[pltpu.VMEM((keys, LANES), BF16), pltpu.VMEM((keys, LANES), F32)],
        ),
        out_shape=[
            jax.ShapeDtypeStruct(queries.shape, BF16),
            jax.ShapeDtypeStruct(kv.shape, F32),
        ],
        compiler_params=pltpu.CompilerParams(vmem_limit_bytes=40 * 1024 * 1024),
    )(places, queries, grad, attended, logs, kv, first, cosine, sine)


def rms_forward(values, gain):
    factor = lax.rsqrt(jnp.mean(values * values, -1, keepdims=True) + EPS)
    normed = values * factor
    return factor, normed, (normed * gain).astype(BF16)


def rms_backward(grad_normed, factor, normed, gain):
    gain_grad = jnp.sum(grad_normed * normed, 0)
    scaled = grad_normed * gain
    return gain_grad, factor * (scaled - normed * jnp.mean(scaled * normed, -1, keepdims=True))


def on_device(
    reps,
    shards,
    hidden_in,
    segments,
    cotangent,
    qkv_weight,
    out_weight,
    gate_up_weight,
    down_weight,
    attn_gain,
    ffn_gain,
):
    ring = Ring(shards)
    chips = ring.chips
    twin_map = [(i, i ^ 1) for i in range(reps)]
    side = lax.axis_index("rep") % 2
    side_groups = [list(range(s, reps, 2)) for s in range(2)]

    def twin(value):
        return lax.ppermute(value, "rep", twin_map)

    def rest_of_reps(value):
        if reps == 2:
            return value
        return lax.psum(value, "rep", axis_index_groups=side_groups)

    def over_reps(value):
        mine = rest_of_reps(value).astype(BF16)
        return mine.astype(F32) + twin(mine).astype(F32)

    tok = hidden_in.shape[1]
    model = hidden_in.shape[2]
    rows = model // shards
    seg_row = segments[0]
    length = seg_row.shape[0]
    qsize = HEADS * HEAD_DIM
    ff = down_weight.shape[0] * shards
    wide = ff // chips

    gains = lax.all_gather(jnp.stack([attn_gain, ffn_gain]), "shard", axis=1, tiled=True)
    gain_one = gains[0].astype(F32)
    gain_two = gains[1].astype(F32)
    qkv_own, qkv_sib = ring.gather_both(qkv_weight)

    offset = ring.index * tok
    local_seg = lax.dynamic_slice_in_dim(seg_row, offset, tok)
    starts = jnp.sum((seg_row[None, :] < local_seg[:, None]).astype(jnp.int32), 1)
    positions = offset + jnp.arange(tok, dtype=jnp.int32) - starts
    freqs = jnp.exp(
        (jnp.arange(LANES) % (HEAD_DIM // 2)).astype(F32) * (-2.0 * math.log(10000.0) / HEAD_DIM)
    )
    angles = positions.astype(F32)[:, None] * freqs[None, :]
    cosine, sine = jnp.cos(angles), jnp.sin(angles)
    blocks = min(REACH // tok, shards - 1) + 1
    first = (starts - offset + (blocks - 1) * tok)[None, :]
    device = (ring.index + jnp.arange(1 - blocks, 1)) % shards
    place_of = jnp.asarray([ring.place[i] for i in range(chips)], jnp.int32)
    places = (
        jnp.abs(device % 2 - ring.core) * chips + (place_of[device // 2] - ring.at) % chips
    ).astype(jnp.int32)

    hidden32 = hidden_in[0].astype(F32)
    factor_one, normed_one, input_one = rms_forward(hidden32, gain_one)
    in_own, in_sib = (ring.to_ring(v, 1) for v in ring.split_cores(input_one, 1))

    def by_blocks(own, sib, own_blocks, sib_blocks):
        total = None
        for k in sorted(range(chips), key=lambda k: min(k, chips - k)):
            for value, weights in ((own, own_blocks), (sib, sib_blocks)):
                term = dot(value[:, k * rows : (k + 1) * rows], weights[k])
                total = term if total is None else total + term
        return total

    projections = by_blocks(in_own, in_sib, qkv_own, qkv_sib)
    kv_local = small_kernel(
        kv_prepare_kernel, KV_HEADS * LANES, BF16, projections[:, qsize:], cosine, sine
    )
    kv_own, kv_sib = ring.gather_both(kv_local)
    kv = jnp.stack(kv_own + kv_sib)
    out_own, out_sib = ring.gather_both(after(out_weight, qkv_own[ring.half]))
    queries, attended, logs = attend(places, projections[:, :qsize], kv, first, cosine, sine)
    att_own, att_sib = (ring.to_ring(v, 1) for v in ring.split_cores(attended, 1))
    residual = hidden32 + by_blocks(att_own, att_sib, out_own, out_sib)
    factor_two, normed_two, input_two = rms_forward(residual, gain_two)

    half = rows // 2
    mine = lax.dynamic_slice_in_dim(
        after(gate_up_weight, out_own[ring.half]), side * half, half, 0
    )
    mine = mine.reshape(half, 2, chips, wide).transpose(2, 1, 0, 3)
    mine = lax.all_to_all(mine, "shard", 0, 0, axis_index_groups=ring.core_groups, tiled=True)
    theirs = twin(mine)
    gu_own = jnp.concatenate([pick(side, mine, theirs), pick(side, theirs, mine)], 2)
    gu_own = gu_own.transpose(1, 0, 2, 3).reshape(2, chips * rows, wide)
    gu_sib = ring.swap(gu_own)
    gate_up = jnp.concatenate([gu_own, gu_sib], 1)
    down_sib = ring.swap(down_weight)
    down = jnp.concatenate(
        [pick(ring.core, down_weight, down_sib), pick(ring.core, down_sib, down_weight)], 0
    )

    cot = jnp.concatenate(ring.gather(after(cotangent[0], out_own[ring.half])), 0)
    two = jnp.concatenate(ring.gather(jnp.concatenate(ring.split_cores(input_two, 1), 1)), 0)
    gate = dot(two, gate_up[0])
    upward = dot(two, gate_up[1])
    sigma = jax.nn.sigmoid(gate)
    activation = (gate * sigma * upward).astype(BF16)
    grad_activation = dot(cot, down, ((1,), (1,)))
    grad_gate = (grad_activation * upward * (sigma * (1.0 + gate * (1.0 - sigma)))).astype(BF16)
    grad_up = (grad_activation * gate * sigma).astype(BF16)
    grad_two = dot(grad_gate, gate_up[0], ((1,), (1,))) + dot(grad_up, gate_up[1], ((1,), (1,)))

    def cut(value):
        return [value[k * tok : (k + 1) * tok] for k in range(chips)]

    grad_two = ring.scatter(cut(grad_two))
    grad_input_two = ring.join_cores(grad_two[:, : model // 2], grad_two[:, model // 2 :], 1)
    ffn_out = ring.scatter(cut(after(dot(activation, down), grad_two)))
    hidden_out = (residual + ffn_out).astype(BF16)
    gain_two_term, grad_back_two = rms_backward(grad_input_two, factor_two, normed_two, gain_two)
    grad_residual = cotangent[0].astype(F32) + grad_back_two
    residual_half = grad_residual.astype(BF16)

    down_term = dot(activation, cot, ((0,), (0,)))
    down_rows = down_weight.shape[0]
    keep = pick(ring.core, down_term[:down_rows], down_term[down_rows:])
    give = pick(ring.core, down_term[down_rows:], down_term[:down_rows]).astype(BF16)
    grad_down = over_reps(keep + ring.swap(give).astype(F32))
    gu_term = jnp.stack([dot(two, grad_gate, ((0,), (0,))), dot(two, grad_up, ((0,), (0,)))])
    middle = chips * rows
    gu_term = gu_term[:, :middle] + ring.swap(gu_term[:, middle:].astype(BF16)).astype(F32)
    gu_term = gu_term.reshape(2, chips, rows, wide)
    keep = pick(side, gu_term[:, :, :half], gu_term[:, :, half:])
    give = pick(side, gu_term[:, :, half:], gu_term[:, :, :half]).astype(BF16)
    keep = rest_of_reps(keep + twin(give).astype(F32)).astype(BF16)
    keep = lax.all_to_all(
        keep.transpose(1, 0, 2, 3), "shard", 0, 0, axis_index_groups=ring.core_groups, tiled=True
    )
    keep = keep.transpose(2, 1, 0, 3).reshape(half, 2 * ff)
    give = twin(keep)
    grad_gate_up = jnp.concatenate([pick(side, keep, give), pick(side, give, keep)], 0)
    grad_gate_up = grad_gate_up.astype(F32)

    def token_terms(inputs, grads, gain_term):
        own, sib = (ring.to_ring(v, 1) for v in ring.split_cores(inputs, 1))
        gain_own, gain_sib = (ring.to_ring(v, 0) for v in ring.split_cores(gain_term, 0))

        def with_gain(term, gain):
            extra = jnp.concatenate([gain[:, None], jnp.zeros((gain.shape[0], LANES - 1), F32)], 1)
            return jnp.concatenate([term, extra], 1)

        give = with_gain(dot(sib, grads, ((0,), (0,))), gain_sib).astype(BF16)
        keep = with_gain(dot(own, grads, ((0,), (0,))), gain_own) + ring.swap(give).astype(F32)
        parts = [keep[k * rows : (k + 1) * rows] for k in range(chips)]
        total = over_reps(ring.scatter(parts))
        return total[:, :-LANES], total[:, -LANES]

    out_all = jnp.concatenate(out_own + out_sib, 0)
    grad_att = dot(residual_half, out_all, ((1,), (1,)))
    grad_attended = ring.join_cores(
        ring.from_ring(grad_att[:, : qsize // 2], 1),
        ring.from_ring(grad_att[:, qsize // 2 :], 1),
        1,
    ).astype(BF16)
    grad_out, grad_ffn_gain = token_terms(attended, residual_half, gain_two_term)
    grad_queries, grad_kv = attend_back(
        places, queries, grad_attended, attended, logs, kv, first, cosine, sine
    )
    grad_kv = grad_kv[:chips] + ring.swap(grad_kv[chips:].astype(BF16)).astype(F32)
    grad_kv = ring.scatter([grad_kv[k] for k in range(chips)])
    grad_kv = small_kernel(
        kv_finish_kernel, 2 * KV_HEADS * HEAD_DIM, BF16, grad_kv, cosine, sine
    )
    grad_projections = jnp.concatenate([grad_queries, grad_kv], 1)
    qkv_all = jnp.concatenate(qkv_own + qkv_sib, 0)
    grad_one = dot(grad_projections, qkv_all, ((1,), (1,)))
    grad_input_one = ring.join_cores(
        ring.from_ring(grad_one[:, : model // 2], 1),
        ring.from_ring(grad_one[:, model // 2 :], 1),
        1,
    )
    gain_one_term, grad_back_one = rms_backward(grad_input_one, factor_one, normed_one, gain_one)
    grad_hidden = (grad_residual + grad_back_one).astype(BF16)
    grad_qkv, grad_attn_gain = token_terms(input_one, grad_projections, gain_one_term)
    return (
        hidden_out[None],
        grad_hidden[None],
        grad_qkv,
        grad_out,
        grad_gate_up,
        grad_down,
        grad_attn_gain,
        grad_ffn_gain,
    )


def solution(mesh):
    reps, shards = mesh.shape["rep"], mesh.shape["shard"]

    def layer(*args):
        return on_device(reps, shards, *args)

    return jax.shard_map(
        layer,
        mesh=mesh,
        in_specs=(
            P("rep", "shard", None),
            P("rep", None),
            P("rep", "shard", None),
            P("shard", None),
            P("shard", None),
            P("shard", None),
            P("shard", None),
            P("shard"),
            P("shard"),
        ),
        out_specs=(
            P("rep", "shard", None),
            P("rep", "shard", None),
            P("shard", None),
            P("shard", None),
            P("shard", None),
            P("shard", None),
            P("shard"),
            P("shard"),
        ),
        check_vma=False,
    )
```

time: 3030 us -> 948 us (0.31)
  waiting for transfers between devices: 2260 us -> 341 us
  matrix products: 412 us -> 115 us
  starting transfers between devices: 0.77 us -> 120 us
  local copies, waits for them, and re-layouts: 97.3 us -> 186 us
  loops' own time: 84.2 us -> 0 us
  blocking collectives: 106 us -> 21.8 us
  Pallas kernels: 0 us -> 51.4 us
  other arithmetic: 43.3 us -> 93.8 us
    reduce_scatter x6 -> x0, waiting for transfers between devices: 1710 us -> none  [the longest x1 840 us: on_device(): lax.psum_scatter(gate_up_term, 'shard', scatter_dimension=0, tiled=True)]
    all_gather x6 -> x0, waiting for transfers between devices: 372 us -> none  [the longest x1 158 us: on_device(): lax.all_gather(gate_up_weight, 'shard', axis=0, tiled=True)]
    ppermute x0 -> x117, waiting for transfers between devices: none -> 319 us  [the longest x15 76.3 us: scatter(): ccw = lax.ppermute(back.astype(BF16), 'shard', self.back).astype(F32)]
    dot_general x124 -> x47, matrix products: 412 us -> 115 us  [dot(): return lax.dot_general(a, b, (dims, ((), ())), preferred_element_type=F32)]
    psum x1 -> x0, waiting for transfers between devices: 170 us -> none  [on_device(): attn_parts = lax.psum((attn_parts[0], attn_parts[1], attn_parts[2]), 'rep')]
    ppermute x0 -> x117, starting transfers between devices: none -> 111 us  [the longest x15 20.6 us: gather(): cw = lax.ppermute(cw, 'shard', self.ahead)]
    another operation x2 -> x0, loops' own time: 84.2 us -> none  [the longest x1 42.2 us: on_device(): lax.scan(backward_pair, (zero_acc, zero_acc), (query_pairs, grad_pairs, p...]
    unnamed x1 -> x0, blocking collectives: 58.5 us -> none
  transfers between devices with their start and end apart: 13 -> 119, of which waited for: 12 -> 58; matrix products, arithmetic and copies ran while one was open for 8% -> 38% of each run, Pallas kernels for 0% -> 5%
where the time goes in v1:
time: 948 us; the launch traced here: 934 us
  waiting for transfers between devices  341 us (36%)
  local copies, waits for them, and re-layouts  186 us (20%)
  starting transfers between devices  120 us (13%)
  matrix products  115 us (12%)
  other arithmetic  93.8 us (10%)
  Pallas kernels  51.4 us (5%)
  blocking collectives  21.8 us (2%)
    dot_general x47, matrix products, dot(): return lax.dot_general(a, b, (dims, ((), ())), preferred_element_type=F32)  115 us
    ppermute x15, waiting for transfers between devices, scatter(): ccw = lax.ppermute(back.astype(BF16), 'shard', self.back).astype(F32)  76.3 us
    ppermute x15, waiting for transfers between devices, scatter(): cw = lax.ppermute(ahead.astype(BF16), 'shard', self.ahead).astype(F32)  72.1 us
    unnamed x382, local copies, waits for them, and re-layouts  66.3 us
    ppermute x6, waiting for transfers between devices, twin(): return lax.ppermute(value, 'rep', twin_map)  54.9 us
    ppermute x15, waiting for transfers between devices, gather(): ccw = lax.ppermute(ccw, 'shard', self.back)  44.7 us
    concatenate x4, local copies, waits for them, and re-layouts, with_gain(): return jnp.concatenate([term, extra], 1)  39.6 us
    pallas_call x1, Pallas kernels, attend_back(): pl.pallas_call(attend_back_kernel, grid_spec=pltpu.PrefetchScalarGridSpec...  24 us
  transfers between devices with their start and end apart: 119, of which 58 were waited for; matrix products, arithmetic and copies ran while one was open for 38% of the time, Pallas kernels for 5%

profile of v1, /device:TPU:0, one launch (start us, length us, event | category | flops | bytes accessed | tf_op | source)
XLA Modules:
  0.0 934.2 jit_solution(9444271707525356506)
XLA Ops:
  13.7 21.8 %all_gather.3 = bf16[2,2048]{1,0:T(2,128)(2,1)S(1)} all-gather(bf16[2,128]{1,0:T(2,128)(2,1)S(1)} %pad_maximum_fusion.24), channel_id=1, replica_groups=mesh['rep'=2,'shard'=16] {'shard'}, dimensions={1}, use_global_device_ids=true | all-gather | bytes 8704 | tf_op jit(solution)/shard_map/all_gather | solution.py:402
  55.2 8.5 collective-permute-done.5
  73.4 6.4 collective-permute-done.9
  161.9 23.7 %shard_map.171 = (bf16[128,2048]{1,0:T(8,128)(2,1)S(1)}, bf16[128,2048]{1,0:T(8,128)(2,1)S(1)}, f32[16,1,256]{2,1,0:T(1,128)S(1)}) custom-call(s32[9]{0:T(128)S(1)} %copy-done.11, f32[128,2048]{1,0:T(8,128)S(1)} %slice.1204.proj_ref, bf16[16,128,512]{2,1,0:T(8,128)(2,1)S(1)} %constant_dynamic-update-slice_fusion.30.kv_ref, s32[1,128]{1,0:T(1,128)S(1)} %copy-done.13, ...), custom_call_target="tpu_custom_call" | custom-call | tf_op jit(solution)/shard_map/pallas_call | solution.py:290
  249.0 22.4 %all-to-all-done = bf16[8,2,64,704]{3,1,2,0:T(2,128)(2,1)} async-done(((bf16[8,2,64,704]{3,1,2,0:T(2,128)(2,1)}), bf16[8,2,64,704]{3,1,2,0:T(2,128)(2,1)}, u32[]{:S(2)}, u32[]{:S(2)}) %all-to-all-start) | async-done | bytes 1441824 | tf_op jit(solution)/shard_map/all_to_all | solution.py:453
  284.4 7.1 collective-permute-done.63
  294.0 9.6 %collective-permute-done.56 = bf16[8,2,64,704]{3,1,2,0:T(2,128)(2,1)} collective-permute-done((bf16[8,2,64,704]{3,1,2,0:T(2,128)(2,1)}, bf16[8,2,64,704]{3,1,2,0:T(2,128)(2,1)}, u32[]{:S(2)}, u32[]{:S(2)}) %collective-permute-start.56) | collective-permute-done | bytes 1441824 | tf_op jit(solution)/shard_map/ppermute | solution.py:382
  305.7 5.8 pad_maximum_fusion.1
  311.5 8.6 copy.126
  330.4 6.3 collective-permute-done.61
  339.1 8.8 collective-permute-done.49
  356.1 8.1 collective-permute-done.50
  378.2 7.4 concatenate.163
  385.6 6.1 fusion.65
  391.8 6.8 multiply_convert_fusion.1
  398.6 5.9 fusion.63
  404.5 7.1 fusion.210
  427.8 6.0 collective-permute-done.68
  438.9 6.2 collective-permute-done.69
  462.1 6.2 collective-permute-done.74
  483.9 7.7 collective-permute-done.76
  526.4 6.6 fusion.194
  544.9 24.0 %shard_map.172 = (bf16[128,2048]{1,0:T(8,128)(2,1)S(1)}, f32[16,128,512]{2,1,0:T(8,128)S(1)}) custom-call(s32[9]{0:T(128)S(1)} %copy-done.12, bf16[128,2048]{1,0:T(8,128)(2,1)S(1)} %copy-done.10, bf16[128,2048]{1,0:T(8,128)(2,1)S(1)} %copy-done.6, bf16[128,2048]{1,0:T(8,128)(2,1)S(1)} %get-tuple-element.17.att_ref, ...), custom_call_target="tpu_custom_call" | custom-call | tf_op jit(solution)/shard_map/pallas_call | solution.py:324
  569.2 6.6 add_convert_fusion.1
  577.3 6.7 fusion.1
  584.0 6.4 copy.127
  603.2 7.4 collective-permute-done.116
  616.7 26.2 %collective-permute-done.113 = bf16[2,8,64,704]{3,2,1,0:T(8,128)(2,1)S(1)} collective-permute-done((bf16[2,8,64,704]{3,2,1,0:T(8,128)(2,1)S(1)}, bf16[2,8,64,704]{3,2,1,0:T(8,128)(2,1)S(1)}, u32[]{:S(2)}, u32[]{:S(2)}) %collective-permute-start.113) | collective-permute-done | bytes 1441824 | tf_op jit(solution)/shard_map/ppermute | solution.py:382
  657.2 15.2 %collective-permute-done.90 = bf16[128,512]{1,0:T(8,128)(2,1)S(1)} collective-permute-done((bf16[128,512]{1,0:T(8,128)(2,1)S(1)}, bf16[128,512]{1,0:T(8,128)(2,1)S(1)}, u32[]{:S(2)}, u32[]{:S(2)}) %collective-permute-start.90) | collective-permute-done | bytes 131104 | tf_op jit(solution)/shard_map/ppermute | solution.py:92
  673.3 6.7 collective-permute-start.91
  683.3 10.0 %collective-permute-done.91 = bf16[128,512]{1,0:T(8,128)(2,1)S(1)} collective-permute-done((bf16[128,512]{1,0:T(8,128)(2,1)S(1)}, bf16[128,512]{1,0:T(8,128)(2,1)S(1)}, u32[]{:S(2)}, u32[]{:S(2)}) %collective-permute-start.91) | collective-permute-done | bytes 131104 | tf_op jit(solution)/shard_map/ppermute | solution.py:92
  696.9 7.5 fusion.83
  713.1 8.0 concatenate.194
  739.9 9.1 concatenate.188
  749.3 10.2 %concatenate.192 = f32[1024,2176]{1,0:T(8,128)} concatenate(f32[1024,2048]{1,0:T(8,128)} %fusion.78, f32[1024,1]{1,0:T(8,128)} %copy.120, f32[1024,127]{1,0:T(8,128)S(1)} %broadcast.348), dimensions={1} | concatenate | bytes 17825792 | tf_op jit(solution)/shard_map/concatenate | solution.py:512
  759.4 6.3 fusion.81
  765.8 12.3 %concatenate.186 = f32[1024,2688]{1,0:T(8,128)} concatenate(f32[1024,2560]{1,0:T(8,128)} %fusion.81, f32[1024,1]{1,0:T(8,128)S(1)} %copy.118, f32[1024,127]{1,0:T(8,128)S(1)} %broadcast.348), dimensions={1} | concatenate | bytes 22020096 | tf_op jit(solution)/shard_map/concatenate | solution.py:512
  782.1 10.8 %fusion.199 = (bf16[1024,2176]{1,0:T(8,128)(2,1)}, f32[1024,2176]{1,0:T(8,128)}) fusion(f32[1024,2176]{1,0:T(8,128)} %concatenate.192, bf16[1024,2176]{1,0:T(8,128)(2,1)} %collective-permute-done.102), kind=kLoop, calls=%fused_computation.608 | loop fusion | flops 6684672 | bytes 26738688 | tf_op jit(solution)/shard_map/convert.11
  805.5 6.5 fusion.200
  816.1 7.1 collective-permute-done.93
  827.2 8.0 collective-permute-done.104
  837.5 12.4 %collective-permute-done.94 = bf16[128,2688]{1,0:T(8,128)(2,1)S(1)} collective-permute-done((bf16[128,2688]{1,0:T(8,128)(2,1)S(1)}, bf16[128,2688]{1,0:T(8,128)(2,1)S(1)}, u32[]{:S(2)}, u32[]{:S(2)}) %collective-permute-start.94) | collective-permute-done | bytes 688160 | tf_op jit(solution)/shard_map/ppermute | solution.py:91
  851.8 10.0 %collective-permute-done.105 = bf16[128,2176]{1,0:T(8,128)(2,1)S(1)} collective-permute-done((bf16[128,2176]{1,0:T(8,128)(2,1)S(1)}, bf16[128,2176]{1,0:T(8,128)(2,1)S(1)}, u32[]{:S(2)}, u32[]{:S(2)}) %collective-permute-start.105) | collective-permute-done | bytes 557088 | tf_op jit(solution)/shard_map/ppermute | solution.py:91
  864.2 12.4 %collective-permute-done.95 = bf16[128,2688]{1,0:T(8,128)(2,1)S(1)} collective-permute-done((bf16[128,2688]{1,0:T(8,128)(2,1)S(1)}, bf16[128,2688]{1,0:T(8,128)(2,1)S(1)}, u32[]{:S(2)}, u32[]{:S(2)}) %collective-permute-start.95) | collective-permute-done | bytes 688160 | tf_op jit(solution)/shard_map/ppermute | solution.py:91
  879.9 15.4 %collective-permute-done.99 = bf16[128,2688]{1,0:T(8,128)(2,1)S(1)} collective-permute-done((bf16[128,2688]{1,0:T(8,128)(2,1)S(1)}, bf16[128,2688]{1,0:T(8,128)(2,1)S(1)}, u32[]{:S(2)}, u32[]{:S(2)}) %collective-permute-start.99) | collective-permute-done | bytes 688160 | tf_op jit(solution)/shard_map/ppermute | solution.py:92
  896.3 11.0 %collective-permute-done.110 = bf16[128,2176]{1,0:T(8,128)(2,1)S(1)} collective-permute-done((bf16[128,2176]{1,0:T(8,128)(2,1)S(1)}, bf16[128,2176]{1,0:T(8,128)(2,1)S(1)}, u32[]{:S(2)}, u32[]{:S(2)}) %collective-permute-start.110) | collective-permute-done | bytes 557088 | tf_op jit(solution)/shard_map/ppermute | solution.py:92
  908.1 9.4 %collective-permute-done.100 = bf16[128,2688]{1,0:T(8,128)(2,1)S(1)} collective-permute-done((bf16[128,2688]{1,0:T(8,128)(2,1)S(1)}, bf16[128,2688]{1,0:T(8,128)(2,1)S(1)}, u32[]{:S(2)}, u32[]{:S(2)}) %collective-permute-start.100) | collective-permute-done | bytes 688160 | tf_op jit(solution)/shard_map/ppermute | solution.py:92
  920.1 11.7 %collective-permute-done.101 = bf16[128,2688]{1,0:T(8,128)(2,1)S(1)} collective-permute-done((bf16[128,2688]{1,0:T(8,128)(2,1)S(1)}, bf16[128,2688]{1,0:T(8,128)(2,1)S(1)}, u32[]{:S(2)}, u32[]{:S(2)}) %collective-permute-start.101) | collective-permute-done | bytes 688160 | tf_op jit(solution)/shard_map/ppermute | solution.py:382
  (796 shorter events, 448.0 us)
Async XLA Ops:
  0.7 45.8 %collective-permute-start.1 = (bf16[128,2560]{1,0:T(8,128)(2,1)}, bf16[128,2560]{1,0:T(8,128)(2,1)}, u32[]{:S(2)}, u32[]{:S(2)}) collective-permute-start(bf16[128,2560]{1,0:T(8,128)(2,1)} %param.14), channel_id=1, source_target_pairs={{0,2},{1,3},{2,6},{3,7},{4,0},{5,1},{6,10},{7,11},{8,4},{9,5},{10,... | collective-permute-start | bytes 1966088 | tf_op jit(solution)/shard_map/ppermute | solution.py:68
  3.7 46.9 %collective-permute-start = (bf16[128,2560]{1,0:T(8,128)(2,1)}, bf16[128,2560]{1,0:T(8,128)(2,1)}, u32[]{:S(2)}, u32[]{:S(2)}) collective-permute-start(bf16[128,2560]{1,0:T(8,128)(2,1)} %param.14), channel_id=1, source_target_pairs={{0,1},{1,0},{2,3},{3,2},{4,5},{5,4},{6,7},{7,6},{8,9},{9,8},{10,11... | collective-permute-start | bytes 1966088 | tf_op jit(solution)/shard_map/ppermute | solution.py:59
  3.7 43.7 %collective-permute-start.3 = (bf16[128,2560]{1,0:T(8,128)(2,1)}, bf16[128,2560]{1,0:T(8,128)(2,1)}, u32[]{:S(2)}, u32[]{:S(2)}) collective-permute-start(bf16[128,2560]{1,0:T(8,128)(2,1)} %param.14), channel_id=1, source_target_pairs={{0,4},{1,5},{2,0},{3,1},{4,8},{5,9},{6,2},{7,3},{8,12},{9,13},{10,... | collective-permute-start | bytes 1966088 | tf_op jit(solution)/shard_map/ppermute | solution.py:66
  3.9 66.3 %collective-permute-start.58 = (bf16[352,2048]{1,0:T(8,128)(2,1)}, bf16[352,2048]{1,0:T(8,128)(2,1)}, u32[]{:S(2)}, u32[]{:S(2)}) collective-permute-start(bf16[352,2048]{1,0:T(8,128)(2,1)} %param.17), channel_id=1, source_target_pairs={{0,1},{1,0},{2,3},{3,2},{4,5},{5,4},{6,7},{7,6},{8,9},{9,8},{10,11... | collective-permute-start | bytes 4325384 | tf_op jit(solution)/shard_map/ppermute | solution.py:59
  84.1 22.2 %collective-permute-start.10 = (bf16[128,2560]{1,0:T(8,128)(2,1)S(1)}, bf16[128,2560]{1,0:T(8,128)(2,1)S(1)}, u32[]{:S(2)}, u32[]{:S(2)}) collective-permute-start(bf16[128,2560]{1,0:T(8,128)(2,1)S(1)} %collective-permute-done.9), channel_id=1, source_target_pairs={{0,1},{1,0},{2,3},{3,2},{4,5},{5,4},{6,7},{7,6},{8,9},{9,8},{10,11... | collective-permute-start | bytes 1966088 | tf_op jit(solution)/shard_map/ppermute | solution.py:59
  84.2 28.4 %collective-permute-start.12 = (bf16[128,2560]{1,0:T(8,128)(2,1)S(1)}, bf16[128,2560]{1,0:T(8,128)(2,1)S(1)}, u32[]{:S(2)}, u32[]{:S(2)}) collective-permute-start(bf16[128,2560]{1,0:T(8,128)(2,1)S(1)} %collective-permute-done.11), channel_id=1, source_target_pairs={{0,1},{1,0},{2,3},{3,2},{4,5},{5,4},{6,7},{7,6},{8,9},{9,8},{10,11... | collective-permute-start | bytes 1966088 | tf_op jit(solution)/shard_map/ppermute | solution.py:59
  95.8 101.6 %collective-permute-start.32 = (bf16[128,2048]{1,0:T(8,128)(2,1)}, bf16[128,2048]{1,0:T(8,128)(2,1)}, u32[]{:S(2)}, u32[]{:S(2)}) collective-permute-start(bf16[128,2048]{1,0:T(8,128)(2,1)} %param.15), channel_id=1, source_target_pairs={{0,1},{1,0},{2,3},{3,2},{4,5},{5,4},{6,7},{7,6},{8,9},{9,8},{10,11... | collective-permute-start | bytes 1572872 | tf_op jit(solution)/shard_map/ppermute | solution.py:59
  108.2 51.8 %collective-permute-start.39 = (bf16[128,2048]{1,0:T(8,128)(2,1)}, bf16[128,2048]{1,0:T(8,128)(2,1)}, u32[]{:S(2)}, u32[]{:S(2)}) collective-permute-start(bf16[128,2048]{1,0:T(8,128)(2,1)} %collective-permute-done.35), channel_id=1, source_target_pairs={{0,4},{1,5},{2,0},{3,1},{4,8},{5,9},{6,2},{7,3},{8,12},{9,13},{10,... | collective-permute-start | bytes 1572872 | tf_op jit(solution)/shard_map/ppermute | solution.py:66
  109.4 28.2 %collective-permute-start.37 = (bf16[128,2048]{1,0:T(8,128)(2,1)}, bf16[128,2048]{1,0:T(8,128)(2,1)}, u32[]{:S(2)}, u32[]{:S(2)}) collective-permute-start(bf16[128,2048]{1,0:T(8,128)(2,1)} %collective-permute-done.33), channel_id=1, source_target_pairs={{0,2},{1,3},{2,6},{3,7},{4,0},{5,1},{6,10},{7,11},{8,4},{9,5},{10,... | collective-permute-start | bytes 1572872 | tf_op jit(solution)/shard_map/ppermute | solution.py:68
  126.8 82.2 %collective-permute-start.36 = (bf16[128,2048]{1,0:T(8,128)(2,1)}, bf16[128,2048]{1,0:T(8,128)(2,1)}, u32[]{:S(2)}, u32[]{:S(2)}) collective-permute-start(bf16[128,2048]{1,0:T(8,128)(2,1)} %collective-permute-done.35), channel_id=1, source_target_pairs={{0,1},{1,0},{2,3},{3,2},{4,5},{5,4},{6,7},{7,6},{8,9},{9,8},{10,11... | collective-permute-start | bytes 1572872 | tf_op jit(solution)/shard_map/ppermute | solution.py:59
  142.6 61.6 %collective-permute-start.34 = (bf16[128,2048]{1,0:T(8,128)(2,1)}, bf16[128,2048]{1,0:T(8,128)(2,1)}, u32[]{:S(2)}, u32[]{:S(2)}) collective-permute-start(bf16[128,2048]{1,0:T(8,128)(2,1)} %collective-permute-done.33), channel_id=1, source_target_pairs={{0,1},{1,0},{2,3},{3,2},{4,5},{5,4},{6,7},{7,6},{8,9},{9,8},{10,11... | collective-permute-start | bytes 1572872 | tf_op jit(solution)/shard_map/ppermute | solution.py:59
  161.1 46.2 %collective-permute-start.43 = (bf16[128,2048]{1,0:T(8,128)(2,1)}, bf16[128,2048]{1,0:T(8,128)(2,1)}, u32[]{:S(2)}, u32[]{:S(2)}) collective-permute-start(bf16[128,2048]{1,0:T(8,128)(2,1)} %collective-permute-done.39), channel_id=1, source_target_pairs={{0,4},{1,5},{2,0},{3,1},{4,8},{5,9},{6,2},{7,3},{8,12},{9,13},{10,... | collective-permute-start | bytes 1572872 | tf_op jit(solution)/shard_map/ppermute | solution.py:66
  161.8 76.0 %collective-permute-start.40 = (bf16[128,2048]{1,0:T(8,128)(2,1)}, bf16[128,2048]{1,0:T(8,128)(2,1)}, u32[]{:S(2)}, u32[]{:S(2)}) collective-permute-start(bf16[128,2048]{1,0:T(8,128)(2,1)} %collective-permute-done.39), channel_id=1, source_target_pairs={{0,1},{1,0},{2,3},{3,2},{4,5},{5,4},{6,7},{7,6},{8,9},{9,8},{10,11... | collective-permute-start | bytes 1572872 | tf_op jit(solution)/shard_map/ppermute | solution.py:59
  204.3 32.2 %collective-permute-start.38 = (bf16[128,2048]{1,0:T(8,128)(2,1)}, bf16[128,2048]{1,0:T(8,128)(2,1)}, u32[]{:S(2)}, u32[]{:S(2)}) collective-permute-start(bf16[128,2048]{1,0:T(8,128)(2,1)} %collective-permute-done.37), channel_id=1, source_target_pairs={{0,1},{1,0},{2,3},{3,2},{4,5},{5,4},{6,7},{7,6},{8,9},{9,8},{10,11... | collective-permute-start | bytes 1572872 | tf_op jit(solution)/shard_map/ppermute | solution.py:59
  228.7 42.8 %all-to-all-start = ((bf16[8,2,64,704]{3,1,2,0:T(2,128)(2,1)}), bf16[8,2,64,704]{3,1,2,0:T(2,128)(2,1)}, u32[]{:S(2)}, u32[]{:S(2)}) async-start(bf16[8,2,64,704]{3,1,2,0:T(2,128)(2,1)} %copy.110), calls=%async_computation | async-start | bytes 3145728 | tf_op jit(solution)/shard_map/all_to_all | solution.py:453
  240.6 32.9 %collective-permute-start.62 = (bf16[128,2048]{1,0:T(8,128)(2,1)}, bf16[128,2048]{1,0:T(8,128)(2,1)}, u32[]{:S(2)}, u32[]{:S(2)}) collective-permute-start(bf16[128,2048]{1,0:T(8,128)(2,1)} %bitcast.38), channel_id=1, source_target_pairs={{0,4},{1,5},{2,0},{3,1},{4,8},{5,9},{6,2},{7,3},{8,12},{9,13},{10,... | collective-permute-start | bytes 1572872 | tf_op jit(solution)/shard_map/ppermute | solution.py:66
  242.6 40.6 %collective-permute-start.59 = (bf16[128,2048]{1,0:T(8,128)(2,1)}, bf16[128,2048]{1,0:T(8,128)(2,1)}, u32[]{:S(2)}, u32[]{:S(2)}) collective-permute-start(bf16[128,2048]{1,0:T(8,128)(2,1)} %bitcast.38), channel_id=1, source_target_pairs={{0,2},{1,3},{2,6},{3,7},{4,0},{5,1},{6,10},{7,11},{8,4},{9,5},{10,... | collective-permute-start | bytes 1572872 | tf_op jit(solution)/shard_map/ppermute | solution.py:68
  271.5 32.2 %collective-permute-start.56 = (bf16[8,2,64,704]{3,1,2,0:T(2,128)(2,1)}, bf16[8,2,64,704]{3,1,2,0:T(2,128)(2,1)}, u32[]{:S(2)}, u32[]{:S(2)}) collective-permute-start(bf16[8,2,64,704]{3,1,2,0:T(2,128)(2,1)} %all-to-all-done), channel_id=1, source_target_pairs={{0,16},{16,0},{1,17},{17,1},{2,18},{18,2},{3,19},{19,3},{4,20},{20... | collective-permute-start | bytes 4325384 | tf_op jit(solution)/shard_map/ppermute | solution.py:382
  280.6 43.5 %collective-permute-start.51 = (bf16[128,2048]{0,1:T(8,128)(2,1)S(1)}, bf16[128,2048]{0,1:T(8,128)(2,1)S(1)}, u32[]{:S(2)}, u32[]{:S(2)}) collective-permute-start(bf16[128,2048]{0,1:T(8,128)(2,1)S(1)} %pad_maximum_fusion.13), channel_id=1, source_target_pairs={{0,4},{1,5},{2,0},{3,1},{4,8},{5,9},{6,2},{7,3},{8,12},{9,13},{10,... | collective-permute-start | bytes 1572872 | tf_op jit(solution)/shard_map/ppermute | solution.py:66
  283.2 40.9 %collective-permute-start.48 = (bf16[128,2048]{0,1:T(8,128)(2,1)S(1)}, bf16[128,2048]{0,1:T(8,128)(2,1)}, u32[]{:S(2)}, u32[]{:S(2)}) collective-permute-start(bf16[128,2048]{0,1:T(8,128)(2,1)S(1)} %pad_maximum_fusion.13), channel_id=1, source_target_pairs={{0,2},{1,3},{2,6},{3,7},{4,0},{5,1},{6,10},{7,11},{8,4},{9,5},{10,... | collective-permute-start | bytes 1572872 | tf_op jit(solution)/shard_map/ppermute | solution.py:68
  283.2 38.1 %collective-permute-start.60 = (bf16[128,2048]{1,0:T(8,128)(2,1)}, bf16[128,2048]{1,0:T(8,128)(2,1)}, u32[]{:S(2)}, u32[]{:S(2)}) collective-permute-start(bf16[128,2048]{1,0:T(8,128)(2,1)} %collective-permute-done.59), channel_id=1, source_target_pairs={{0,2},{1,3},{2,6},{3,7},{4,0},{5,1},{6,10},{7,11},{8,4},{9,5},{10,... | collective-permute-start | bytes 1572872 | tf_op jit(solution)/shard_map/ppermute | solution.py:68
  291.5 37.6 %collective-permute-start.64 = (bf16[128,2048]{1,0:T(8,128)(2,1)}, bf16[128,2048]{1,0:T(8,128)(2,1)S(1)}, u32[]{:S(2)}, u32[]{:S(2)}) collective-permute-start(bf16[128,2048]{1,0:T(8,128)(2,1)} %collective-permute-done.63), channel_id=1, source_target_pairs={{0,4},{1,5},{2,0},{3,1},{4,8},{5,9},{6,2},{7,3},{8,12},{9,13},{10,... | collective-permute-start | bytes 1572872 | tf_op jit(solution)/shard_map/ppermute | solution.py:66
  320.2 65.4 %collective-permute-start.57 = (bf16[2,1024,704]{1,2,0:T(8,128)(2,1)}, bf16[2,1024,704]{1,2,0:T(8,128)(2,1)}, u32[]{:S(2)}, u32[]{:S(2)}) collective-permute-start(bf16[2,1024,704]{1,2,0:T(8,128)(2,1)} %copy.126), channel_id=1, source_target_pairs={{0,1},{1,0},{2,3},{3,2},{4,5},{5,4},{6,7},{7,6},{8,9},{9,8},{10,11... | collective-permute-start | bytes 8650760 | tf_op jit(solution)/shard_map/ppermute | solution.py:59
  324.1 23.8 %collective-permute-start.49 = (bf16[128,2048]{0,1:T(8,128)(2,1)}, bf16[128,2048]{0,1:T(8,128)(2,1)S(1)}, u32[]{:S(2)}, u32[]{:S(2)}) collective-permute-start(bf16[128,2048]{0,1:T(8,128)(2,1)} %collective-permute-done.48), channel_id=1, source_target_pairs={{0,2},{1,3},{2,6},{3,7},{4,0},{5,1},{6,10},{7,11},{8,4},{9,5},{10,... | collective-permute-start | bytes 1572872 | tf_op jit(solution)/shard_map/ppermute | solution.py:68
  329.2 21.2 %collective-permute-start.65 = (bf16[64,2048]{1,0:T(8,128)(2,1)S(1)}, bf16[64,2048]{1,0:T(8,128)(2,1)S(1)}, u32[]{:S(2)}, u32[]{:S(2)}) collective-permute-start(bf16[64,2048]{1,0:T(8,128)(2,1)S(1)} %slice.1233), channel_id=1, source_target_pairs={{0,4},{1,5},{2,0},{3,1},{4,8},{5,9},{6,2},{7,3},{8,12},{9,13},{10,... | collective-permute-start | bytes 786440 | tf_op jit(solution)/shard_map/ppermute | solution.py:70
  504.8 64.4 %collective-permute-start.115 = (bf16[352,2048]{1,0:T(8,128)(2,1)}, bf16[352,2048]{1,0:T(8,128)(2,1)}, u32[]{:S(2)}, u32[]{:S(2)}) collective-permute-start(bf16[352,2048]{1,0:T(8,128)(2,1)} %select_convert_fusion.1), channel_id=1, source_target_pairs={{0,1},{1,0},{2,3},{3,2},{4,5},{5,4},{6,7},{7,6},{8,9},{9,8},{10,11... | collective-permute-start | bytes 4325384 | tf_op jit(solution)/shard_map/ppermute | solution.py:59
  506.9 70.4 %collective-permute-start.112 = (bf16[2,1024,704]{1,2,0:T(8,128)(2,1)}, bf16[2,1024,704]{1,2,0:T(8,128)(2,1)}, u32[]{:S(2)}, u32[]{:S(2)}) collective-permute-start(bf16[2,1024,704]{1,2,0:T(8,128)(2,1)} %fusion.2), channel_id=1, source_target_pairs={{0,1},{1,0},{2,3},{3,2},{4,5},{5,4},{6,7},{7,6},{8,9},{9,8},{10,11... | collective-permute-start | bytes 8650760 | tf_op jit(solution)/shard_map/ppermute | solution.py:59
  569.1 25.3 %collective-permute-start.83 = (bf16[8,128,512]{2,1,0:T(8,128)(2,1)S(1)}, bf16[8,128,512]{2,1,0:T(8,128)(2,1)}, u32[]{:S(2)}, u32[]{:S(2)}) collective-permute-start(bf16[8,128,512]{2,1,0:T(8,128)(2,1)S(1)} %slice.1765), channel_id=1, source_target_pairs={{0,1},{1,0},{2,3},{3,2},{4,5},{5,4},{6,7},{7,6},{8,9},{9,8},{10,11... | collective-permute-start | bytes 3145736 | tf_op jit(solution)/shard_map/ppermute | solution.py:59
  575.8 34.8 %collective-permute-start.116 = (bf16[352,2048]{1,0:T(8,128)(2,1)}, bf16[352,2048]{1,0:T(8,128)(2,1)}, u32[]{:S(2)}, u32[]{:S(2)}) collective-permute-start(bf16[352,2048]{1,0:T(8,128)(2,1)} %add_convert_fusion.1), channel_id=1, source_target_pairs={{0,16},{16,0},{1,17},{17,1},{2,18},{18,2},{3,19},{19,3},{4,20},{20... | collective-permute-start | bytes 4325384 | tf_op jit(solution)/shard_map/ppermute | solution.py:382
  593.7 49.2 %collective-permute-start.113 = (bf16[2,8,64,704]{3,2,1,0:T(8,128)(2,1)S(1)}, bf16[2,8,64,704]{3,2,1,0:T(8,128)(2,1)S(1)}, u32[]{:S(2)}, u32[]{:S(2)}) collective-permute-start(bf16[2,8,64,704]{3,2,1,0:T(8,128)(2,1)S(1)} %select_convert_fusion), channel_id=1, source_target_pairs={{0,16},{16,0},{1,17},{17,1},{2,18},{18,2},{3,19},{19,3},{4,20},{20... | collective-permute-start | bytes 4325384 | tf_op jit(solution)/shard_map/ppermute | solution.py:382
  614.5 34.9 %collective-permute-start.89 = (bf16[128,512]{1,0:T(8,128)(2,1)S(1)}, bf16[128,512]{1,0:T(8,128)(2,1)S(1)}, u32[]{:S(2)}, u32[]{:S(2)}) collective-permute-start(bf16[128,512]{1,0:T(8,128)(2,1)S(1)} %pad_maximum_fusion.23), channel_id=1, source_target_pairs={{0,2},{1,3},{2,6},{3,7},{4,0},{5,1},{6,10},{7,11},{8,4},{9,5},{10,... | collective-permute-start | bytes 393224 | tf_op jit(solution)/shard_map/ppermute | solution.py:92
  615.5 33.9 %collective-permute-start.86 = (bf16[128,512]{1,0:T(8,128)(2,1)S(1)}, bf16[128,512]{1,0:T(8,128)(2,1)S(1)}, u32[]{:S(2)}, u32[]{:S(2)}) collective-permute-start(bf16[128,512]{1,0:T(8,128)(2,1)S(1)} %fusion.72), channel_id=1, source_target_pairs={{0,4},{1,5},{2,0},{3,1},{4,8},{5,9},{6,2},{7,3},{8,12},{9,13},{10,... | collective-permute-start | bytes 393224 | tf_op jit(solution)/shard_map/ppermute | solution.py:91
  644.9 76.4 %all-to-all-start.1 = ((bf16[8,2,64,704]{3,2,1,0:T(8,128)(2,1)}), bf16[8,2,64,704]{3,2,1,0:T(8,128)(2,1)}, u32[]{:S(2)}, u32[]{:S(2)}) async-start(bf16[8,2,64,704]{3,2,1,0:T(8,128)(2,1)} %copy.124), calls=%async_computation.1 | async-start | bytes 3145728 | tf_op jit(solution)/shard_map/all_to_all | solution.py:498
  650.6 21.8 %collective-permute-start.90 = (bf16[128,512]{1,0:T(8,128)(2,1)S(1)}, bf16[128,512]{1,0:T(8,128)(2,1)S(1)}, u32[]{:S(2)}, u32[]{:S(2)}) collective-permute-start(bf16[128,512]{1,0:T(8,128)(2,1)S(1)} %get-tuple-element.78), channel_id=1, source_target_pairs={{0,2},{1,3},{2,6},{3,7},{4,0},{5,1},{6,10},{7,11},{8,4},{9,5},{10,... | collective-permute-start | bytes 393224 | tf_op jit(solution)/shard_map/ppermute | solution.py:92
  657.1 26.2 %collective-permute-start.87 = (bf16[128,512]{1,0:T(8,128)(2,1)S(1)}, bf16[128,512]{1,0:T(8,128)(2,1)S(1)}, u32[]{:S(2)}, u32[]{:S(2)}) collective-permute-start(bf16[128,512]{1,0:T(8,128)(2,1)S(1)} %get-tuple-element.77), channel_id=1, source_target_pairs={{0,4},{1,5},{2,0},{3,1},{4,8},{5,9},{6,2},{7,3},{8,12},{9,13},{10,... | collective-permute-start | bytes 393224 | tf_op jit(solution)/shard_map/ppermute | solution.py:91
  721.1 61.0 %collective-permute-start.102 = (bf16[1024,2176]{1,0:T(8,128)(2,1)}, bf16[1024,2176]{1,0:T(8,128)(2,1)}, u32[]{:S(2)}, u32[]{:S(2)}) collective-permute-start(bf16[1024,2176]{1,0:T(8,128)(2,1)} %concatenate.194), channel_id=1, source_target_pairs={{0,1},{1,0},{2,3},{3,2},{4,5},{5,4},{6,7},{7,6},{8,9},{9,8},{10,11... | collective-permute-start | bytes 13369352 | tf_op jit(solution)/shard_map/ppermute | solution.py:59
  728.9 51.7 %collective-permute-start.114 = (bf16[64,11264]{1,0:T(8,128)(2,1)}, bf16[64,11264]{1,0:T(8,128)(2,1)}, u32[]{:S(2)}, u32[]{:S(2)}) collective-permute-start(bf16[64,11264]{1,0:T(8,128)(2,1)} %reshape.546), channel_id=1, source_target_pairs={{0,16},{16,0},{1,17},{17,1},{2,18},{18,2},{3,19},{19,3},{4,20},{20... | collective-permute-start | bytes 4325384 | tf_op jit(solution)/shard_map/ppermute | solution.py:382
  749.0 56.5 %collective-permute-start.92 = (bf16[1024,2688]{1,0:T(8,128)(2,1)}, bf16[1024,2688]{1,0:T(8,128)(2,1)}, u32[]{:S(2)}, u32[]{:S(2)}) collective-permute-start(bf16[1024,2688]{1,0:T(8,128)(2,1)} %concatenate.188), channel_id=1, source_target_pairs={{0,1},{1,0},{2,3},{3,2},{4,5},{5,4},{6,7},{7,6},{8,9},{9,8},{10,11... | collective-permute-start | bytes 16515080 | tf_op jit(solution)/shard_map/ppermute | solution.py:59
  805.2 46.6 %collective-permute-start.108 = (bf16[128,2176]{1,0:T(8,128)(2,1)S(1)}, bf16[128,2176]{1,0:T(8,128)(2,1)S(1)}, u32[]{:S(2)}, u32[]{:S(2)}) collective-permute-start(bf16[128,2176]{1,0:T(8,128)(2,1)S(1)} %pad_maximum_fusion.12), channel_id=1, source_target_pairs={{0,2},{1,3},{2,6},{3,7},{4,0},{5,1},{6,10},{7,11},{8,4},{9,5},{10,... | collective-permute-start | bytes 1671176 | tf_op jit(solution)/shard_map/ppermute | solution.py:92
  814.3 20.9 %collective-permute-start.104 = (bf16[128,2176]{1,0:T(8,128)(2,1)S(1)}, bf16[128,2176]{1,0:T(8,128)(2,1)S(1)}, u32[]{:S(2)}, u32[]{:S(2)}) collective-permute-start(bf16[128,2176]{1,0:T(8,128)(2,1)S(1)} %pad_maximum_fusion.11), channel_id=1, source_target_pairs={{0,4},{1,5},{2,0},{3,1},{4,8},{5,9},{6,2},{7,3},{8,12},{9,13},{10,... | collective-permute-start | bytes 1671176 | tf_op jit(solution)/shard_map/ppermute | solution.py:91
  826.5 23.4 %collective-permute-start.94 = (bf16[128,2688]{1,0:T(8,128)(2,1)S(1)}, bf16[128,2688]{1,0:T(8,128)(2,1)S(1)}, u32[]{:S(2)}, u32[]{:S(2)}) collective-permute-start(bf16[128,2688]{1,0:T(8,128)(2,1)S(1)} %pad_maximum_fusion.8), channel_id=1, source_target_pairs={{0,4},{1,5},{2,0},{3,1},{4,8},{5,9},{6,2},{7,3},{8,12},{9,13},{10,... | collective-permute-start | bytes 2064392 | tf_op jit(solution)/shard_map/ppermute | solution.py:91
  835.3 26.6 %collective-permute-start.105 = (bf16[128,2176]{1,0:T(8,128)(2,1)S(1)}, bf16[128,2176]{1,0:T(8,128)(2,1)S(1)}, u32[]{:S(2)}, u32[]{:S(2)}) collective-permute-start(bf16[128,2176]{1,0:T(8,128)(2,1)S(1)} %fusion.32), channel_id=1, source_target_pairs={{0,4},{1,5},{2,0},{3,1},{4,8},{5,9},{6,2},{7,3},{8,12},{9,13},{10,... | collective-permute-start | bytes 1671176 | tf_op jit(solution)/shard_map/ppermute | solution.py:91
  837.1 27.1 %collective-permute-start.98 = (bf16[128,2688]{1,0:T(8,128)(2,1)S(1)}, bf16[128,2688]{1,0:T(8,128)(2,1)S(1)}, u32[]{:S(2)}, u32[]{:S(2)}) collective-permute-start(bf16[128,2688]{1,0:T(8,128)(2,1)S(1)} %pad_maximum_fusion.9), channel_id=1, source_target_pairs={{0,2},{1,3},{2,6},{3,7},{4,0},{5,1},{6,10},{7,11},{8,4},{9,5},{10,... | collective-permute-start | bytes 2064392 | tf_op jit(solution)/shard_map/ppermute | solution.py:92
  850.0 26.6 %collective-permute-start.95 = (bf16[128,2688]{1,0:T(8,128)(2,1)S(1)}, bf16[128,2688]{1,0:T(8,128)(2,1)S(1)}, u32[]{:S(2)}, u32[]{:S(2)}) collective-permute-start(bf16[128,2688]{1,0:T(8,128)(2,1)S(1)} %fusion.26), channel_id=1, source_target_pairs={{0,4},{1,5},{2,0},{3,1},{4,8},{5,9},{6,2},{7,3},{8,12},{9,13},{10,... | collective-permute-start | bytes 2064392 | tf_op jit(solution)/shard_map/ppermute | solution.py:91
  862.1 34.2 %collective-permute-start.106 = (bf16[128,2176]{1,0:T(8,128)(2,1)S(1)}, bf16[128,2176]{1,0:T(8,128)(2,1)S(1)}, u32[]{:S(2)}, u32[]{:S(2)}) collective-permute-start(bf16[128,2176]{1,0:T(8,128)(2,1)S(1)} %get-tuple-element.40), channel_id=1, source_target_pairs={{0,4},{1,5},{2,0},{3,1},{4,8},{5,9},{6,2},{7,3},{8,12},{9,13},{10,... | collective-permute-start | bytes 1671176 | tf_op jit(solution)/shard_map/ppermute | solution.py:91
  877.8 29.4 %collective-permute-start.110 = (bf16[128,2176]{1,0:T(8,128)(2,1)S(1)}, bf16[128,2176]{1,0:T(8,128)(2,1)S(1)}, u32[]{:S(2)}, u32[]{:S(2)}) collective-permute-start(bf16[128,2176]{1,0:T(8,128)(2,1)S(1)} %fusion.31), channel_id=1, source_target_pairs={{0,2},{1,3},{2,6},{3,7},{4,0},{5,1},{6,10},{7,11},{8,4},{9,5},{10,... | collective-permute-start | bytes 1671176 | tf_op jit(solution)/shard_map/ppermute | solution.py:92
  879.7 28.4 %collective-permute-start.96 = (bf16[128,2688]{1,0:T(8,128)(2,1)S(1)}, bf16[128,2688]{1,0:T(8,128)(2,1)S(1)}, u32[]{:S(2)}, u32[]{:S(2)}) collective-permute-start(bf16[128,2688]{1,0:T(8,128)(2,1)S(1)} %get-tuple-element.36), channel_id=1, source_target_pairs={{0,4},{1,5},{2,0},{3,1},{4,8},{5,9},{6,2},{7,3},{8,12},{9,13},{10,... | collective-permute-start | bytes 2064392 | tf_op jit(solution)/shard_map/ppermute | solution.py:91
  895.5 21.9 %collective-permute-start.100 = (bf16[128,2688]{1,0:T(8,128)(2,1)S(1)}, bf16[128,2688]{1,0:T(8,128)(2,1)S(1)}, u32[]{:S(2)}, u32[]{:S(2)}) collective-permute-start(bf16[128,2688]{1,0:T(8,128)(2,1)S(1)} %fusion.25), channel_id=1, source_target_pairs={{0,2},{1,3},{2,6},{3,7},{4,0},{5,1},{6,10},{7,11},{8,4},{9,5},{10,... | collective-permute-start | bytes 2064392 | tf_op jit(solution)/shard_map/ppermute | solution.py:92
  (166 other events, 2019.7 us)

commit v2 on v1

v2 whole, which is shorter than its diff:
```python
import math

import jax
import jax.numpy as jnp
import numpy as np
from jax import lax
from jax.experimental import pallas as pl
from jax.experimental.pallas import tpu as pltpu
from jax.sharding import PartitionSpec as P

HEADS = 32
KV_HEADS = 4
HEAD_DIM = 64
REACH = 1024
EPS = 1e-05
F32 = jnp.float32
BF16 = jnp.bfloat16
LANES = 128
SCALE = HEAD_DIM**-0.5
LIMIT = 58 * 1024 * 1024
ROOMY = pltpu.CompilerParams(vmem_limit_bytes=LIMIT)
HELD = pl.BlockSpec(memory_space=pl.ANY)


def dot(a, b, dims=((1,), (0,))):
    return lax.dot_general(a, b, (dims, ((), ())), preferred_element_type=F32)


LAST = ((1,), (1,))
FIRST = ((0,), (0,))


def pick(flag, one, other):
    return jnp.where(flag == 0, one, other)


class Ring:
    def __init__(self, size, window):
        self.size = size
        self.chips = chips = size // 2
        rows = chips // 2
        self.order = [2 * i for i in range(rows)] + [2 * i + 1 for i in reversed(range(rows))]
        self.place = [self.order.index(chip) for chip in range(chips)]
        self.half = chips // 2

        def turned(step):
            return [
                (s, self.order[(self.place[s // 2] + step) % chips] * 2 + s % 2)
                for s in range(size)
            ]

        self.ahead = turned(1)
        self.back = turned(-1)
        self.sibling = [(s, s ^ 1) for s in range(size)]
        self.core_groups = [list(range(core, size, 2)) for core in range(2)]
        self.near, self.place_near, self.cores, self.place_cores, self.window = (
            k * size for k in range(5)
        )
        self.core_at = self.window + window
        self.side_at = self.core_at + 1
        table = []
        for side in range(2):
            for s in range(size):
                chip, core = s // 2, s % 2
                at = self.place[chip]
                near = [
                    self.order[(at + j) % chips] * 2 + (core ^ other)
                    for other in range(2)
                    for j in range(chips)
                ]
                cores = [j * 2 + (core ^ other) for other in range(2) for j in range(chips)]
                place_near = [near.index(d) for d in range(size)]
                place_cores = [cores.index(d) for d in range(size)]
                seen = [place_near[(s + 1 - window + b) % size] for b in range(window)]
                table.append(near + place_near + cores + place_cores + seen + [core, side])
        self.index = lax.axis_index("shard")
        self.side = lax.axis_index("rep") % 2
        self.table = lax.dynamic_index_in_dim(
            jnp.asarray(np.array(table, np.int32)), self.side * size + self.index, 0, False
        )

    def swap(self, value):
        return lax.ppermute(value, "shard", self.sibling)

    def gather(self, block, ties=None):
        n, h = self.chips, block.shape[0] // 2
        cw = ccw = block
        found = [(0, 0, block)]
        for k in range(1, self.half):
            if ties and k in ties:
                cw, ccw = after(cw, *ties[k]), after(ccw, *ties[k])
            cw = lax.ppermute(cw, "shard", self.ahead)
            ccw = lax.ppermute(ccw, "shard", self.back)
            found += [(n - k, 0, cw), (k, 0, ccw)]
        top = lax.ppermute(cw[:h], "shard", self.ahead)
        low = lax.ppermute(ccw[h:], "shard", self.back)
        return found + [(self.half, 0, top), (self.half, h, low)]

    def gather_both(self, block):
        own = self.gather(block)
        other = [(k + self.chips, row, self.swap(piece)) for k, row, piece in own]
        return own + other, [piece for _, _, piece in own]

    def scatter(self, parts, ties=None):
        n, m = self.chips, self.half
        h = parts[0].shape[0] // 2
        cw, ccw = parts[m][:h].astype(BF16), parts[m][h:].astype(BF16)
        marks = []
        for k in range(m - 1, -1, -1):
            if ties:
                others = ties(m - k, marks)
                if others:
                    cw, ccw = after(cw, *others), after(ccw, *others)
            cw = lax.ppermute(cw, "shard", self.ahead)
            ccw = lax.ppermute(ccw, "shard", self.back)
            marks.append((cw, ccw))
            if k == 0:
                return parts[0].astype(F32) + cw.astype(F32) + ccw.astype(F32), marks
            ahead, back = parts[k].astype(F32), parts[n - k].astype(F32)
            if k == m - 1:
                ahead = jnp.concatenate([ahead[:h] + cw.astype(F32), ahead[h:]], 0)
                back = jnp.concatenate([back[:h], back[h:] + ccw.astype(F32)], 0)
            else:
                ahead, back = ahead + cw.astype(F32), back + ccw.astype(F32)
            cw, ccw = ahead.astype(BF16), back.astype(BF16)


def whole(shape):
    return pl.BlockSpec(shape, lambda *_: (0,) * len(shape))


def shaped(shape, kind):
    return jax.ShapeDtypeStruct(shape, kind)


def call(kernel, table, ins, outs, pieces=(), scratch=(), others=()):
    count, more, extra = len(ins), len(pieces), len(others)

    def body(table_ref, *refs):
        behind = count + more + extra
        kernel(
            table_ref,
            refs[:count],
            refs[count : count + more],
            refs[behind : behind + len(outs)],
            refs[behind + len(outs) :],
        )

    return pl.pallas_call(
        body,
        grid_spec=pltpu.PrefetchScalarGridSpec(
            num_scalar_prefetch=1,
            grid=(1,),
            in_specs=[whole(v.shape) for v in ins] + [HELD] * (more + extra),
            out_specs=[whole(v.shape) for v in outs],
            scratch_shapes=list(scratch),
        ),
        out_shape=list(outs),
        compiler_params=ROOMY,
    )(table, *ins, *pieces, *others)


def after(value, *others):
    return pl.pallas_call(
        lambda *refs: None,
        in_specs=[HELD] * (1 + len(others)),
        out_specs=HELD,
        out_shape=shaped(value.shape, value.dtype),
        input_output_aliases={0: 0},
    )(value, *others)


def fetches(pieces, refs, buffer, sems):
    return [
        pltpu.make_async_copy(
            ref, buffer.at[k, pl.ds(row, ref.shape[0])], sems.at[n]
        )
        for n, ((k, row, _), ref) in enumerate(zip(pieces, refs))
    ]


def block_at(place):
    return pl.ds(pl.multiple_of(place * LANES, LANES), LANES)


def columns(block):
    return slice(block * LANES, (block + 1) * LANES)


def lane_low(shape):
    return lax.broadcasted_iota(jnp.int32, shape, len(shape) - 1) % LANES < HEAD_DIM


def rotated(values):
    quarter = HEAD_DIM // 2
    first = lax.broadcasted_iota(jnp.int32, values.shape, 1) % HEAD_DIM < quarter
    return jnp.where(
        first, -pltpu.roll(values, LANES - quarter, 1), pltpu.roll(values, quarter, 1)
    )


def pack_weight(weight, gain_one, gain_two, table):
    def kernel(_, ins, pieces, outs, scratch):
        weight_ref, one_ref, two_ref = ins
        width = weight_ref.shape[1]
        outs[0][:, :width] = weight_ref[...]
        lane = lax.broadcasted_iota(jnp.int32, (weight_ref.shape[0], LANES), 1)
        block = jnp.where(lane == 0, one_ref[...], jnp.where(lane == 1, two_ref[...], 0.0))
        outs[0][:, width:] = block.astype(BF16)

    rows, width = weight.shape
    gains = [g.astype(F32)[:, None] for g in (gain_one, gain_two)]
    return call(kernel, table, [weight, *gains], [shaped((rows, width + LANES), BF16)])[0]


def project(ring, hidden, cosine, sine, pieces, width, others):
    size = ring.size
    rows, model = hidden.shape
    qsize = HEADS * HEAD_DIM
    step = 2 * LANES

    def kernel(table, ins, refs, outs, scratch):
        hidden_ref, cos_ref, sin_ref = ins
        q_ref, kv_ref, input_ref, factor_ref, gain_ref = outs
        buffer, sems = scratch
        copies = fetches(pieces, refs, buffer, sems)
        for copy in copies:
            copy.start()
        values = hidden_ref[...].astype(F32)
        factor = lax.rsqrt(jnp.mean(values * values, -1, keepdims=True) + EPS)
        factor_ref[...] = jnp.broadcast_to(factor, factor_ref.shape)
        for copy in copies:
            copy.wait()
        for k in range(size):
            gains = jnp.transpose(buffer[k, :, width : width + LANES].astype(F32))
            gain_ref[:, columns(k)] = gains[:8]
            part = hidden_ref[:, block_at(table[ring.near + k])].astype(F32)
            input_ref[:, columns(k)] = (part * factor * gains[:1]).astype(BF16)
        inputs = input_ref[...]
        for start in range(0, qsize, step):
            weights = buffer[:, :, start : start + step].reshape(model, step)
            q_ref[:, start : start + step] = dot(inputs, weights)
        weights = buffer[:, :, qsize:width].reshape(model, width - qsize)
        proj = dot(inputs, weights)
        for pair in range(KV_HEADS // 2):
            keys = proj[:, columns(pair)]
            keys = keys * cos_ref[...] + rotated(keys) * sin_ref[...]
            heads = proj[:, columns(KV_HEADS // 2 + pair)]
            low = lane_low(keys.shape)
            one = jnp.where(low, keys, pltpu.roll(heads, HEAD_DIM, 1))
            two = jnp.where(low, pltpu.roll(keys, HEAD_DIM, 1), heads)
            kv_ref[:, columns(2 * pair)] = one.astype(BF16)
            kv_ref[:, columns(2 * pair + 1)] = two.astype(BF16)

    return call(
        kernel,
        ring.table,
        [hidden, cosine, sine],
        [
            shaped((rows, qsize), F32),
            shaped((rows, KV_HEADS * LANES), BF16),
            shaped((rows, model), BF16),
            shaped((rows, LANES), F32),
            shaped((8, model), F32),
        ],
        [piece for _, _, piece in pieces],
        [
            pltpu.VMEM((size, rows, width + LANES), BF16),
            pltpu.SemaphoreType.DMA((len(pieces),)),
        ],
        others,
    )


def stack_blocks(ring, pieces, others):
    rows, width = pieces[0][2].shape

    def body(*refs):
        copies = fetches(pieces, refs[: len(pieces)], refs[-2], refs[-1])
        for copy in copies:
            copy.start()
        for copy in copies:
            copy.wait()

    return pl.pallas_call(
        body,
        in_specs=[HELD] * (len(pieces) + len(others)),
        out_specs=pl.BlockSpec(memory_space=pltpu.VMEM),
        out_shape=shaped((ring.chips, rows, width), pieces[0][2].dtype),
        scratch_shapes=[pltpu.SemaphoreType.DMA((len(pieces),))],
        compiler_params=ROOMY,
    )(*[piece for _, _, piece in pieces], *others)


def project_out(ring, attended, hidden, gains, pieces, others):
    size = ring.size
    rows, model = hidden.shape
    step = 2 * LANES

    def kernel(table, ins, refs, outs, scratch):
        att_ref, hidden_ref, gain_ref = ins
        residual_ref, factor_ref, input_ref = outs
        buffer, sems = scratch
        copies = fetches(pieces, refs, buffer, sems)
        for copy in copies:
            copy.start()
        for copy in copies:
            copy.wait()
        inputs = att_ref[...]
        squares = jnp.zeros((rows, 1), F32)
        for start in range(0, model, step):
            weights = buffer[:, :, start : start + step].reshape(model, step)
            part = hidden_ref[:, start : start + step].astype(F32) + dot(inputs, weights)
            residual_ref[:, start : start + step] = part
            squares += jnp.sum(part * part, -1, keepdims=True)
        factor = lax.rsqrt(squares * (1.0 / model) + EPS)
        factor_ref[...] = jnp.broadcast_to(factor, factor_ref.shape)
        for k in range(size):
            device = table[ring.cores + k]
            gain = gain_ref[1:2, block_at(table[ring.place_near + device])]
            part = residual_ref[:, block_at(device)] * factor
            input_ref[:, columns(k)] = (part * gain).astype(BF16)

    return call(
        kernel,
        ring.table,
        [attended, hidden, gains],
        [shaped((rows, model), F32), shaped((rows, LANES), F32), shaped((rows, model), BF16)],
        [piece for _, _, piece in pieces],
        [
            pltpu.VMEM((size, rows, model), BF16),
            pltpu.SemaphoreType.DMA((len(pieces),)),
        ],
        others,
    )


def back_out(ring, grad_two, residual, factor, gains, cot, pieces, others):
    size = ring.size
    rows, model = residual.shape

    def kernel(table, ins, refs, outs, scratch):
        grad_ref, residual_ref, factor_ref, gain_ref, cot_ref = ins
        grad_res_ref, half_ref, att_ref, term_ref = outs
        buffer, sems = scratch
        copies = fetches(pieces, refs, buffer, sems)
        for copy in copies:
            copy.start()
        factor = factor_ref[...]
        mean = jnp.zeros((rows, 1), F32)
        for d in range(size):
            place = block_at(table[ring.place_near + d])
            grad = grad_ref[:, block_at(table[ring.place_cores + d])]
            normed = residual_ref[:, columns(d)] * factor
            product = grad * normed
            term_ref[:, place] = jnp.broadcast_to(
                jnp.sum(product, 0, keepdims=True), (8, LANES)
            )
            mean += jnp.sum(product * gain_ref[1:2, place], -1, keepdims=True)
        mean *= 1.0 / model
        for d in range(size):
            place = block_at(table[ring.place_near + d])
            grad = grad_ref[:, block_at(table[ring.place_cores + d])] * gain_ref[1:2, place]
            normed = residual_ref[:, columns(d)] * factor
            total = cot_ref[:, columns(d)].astype(F32) + factor * (grad - normed * mean)
            grad_res_ref[:, columns(d)] = total
            half_ref[:, columns(d)] = total.astype(BF16)
        for copy in copies:
            copy.wait()
        halves = half_ref[...]
        for k in range(0, size, 2):
            weights = buffer[k : k + 2].reshape(2 * rows, model)
            att_ref[:, k * LANES : (k + 2) * LANES] = dot(halves, weights, LAST).astype(BF16)

    return call(
        kernel,
        ring.table,
        [grad_two, residual, factor, gains, cot],
        [
            shaped((rows, model), F32),
            shaped((rows, model), BF16),
            shaped((rows, model), BF16),
            shaped((8, model), F32),
        ],
        [piece for _, _, piece in pieces],
        [
            pltpu.VMEM((size, rows, model), BF16),
            pltpu.SemaphoreType.DMA((len(pieces),)),
        ],
        others,
    )


def finish_kv(ring, grad, cosine, sine, others):
    def kernel(table, ins, refs, outs, scratch):
        grad_ref, cos_ref, sin_ref = ins
        for pair in range(KV_HEADS // 2):
            one = grad_ref[:, columns(2 * pair)]
            two = grad_ref[:, columns(2 * pair + 1)]
            low = lane_low(one.shape)
            keys = jnp.where(low, one, pltpu.roll(two, HEAD_DIM, 1))
            values = jnp.where(low, pltpu.roll(one, HEAD_DIM, 1), two)
            keys = keys * cos_ref[...] - rotated(keys) * sin_ref[...]
            outs[0][:, columns(pair)] = keys.astype(BF16)
            outs[0][:, columns(KV_HEADS // 2 + pair)] = values.astype(BF16)

    rows = grad.shape[0]
    return call(
        kernel,
        ring.table,
        [grad, cosine, sine],
        [shaped((rows, 2 * KV_HEADS * HEAD_DIM), BF16)],
        others=others,
    )[0]


def back_project(
    ring, grad_queries, grad_kv, hidden, factor, gains, grad_residual, pieces, width, others
):
    size = ring.size
    rows, model = hidden.shape
    qsize = grad_queries.shape[1]

    def kernel(table, ins, refs, outs, scratch):
        gq_ref, gkv_ref, hidden_ref, factor_ref, gain_ref, grad_res_ref = ins
        grad_ref, term_ref = outs
        buffer, sems, total = scratch
        copies = fetches(pieces, refs, buffer, sems)
        for copy in copies:
            copy.start()
        for copy in copies:
            copy.wait()
        queries, keys = gq_ref[...], gkv_ref[...]
        for k in range(0, size, 2):
            weights = buffer[k : k + 2].reshape(2 * rows, width + LANES)
            total[:, k * LANES : (k + 2) * LANES] = dot(
                queries, weights[:, :qsize], LAST
            ) + dot(keys, weights[:, qsize:width], LAST)
        factor = factor_ref[...]
        mean = jnp.zeros((rows, 1), F32)
        for k in range(size):
            normed = hidden_ref[:, block_at(table[ring.near + k])].astype(F32) * factor
            product = total[:, columns(k)] * normed
            term_ref[:, columns(k)] = jnp.broadcast_to(
                jnp.sum(product, 0, keepdims=True), (8, LANES)
            )
            mean += jnp.sum(product * gain_ref[:1, columns(k)], -1, keepdims=True)
        mean *= 1.0 / model
        for k in range(size):
            place = block_at(table[ring.near + k])
            normed = hidden_ref[:, place].astype(F32) * factor
            scaled = total[:, columns(k)] * gain_ref[:1, columns(k)]
            back = grad_res_ref[:, place] + factor * (scaled - normed * mean)
            grad_ref[:, place] = back.astype(BF16)

    return call(
        kernel,
        ring.table,
        [grad_queries, grad_kv, hidden, factor, gains, grad_residual],
        [shaped((rows, model), BF16), shaped((8, model), F32)],
        [piece for _, _, piece in pieces],
        [
            pltpu.VMEM((size, rows, width + LANES), BF16),
            pltpu.SemaphoreType.DMA((len(pieces),)),
            pltpu.VMEM((rows, model), F32),
        ],
        others,
    )


def cut_columns(ring, weight, wide):
    rows = weight.shape[0]
    half = rows // 2

    def kernel(table, ins, refs, outs, scratch):
        upper = table[ring.side_at] == 0
        for chip in range(ring.chips):
            for part in range(2):
                start = (part * ring.chips + chip) * wide
                block = ins[0][:, start : start + wide].astype(F32)
                outs[0][chip, part] = jnp.where(upper, block[:half], block[half:]).astype(BF16)

    return call(
        kernel, ring.table, [weight], [shaped((ring.chips, 2, half, wide), BF16)]
    )[0]


def join_columns(ring, mine, theirs):
    chips, parts, half, wide = mine.shape

    def kernel(table, ins, refs, outs, scratch):
        flip = table[ring.side_at] == 0
        for chip in range(chips):
            for part in range(parts):
                start = (part * chips + chip) * wide
                one, two = ins[0][chip, part].astype(F32), ins[1][chip, part].astype(F32)
                outs[0][:half, start : start + wide] = jnp.where(flip, one, two)
                outs[0][half:, start : start + wide] = jnp.where(flip, two, one)

    return call(
        kernel,
        ring.table,
        [mine, theirs],
        [shaped((2 * half, parts * chips * wide), F32)],
    )[0]


def give_terms(ring, inputs, grads, others=()):
    tokens, model = inputs.shape
    chips, count, extra = ring.chips, len(grads), len(others)
    rows = model // ring.size

    def body(input_ref, *refs):
        for grad_ref, out_ref in zip(refs[:count], refs[count + extra :]):
            out_ref[...] = dot(input_ref[...], grad_ref[...], FIRST).astype(BF16)

    return pl.pallas_call(
        body,
        grid=(chips,),
        in_specs=[pl.BlockSpec((tokens, rows), lambda i: (0, chips + i))]
        + [whole(g.shape) for g in grads]
        + [HELD] * extra,
        out_specs=[pl.BlockSpec((rows, g.shape[1]), lambda i: (i, 0)) for g in grads],
        out_shape=[shaped((chips * rows, g.shape[1]), BF16) for g in grads],
        compiler_params=ROOMY,
    )(inputs, *grads, *others)


def keep_terms(ring, inputs, grads, gots):
    tokens, model = inputs.shape
    chips, count = ring.chips, len(grads)
    rows = model // ring.size

    def body(input_ref, *refs):
        for part in range(count):
            term = dot(input_ref[...], refs[part][...], FIRST)
            refs[2 * count + part][...] = (term + refs[count + part][...].astype(F32)).astype(BF16)

    blocks = [pl.BlockSpec((rows, g.shape[1]), lambda i: (i, 0)) for g in grads]
    return pl.pallas_call(
        body,
        grid=(chips,),
        in_specs=[pl.BlockSpec((tokens, rows), lambda i: (0, i))]
        + [whole(g.shape) for g in grads]
        + blocks,
        out_specs=blocks,
        out_shape=[shaped((chips * rows, g.shape[1]), BF16) for g in grads],
        compiler_params=ROOMY,
    )(inputs, *grads, *gots)


def halve_terms(ring, inputs, grads, gots):
    tokens, model = inputs.shape
    chips, count = ring.chips, len(grads)
    rows, wide = model // ring.size, grads[0].shape[1]
    half = rows // 2

    def body(table, input_ref, *refs):
        upper = table[ring.side_at] == 0
        keep_ref, give_ref = refs[2 * count :]
        for part in range(count):
            total = dot(input_ref[...], refs[part][...], FIRST)
            total += refs[count + part][...].astype(F32)
            keep_ref[0, part] = jnp.where(upper, total[:half], total[half:])
            give_ref[0, part] = jnp.where(upper, total[half:], total[:half]).astype(BF16)

    return pl.pallas_call(
        body,
        grid_spec=pltpu.PrefetchScalarGridSpec(
            num_scalar_prefetch=1,
            grid=(chips,),
            in_specs=[pl.BlockSpec((tokens, rows), lambda i, _: (0, i))]
            + [whole(g.shape) for g in grads]
            + [pl.BlockSpec((rows, wide), lambda i, _: (i, 0))] * count,
            out_specs=[pl.BlockSpec((1, count, half, wide), lambda i, _: (i, 0, 0, 0))] * 2,
        ),
        out_shape=[shaped((chips, count, half, wide), kind) for kind in (F32, BF16)],
        compiler_params=ROOMY,
    )(ring.table, inputs, *grads, *gots)


def down_terms(ring, activation, cot, others):
    tokens, wide = activation.shape
    model = cot.shape[1]
    step, half = 2 * LANES, wide // 2

    def body(table, act_ref, cot_ref, *refs):
        keep_ref, give_ref = refs[len(others) :]
        total = dot(act_ref[...], cot_ref[...], FIRST)
        first = table[ring.core_at] == 0
        keep_ref[...] = jnp.where(first, total[:half], total[half:])
        give_ref[...] = jnp.where(first, total[half:], total[:half]).astype(BF16)

    return pl.pallas_call(
        body,
        grid_spec=pltpu.PrefetchScalarGridSpec(
            num_scalar_prefetch=1,
            grid=(model // step,),
            in_specs=[whole(activation.shape), pl.BlockSpec((tokens, step), lambda i, _: (0, i))]
            + [HELD] * len(others),
            out_specs=[pl.BlockSpec((half, step), lambda i, _: (0, i))] * 2,
        ),
        out_shape=[shaped((half, model), kind) for kind in (F32, BF16)],
        compiler_params=ROOMY,
    )(ring.table, activation, cot, *others)


def down_project(activation, down, others):
    tokens, wide = activation.shape
    model = down.shape[1]
    step = 2 * LANES

    def body(act_ref, down_ref, *refs):
        refs[-1][...] = dot(act_ref[...], down_ref[...]).astype(BF16)

    return pl.pallas_call(
        body,
        grid=(tokens // step,),
        in_specs=[pl.BlockSpec((step, wide), lambda i: (i, 0)), whole(down.shape)]
        + [HELD] * len(others),
        out_specs=pl.BlockSpec((step, model), lambda i: (i, 0)),
        out_shape=shaped((tokens, model), BF16),
        compiler_params=ROOMY,
    )(activation, down, *others)


def join_rows(ring, mine, theirs):
    rows, wide = mine.shape

    def body(table, mine_ref, theirs_ref, out_ref, sems):
        core = table[ring.core_at]
        copies = []
        for n, (place, ref) in enumerate(((core, mine_ref), (1 - core, theirs_ref))):
            target = out_ref.at[pl.ds(pl.multiple_of(place * rows, 16), rows)]
            copies.append(pltpu.make_async_copy(ref, target, sems.at[n]))
        for copy in copies:
            copy.start()
        for copy in copies:
            copy.wait()

    return pl.pallas_call(
        body,
        grid_spec=pltpu.PrefetchScalarGridSpec(
            num_scalar_prefetch=1,
            grid=(1,),
            in_specs=[HELD] * 2,
            out_specs=whole((2 * rows, wide)),
            scratch_shapes=[pltpu.SemaphoreType.DMA((2,))],
        ),
        out_shape=shaped((2 * rows, wide), mine.dtype),
        compiler_params=ROOMY,
    )(ring.table, mine, theirs)


def feed_forward(ring, twos, cots, weights, down, others):
    chips = ring.chips
    tok, model = twos[0][2].shape
    _, _, half, wide = weights[0].shape
    steps = chips // 2
    chunk = 2 * tok
    count = len(twos)

    def body(table, *refs):
        two_refs, cot_refs = refs[:count], refs[count : 2 * count]
        weight_refs = refs[2 * count : 2 * count + 4]
        down_ref = refs[2 * count + 4]
        outs = refs[2 * count + 5 + len(others) :]
        act_ref, gate_ref, up_ref, grad_ref, two_out, cot_out = outs[:6]
        two_buf, cot_buf, weight_buf, down_buf, two_sems, cot_sems, weight_sems = outs[6:]
        step = pl.program_id(0)
        side = table[ring.side_at]
        moves = [pltpu.make_async_copy(down_ref, down_buf, weight_sems.at[8])]
        for n, ref in enumerate(weight_refs):
            place = side if n % 2 == 0 else 1 - side
            for part in range(2):
                target = weight_buf.at[part, pl.ds(n // 2 * chips, chips), place]
                sem = weight_sems.at[2 * n + part]
                moves.append(pltpu.make_async_copy(ref.at[:, part], target, sem))
        blocks = fetches(twos, two_refs, two_buf, two_sems)
        blocks += fetches(cots, cot_refs, cot_buf, cot_sems)

        @pl.when(step == 0)
        def _():
            for move in moves + blocks:
                move.start()
            for move in moves:
                move.wait()

        for at in range(steps):

            @pl.when(step == at)
            def _():
                for (slot, _, _), block in zip(twos + cots, blocks):
                    if slot // 2 == at:
                        block.wait()

        two = two_buf[pl.ds(step * 2, 2)].reshape(chunk, model)
        cot = cot_buf[pl.ds(step * 2, 2)].reshape(chunk, model)
        two_out[...] = two
        cot_out[...] = cot
        gate_weight = weight_buf[0].reshape(model, wide)
        up_weight = weight_buf[1].reshape(model, wide)
        gate = dot(two, gate_weight)
        upward = dot(two, up_weight)
        grad = dot(cot, down_buf[...], LAST)
        sigma = jax.nn.sigmoid(gate)
        act_ref[...] = (gate * sigma * upward).astype(BF16)
        grad_gate = (grad * upward * (sigma * (1.0 + gate * (1.0 - sigma)))).astype(BF16)
        grad_up = (grad * gate * sigma).astype(BF16)
        gate_ref[...] = grad_gate
        up_ref[...] = grad_up
        grad_two = dot(grad_gate, gate_weight, LAST) + dot(grad_up, up_weight, LAST)
        grad_ref[...] = grad_two.astype(BF16)

    def out(width):
        return pl.BlockSpec((chunk, width), lambda i, _: (i, 0))

    widths = (wide, wide, wide, model, model, model)
    kinds = (BF16,) * 6
    return pl.pallas_call(
        body,
        grid_spec=pltpu.PrefetchScalarGridSpec(
            num_scalar_prefetch=1,
            grid=(steps,),
            in_specs=[HELD] * (2 * count + 5 + len(others)),
            out_specs=[out(w) for w in widths],
            scratch_shapes=[
                pltpu.VMEM((chips, tok, model), BF16),
                pltpu.VMEM((chips, tok, model), BF16),
                pltpu.VMEM((2, 2 * chips, 2, half, wide), BF16),
                pltpu.VMEM(down.shape, BF16),
                pltpu.SemaphoreType.DMA((count,)),
                pltpu.SemaphoreType.DMA((count,)),
                pltpu.SemaphoreType.DMA((9,)),
            ],
        ),
        out_shape=[shaped((chips * tok, w), kind) for w, kind in zip(widths, kinds)],
        compiler_params=ROOMY,
    )(
        ring.table,
        *[piece for _, _, piece in twos],
        *[piece for _, _, piece in cots],
        *weights,
        down,
        *others,
    )


def load_window(table, at, own_ref, other_ref, window, rows):
    chips = own_ref.shape[0]
    for b in range(window.shape[0] // rows):
        place = table[at + b]
        target = window.at[b * rows : (b + 1) * rows, :]

        @pl.when(place < chips)
        def _():
            target[...] = own_ref[place]

        @pl.when(place >= chips)
        def _():
            target[...] = other_ref[place - chips]


def allowed_pairs(first_ref, reach, keys, rows):
    key = lax.broadcasted_iota(jnp.int32, (keys, rows), 0)
    token = lax.broadcasted_iota(jnp.int32, (keys, rows), 1)
    allowed = (key >= first_ref[...]) & (key <= token + reach)
    return jnp.concatenate([allowed, allowed], 1)


def stacked(block, low_side):
    turned = pltpu.roll(block, HEAD_DIM, 1)
    low = lane_low(block.shape)
    if low_side:
        one, two = jnp.where(low, block, 0.0), jnp.where(low, turned, 0.0)
    else:
        one, two = jnp.where(low, 0.0, turned), jnp.where(low, 0.0, block)
    return jnp.concatenate([one, two], 0).astype(BF16)


def attend_kernel(
    ring, table, proj_ref, own_ref, other_ref, first_ref, cos_ref, sin_ref, q_ref, out_ref, log_ref, window
):
    rows = proj_ref.shape[0]
    keys = window.shape[0]

    @pl.when(pl.program_id(1) == 0)
    def _():
        load_window(table, ring.window, own_ref, other_ref, window, rows)

    block = proj_ref[...]
    block = block * cos_ref[...] + rotated(block) * sin_ref[...]
    q_ref[...] = block.astype(BF16)
    queries = stacked(block, True)
    score = dot(window[...], queries, LAST) * SCALE
    allowed = allowed_pairs(first_ref, keys - rows, keys, rows)
    score = jnp.where(allowed, score, -jnp.inf)
    top = jnp.max(score, 0, keepdims=True)
    expon = jnp.exp(score - top)
    total = jnp.sum(expon, 0, keepdims=True)
    log_ref[0] = top + jnp.log(total)
    probs = (expon * (1.0 / total)).astype(BF16)
    out = dot(probs, window[...], FIRST)
    one, two = out[:rows], out[rows:]
    out_ref[...] = jnp.where(lane_low(one.shape), pltpu.roll(one, HEAD_DIM, 1), two).astype(BF16)


def attend_back_kernel(
    ring,
    table,
    q_ref,
    grad_ref,
    att_ref,
    log_ref,
    own_ref,
    other_ref,
    first_ref,
    cos_ref,
    sin_ref,
    gq_ref,
    gown_ref,
    gother_ref,
    window,
    total,
):
    rows = q_ref.shape[0]
    keys = window.shape[0]
    chips = own_ref.shape[0]
    step = pl.program_id(1)

    @pl.when(step == 0)
    def _():
        load_window(table, ring.window, own_ref, other_ref, window, rows)
        total[...] = jnp.zeros_like(total)

    grad = grad_ref[...].astype(F32)
    queries = stacked(q_ref[...].astype(F32), True)
    grads = stacked(grad, False)
    product = jnp.transpose(grad * att_ref[...].astype(F32))
    delta = jnp.concatenate(
        [
            jnp.sum(product[:HEAD_DIM], 0, keepdims=True),
            jnp.sum(product[HEAD_DIM:], 0, keepdims=True),
        ],
        1,
    )
    score = dot(window[...], queries, LAST) * SCALE
    allowed = allowed_pairs(first_ref, keys - rows, keys, rows)
    probs = jnp.where(allowed, jnp.exp(score - log_ref[0]), 0.0)
    grad_probs = dot(window[...], grads, LAST)
    grad_scores = (probs * (grad_probs - delta) * SCALE).astype(BF16)
    total[...] += dot(grad_scores, queries) + dot(probs.astype(BF16), grads)
    grad_queries = dot(grad_scores, window[...], FIRST)
    one, two = grad_queries[:rows], grad_queries[rows:]
    block = jnp.where(lane_low(one.shape), one, pltpu.roll(two, HEAD_DIM, 1))
    gq_ref[...] = (block * cos_ref[...] - rotated(block) * sin_ref[...]).astype(BF16)

    @pl.when(step == pl.num_programs(1) - 1)
    def _():
        gown_ref[...] = jnp.zeros_like(gown_ref)
        gother_ref[...] = jnp.zeros_like(gother_ref)
        for b in range(keys // rows):
            place = table[ring.window + b]
            block = total[b * rows : (b + 1) * rows, :]

            @pl.when(place < chips)
            def _():
                gown_ref[place] = block

            @pl.when(place >= chips)
            def _():
                gother_ref[place - chips] = block.astype(BF16)


def attention_call(kernel, ring, groups, ins, outs, scratch, before, others):
    start, stop = groups
    inner = HEADS // KV_HEADS // 2
    given = len(ins)

    def body(table, *refs):
        kernel(ring, table, *refs[:given], *refs[given + len(before) + len(others) :])

    def spec(entry):
        shape, place = entry
        return pl.BlockSpec(
            shape, lambda g, i, table: place(g + start, (g + start) * inner + i, table)
        )

    return pl.pallas_call(
        body,
        grid_spec=pltpu.PrefetchScalarGridSpec(
            num_scalar_prefetch=1,
            grid=(stop - start, inner),
            in_specs=[spec(entry) for _, entry in ins] + [HELD] * (len(before) + len(others)),
            out_specs=[spec(entry) for _, entry in outs],
            scratch_shapes=scratch,
        ),
        out_shape=[shape for shape, _ in outs],
        input_output_aliases={1 + given + k: k for k in range(len(before))},
        compiler_params=ROOMY,
    )(ring.table, *[value for value, _ in ins], *before, *others)


def attention_specs(ring, rows):
    return (
        ((rows, LANES), lambda g, pair, table: (0, pair)),
        ((rows, LANES), lambda g, pair, table: (0, table[ring.place_near + pair])),
        ((1, 1, 2 * rows), lambda g, pair, table: (pair, 0, 0)),
        ((ring.chips, rows, LANES), lambda g, pair, table: (0, 0, g)),
        ((1, rows), lambda g, pair, table: (0, 0)),
        ((rows, LANES), lambda g, pair, table: (0, 0)),
    )


def attend(ring, groups, others, keys, proj, own, other, first, cosine, sine, before=()):
    rows = proj.shape[0]
    pairs = HEADS // 2
    block, near_block, log_block, kv_block, row, table = attention_specs(ring, rows)
    return attention_call(
        attend_kernel,
        ring,
        groups,
        [(proj, block), (own, kv_block), (other, kv_block)]
        + [(first, row), (cosine, table), (sine, table)],
        [
            (shaped((rows, pairs * LANES), BF16), block),
            (shaped((rows, pairs * LANES), BF16), near_block),
            (shaped((pairs, 1, 2 * rows), F32), log_block),
        ],
        [pltpu.VMEM((keys, LANES), BF16)],
        before,
        others,
    )


def attend_back(
    ring, groups, others, keys, queries, grad, attended, logs, own, other, first, cosine, sine, before=()
):
    rows = queries.shape[0]
    block, near_block, log_block, kv_block, row, table = attention_specs(ring, rows)
    return attention_call(
        attend_back_kernel,
        ring,
        groups,
        [
            (queries, block),
            (grad, near_block),
            (attended, near_block),
            (logs, log_block),
            (own, kv_block),
            (other, kv_block),
            (first, row),
            (cosine, table),
            (sine, table),
        ],
        [
            (shaped(queries.shape, BF16), block),
            (shaped(own.shape, F32), kv_block),
            (shaped(own.shape, BF16), kv_block),
        ],
        [pltpu.VMEM((keys, LANES), BF16), pltpu.VMEM((keys, LANES), F32)],
        before,
        others,
    )


def on_device(
    reps,
    shards,
    hidden_in,
    segments,
    cotangent,
    qkv_weight,
    out_weight,
    gate_up_weight,
    down_weight,
    attn_gain,
    ffn_gain,
):
    tok = hidden_in.shape[1]
    model = hidden_in.shape[2]
    rows, width = qkv_weight.shape
    blocks = min(REACH // tok, shards - 1) + 1
    ring = Ring(shards, blocks)
    chips = ring.chips
    middle = chips * rows
    ff = down_weight.shape[0] * shards
    wide = ff // chips
    half = rows // 2
    side = ring.side
    twin_map = [(i, i ^ 1) for i in range(reps)]
    side_groups = [list(range(s, reps, 2)) for s in range(2)]
    hidden, cot_local, seg_row = hidden_in[0], cotangent[0], segments[0]
    groups = ((0, KV_HEADS // 2), (KV_HEADS // 2, KV_HEADS))

    def twin(value):
        return lax.ppermute(value, "rep", twin_map)

    def rest_of_reps(value):
        if reps == 2:
            return value
        return lax.psum(value, "rep", axis_index_groups=side_groups)

    def over_reps(value):
        mine = rest_of_reps(value).astype(BF16)
        return mine.astype(F32) + twin(mine).astype(F32)

    def cut(value, size):
        return [value[k * size : (k + 1) * size] for k in range(chips)]

    mine = cut_columns(ring, gate_up_weight, wide)
    mine = lax.all_to_all(
        mine, "shard", 0, 0, axis_index_groups=ring.core_groups, tiled=True
    )

    packed = pack_weight(qkv_weight, attn_gain, ffn_gain, ring.table)
    qkv_pieces, qkv_marks = ring.gather_both(packed)

    offset = ring.index * tok
    local_seg = lax.dynamic_slice_in_dim(seg_row, offset, tok)
    starts = jnp.sum((seg_row[None, :] < local_seg[:, None]).astype(jnp.int32), 1)
    positions = offset + jnp.arange(tok, dtype=jnp.int32) - starts
    freqs = jnp.exp(
        (jnp.arange(LANES) % (HEAD_DIM // 2)).astype(F32) * (-2.0 * math.log(10000.0) / HEAD_DIM)
    )
    angles = positions.astype(F32)[:, None] * freqs[None, :]
    cosine, sine = jnp.cos(angles), jnp.sin(angles)
    first = (starts - offset + (blocks - 1) * tok)[None, :]

    proj, kv_local, input_one, factor_one, gains = project(
        ring, hidden, cosine, sine, qkv_pieces, width, (mine,)
    )
    out_pieces, out_marks = ring.gather_both(after(out_weight, *qkv_marks[-2:]))
    kv_own = stack_blocks(ring, ring.gather(kv_local, {2: out_marks[1:3]}), out_marks[3:5])
    kv_other = ring.swap(kv_own)
    theirs = twin(mine)
    cots = ring.gather(after(cot_local, *out_marks[-2:]))
    tables = (kv_own, kv_other, first, cosine, sine)
    keys = blocks * tok
    kept = attend(ring, groups[0], (), keys, proj, *tables)
    kept = attend(ring, groups[1], tuple(out_marks[5:7]), keys, proj, *tables, kept)
    queries, attended, logs = kept
    residual, factor_two, input_two = project_out(ring, attended, hidden, gains, out_pieces, ())

    twos = ring.gather(input_two)
    weights = (mine, theirs, ring.swap(mine), ring.swap(theirs))
    down = join_rows(ring, down_weight, ring.swap(down_weight))
    activation, grad_gate, grad_up, grad_two, two, cot = feed_forward(
        ring, twos, cots, weights, down, ()
    )
    grad_two, two_marks = ring.scatter(cut(grad_two, tok))

    ffn_term = down_project(activation, down, two_marks[0])
    gu_gots = [ring.swap(v) for v in give_terms(ring, two, (grad_gate, grad_up), (ffn_term,))]
    down_keep, down_give = down_terms(ring, activation, cot, two_marks[1])
    down_keep = rest_of_reps(down_keep + ring.swap(down_give).astype(F32)).astype(BF16)
    gu_keep, gu_give = halve_terms(ring, two, (grad_gate, grad_up), gu_gots)
    gu_recv = twin(gu_give)
    gu_sum = rest_of_reps(gu_keep + gu_recv.astype(F32)).astype(BF16)
    down_recv = twin(down_keep)
    grad_down = down_keep.astype(F32) + down_recv.astype(F32)

    grad_residual, residual_half, grad_attended, gain_two_term = back_out(
        ring,
        grad_two,
        residual,
        factor_two,
        gains,
        cot_local,
        out_pieces,
        (ffn_term, gu_give),
    )
    (out_give,) = give_terms(ring, attended, (residual_half,))
    out_got = ring.swap(out_give)
    tables = (logs, kv_own, kv_other, first, cosine, sine)

    done = []

    def ffn_ties(step, marks):
        if step == 1:
            return two_marks[-1]
        if step == 2:
            return ()
        others = {3: (*marks[0], out_give), 4: (*marks[1], gu_sum)}[step]
        before = done[-1] if done else ()
        done.append(
            attend_back(
                ring, groups[step - 3], others, keys, queries, grad_attended, attended, *tables, before
            )
        )
        return (done[-1][0],)

    ffn_out, ffn_marks = ring.scatter(cut(ffn_term, tok), ffn_ties)
    hidden_out = (residual + ffn_out).astype(BF16)
    grad_queries, kv_keep, kv_give = done[-1]
    out_keep, out_send = halve_terms(ring, attended, (residual_half,), (out_got,))
    out_recv = twin(out_send)
    gu_sum = lax.all_to_all(
        gu_sum, "shard", 0, 0, axis_index_groups=ring.core_groups, tiled=True
    )
    (query_give,) = give_terms(ring, input_one, (grad_queries,))
    kv_give = after(kv_give, query_give, out_send)
    kv_keep = kv_keep + ring.swap(kv_give).astype(F32)
    query_got = ring.swap(query_give)
    (query_term,) = keep_terms(ring, input_one, (grad_queries,), (query_got,))
    query_sum, query_marks = ring.scatter(cut(query_term, rows))

    def kv_ties(step, marks):
        return {3: (query_got,), 4: query_marks[0]}.get(step, ())

    grad_kv, kv_marks = ring.scatter([kv_keep[k] for k in range(chips)], kv_ties)
    out_term = (out_keep + out_recv.astype(F32)).astype(BF16).reshape(chips * half, model)
    out_sum, out_marks = ring.scatter(cut(after(out_term, *ffn_marks[3]), half))
    grad_kv = finish_kv(
        ring, grad_kv, cosine, sine, (*query_marks[1], *ffn_marks[3], *out_marks[0], gu_sum)
    )
    (kv_give,) = give_terms(ring, input_one, (grad_kv,))
    (kv_term,) = keep_terms(ring, input_one, (grad_kv,), (ring.swap(kv_give),))
    gu_other = twin(gu_sum)
    grad_hidden, gain_one_term = back_project(
        ring,
        grad_queries,
        grad_kv,
        hidden,
        factor_one,
        gains,
        grad_residual,
        qkv_pieces,
        width,
        (*out_marks[1], *query_marks[2]),
    )
    gain_terms = jnp.concatenate([gain_one_term[:1], gain_two_term[:1]], 0)
    gain_terms = gain_terms[:, :middle] + ring.swap(gain_terms[:, middle:])
    below = gain_terms.reshape(2, chips, rows).transpose(1, 0, 2).reshape(chips, 1, 2 * rows)
    below = jnp.pad(below, ((0, 0), (0, 15), (0, kv_term.shape[1] - 2 * rows)))
    below = below.astype(BF16)
    parts = [jnp.concatenate([part, below[k]], 0) for k, part in enumerate(cut(kv_term, rows))]
    kv_sum, _ = ring.scatter(parts)
    kv_sum = over_reps(kv_sum)
    grad_qkv = jnp.concatenate([over_reps(query_sum), kv_sum[:rows]], 1)
    out_sum = rest_of_reps(out_sum).astype(BF16)
    out_other = twin(out_sum)
    grad_out = jnp.concatenate([pick(side, out_sum, out_other), pick(side, out_other, out_sum)], 0)
    return (
        hidden_out[None],
        grad_hidden[None],
        grad_qkv,
        grad_out.astype(F32),
        join_columns(ring, gu_sum, gu_other),
        grad_down,
        kv_sum[rows, :rows],
        kv_sum[rows, rows : 2 * rows],
    )


def solution(mesh):
    reps, shards = mesh.shape["rep"], mesh.shape["shard"]

    def layer(*args):
        return on_device(reps, shards, *args)

    return jax.shard_map(
        layer,
        mesh=mesh,
        in_specs=(
            P("rep", "shard", None),
            P("rep", None),
            P("rep", "shard", None),
            P("shard", None),
            P("shard", None),
            P("shard", None),
            P("shard", None),
            P("shard"),
            P("shard"),
        ),
        out_specs=(
            P("rep", "shard", None),
            P("rep", "shard", None),
            P("shard", None),
            P("shard", None),
            P("shard", None),
            P("shard", None),
            P("shard"),
            P("shard"),
        ),
        check_vma=False,
    )
```

time: 948 us -> 759 us (0.80)
  Pallas kernels: 51.4 us -> 225 us
  local copies, waits for them, and re-layouts: 186 us -> 39 us
  matrix products: 115 us -> 0 us
  waiting for transfers between devices: 341 us -> 291 us
  other arithmetic: 93.8 us -> 67.8 us
  blocking collectives: 21.8 us -> 0 us
    pallas_call x4 -> x41, Pallas kernels: 51.4 us -> 225 us  [the longest x4 57.2 us: attention_call(): pl.pallas_call(body, grid_spec=pltpu.PrefetchScalarGridSpec(num_scalar_pr...]
    dot_general x47 -> x0, matrix products: 115 us -> none  [dot(): return lax.dot_general(a, b, (dims, ((), ())), preferred_element_type=F32)]
    ppermute x40 -> x48, waiting for transfers between devices: 171 us -> 73.4 us  [the longest x24 41.3 us: scatter(): cw = lax.ppermute(cw, 'shard', self.ahead)]
    ppermute x15, waiting for transfers between devices: 44.7 us -> 132 us  [gather(): ccw = lax.ppermute(ccw, 'shard', self.back)]
    unnamed x382 -> x161, local copies, waits for them, and re-layouts: 66.3 us -> 12 us
    concatenate x21 -> x0, local copies, waits for them, and re-layouts: 50.9 us -> none  [the longest x4 39.6 us: with_gain(): return jnp.concatenate([term, extra], 1)]
    reshape x8 -> x1, local copies, waits for them, and re-layouts: 29.2 us -> 0.01 us  [on_device(): gain_terms.reshape(2, chips, rows).transpose(1, 0, 2)]
    convert_element_type x20 -> x23, other arithmetic: 14.5 us -> 37.2 us  [the longest x18 24.4 us: scatter(): cw, ccw = (ahead.astype(BF16), back.astype(BF16))]
  transfers between devices with their start and end apart: 119 -> 128, of which waited for: 58 -> 43; matrix products, arithmetic and copies ran while one was open for 38% -> 11% of each run, Pallas kernels for 5% -> 24%
where the time goes in v2:
time: 759 us; the launch traced here: 749 us
  waiting for transfers between devices  291 us (38%)
  Pallas kernels  225 us (30%)
  starting transfers between devices  124 us (16%)
  other arithmetic  67.8 us (9%)
  local copies, waits for them, and re-layouts  39 us (5%)
    ppermute x15, waiting for transfers between devices, gather(): ccw = lax.ppermute(ccw, 'shard', self.back)  132 us
    ppermute x8, waiting for transfers between devices, twin(): return lax.ppermute(value, 'rep', twin_map)  58 us
    pallas_call x4, Pallas kernels, attention_call(): pl.pallas_call(body, grid_spec=pltpu.PrefetchScalarGridSpec(num_scalar_pr...  57.2 us
    pallas_call x8, Pallas kernels, call(): pl.pallas_call(body, grid_spec=pltpu.PrefetchScalarGridSpec(num_scalar_pr...  53.7 us
    ppermute x24, waiting for transfers between devices, scatter(): cw = lax.ppermute(cw, 'shard', self.ahead)  41.3 us
    ppermute x24, waiting for transfers between devices, scatter(): ccw = lax.ppermute(ccw, 'shard', self.back)  32.1 us
    pallas_call x1, Pallas kernels, feed_forward(): pl.pallas_call(body, grid_spec=pltpu.PrefetchScalarGridSpec(num_scalar_pr...  28.6 us
    ppermute x24, starting transfers between devices, scatter(): cw = lax.ppermute(cw, 'shard', self.ahead)  28.1 us
  transfers between devices with their start and end apart: 128, of which 43 were waited for; matrix products, arithmetic and copies ran while one was open for 11% of the time, Pallas kernels for 24%

profile of v2, /device:TPU:0, one launch (start us, length us, event | category | flops | bytes accessed | tf_op | source)
XLA Modules:
  0.0 748.6 jit_solution(15120502710264831467)
XLA Ops:
  12.3 15.6 %collective-permute-done.1.refs_5_.refs_8_ = bf16[128,2688]{1,0:T(8,128)(2,1)S(1)} collective-permute-done((bf16[128,2688]{1,0:T(8,128)(2,1)}, bf16[128,2688]{1,0:T(8,128)(2,1)S(1)}, u32[]{:S(2)}, u32[]{:S(2)}) %collective-permute-start.1) | collective-permute-done | bytes 688160 | tf_op jit(solution)/shard_map/ppermute | solution.py:93
  30.0 4.1 shard_map.162
  34.1 6.1 all-to-all-start
  40.3 10.6 %collective-permute-done.3.refs_7_.refs_10_ = bf16[128,2688]{1,0:T(8,128)(2,1)} collective-permute-done((bf16[128,2688]{1,0:T(8,128)(2,1)S(1)}, bf16[128,2688]{1,0:T(8,128)(2,1)}, u32[]{:S(2)}, u32[]{:S(2)}) %collective-permute-start.3) | collective-permute-done | bytes 688160 | tf_op jit(solution)/shard_map/ppermute | solution.py:93
  54.9 29.8 %collective-permute-done.5.refs_9_.refs_12_ = bf16[128,2688]{1,0:T(8,128)(2,1)S(1)} collective-permute-done((bf16[128,2688]{1,0:T(8,128)(2,1)}, bf16[128,2688]{1,0:T(8,128)(2,1)S(1)}, u32[]{:S(2)}, u32[]{:S(2)}) %collective-permute-start.5) | collective-permute-done | bytes 688160 | tf_op jit(solution)/shard_map/ppermute | solution.py:93
  87.6 7.2 collective-permute-start.6
  94.8 8.6 %collective-permute-done.7.refs_11_.refs_2_.refs_14_ = bf16[64,2688]{1,0:T(8,128)(2,1)S(1)} collective-permute-done((bf16[64,2688]{1,0:T(8,128)(2,1)S(1)}, bf16[64,2688]{1,0:T(8,128)(2,1)S(1)}, u32[]{:S(2)}, u32[]{:S(2)}) %collective-permute-start.7) | collective-permute-done | bytes 344096 | tf_op jit(solution)/shard_map/ppermute | solution.py:96
  108.5 10.3 %collective-permute-done.20.refs_2_.refs_5_.refs_7_ = bf16[128,2048]{1,0:T(8,128)(2,1)} collective-permute-done((bf16[128,2048]{1,0:T(8,128)(2,1)}, bf16[128,2048]{1,0:T(8,128)(2,1)}, u32[]{:S(2)}, u32[]{:S(2)}) %collective-permute-start.20) | collective-permute-done | bytes 524320 | tf_op jit(solution)/shard_map/ppermute | solution.py:93
  123.7 8.7 %shard_map.163 = (f32[128,2048]{1,0:T(8,128)}, bf16[128,512]{1,0:T(8,128)(2,1)}, bf16[128,2048]{1,0:T(8,128)(2,1)}, f32[128,128]{1,0:T(8,128)}, f32[8,2048]{1,0:T(8,128)}) custom-call(s32[75]{0:T(128)} %dynamic-slice_bitcast_fusion.1.table_ref.table, bf16[128,2048]{1,0:T(8,128)(2,1)} %bitcast.100, f32[128,128]{1,0:T(8,128)} %get-tuple-element.155.refs_1_.refs_4_.refs_7_, ...), custom_call_target="tpu_custom_call" | custom-call | tf_op jit(solution)/shard_map/pallas_call | solution.py:149
  147.2 11.3 %collective-permute-done.24.refs_6_ = bf16[128,512]{1,0:T(8,128)(2,1)S(1)} collective-permute-done((bf16[128,512]{1,0:T(8,128)(2,1)S(1)}, bf16[128,512]{1,0:T(8,128)(2,1)S(1)}, u32[]{:S(2)}, u32[]{:S(2)}) %collective-permute-start.24) | collective-permute-done | bytes 131104 | tf_op jit(solution)/shard_map/ppermute | solution.py:93
  175.1 5.1 collective-permute-done.33.refs_11_.refs_2_.refs_13_
  188.0 14.1 %shard_map.168 = (bf16[128,2048]{1,0:T(8,128)(2,1)}, bf16[128,2048]{1,0:T(8,128)(2,1)}, f32[16,1,256]{2,1,0:T(1,128)}) custom-call(s32[75]{0:T(128)} %dynamic-slice_bitcast_fusion.1.table_ref.table, f32[128,2048]{1,0:T(8,128)} %get-tuple-element.48.refs_0_, bf16[8,128,512]{2,1,0:T(8,128)(2,1)} %shard_map.167.refs_1_.refs_4_, bf16[8,128,512]{2,1,0:T(8,128)(2,1)} %copy-done.1, ...), custom_call_target="tpu_custom_call" | custom-call | tf_op jit(solution)/shard_map/pallas_call | solution.py:889
  202.0 14.1 %shard_map.169 = (bf16[128,2048]{1,0:T(8,128)(2,1)}, bf16[128,2048]{1,0:T(8,128)(2,1)}, f32[16,1,256]{2,1,0:T(1,128)}) custom-call(s32[75]{0:T(128)} %dynamic-slice_bitcast_fusion.1.table_ref.table, f32[128,2048]{1,0:T(8,128)} %get-tuple-element.48.refs_0_, ...), custom_call_target="tpu_custom_call", output_to_operand_aliasing={{0}: (7, {}), {1}: (8, {}), {2}: (9, {})} | custom-call | tf_op jit(solution)/shard_map/pallas_call | solution.py:889
  216.9 7.9 %shard_map.170 = (f32[128,2048]{1,0:T(8,128)}, f32[128,128]{1,0:T(8,128)}, bf16[128,2048]{1,0:T(8,128)(2,1)}) custom-call(s32[75]{0:T(128)} %dynamic-slice_bitcast_fusion.1.table_ref.table, bf16[128,2048]{1,0:T(8,128)(2,1)} %get-tuple-element.53.refs_0_.input_ref.refs_2_, bf16[128,2048]{1,0:T(8,128)(2,1)} %bitcast.101, ...), custom_call_target="tpu_custom_call" | custom-call | tf_op jit(solution)/shard_map/pallas_call | solution.py:149
  229.0 10.9 %collective-permute-done.44.refs_2_ = bf16[128,2048]{1,0:T(8,128)(2,1)S(1)} collective-permute-done((bf16[128,2048]{1,0:T(8,128)(2,1)}, bf16[128,2048]{1,0:T(8,128)(2,1)S(1)}, u32[]{:S(2)}, u32[]{:S(2)}) %collective-permute-start.44) | collective-permute-done | bytes 524320 | tf_op jit(solution)/shard_map/ppermute | solution.py:93
  242.0 9.2 %collective-permute-done.54.refs_13_ = bf16[128,2048]{1,0:T(8,128)(2,1)S(1)} collective-permute-done((bf16[128,2048]{1,0:T(8,128)(2,1)S(1)}, bf16[128,2048]{1,0:T(8,128)(2,1)S(1)}, u32[]{:S(2)}, u32[]{:S(2)}) %collective-permute-start.54) | collective-permute-done | bytes 524320 | tf_op jit(solution)/shard_map/ppermute | solution.py:93
  252.5 8.9 %collective-permute-done.46.refs_4_ = bf16[128,2048]{1,0:T(8,128)(2,1)S(1)} collective-permute-done((bf16[128,2048]{1,0:T(8,128)(2,1)S(1)}, bf16[128,2048]{1,0:T(8,128)(2,1)S(1)}, u32[]{:S(2)}, u32[]{:S(2)}) %collective-permute-start.46) | collective-permute-done | bytes 524320 | tf_op jit(solution)/shard_map/ppermute | solution.py:93
  263.5 11.0 %collective-permute-done.56.refs_15_ = bf16[128,2048]{1,0:T(8,128)(2,1)S(1)} collective-permute-done((bf16[128,2048]{1,0:T(8,128)(2,1)S(1)}, bf16[128,2048]{1,0:T(8,128)(2,1)S(1)}, u32[]{:S(2)}, u32[]{:S(2)}) %collective-permute-start.56) | collective-permute-done | bytes 524320 | tf_op jit(solution)/shard_map/ppermute | solution.py:93
  278.1 8.5 %collective-permute-done.48.refs_6_ = bf16[128,2048]{1,0:T(8,128)(2,1)S(1)} collective-permute-done((bf16[128,2048]{1,0:T(8,128)(2,1)S(1)}, bf16[128,2048]{1,0:T(8,128)(2,1)S(1)}, u32[]{:S(2)}, u32[]{:S(2)}) %collective-permute-start.48) | collective-permute-done | bytes 524320 | tf_op jit(solution)/shard_map/ppermute | solution.py:93
  300.0 28.6 %shard_map.173 = (bf16[1024,704]{1,0:T(8,128)(2,1)}, bf16[1024,704]{1,0:T(8,128)(2,1)}, bf16[1024,704]{1,0:T(8,128)(2,1)}, bf16[1024,2048]{1,0:T(8,128)(2,1)}, b...) custom-call(s32[75]{0:T(128)} %dynamic-slice_bitcast_fusion.1.table_ref.table, ...), custom_call_target="tpu_custom_call" | custom-call | tf_op jit(solution)/shard_map/pallas_call | solution.py:720
  332.0 4.8 collective-permute-done.64.refs_1_
  341.3 9.5 %collective-permute-done.68.refs_1_ = bf16[128,2048]{1,0:T(8,128)(2,1)S(1)} collective-permute-done((bf16[128,2048]{1,0:T(8,128)(2,1)S(1)}, bf16[128,2048]{1,0:T(8,128)(2,1)S(1)}, u32[]{:S(2)}, u32[]{:S(2)}) %collective-permute-start.68) | collective-permute-done | bytes 524320 | tf_op jit(solution)/shard_map/ppermute | solution.py:115
  352.5 8.9 %collective-permute-done.69 = bf16[128,2048]{1,0:T(8,128)(2,1)S(1)} collective-permute-done((bf16[128,2048]{1,0:T(8,128)(2,1)S(1)}, bf16[128,2048]{1,0:T(8,128)(2,1)S(1)}, u32[]{:S(2)}, u32[]{:S(2)}) %collective-permute-start.69) | collective-permute-done | bytes 524320 | tf_op jit(solution)/shard_map/ppermute | solution.py:115
  365.6 7.2 shard_map.174.refs_2_.refs_23_
  372.8 9.0 %shard_map.176 = (bf16[1024,704]{1,0:T(8,128)(2,1)}, bf16[1024,704]{1,0:T(8,128)(2,1)}) custom-call(bf16[1024,2048]{1,0:T(8,128)(2,1)} %get-tuple-element.61.input_ref, bf16[1024,704]{1,0:T(8,128)(2,1)} %get-tuple-element.62.refs_0_, bf16[1024,704]{1,0:T(8,128)(2,1)} %get-tuple-element.63.refs_1_, bf16[1024,2048]{1,0:T(8,128)(2,1)} %shard_map.174.refs_2_.refs_23_), custom_call_target="tpu_custom_call" | custom-call | tf_op jit(solution)/shard_map/pallas_call | solution.py:517
  394.1 11.2 %shard_map.177 = (f32[8,2,64,704]{3,2,1,0:T(8,128)}, bf16[8,2,64,704]{3,2,1,0:T(8,128)(2,1)}) custom-call(s32[75]{0:T(128)} %dynamic-slice_bitcast_fusion.1.table_ref.table, bf16[1024,2048]{1,0:T(8,128)(2,1)} %get-tuple-element.61.input_ref, bf16[1024,704]{1,0:T(8,128)(2,1)} %get-tuple-element.62.refs_0_, bf16[1024,704]{1,0:T(8,128)(2,1)} %get-tuple-element.63.refs_1_, ...), custom_call_target="tpu_custom_call" | custom-call | tf_op jit(solution)/shard_map/pallas_call | solution.py:567
  407.8 10.2 %shard_map.178 = (f32[128,2048]{1,0:T(8,128)}, bf16[128,2048]{1,0:T(8,128)(2,1)}, bf16[128,2048]{1,0:T(8,128)(2,1)}, f32[8,2048]{1,0:T(8,128)}) custom-call(s32[75]{0:T(128)} %dynamic-slice_bitcast_fusion.1.table_ref.table, f32[128,2048]{1,0:T(8,128)} %convert_add_fusion.3.refs_0_, f32[128,2048]{1,0:T(8,128)} %get-tuple-element.55.refs_1_, ...), custom_call_target="tpu_custom_call" | custom-call | tf_op jit(solution)/shard_map/pallas_call | solution.py:149
  418.0 6.4 shard_map.180.refs_11_
  429.0 6.4 collective-permute-done.71.refs_9_
  437.8 10.2 %shard_map.201 = (f32[352,2048]{1,0:T(8,128)}, bf16[352,2048]{1,0:T(8,128)(2,1)}) custom-call(s32[75]{0:T(128)} %dynamic-slice_bitcast_fusion.1.table_ref.table, bf16[1024,704]{1,0:T(8,128)(2,1)} %get-tuple-element.57.act_ref, bf16[1024,2048]{1,0:T(8,128)(2,1)} %get-tuple-element.85.cot_ref, bf16[128,2048]{1,0:T(8,128)(2,1)} %copy-done.33, ...), custom_call_target="tpu_custom_call" | custom-call | tf_op jit(solution)/shard_map/pallas_call | solution.py:594
  450.6 14.5 %shard_map.181 = (bf16[128,2048]{1,0:T(8,128)(2,1)}, f32[8,128,512]{2,1,0:T(8,128)}, bf16[8,128,512]{2,1,0:T(8,128)(2,1)}) custom-call(s32[75]{0:T(128)} %dynamic-slice_bitcast_fusion.1.table_ref.table, bf16[128,2048]{1,0:T(8,128)(2,1)} %get-tuple-element.59.refs_0_, bf16[128,2048]{1,0:T(8,128)(2,1)} %get-tuple-element.67.refs_1_, ...), custom_call_target="tpu_custom_call" | custom-call | tf_op jit(solution)/shard_map/pallas_call | solution.py:889
  471.8 10.8 %collective-permute-done.76 = bf16[128,2048]{1,0:T(8,128)(2,1)S(1)} collective-permute-done((bf16[128,2048]{1,0:T(8,128)(2,1)}, bf16[128,2048]{1,0:T(8,128)(2,1)S(1)}, u32[]{:S(2)}, u32[]{:S(2)}) %collective-permute-start.76) | collective-permute-done | bytes 524320 | tf_op jit(solution)/shard_map/ppermute | solution.py:114
  485.3 14.5 %shard_map.183 = (bf16[128,2048]{1,0:T(8,128)(2,1)}, f32[8,128,512]{2,1,0:T(8,128)}, bf16[8,128,512]{2,1,0:T(8,128)(2,1)}) custom-call(s32[75]{0:T(128)} %dynamic-slice_bitcast_fusion.1.table_ref.table, bf16[128,2048]{1,0:T(8,128)(2,1)} %get-tuple-element.59.refs_0_, ...), custom_call_target="tpu_custom_call", output_to_operand_aliasing={{0}: (10, {}), {1}: (11, {}), {2}: (12, {})} | custom-call | tf_op jit(solution)/shard_map/pallas_call | solution.py:889
  499.8 6.4 shard_map.187.refs_1_
  509.9 9.1 %shard_map.188 = (f32[8,1,64,2048]{3,2,1,0:T(8,128)}, bf16[8,1,64,2048]{3,2,1,0:T(8,128)(2,1)}) custom-call(s32[75]{0:T(128)} %dynamic-slice_bitcast_fusion.1.table_ref.table, bf16[128,2048]{1,0:T(8,128)(2,1)} %get-tuple-element.53.refs_0_.input_ref.refs_2_, bf16[128,2048]{1,0:T(8,128)(2,1)} %get-tuple-element.69.refs_0_, ...), custom_call_target="tpu_custom_call" | custom-call | tf_op jit(solution)/shard_map/pallas_call | solution.py:567
  531.5 24.3 %collective-permute-done.125 = bf16[352,2048]{1,0:T(8,128)(2,1)} collective-permute-done((bf16[352,2048]{1,0:T(8,128)(2,1)S(1)}, bf16[352,2048]{1,0:T(8,128)(2,1)}, u32[]{:S(2)}, u32[]{:S(2)}) %collective-permute-start.125) | collective-permute-done | bytes 1441824 | tf_op jit(solution)/shard_map/ppermute | solution.py:997
  567.1 8.7 %collective-permute-done.85 = bf16[128,512]{1,0:T(8,128)(2,1)S(1)} collective-permute-done((bf16[128,512]{1,0:T(8,128)(2,1)S(1)}, bf16[128,512]{1,0:T(8,128)(2,1)S(1)}, u32[]{:S(2)}, u32[]{:S(2)}) %collective-permute-start.85) | collective-permute-done | bytes 131104 | tf_op jit(solution)/shard_map/ppermute | solution.py:114
  579.7 7.9 %shard_map.191 = bf16[1024,2048]{1,0:T(8,128)(2,1)} custom-call(bf16[128,2048]{1,0:T(8,128)(2,1)} %get-tuple-element.77.input_ref, bf16[128,2048]{1,0:T(8,128)(2,1)} %get-tuple-element.74.refs_1_.refs_0_, bf16[1024,2048]{1,0:T(8,128)(2,1)} %collective-permute-done.86.refs_1_), custom_call_target="tpu_custom_call" | custom-call | tf_op jit(solution)/shard_map/pallas_call | solution.py:540
  591.8 6.9 collective-permute-done.123.refs_1_
  602.6 6.0 shard_map.200
  619.6 22.2 %collective-permute-done.97 = bf16[8,1,64,2048]{3,2,1,0:T(8,128)(2,1)} collective-permute-done((bf16[8,1,64,2048]{3,2,1,0:T(8,128)(2,1)}, bf16[8,1,64,2048]{3,2,1,0:T(8,128)(2,1)}, u32[]{:S(2)}, u32[]{:S(2)}) %collective-permute-start.97) | collective-permute-done | bytes 2097184 | tf_op jit(solution)/shard_map/ppermute | solution.py:997
  641.9 4.9 add_convert_fusion
  665.5 5.5 shard_map.198
  678.9 11.4 %shard_map.197 = (bf16[128,2048]{1,0:T(8,128)(2,1)}, f32[8,2048]{1,0:T(8,128)}) custom-call(s32[75]{0:T(128)} %dynamic-slice_bitcast_fusion.1.table_ref.table, bf16[128,2048]{1,0:T(8,128)(2,1)} %get-tuple-element.74.refs_1_.refs_0_, bf16[128,512]{1,0:T(8,128)(2,1)} %shard_map.196.refs_1_.refs_0_, bf16[128,2048]{1,0:T(8,128)(2,1)} %bitcast.102, ...), custom_call_target="tpu_custom_call" | custom-call | tf_op jit(solution)/shard_map/pallas_call | solution.py:149
  694.6 6.5 collective-permute-done.120
  705.5 6.1 shard_map.199
  731.9 4.3 collective-permute-done.111
  742.1 4.5 collective-permute-done.117
  (503 shorter events, 257.5 us)
Async XLA Ops:
  28.0 23.0 %collective-permute-start.3 = (bf16[128,2688]{1,0:T(8,128)(2,1)S(1)}, bf16[128,2688]{1,0:T(8,128)(2,1)}, u32[]{:S(2)}, u32[]{:S(2)}) collective-permute-start(bf16[128,2688]{1,0:T(8,128)(2,1)S(1)} %collective-permute-done.1.refs_5_.refs_8_), channel_id=1, source_target_pairs={{0,2},{1,3},{2,6},{3,7},{4,0},{5,1},{6,10},{7,11},{8,4},{9,5},{10,... | collective-permute-start | bytes 2064392 | tf_op jit(solution)/shard_map/ppermute | solution.py:93
  29.6 24.6 %collective-permute-start.2 = (bf16[128,2688]{1,0:T(8,128)(2,1)}, bf16[128,2688]{1,0:T(8,128)(2,1)}, u32[]{:S(2)}, u32[]{:S(2)}) collective-permute-start(bf16[128,2688]{1,0:T(8,128)(2,1)} %collective-permute-done.refs_4_.refs_7_), channel_id=1, source_target_pairs={{0,4},{1,5},{2,0},{3,1},{4,8},{5,9},{6,2},{7,3},{8,12},{9,13},{10,... | collective-permute-start | bytes 2064392 | tf_op jit(solution)/shard_map/ppermute | solution.py:92
  34.1 88.1 %all-to-all-start = ((bf16[8,2,64,704]{3,2,1,0:T(8,128)(2,1)}), bf16[8,2,64,704]{3,2,1,0:T(8,128)(2,1)S(1)}, u32[]{:S(2)}, u32[]{:S(2)}) async-start(bf16[8,2,64,704]{3,2,1,0:T(8,128)(2,1)} %shard_map.162), calls=%async_computation | async-start | bytes 3145728 | tf_op jit(solution)/shard_map/all_to_all | solution.py:1012
  50.9 33.8 %collective-permute-start.5 = (bf16[128,2688]{1,0:T(8,128)(2,1)}, bf16[128,2688]{1,0:T(8,128)(2,1)S(1)}, u32[]{:S(2)}, u32[]{:S(2)}) collective-permute-start(bf16[128,2688]{1,0:T(8,128)(2,1)} %collective-permute-done.3.refs_7_.refs_10_), channel_id=1, source_target_pairs={{0,2},{1,3},{2,6},{3,7},{4,0},{5,1},{6,10},{7,11},{8,4},{9,5},{10,... | collective-permute-start | bytes 2064392 | tf_op jit(solution)/shard_map/ppermute | solution.py:93
  54.3 30.5 %collective-permute-start.4 = (bf16[128,2688]{1,0:T(8,128)(2,1)}, bf16[128,2688]{1,0:T(8,128)(2,1)S(1)}, u32[]{:S(2)}, u32[]{:S(2)}) collective-permute-start(bf16[128,2688]{1,0:T(8,128)(2,1)} %collective-permute-done.2.refs_6_.refs_9_), channel_id=1, source_target_pairs={{0,4},{1,5},{2,0},{3,1},{4,8},{5,9},{6,2},{7,3},{8,12},{9,13},{10,... | collective-permute-start | bytes 2064392 | tf_op jit(solution)/shard_map/ppermute | solution.py:92
  54.3 33.3 %collective-permute-start.10 = (bf16[128,2688]{1,0:T(8,128)(2,1)}, bf16[128,2688]{1,0:T(8,128)(2,1)S(1)}, u32[]{:S(2)}, u32[]{:S(2)}) collective-permute-start(bf16[128,2688]{1,0:T(8,128)(2,1)} %copy-done.17), channel_id=1, source_target_pairs={{0,1},{1,0},{2,3},{3,2},{4,5},{5,4},{6,7},{7,6},{8,9},{9,8},{10,11... | collective-permute-start | bytes 2064392 | tf_op jit(solution)/shard_map/ppermute | solution.py:83
  54.3 50.4 %collective-permute-start.9 = (bf16[128,2688]{1,0:T(8,128)(2,1)}, bf16[128,2688]{1,0:T(8,128)(2,1)}, u32[]{:S(2)}, u32[]{:S(2)}) collective-permute-start(bf16[128,2688]{1,0:T(8,128)(2,1)} %collective-permute-done.refs_4_.refs_7_), channel_id=1, source_target_pairs={{0,1},{1,0},{2,3},{3,2},{4,5},{5,4},{6,7},{7,6},{8,9},{9,8},{10,11... | collective-permute-start | bytes 2064392 | tf_op jit(solution)/shard_map/ppermute | solution.py:83
  54.8 52.3 %collective-permute-start.12 = (bf16[128,2688]{1,0:T(8,128)(2,1)}, bf16[128,2688]{1,0:T(8,128)(2,1)}, u32[]{:S(2)}, u32[]{:S(2)}) collective-permute-start(bf16[128,2688]{1,0:T(8,128)(2,1)} %collective-permute-done.3.refs_7_.refs_10_), channel_id=1, source_target_pairs={{0,1},{1,0},{2,3},{3,2},{4,5},{5,4},{6,7},{7,6},{8,9},{9,8},{10,11... | collective-permute-start | bytes 2064392 | tf_op jit(solution)/shard_map/ppermute | solution.py:83
  118.9 23.1 %collective-permute-start.28 = (bf16[128,2048]{1,0:T(8,128)(2,1)}, bf16[128,2048]{1,0:T(8,128)(2,1)}, u32[]{:S(2)}, u32[]{:S(2)}) collective-permute-start(bf16[128,2048]{1,0:T(8,128)(2,1)} %collective-permute-done.20.refs_2_.refs_5_.refs_7_), channel_id=1, source_target_pairs={{0,2},{1,3},{2,6},{3,7},{4,0},{5,1},{6,10},{7,11},{8,4},{9,5},{10,... | collective-permute-start | bytes 1572872 | tf_op jit(solution)/shard_map/ppermute | solution.py:93
  121.1 38.7 %collective-permute-start.34 = (bf16[128,2048]{1,0:T(8,128)(2,1)}, bf16[128,2048]{1,0:T(8,128)(2,1)}, u32[]{:S(2)}, u32[]{:S(2)}) collective-permute-start(bf16[128,2048]{1,0:T(8,128)(2,1)} %shard_map.164.refs_3_.refs_5_), channel_id=1, source_target_pairs={{0,1},{1,0},{2,3},{3,2},{4,5},{5,4},{6,7},{7,6},{8,9},{9,8},{10,11... | collective-permute-start | bytes 1572872 | tf_op jit(solution)/shard_map/ppermute | solution.py:83
  121.1 25.9 %collective-permute-start.27 = (bf16[128,2048]{1,0:T(8,128)(2,1)}, bf16[128,2048]{1,0:T(8,128)(2,1)}, u32[]{:S(2)}, u32[]{:S(2)}) collective-permute-start(bf16[128,2048]{1,0:T(8,128)(2,1)} %collective-permute-done.19.refs_1_.refs_4_.refs_6_), channel_id=1, source_target_pairs={{0,4},{1,5},{2,0},{3,1},{4,8},{5,9},{6,2},{7,3},{8,12},{9,13},{10,... | collective-permute-start | bytes 1572872 | tf_op jit(solution)/shard_map/ppermute | solution.py:92
  141.9 29.4 %collective-permute-start.31 = (bf16[128,2048]{1,0:T(8,128)(2,1)}, bf16[128,2048]{1,0:T(8,128)(2,1)S(1)}, u32[]{:S(2)}, u32[]{:S(2)}) collective-permute-start(bf16[128,2048]{1,0:T(8,128)(2,1)} %collective-permute-done.28.refs_10_.refs_7_.refs_9_), channel_id=1, source_target_pairs={{0,2},{1,3},{2,6},{3,7},{4,0},{5,1},{6,10},{7,11},{8,4},{9,5},{10,... | collective-permute-start | bytes 1572872 | tf_op jit(solution)/shard_map/ppermute | solution.py:93
  147.1 24.3 %collective-permute-start.30 = (bf16[128,2048]{1,0:T(8,128)(2,1)}, bf16[128,2048]{1,0:T(8,128)(2,1)}, u32[]{:S(2)}, u32[]{:S(2)}) collective-permute-start(bf16[128,2048]{1,0:T(8,128)(2,1)} %collective-permute-done.27.refs_9_.refs_6_.refs_8_), channel_id=1, source_target_pairs={{0,4},{1,5},{2,0},{3,1},{4,8},{5,9},{6,2},{7,3},{8,12},{9,13},{10,... | collective-permute-start | bytes 1572872 | tf_op jit(solution)/shard_map/ppermute | solution.py:92
  147.2 26.6 %collective-permute-start.36 = (bf16[128,2048]{1,0:T(8,128)(2,1)}, bf16[128,2048]{1,0:T(8,128)(2,1)S(1)}, u32[]{:S(2)}, u32[]{:S(2)}) collective-permute-start(bf16[128,2048]{1,0:T(8,128)(2,1)} %collective-permute-done.20.refs_2_.refs_5_.refs_7_), channel_id=1, source_target_pairs={{0,1},{1,0},{2,3},{3,2},{4,5},{5,4},{6,7},{7,6},{8,9},{9,8},{10,11... | collective-permute-start | bytes 1572872 | tf_op jit(solution)/shard_map/ppermute | solution.py:83
  182.4 59.6 %collective-permute-start.59 = (bf16[8,2,64,704]{3,2,1,0:T(8,128)(2,1)S(1)}, bf16[8,2,64,704]{3,2,1,0:T(8,128)(2,1)}, u32[]{:S(2)}, u32[]{:S(2)}) collective-permute-start(bf16[8,2,64,704]{3,2,1,0:T(8,128)(2,1)S(1)} %copy-done.3), channel_id=1, source_target_pairs={{0,16},{16,0},{1,17},{17,1},{2,18},{18,2},{3,19},{19,3},{4,20},{20... | collective-permute-start | bytes 4325384 | tf_op jit(solution)/shard_map/ppermute | solution.py:997
  184.7 42.2 %collective-permute-start.52 = (bf16[128,2048]{1,0:T(8,128)(2,1)}, bf16[128,2048]{1,0:T(8,128)(2,1)S(1)}, u32[]{:S(2)}, u32[]{:S(2)}) collective-permute-start(bf16[128,2048]{1,0:T(8,128)(2,1)} %shard_map.171.refs_9_), channel_id=1, source_target_pairs={{0,2},{1,3},{2,6},{3,7},{4,0},{5,1},{6,10},{7,11},{8,4},{9,5},{10,... | collective-permute-start | bytes 1572872 | tf_op jit(solution)/shard_map/ppermute | solution.py:93
  186.5 29.6 %collective-permute-start.42 = (bf16[64,2048]{1,0:T(8,128)(2,1)}, bf16[64,2048]{1,0:T(8,128)(2,1)S(1)}, u32[]{:S(2)}, u32[]{:S(2)}) collective-permute-start(bf16[64,2048]{1,0:T(8,128)(2,1)} %copy-done.21), channel_id=1, source_target_pairs={{0,1},{1,0},{2,3},{3,2},{4,5},{5,4},{6,7},{7,6},{8,9},{9,8},{10,11... | collective-permute-start | bytes 786440 | tf_op jit(solution)/shard_map/ppermute | solution.py:83
  186.5 29.6 %collective-permute-start.41 = (bf16[64,2048]{1,0:T(8,128)(2,1)}, bf16[64,2048]{1,0:T(8,128)(2,1)S(1)}, u32[]{:S(2)}, u32[]{:S(2)}) collective-permute-start(bf16[64,2048]{1,0:T(8,128)(2,1)} %collective-permute-done.32.refs_10_.refs_1_.refs_12_), channel_id=1, source_target_pairs={{0,1},{1,0},{2,3},{3,2},{4,5},{5,4},{6,7},{7,6},{8,9},{9,8},{10,11... | collective-permute-start | bytes 786440 | tf_op jit(solution)/shard_map/ppermute | solution.py:83
  187.0 41.3 %collective-permute-start.51 = (bf16[128,2048]{1,0:T(8,128)(2,1)}, bf16[128,2048]{1,0:T(8,128)(2,1)S(1)}, u32[]{:S(2)}, u32[]{:S(2)}) collective-permute-start(bf16[128,2048]{1,0:T(8,128)(2,1)} %shard_map.171.refs_9_), channel_id=1, source_target_pairs={{0,4},{1,5},{2,0},{3,1},{4,8},{5,9},{6,2},{7,3},{8,12},{9,13},{10,... | collective-permute-start | bytes 1572872 | tf_op jit(solution)/shard_map/ppermute | solution.py:92
  227.0 24.2 %collective-permute-start.54 = (bf16[128,2048]{1,0:T(8,128)(2,1)S(1)}, bf16[128,2048]{1,0:T(8,128)(2,1)S(1)}, u32[]{:S(2)}, u32[]{:S(2)}) collective-permute-start(bf16[128,2048]{1,0:T(8,128)(2,1)S(1)} %collective-permute-done.52.refs_11_), channel_id=1, source_target_pairs={{0,2},{1,3},{2,6},{3,7},{4,0},{5,1},{6,10},{7,11},{8,4},{9,5},{10,... | collective-permute-start | bytes 1572872 | tf_op jit(solution)/shard_map/ppermute | solution.py:93
  228.3 24.3 %collective-permute-start.53 = (bf16[128,2048]{1,0:T(8,128)(2,1)S(1)}, bf16[128,2048]{1,0:T(8,128)(2,1)S(1)}, u32[]{:S(2)}, u32[]{:S(2)}) collective-permute-start(bf16[128,2048]{1,0:T(8,128)(2,1)S(1)} %collective-permute-done.51.refs_10_), channel_id=1, source_target_pairs={{0,4},{1,5},{2,0},{3,1},{4,8},{5,9},{6,2},{7,3},{8,12},{9,13},{10,... | collective-permute-start | bytes 1572872 | tf_op jit(solution)/shard_map/ppermute | solution.py:92
  242.0 48.1 %collective-permute-start.62 = (bf16[352,2048]{1,0:T(8,128)(2,1)}, bf16[352,2048]{1,0:T(8,128)(2,1)S(1)}, u32[]{:S(2)}, u32[]{:S(2)}) collective-permute-start(bf16[352,2048]{1,0:T(8,128)(2,1)} %mine_ref.1), channel_id=1, source_target_pairs={{0,1},{1,0},{2,3},{3,2},{4,5},{5,4},{6,7},{7,6},{8,9},{9,8},{10,11... | collective-permute-start | bytes 4325384 | tf_op jit(solution)/shard_map/ppermute | solution.py:83
  251.2 39.4 %collective-permute-start.60 = (bf16[8,2,64,704]{3,2,1,0:T(8,128)(2,1)S(1)}, bf16[8,2,64,704]{3,2,1,0:T(8,128)(2,1)S(1)}, u32[]{:S(2)}, u32[]{:S(2)}) collective-permute-start(bf16[8,2,64,704]{3,2,1,0:T(8,128)(2,1)S(1)} %copy-done.3), channel_id=1, source_target_pairs={{0,1},{1,0},{2,3},{3,2},{4,5},{5,4},{6,7},{7,6},{8,9},{9,8},{10,11... | collective-permute-start | bytes 4325384 | tf_op jit(solution)/shard_map/ppermute | solution.py:83
  252.5 43.8 %collective-permute-start.61 = (bf16[8,2,64,704]{3,2,1,0:T(8,128)(2,1)}, bf16[8,2,64,704]{3,2,1,0:T(8,128)(2,1)S(1)}, u32[]{:S(2)}, u32[]{:S(2)}) collective-permute-start(bf16[8,2,64,704]{3,2,1,0:T(8,128)(2,1)} %collective-permute-done.59.refs_19_), channel_id=1, source_target_pairs={{0,1},{1,0},{2,3},{3,2},{4,5},{5,4},{6,7},{7,6},{8,9},{9,8},{10,11... | collective-permute-start | bytes 4325384 | tf_op jit(solution)/shard_map/ppermute | solution.py:83
  424.4 85.5 %collective-permute-start.82 = (bf16[1024,2048]{1,0:T(8,128)(2,1)}, bf16[1024,2048]{1,0:T(8,128)(2,1)}, u32[]{:S(2)}, u32[]{:S(2)}) collective-permute-start(bf16[1024,2048]{1,0:T(8,128)(2,1)} %shard_map.180.refs_11_), channel_id=1, source_target_pairs={{0,1},{1,0},{2,3},{3,2},{4,5},{5,4},{6,7},{7,6},{8,9},{9,8},{10,11... | collective-permute-start | bytes 12582920 | tf_op jit(solution)/shard_map/ppermute | solution.py:83
  428.5 40.2 %collective-permute-start.78 = (bf16[8,2,64,704]{3,2,1,0:T(8,128)(2,1)}, bf16[8,2,64,704]{3,2,1,0:T(8,128)(2,1)}, u32[]{:S(2)}, u32[]{:S(2)}) collective-permute-start(bf16[8,2,64,704]{3,2,1,0:T(8,128)(2,1)} %get-tuple-element.66.refs_24_), channel_id=1, source_target_pairs={{0,16},{16,0},{1,17},{17,1},{2,18},{18,2},{3,19},{19,3},{4,20},{20... | collective-permute-start | bytes 4325384 | tf_op jit(solution)/shard_map/ppermute | solution.py:997
  437.4 27.7 %collective-permute-start.72 = (bf16[128,2048]{1,0:T(8,128)(2,1)S(1)}, bf16[128,2048]{1,0:T(8,128)(2,1)S(1)}, u32[]{:S(2)}, u32[]{:S(2)}) collective-permute-start(bf16[128,2048]{1,0:T(8,128)(2,1)S(1)} %pad_maximum_fusion.3), channel_id=1, source_target_pairs={{0,4},{1,5},{2,0},{3,1},{4,8},{5,9},{6,2},{7,3},{8,12},{9,13},{10,... | collective-permute-start | bytes 1572872 | tf_op jit(solution)/shard_map/ppermute | solution.py:114
  448.0 71.5 %collective-permute-start.124 = (bf16[352,2048]{1,0:T(8,128)(2,1)}, bf16[352,2048]{1,0:T(8,128)(2,1)}, u32[]{:S(2)}, u32[]{:S(2)}) collective-permute-start(bf16[352,2048]{1,0:T(8,128)(2,1)} %get-tuple-element.87), channel_id=1, source_target_pairs={{0,1},{1,0},{2,3},{3,2},{4,5},{5,4},{6,7},{7,6},{8,9},{9,8},{10,11... | collective-permute-start | bytes 4325384 | tf_op jit(solution)/shard_map/ppermute | solution.py:83
  448.9 22.8 %collective-permute-start.77 = (bf16[128,2048]{1,0:T(8,128)(2,1)}, bf16[128,2048]{1,0:T(8,128)(2,1)}, u32[]{:S(2)}, u32[]{:S(2)}) collective-permute-start(bf16[128,2048]{1,0:T(8,128)(2,1)} %pad_maximum_fusion.4), channel_id=1, source_target_pairs={{0,2},{1,3},{2,6},{3,7},{4,0},{5,1},{6,10},{7,11},{8,4},{9,5},{10,... | collective-permute-start | bytes 1572872 | tf_op jit(solution)/shard_map/ppermute | solution.py:115
  506.3 71.7 %collective-permute-start.86 = (bf16[1024,2048]{1,0:T(8,128)(2,1)}, bf16[1024,2048]{1,0:T(8,128)(2,1)}, u32[]{:S(2)}, u32[]{:S(2)}) collective-permute-start(bf16[1024,2048]{1,0:T(8,128)(2,1)} %shard_map.187.refs_1_), channel_id=1, source_target_pairs={{0,1},{1,0},{2,3},{3,2},{4,5},{5,4},{6,7},{7,6},{8,9},{9,8},{10,11... | collective-permute-start | bytes 12582920 | tf_op jit(solution)/shard_map/ppermute | solution.py:83
  506.3 55.0 %all-to-all-start.1 = ((bf16[8,2,64,704]{3,2,1,0:T(8,128)(2,1)}), bf16[8,2,64,704]{3,2,1,0:T(8,128)(2,1)S(1)}, u32[]{:S(2)}, u32[]{:S(2)}) async-start(bf16[8,2,64,704]{3,2,1,0:T(8,128)(2,1)} %add_convert_fusion.1.refs_14_), calls=%async_computation.1 | async-start | bytes 3145728 | tf_op jit(solution)/shard_map/all_to_all | solution.py:1098
  522.2 33.7 %collective-permute-start.125 = (bf16[352,2048]{1,0:T(8,128)(2,1)S(1)}, bf16[352,2048]{1,0:T(8,128)(2,1)}, u32[]{:S(2)}, u32[]{:S(2)}) collective-permute-start(bf16[352,2048]{1,0:T(8,128)(2,1)S(1)} %add_convert_fusion.2), channel_id=1, source_target_pairs={{0,16},{16,0},{1,17},{17,1},{2,18},{18,2},{3,19},{19,3},{4,20},{20... | collective-permute-start | bytes 4325384 | tf_op jit(solution)/shard_map/ppermute | solution.py:997
  523.6 40.8 %collective-permute-start.80 = (bf16[128,2048]{1,0:T(8,128)(2,1)S(1)}, bf16[128,2048]{1,0:T(8,128)(2,1)}, u32[]{:S(2)}, u32[]{:S(2)}) collective-permute-start(bf16[128,2048]{1,0:T(8,128)(2,1)S(1)} %copy-done.31), channel_id=1, source_target_pairs={{0,2},{1,3},{2,6},{3,7},{4,0},{5,1},{6,10},{7,11},{8,4},{9,5},{10,... | collective-permute-start | bytes 1572872 | tf_op jit(solution)/shard_map/ppermute | solution.py:115
  529.5 31.7 %collective-permute-start.84 = (bf16[64,512]{1,0:T(8,128)(2,1)}, bf16[64,512]{1,0:T(8,128)(2,1)}, u32[]{:S(2)}, u32[]{:S(2)}) collective-permute-start(bf16[64,512]{1,0:T(8,128)(2,1)} %get-tuple-element.138), channel_id=1, source_target_pairs={{0,4},{1,5},{2,0},{3,1},{4,8},{5,9},{6,2},{7,3},{8,12},{9,13},{10,... | collective-permute-start | bytes 196616 | tf_op jit(solution)/shard_map/ppermute | solution.py:114
  529.9 31.9 %collective-permute-start.91 = (bf16[64,512]{1,0:T(8,128)(2,1)}, bf16[64,512]{1,0:T(8,128)(2,1)}, u32[]{:S(2)}, u32[]{:S(2)}) collective-permute-start(bf16[64,512]{1,0:T(8,128)(2,1)} %get-tuple-element.139), channel_id=1, source_target_pairs={{0,2},{1,3},{2,6},{3,7},{4,0},{5,1},{6,10},{7,11},{8,4},{9,5},{10,... | collective-permute-start | bytes 196616 | tf_op jit(solution)/shard_map/ppermute | solution.py:115
  559.3 30.4 %collective-permute-start.79 = (bf16[128,2048]{1,0:T(8,128)(2,1)}, bf16[128,2048]{1,0:T(8,128)(2,1)S(1)}, u32[]{:S(2)}, u32[]{:S(2)}) collective-permute-start(bf16[128,2048]{1,0:T(8,128)(2,1)} %shard_map.184), channel_id=1, source_target_pairs={{0,4},{1,5},{2,0},{3,1},{4,8},{5,9},{6,2},{7,3},{8,12},{9,13},{10,... | collective-permute-start | bytes 1572872 | tf_op jit(solution)/shard_map/ppermute | solution.py:114
  561.2 37.5 %collective-permute-start.123 = (bf16[8,2,64,704]{3,2,1,0:T(8,128)(2,1)S(1)}, bf16[8,2,64,704]{3,2,1,0:T(8,128)(2,1)}, u32[]{:S(2)}, u32[]{:S(2)}) collective-permute-start(bf16[8,2,64,704]{3,2,1,0:T(8,128)(2,1)S(1)} %all-to-all-done.1.refs_9_.refs_0_), channel_id=1, source_target_pairs={{0,16},{16,0},{1,17},{17,1},{2,18},{18,2},{3,19},{19,3},{4,20},{20... | collective-permute-start | bytes 4325384 | tf_op jit(solution)/shard_map/ppermute | solution.py:997
  566.5 24.7 %collective-permute-start.81 = (bf16[128,2048]{1,0:T(8,128)(2,1)}, bf16[128,2048]{1,0:T(8,128)(2,1)S(1)}, u32[]{:S(2)}, u32[]{:S(2)}) collective-permute-start(bf16[128,2048]{1,0:T(8,128)(2,1)} %shard_map.186), channel_id=1, source_target_pairs={{0,2},{1,3},{2,6},{3,7},{4,0},{5,1},{6,10},{7,11},{8,4},{9,5},{10,... | collective-permute-start | bytes 1572872 | tf_op jit(solution)/shard_map/ppermute | solution.py:115
  575.8 66.0 %collective-permute-start.97 = (bf16[8,1,64,2048]{3,2,1,0:T(8,128)(2,1)}, bf16[8,1,64,2048]{3,2,1,0:T(8,128)(2,1)}, u32[]{:S(2)}, u32[]{:S(2)}) collective-permute-start(bf16[8,1,64,2048]{3,2,1,0:T(8,128)(2,1)} %get-tuple-element.78.refs_2_), channel_id=1, source_target_pairs={{0,16},{16,0},{1,17},{17,1},{2,18},{18,2},{3,19},{19,3},{4,20},{20... | collective-permute-start | bytes 6291464 | tf_op jit(solution)/shard_map/ppermute | solution.py:997
  577.9 30.8 %collective-permute-start.92 = (bf16[128,512]{1,0:T(8,128)(2,1)S(1)}, bf16[128,512]{1,0:T(8,128)(2,1)}, u32[]{:S(2)}, u32[]{:S(2)}) collective-permute-start(bf16[128,512]{1,0:T(8,128)(2,1)S(1)} %pad_maximum_fusion.11), channel_id=1, source_target_pairs={{0,2},{1,3},{2,6},{3,7},{4,0},{5,1},{6,10},{7,11},{8,4},{9,5},{10,... | collective-permute-start | bytes 393224 | tf_op jit(solution)/shard_map/ppermute | solution.py:115
  613.2 43.6 %collective-permute-start.95 = (bf16[128,2048]{1,0:T(8,128)(2,1)}, bf16[128,2048]{1,0:T(8,128)(2,1)S(1)}, u32[]{:S(2)}, u32[]{:S(2)}) collective-permute-start(bf16[128,2048]{1,0:T(8,128)(2,1)} %pad_maximum_fusion.5), channel_id=1, source_target_pairs={{0,4},{1,5},{2,0},{3,1},{4,8},{5,9},{6,2},{7,3},{8,12},{9,13},{10,... | collective-permute-start | bytes 1572872 | tf_op jit(solution)/shard_map/ppermute | solution.py:114
  615.5 41.3 %collective-permute-start.96 = (bf16[128,2048]{1,0:T(8,128)(2,1)}, bf16[128,2048]{1,0:T(8,128)(2,1)S(1)}, u32[]{:S(2)}, u32[]{:S(2)}) collective-permute-start(bf16[128,2048]{1,0:T(8,128)(2,1)} %pad_maximum_fusion.6), channel_id=1, source_target_pairs={{0,2},{1,3},{2,6},{3,7},{4,0},{5,1},{6,10},{7,11},{8,4},{9,5},{10,... | collective-permute-start | bytes 1572872 | tf_op jit(solution)/shard_map/ppermute | solution.py:115
  616.0 32.2 %collective-permute-start.90 = (bf16[128,512]{1,0:T(8,128)(2,1)}, bf16[128,512]{1,0:T(8,128)(2,1)S(1)}, u32[]{:S(2)}, u32[]{:S(2)}) collective-permute-start(bf16[128,512]{1,0:T(8,128)(2,1)} %shard_map.192), channel_id=1, source_target_pairs={{0,4},{1,5},{2,0},{3,1},{4,8},{5,9},{6,2},{7,3},{8,12},{9,13},{10,... | collective-permute-start | bytes 393224 | tf_op jit(solution)/shard_map/ppermute | solution.py:114
  619.1 30.9 %collective-permute-start.94 = (bf16[128,512]{1,0:T(8,128)(2,1)}, bf16[128,512]{1,0:T(8,128)(2,1)}, u32[]{:S(2)}, u32[]{:S(2)}) collective-permute-start(bf16[128,512]{1,0:T(8,128)(2,1)} %shard_map.194), channel_id=1, source_target_pairs={{0,2},{1,3},{2,6},{3,7},{4,0},{5,1},{6,10},{7,11},{8,4},{9,5},{10,... | collective-permute-start | bytes 393224 | tf_op jit(solution)/shard_map/ppermute | solution.py:115
  671.0 33.6 %collective-permute-start.107 = (bf16[1024,512]{1,0:T(8,128)(2,1)}, bf16[1024,512]{1,0:T(8,128)(2,1)S(1)}, u32[]{:S(2)}, u32[]{:S(2)}) collective-permute-start(bf16[1024,512]{1,0:T(8,128)(2,1)} %shard_map.198), channel_id=1, source_target_pairs={{0,1},{1,0},{2,3},{3,2},{4,5},{5,4},{6,7},{7,6},{8,9},{9,8},{10,11... | collective-permute-start | bytes 3145736 | tf_op jit(solution)/shard_map/ppermute | solution.py:83
  675.9 26.6 %collective-permute-start.104 = (bf16[128,2048]{1,0:T(8,128)(2,1)}, bf16[128,2048]{1,0:T(8,128)(2,1)S(1)}, u32[]{:S(2)}, u32[]{:S(2)}) collective-permute-start(bf16[128,2048]{1,0:T(8,128)(2,1)} %get-tuple-element.90), channel_id=1, source_target_pairs={{0,4},{1,5},{2,0},{3,1},{4,8},{5,9},{6,2},{7,3},{8,12},{9,13},{10,... | collective-permute-start | bytes 1572872 | tf_op jit(solution)/shard_map/ppermute | solution.py:114
  677.4 25.1 %collective-permute-start.105 = (bf16[128,2048]{1,0:T(8,128)(2,1)S(1)}, bf16[128,2048]{1,0:T(8,128)(2,1)}, u32[]{:S(2)}, u32[]{:S(2)}) collective-permute-start(bf16[128,2048]{1,0:T(8,128)(2,1)S(1)} %get-tuple-element.91), channel_id=1, source_target_pairs={{0,2},{1,3},{2,6},{3,7},{4,0},{5,1},{6,10},{7,11},{8,4},{9,5},{10,... | collective-permute-start | bytes 1572872 | tf_op jit(solution)/shard_map/ppermute | solution.py:115
  704.0 38.0 %collective-permute-start.106 = (bf16[128,2048]{1,0:T(8,128)(2,1)S(1)}, bf16[128,2048]{1,0:T(8,128)(2,1)S(1)}, u32[]{:S(2)}, u32[]{:S(2)}) collective-permute-start(bf16[128,2048]{1,0:T(8,128)(2,1)S(1)} %add_convert_fusion.3), channel_id=1, source_target_pairs={{0,16},{16,0},{1,17},{17,1},{2,18},{18,2},{3,19},{19,3},{4,20},{20... | collective-permute-start | bytes 1572872 | tf_op jit(solution)/shard_map/ppermute | solution.py:997
  (158 other events, 1801.3 us)

commit v3 on v2

--- a/solution.py
+++ b/solution.py
@@ -20,6 +20,12 @@
 LIMIT = 58 * 1024 * 1024
 ROOMY = pltpu.CompilerParams(vmem_limit_bytes=LIMIT)
 HELD = pl.BlockSpec(memory_space=pl.ANY)
+
+
+def takes(micros):
+    return pl.CostEstimate(
+        flops=int(micros * 1.1e9), bytes_accessed=int(micros * 3.3e6), transcendentals=0
+    )
 
 
 def dot(a, b, dims=((1,), (0,))):
@@ -96,15 +102,16 @@
         low = lax.ppermute(ccw[h:], "shard", self.back)
         return found + [(self.half, 0, top), (self.half, h, low)]
 
-    def gather_both(self, block):
-        own = self.gather(block)
+    def gather_both(self, block, ties=None):
+        own = self.gather(block, ties)
         other = [(k + self.chips, row, self.swap(piece)) for k, row, piece in own]
         return own + other, [piece for _, _, piece in own]
 
     def scatter(self, parts, ties=None):
         n, m = self.chips, self.half
-        h = parts[0].shape[0] // 2
-        cw, ccw = parts[m][:h].astype(BF16), parts[m][h:].astype(BF16)
+        rows = parts.shape[0] // n
+        h = rows // 2
+        cw, ccw = parts[m * rows : m * rows + h], parts[m * rows + h : (m + 1) * rows]
         marks = []
         for k in range(m - 1, -1, -1):
             if ties:
@@ -114,15 +121,41 @@
             cw = lax.ppermute(cw, "shard", self.ahead)
             ccw = lax.ppermute(ccw, "shard", self.back)
             marks.append((cw, ccw))
-            if k == 0:
-                return parts[0].astype(F32) + cw.astype(F32) + ccw.astype(F32), marks
-            ahead, back = parts[k].astype(F32), parts[n - k].astype(F32)
-            if k == m - 1:
-                ahead = jnp.concatenate([ahead[:h] + cw.astype(F32), ahead[h:]], 0)
-                back = jnp.concatenate([back[:h], back[h:] + ccw.astype(F32)], 0)
-            else:
-                ahead, back = ahead + cw.astype(F32), back + ccw.astype(F32)
-            cw, ccw = ahead.astype(BF16), back.astype(BF16)
+            if k > 0:
+                cw, ccw = add_step(parts, rows, k, n - k, cw, ccw)
+        return (parts, cw, ccw), marks
+
+
+def add_step(parts, rows, ahead, back, cw, ccw):
+    width = parts.shape[1]
+    got = cw.shape[0]
+
+    def body(ahead_ref, back_ref, cw_ref, ccw_ref, one_ref, two_ref):
+        if got < rows:
+            one_ref[got:] = ahead_ref[got:]
+            two_ref[: rows - ccw.shape[0]] = back_ref[: rows - ccw.shape[0]]
+        last = rows - ccw.shape[0]
+        one_ref[:got] = (ahead_ref[:got].astype(F32) + cw_ref[...].astype(F32)).astype(BF16)
+        two_ref[last:] = (back_ref[last:].astype(F32) + ccw_ref[...].astype(F32)).astype(BF16)
+
+    return pl.pallas_call(
+        body,
+        grid=(1,),
+        in_specs=[
+            pl.BlockSpec((rows, width), lambda _: (ahead, 0)),
+            pl.BlockSpec((rows, width), lambda _: (back, 0)),
+            whole(cw.shape),
+            whole(ccw.shape),
+        ],
+        out_specs=[whole((rows, width))] * 2,
+        out_shape=[shaped((rows, width), BF16)] * 2,
+        cost_estimate=takes(0.875), compiler_params=ROOMY,
+    )(parts, parts, cw, ccw)
+
+
+def summed(sums):
+    parts, cw, ccw = sums
+    return parts[: cw.shape[0]].astype(F32) + cw.astype(F32) + ccw.astype(F32)
 
 
 def whole(shape):
@@ -133,7 +166,7 @@
     return jax.ShapeDtypeStruct(shape, kind)
 
 
-def call(kernel, table, ins, outs, pieces=(), scratch=(), others=()):
+def call(kernel, table, ins, outs, pieces=(), scratch=(), others=(), cost=3):
     count, more, extra = len(ins), len(pieces), len(others)
 
     def body(table_ref, *refs):
@@ -157,6 +190,7 @@
         ),
         out_shape=list(outs),
         compiler_params=ROOMY,
+        cost_estimate=takes(cost),
     )(table, *ins, *pieces, *others)
 
 
@@ -199,18 +233,19 @@
     )
 
 
-def pack_weight(weight, gain_one, gain_two, table):
-    def kernel(_, ins, pieces, outs, scratch):
-        weight_ref, one_ref, two_ref = ins
-        width = weight_ref.shape[1]
-        outs[0][:, :width] = weight_ref[...]
-        lane = lax.broadcasted_iota(jnp.int32, (weight_ref.shape[0], LANES), 1)
+def pack_weight(weight, gain_one, gain_two):
+    rows, width = weight.shape
+
+    def body(weight_ref, one_ref, two_ref, out_ref):
+        out_ref[:, :width] = weight_ref[...]
+        lane = lax.broadcasted_iota(jnp.int32, (rows, LANES), 1)
         block = jnp.where(lane == 0, one_ref[...], jnp.where(lane == 1, two_ref[...], 0.0))
-        outs[0][:, width:] = block.astype(BF16)
-
-    rows, width = weight.shape
+        out_ref[:, width:] = block.astype(BF16)
+
     gains = [g.astype(F32)[:, None] for g in (gain_one, gain_two)]
-    return call(kernel, table, [weight, *gains], [shaped((rows, width + LANES), BF16)])[0]
+    return pl.pallas_call(body, out_shape=shaped((rows, width + LANES), BF16), cost_estimate=takes(3), compiler_params=ROOMY)(
+        weight, *gains
+    )
 
 
 def project(ring, hidden, cosine, sine, pieces, width, others):
@@ -269,6 +304,7 @@
             pltpu.SemaphoreType.DMA((len(pieces),)),
         ],
         others,
+        9,
     )
 
 
@@ -288,7 +324,7 @@
         out_specs=pl.BlockSpec(memory_space=pltpu.VMEM),
         out_shape=shaped((ring.chips, rows, width), pieces[0][2].dtype),
         scratch_shapes=[pltpu.SemaphoreType.DMA((len(pieces),))],
-        compiler_params=ROOMY,
+        cost_estimate=takes(2.5), compiler_params=ROOMY,
     )(*[piece for _, _, piece in pieces], *others)
 
 
@@ -332,25 +368,29 @@
             pltpu.SemaphoreType.DMA((len(pieces),)),
         ],
         others,
-    )
-
-
-def back_out(ring, grad_two, residual, factor, gains, cot, pieces, others):
+        8,
+    )
+
+
+def back_out(ring, sums, residual, factor, gains, cot, pieces, others):
     size = ring.size
     rows, model = residual.shape
 
     def kernel(table, ins, refs, outs, scratch):
-        grad_ref, residual_ref, factor_ref, gain_ref, cot_ref = ins
+        own_ref, cw_ref, ccw_ref, residual_ref, factor_ref, gain_ref, cot_ref = ins
         grad_res_ref, half_ref, att_ref, term_ref = outs
-        buffer, sems = scratch
+        buffer, sems, total = scratch
         copies = fetches(pieces, refs, buffer, sems)
         for copy in copies:
             copy.start()
         factor = factor_ref[...]
         mean = jnp.zeros((rows, 1), F32)
         for d in range(size):
-            place = block_at(table[ring.place_near + d])
-            grad = grad_ref[:, block_at(table[ring.place_cores + d])]
+            place, source = (
+                block_at(table[order + d]) for order in (ring.place_near, ring.place_cores)
+            )
+            grad = sum(ref[:, source].astype(F32) for ref in (own_ref, cw_ref, ccw_ref))
+            total[:, columns(d)] = grad
             normed = residual_ref[:, columns(d)] * factor
             product = grad * normed
             term_ref[:, place] = jnp.broadcast_to(
@@ -360,11 +400,11 @@
         mean *= 1.0 / model
         for d in range(size):
             place = block_at(table[ring.place_near + d])
-            grad = grad_ref[:, block_at(table[ring.place_cores + d])] * gain_ref[1:2, place]
+            grad = total[:, columns(d)] * gain_ref[1:2, place]
             normed = residual_ref[:, columns(d)] * factor
-            total = cot_ref[:, columns(d)].astype(F32) + factor * (grad - normed * mean)
-            grad_res_ref[:, columns(d)] = total
-            half_ref[:, columns(d)] = total.astype(BF16)
+            back = cot_ref[:, columns(d)].astype(F32) + factor * (grad - normed * mean)
+            grad_res_ref[:, columns(d)] = back
+            half_ref[:, columns(d)] = back.astype(BF16)
         for copy in copies:
             copy.wait()
         halves = half_ref[...]
@@ -375,7 +415,7 @@
     return call(
         kernel,
         ring.table,
-        [grad_two, residual, factor, gains, cot],
+        [sums[0][:rows], sums[1], sums[2], residual, factor, gains, cot],
         [
             shaped((rows, model), F32),
             shaped((rows, model), BF16),
@@ -386,17 +426,20 @@
         [
             pltpu.VMEM((size, rows, model), BF16),
             pltpu.SemaphoreType.DMA((len(pieces),)),
+            pltpu.VMEM((rows, model), F32),
         ],
         others,
-    )
-
-
-def finish_kv(ring, grad, cosine, sine, others):
+        3.5,
+    )
+
+
+def finish_kv(ring, sums, cosine, sine, others):
     def kernel(table, ins, refs, outs, scratch):
-        grad_ref, cos_ref, sin_ref = ins
+        own_ref, cw_ref, ccw_ref, cos_ref, sin_ref = ins
+        grad = sum(ref[...].astype(F32) for ref in (own_ref, cw_ref, ccw_ref))
         for pair in range(KV_HEADS // 2):
-            one = grad_ref[:, columns(2 * pair)]
-            two = grad_ref[:, columns(2 * pair + 1)]
+            one = grad[:, columns(2 * pair)]
+            two = grad[:, columns(2 * pair + 1)]
             low = lane_low(one.shape)
             keys = jnp.where(low, one, pltpu.roll(two, HEAD_DIM, 1))
             values = jnp.where(low, pltpu.roll(one, HEAD_DIM, 1), two)
@@ -404,11 +447,11 @@
             outs[0][:, columns(pair)] = keys.astype(BF16)
             outs[0][:, columns(KV_HEADS // 2 + pair)] = values.astype(BF16)
 
-    rows = grad.shape[0]
+    rows = sums[1].shape[0]
     return call(
         kernel,
         ring.table,
-        [grad, cosine, sine],
+        [sums[0][:rows], sums[1], sums[2], cosine, sine],
         [shaped((rows, 2 * KV_HEADS * HEAD_DIM), BF16)],
         others=others,
     )[0]
@@ -465,6 +508,7 @@
             pltpu.VMEM((rows, model), F32),
         ],
         others,
+        4.025,
     )
 
 
@@ -485,7 +529,7 @@
     )[0]
 
 
-def join_columns(ring, mine, theirs):
+def join_columns(ring, mine, theirs, others):
     chips, parts, half, wide = mine.shape
 
     def kernel(table, ins, refs, outs, scratch):
@@ -502,13 +546,19 @@
         ring.table,
         [mine, theirs],
         [shaped((2 * half, parts * chips * wide), F32)],
+        others=others,
     )[0]
+
+
+def step_columns(tokens):
+    return (4 if tokens <= LANES else 2) * LANES
 
 
 def give_terms(ring, inputs, grads, others=()):
     tokens, model = inputs.shape
-    chips, count, extra = ring.chips, len(grads), len(others)
-    rows = model // ring.size
+    count, extra = len(grads), len(others)
+    step = step_columns(tokens)
+    steps = model // 2 // step
 
     def body(input_ref, *refs):
         for grad_ref, out_ref in zip(refs[:count], refs[count + extra :]):
@@ -516,37 +566,71 @@
 
     return pl.pallas_call(
         body,
-        grid=(chips,),
-        in_specs=[pl.BlockSpec((tokens, rows), lambda i: (0, chips + i))]
+        grid=(steps,),
+        in_specs=[pl.BlockSpec((tokens, step), lambda i: (0, steps + i))]
         + [whole(g.shape) for g in grads]
         + [HELD] * extra,
-        out_specs=[pl.BlockSpec((rows, g.shape[1]), lambda i: (i, 0)) for g in grads],
-        out_shape=[shaped((chips * rows, g.shape[1]), BF16) for g in grads],
-        compiler_params=ROOMY,
+        out_specs=[pl.BlockSpec((step, g.shape[1]), lambda i: (i, 0)) for g in grads],
+        out_shape=[shaped((model // 2, g.shape[1]), BF16) for g in grads],
+        cost_estimate=takes(2.1), compiler_params=ROOMY,
     )(inputs, *grads, *others)
 
 
 def keep_terms(ring, inputs, grads, gots):
     tokens, model = inputs.shape
-    chips, count = ring.chips, len(grads)
-    rows = model // ring.size
+    count = len(grads)
+    step = step_columns(tokens)
 
     def body(input_ref, *refs):
         for part in range(count):
             term = dot(input_ref[...], refs[part][...], FIRST)
             refs[2 * count + part][...] = (term + refs[count + part][...].astype(F32)).astype(BF16)
 
-    blocks = [pl.BlockSpec((rows, g.shape[1]), lambda i: (i, 0)) for g in grads]
+    blocks = [pl.BlockSpec((step, g.shape[1]), lambda i: (i, 0)) for g in grads]
     return pl.pallas_call(
         body,
-        grid=(chips,),
-        in_specs=[pl.BlockSpec((tokens, rows), lambda i: (0, i))]
+        grid=(model // 2 // step,),
+        in_specs=[pl.BlockSpec((tokens, step), lambda i: (0, i))]
         + [whole(g.shape) for g in grads]
         + blocks,
         out_specs=blocks,
-        out_shape=[shaped((chips * rows, g.shape[1]), BF16) for g in grads],
-        compiler_params=ROOMY,
+        out_shape=[shaped((model // 2, g.shape[1]), BF16) for g in grads],
+        cost_estimate=takes(1.75), compiler_params=ROOMY,
     )(inputs, *grads, *gots)
+
+
+def merge_terms(ring, inputs, grads, got, halves, halves_got):
+    tokens, model = inputs.shape
+    chips, _, half, wide = halves.shape
+    rows = model // ring.size
+    step = step_columns(tokens)
+    each = step // rows
+    high = rows + half
+
+    def body(input_ref, grad_ref, got_ref, half_ref, half_got_ref, out_ref):
+        term = dot(input_ref[...], grad_ref[...], FIRST)
+        for n in range(each):
+            at = slice(n * rows, (n + 1) * rows)
+            total = term[at] + got_ref[at].astype(F32)
+            out_ref[n * high : n * high + rows] = total.astype(BF16)
+            total = half_ref[n, 0] + half_got_ref[n, 0].astype(F32)
+            out_ref[n * high + rows : (n + 1) * high] = total.astype(BF16)
+
+    block = pl.BlockSpec((each, 1, half, wide), lambda i: (i, 0, 0, 0))
+    return pl.pallas_call(
+        body,
+        grid=(chips // each,),
+        in_specs=[
+            pl.BlockSpec((tokens, step), lambda i: (0, i)),
+            whole(grads.shape),
+            pl.BlockSpec((step, wide), lambda i: (i, 0)),
+            block,
+            block,
+        ],
+        out_specs=pl.BlockSpec((each * high, wide), lambda i: (i, 0)),
+        out_shape=shaped((chips * high, wide), BF16),
+        cost_estimate=takes(2), compiler_params=ROOMY,
+    )(inputs, grads, got, halves, halves_got)
 
 
 def halve_terms(ring, inputs, grads, gots):
@@ -554,28 +638,32 @@
     chips, count = ring.chips, len(grads)
     rows, wide = model // ring.size, grads[0].shape[1]
     half = rows // 2
+    step = step_columns(tokens)
+    each = step // rows
 
     def body(table, input_ref, *refs):
         upper = table[ring.side_at] == 0
         keep_ref, give_ref = refs[2 * count :]
         for part in range(count):
-            total = dot(input_ref[...], refs[part][...], FIRST)
-            total += refs[count + part][...].astype(F32)
-            keep_ref[0, part] = jnp.where(upper, total[:half], total[half:])
-            give_ref[0, part] = jnp.where(upper, total[half:], total[:half]).astype(BF16)
+            term = dot(input_ref[...], refs[part][...], FIRST)
+            for n in range(each):
+                at = slice(n * rows, (n + 1) * rows)
+                total = term[at] + refs[count + part][at].astype(F32)
+                keep_ref[n, part] = jnp.where(upper, total[:half], total[half:])
+                give_ref[n, part] = jnp.where(upper, total[half:], total[:half]).astype(BF16)
 
     return pl.pallas_call(
         body,
         grid_spec=pltpu.PrefetchScalarGridSpec(
             num_scalar_prefetch=1,
-            grid=(chips,),
-            in_specs=[pl.BlockSpec((tokens, rows), lambda i, _: (0, i))]
+            grid=(chips // each,),
+            in_specs=[pl.BlockSpec((tokens, step), lambda i, _: (0, i))]
             + [whole(g.shape) for g in grads]
-            + [pl.BlockSpec((rows, wide), lambda i, _: (i, 0))] * count,
-            out_specs=[pl.BlockSpec((1, count, half, wide), lambda i, _: (i, 0, 0, 0))] * 2,
+            + [pl.BlockSpec((step, wide), lambda i, _: (i, 0))] * count,
+            out_specs=[pl.BlockSpec((each, count, half, wide), lambda i, _: (i, 0, 0, 0))] * 2,
         ),
         out_shape=[shaped((chips, count, half, wide), kind) for kind in (F32, BF16)],
-        compiler_params=ROOMY,
+        cost_estimate=takes(3.15), compiler_params=ROOMY,
     )(ring.table, inputs, *grads, *gots)
 
 
@@ -601,7 +689,7 @@
             out_specs=[pl.BlockSpec((half, step), lambda i, _: (0, i))] * 2,
         ),
         out_shape=[shaped((half, model), kind) for kind in (F32, BF16)],
-        compiler_params=ROOMY,
+        cost_estimate=takes(3.5), compiler_params=ROOMY,
     )(ring.table, activation, cot, *others)
 
 
@@ -620,7 +708,7 @@
         + [HELD] * len(others),
         out_specs=pl.BlockSpec((step, model), lambda i: (i, 0)),
         out_shape=shaped((tokens, model), BF16),
-        compiler_params=ROOMY,
+        cost_estimate=takes(2.45), compiler_params=ROOMY,
     )(activation, down, *others)
 
 
@@ -648,7 +736,7 @@
             scratch_shapes=[pltpu.SemaphoreType.DMA((2,))],
         ),
         out_shape=shaped((2 * rows, wide), mine.dtype),
-        compiler_params=ROOMY,
+        cost_estimate=takes(4), compiler_params=ROOMY,
     )(ring.table, mine, theirs)
 
 
@@ -735,7 +823,7 @@
             ],
         ),
         out_shape=[shaped((chips * tok, w), kind) for w, kind in zip(widths, kinds)],
-        compiler_params=ROOMY,
+        cost_estimate=takes(28), compiler_params=ROOMY,
     )(
         ring.table,
         *[piece for _, _, piece in twos],
@@ -865,14 +953,14 @@
 
             @pl.when(place < chips)
             def _():
-                gown_ref[place] = block
+                gown_ref[place] = block.astype(BF16)
 
             @pl.when(place >= chips)
             def _():
                 gother_ref[place - chips] = block.astype(BF16)
 
 
-def attention_call(kernel, ring, groups, ins, outs, scratch, before, others):
+def attention_call(kernel, ring, groups, ins, outs, scratch, before, others, cost):
     start, stop = groups
     inner = HEADS // KV_HEADS // 2
     given = len(ins)
@@ -897,7 +985,7 @@
         ),
         out_shape=[shape for shape, _ in outs],
         input_output_aliases={1 + given + k: k for k in range(len(before))},
-        compiler_params=ROOMY,
+        cost_estimate=takes(cost), compiler_params=ROOMY,
     )(ring.table, *[value for value, _ in ins], *before, *others)
 
 
@@ -930,6 +1018,7 @@
         [pltpu.VMEM((keys, LANES), BF16)],
         before,
         others,
+        14,
     )
 
 
@@ -955,12 +1044,13 @@
         ],
         [
             (shaped(queries.shape, BF16), block),
-            (shaped(own.shape, F32), kv_block),
+            (shaped(own.shape, BF16), kv_block),
             (shaped(own.shape, BF16), kv_block),
         ],
         [pltpu.VMEM((keys, LANES), BF16), pltpu.VMEM((keys, LANES), F32)],
         before,
         others,
+        5,
     )
 
 
@@ -1005,15 +1095,12 @@
         mine = rest_of_reps(value).astype(BF16)
         return mine.astype(F32) + twin(mine).astype(F32)
 
-    def cut(value, size):
-        return [value[k * size : (k + 1) * size] for k in range(chips)]
-
     mine = cut_columns(ring, gate_up_weight, wide)
     mine = lax.all_to_all(
         mine, "shard", 0, 0, axis_index_groups=ring.core_groups, tiled=True
     )
 
-    packed = pack_weight(qkv_weight, attn_gain, ffn_gain, ring.table)
+    packed = pack_weight(qkv_weight, attn_gain, ffn_gain)
     qkv_pieces, qkv_marks = ring.gather_both(packed)
 
     offset = ring.index * tok
@@ -1030,9 +1117,11 @@
     proj, kv_local, input_one, factor_one, gains = project(
         ring, hidden, cosine, sine, qkv_pieces, width, (mine,)
     )
-    out_pieces, out_marks = ring.gather_both(after(out_weight, *qkv_marks[-2:]))
-    kv_own = stack_blocks(ring, ring.gather(kv_local, {2: out_marks[1:3]}), out_marks[3:5])
+    kv_own = stack_blocks(ring, ring.gather(kv_local), ())
     kv_other = ring.swap(kv_own)
+    out_pieces, out_marks = ring.gather_both(
+        after(out_weight, *qkv_marks[-2:]), {2: (kv_local,), 3: (kv_own,)}
+    )
     theirs = twin(mine)
     cots = ring.gather(after(cot_local, *out_marks[-2:]))
     tables = (kv_own, kv_other, first, cosine, sine)
@@ -1048,75 +1137,61 @@
     activation, grad_gate, grad_up, grad_two, two, cot = feed_forward(
         ring, twos, cots, weights, down, ()
     )
-    grad_two, two_marks = ring.scatter(cut(grad_two, tok))
-
-    ffn_term = down_project(activation, down, two_marks[0])
-    gu_gots = [ring.swap(v) for v in give_terms(ring, two, (grad_gate, grad_up), (ffn_term,))]
-    down_keep, down_give = down_terms(ring, activation, cot, two_marks[1])
-    down_keep = rest_of_reps(down_keep + ring.swap(down_give).astype(F32)).astype(BF16)
+    gu_gives = give_terms(ring, two, (grad_gate, grad_up))
+    gu_gots = [ring.swap(v) for v in gu_gives]
     gu_keep, gu_give = halve_terms(ring, two, (grad_gate, grad_up), gu_gots)
+    ffn_term = down_project(activation, down, (gu_give,))
     gu_recv = twin(gu_give)
     gu_sum = rest_of_reps(gu_keep + gu_recv.astype(F32)).astype(BF16)
+    gu_sum = lax.all_to_all(
+        gu_sum, "shard", 0, 0, axis_index_groups=ring.core_groups, tiled=True
+    )
+    grad_two, two_marks = ring.scatter(
+        grad_two, lambda step, _: {3: (gu_give,), 4: (ffn_term,)}.get(step)
+    )
+    down_keep, down_give = down_terms(ring, activation, cot, two_marks[3])
+    down_keep = rest_of_reps(down_keep + ring.swap(down_give).astype(F32)).astype(BF16)
     down_recv = twin(down_keep)
-    grad_down = down_keep.astype(F32) + down_recv.astype(F32)
 
     grad_residual, residual_half, grad_attended, gain_two_term = back_out(
-        ring,
-        grad_two,
-        residual,
-        factor_two,
-        gains,
-        cot_local,
-        out_pieces,
-        (ffn_term, gu_give),
+        ring, grad_two, residual, factor_two, gains, cot_local, out_pieces, (gu_recv,)
     )
     (out_give,) = give_terms(ring, attended, (residual_half,))
     out_got = ring.swap(out_give)
-    tables = (logs, kv_own, kv_other, first, cosine, sine)
-
-    done = []
-
-    def ffn_ties(step, marks):
-        if step == 1:
-            return two_marks[-1]
-        if step == 2:
-            return ()
-        others = {3: (*marks[0], out_give), 4: (*marks[1], gu_sum)}[step]
-        before = done[-1] if done else ()
-        done.append(
-            attend_back(
-                ring, groups[step - 3], others, keys, queries, grad_attended, attended, *tables, before
-            )
-        )
-        return (done[-1][0],)
-
-    ffn_out, ffn_marks = ring.scatter(cut(ffn_term, tok), ffn_ties)
-    hidden_out = (residual + ffn_out).astype(BF16)
-    grad_queries, kv_keep, kv_give = done[-1]
     out_keep, out_send = halve_terms(ring, attended, (residual_half,), (out_got,))
     out_recv = twin(out_send)
-    gu_sum = lax.all_to_all(
-        gu_sum, "shard", 0, 0, axis_index_groups=ring.core_groups, tiled=True
-    )
+    tables = (logs, kv_own, kv_other, first, cosine, sine)
+    ffn_out, ffn_marks = ring.scatter(ffn_term, lambda step, _: two_marks[-1] if step == 1 else ())
+    back = attend_back(
+        ring, groups[0], (), keys, queries, grad_attended, attended, *tables
+    )
+    back = attend_back(
+        ring,
+        groups[1],
+        (*ffn_marks[0], gu_sum, out_send),
+        keys,
+        queries,
+        grad_attended,
+        attended,
+        *tables,
+        back,
+    )
+    grad_queries, kv_keep, kv_give = back
+    gu_other = twin(gu_sum)
     (query_give,) = give_terms(ring, input_one, (grad_queries,))
-    kv_give = after(kv_give, query_give, out_send)
-    kv_keep = kv_keep + ring.swap(kv_give).astype(F32)
     query_got = ring.swap(query_give)
-    (query_term,) = keep_terms(ring, input_one, (grad_queries,), (query_got,))
-    query_sum, query_marks = ring.scatter(cut(query_term, rows))
+    kv_got = ring.swap(after(kv_give, query_give))
+    kv_term = (kv_keep.astype(F32) + kv_got.astype(F32)).astype(BF16)
+    merged = merge_terms(ring, input_one, grad_queries, query_got, out_keep, out_recv)
+    merged_sum, merged_marks = ring.scatter(merged)
 
     def kv_ties(step, marks):
-        return {3: (query_got,), 4: query_marks[0]}.get(step, ())
-
-    grad_kv, kv_marks = ring.scatter([kv_keep[k] for k in range(chips)], kv_ties)
-    out_term = (out_keep + out_recv.astype(F32)).astype(BF16).reshape(chips * half, model)
-    out_sum, out_marks = ring.scatter(cut(after(out_term, *ffn_marks[3]), half))
-    grad_kv = finish_kv(
-        ring, grad_kv, cosine, sine, (*query_marks[1], *ffn_marks[3], *out_marks[0], gu_sum)
-    )
+        return {3: (merged, *ffn_marks[2])}.get(step)
+
+    grad_kv, kv_marks = ring.scatter(kv_term.reshape(chips * tok, -1), kv_ties)
+    grad_kv = finish_kv(ring, grad_kv, cosine, sine, merged_marks[0])
     (kv_give,) = give_terms(ring, input_one, (grad_kv,))
     (kv_term,) = keep_terms(ring, input_one, (grad_kv,), (ring.swap(kv_give),))
-    gu_other = twin(gu_sum)
     grad_hidden, gain_one_term = back_project(
         ring,
         grad_queries,
@@ -1127,26 +1202,32 @@
         grad_residual,
         qkv_pieces,
         width,
-        (*out_marks[1], *query_marks[2]),
+        (*merged_marks[1], *ffn_marks[3]),
     )
     gain_terms = jnp.concatenate([gain_one_term[:1], gain_two_term[:1]], 0)
     gain_terms = gain_terms[:, :middle] + ring.swap(gain_terms[:, middle:])
     below = gain_terms.reshape(2, chips, rows).transpose(1, 0, 2).reshape(chips, 1, 2 * rows)
-    below = jnp.pad(below, ((0, 0), (0, 15), (0, kv_term.shape[1] - 2 * rows)))
-    below = below.astype(BF16)
-    parts = [jnp.concatenate([part, below[k]], 0) for k, part in enumerate(cut(kv_term, rows))]
-    kv_sum, _ = ring.scatter(parts)
-    kv_sum = over_reps(kv_sum)
-    grad_qkv = jnp.concatenate([over_reps(query_sum), kv_sum[:rows]], 1)
-    out_sum = rest_of_reps(out_sum).astype(BF16)
-    out_other = twin(out_sum)
-    grad_out = jnp.concatenate([pick(side, out_sum, out_other), pick(side, out_other, out_sum)], 0)
+    below = jnp.pad(below, ((0, 0), (0, 15), (0, kv_term.shape[1] - 2 * rows))).astype(BF16)
+    parts = jnp.concatenate([kv_term.reshape(chips, rows, -1), below], 1)
+    kv_sum, last_marks = ring.scatter(
+        parts.reshape(chips * (rows + 16), -1),
+        lambda step, _: {3: merged_marks[2]}.get(step),
+    )
+    kv_sum = over_reps(summed(kv_sum))
+    merged_sum = rest_of_reps(summed(merged_sum)).astype(BF16)
+    other = twin(merged_sum)
+    grad_queries = merged_sum[:rows].astype(F32) + other[:rows].astype(F32)
+    grad_qkv = jnp.concatenate([grad_queries, kv_sum[:rows]], 1)
+    mine, theirs = merged_sum[rows:], other[rows:]
+    grad_out = jnp.concatenate([pick(side, mine, theirs), pick(side, theirs, mine)], 0)
+    hidden_out = (residual + summed((ffn_out[0], ffn_out[1], after(ffn_out[2], grad_kv)))).astype(BF16)
+    grad_down = down_keep.astype(F32) + after(down_recv, *last_marks[1]).astype(F32)
     return (
         hidden_out[None],
         grad_hidden[None],
         grad_qkv,
         grad_out.astype(F32),
-        join_columns(ring, gu_sum, gu_other),
+        join_columns(ring, gu_sum, gu_other, (grad_kv,)),
         grad_down,
         kv_sum[rows, :rows],
         kv_sum[rows, rows : 2 * rows],

time: 759 us -> 710 us (0.935)
  other arithmetic: 67.8 us -> 21.5 us
  waiting for transfers between devices: 291 us -> 259 us
  Pallas kernels: 225 us -> 240 us
  local copies, waits for them, and re-layouts: 39 us -> 49.9 us
    ppermute x15, waiting for transfers between devices: 132 us -> 75.2 us  [gather(): ccw = lax.ppermute(ccw, 'shard', self.back)]
    ppermute x15, waiting for transfers between devices: 4.31 us -> 50.4 us  [gather(): cw = lax.ppermute(cw, 'shard', self.ahead)]
    ppermute x8 -> x7, waiting for transfers between devices: 58 us -> 20.4 us  [twin(): return lax.ppermute(value, 'rep', twin_map)]
    convert_element_type x20 -> x2, other arithmetic: 30.3 us -> 1.81 us  [the longest x1 1.52 us: on_device(): merged_sum = rest_of_reps(summed(merged_sum)).astype(BF16)]
    pallas_call x6 -> x22, Pallas kernels: 41.2 us -> 64.8 us  [the longest x15 35.5 us: add_step(): pl.pallas_call(body, grid=(1,), in_specs=[pl.BlockSpec((rows, width), lam...]
    unnamed x161 -> x211, local copies, waits for them, and re-layouts: 12 us -> 28.7 us
    ppermute x24 -> x20, waiting for transfers between devices: 32.1 us -> 48 us  [scatter(): ccw = lax.ppermute(ccw, 'shard', self.back)]
    ppermute x15, starting transfers between devices: 7.08 us -> 22.2 us  [gather(): cw = lax.ppermute(cw, 'shard', self.ahead)]
  transfers between devices with their start and end apart: 128 -> 119, of which waited for: 43 -> 45; matrix products, arithmetic and copies ran while one was open for 11% -> 6% of each run, Pallas kernels for 24% -> 24%
where the time goes in v3:
time: 710 us; the launch traced here: 700 us
  waiting for transfers between devices  259 us (36%)
  Pallas kernels  240 us (34%)
  starting transfers between devices  128 us (18%)
  local copies, waits for them, and re-layouts  49.9 us (7%)
  other arithmetic  21.5 us (3%)
    ppermute x15, waiting for transfers between devices, gather(): ccw = lax.ppermute(ccw, 'shard', self.back)  75.2 us
    pallas_call x4, Pallas kernels, attention_call(): pl.pallas_call(body, grid_spec=pltpu.PrefetchScalarGridSpec(num_scalar_pr...  57.1 us
    pallas_call x7, Pallas kernels, call(): pl.pallas_call(body, grid_spec=pltpu.PrefetchScalarGridSpec(num_scalar_pr...  50.9 us
    ppermute x15, waiting for transfers between devices, gather(): cw = lax.ppermute(cw, 'shard', self.ahead)  50.4 us
    ppermute x20, waiting for transfers between devices, scatter(): ccw = lax.ppermute(ccw, 'shard', self.back)  48 us
    ppermute x20, waiting for transfers between devices, scatter(): cw = lax.ppermute(cw, 'shard', self.ahead)  45.7 us
    pallas_call x15, Pallas kernels, add_step(): pl.pallas_call(body, grid=(1,), in_specs=[pl.BlockSpec((rows, width), lam...  35.5 us
    unnamed x211, local copies, waits for them, and re-layouts  28.7 us
  transfers between devices with their start and end apart: 119, of which 45 were waited for; matrix products, arithmetic and copies ran while one was open for 6% of the time, Pallas kernels for 24%

profile of v3, /device:TPU:0, one launch (start us, length us, event | category | flops | bytes accessed | tf_op | source)
XLA Modules:
  0.0 700.4 jit_solution(16170621048325629881)
XLA Ops:
  11.6 14.5 %collective-permute-done.1.refs_5_.refs_8_ = bf16[128,2688]{1,0:T(8,128)(2,1)} collective-permute-done((bf16[128,2688]{1,0:T(8,128)(2,1)}, bf16[128,2688]{1,0:T(8,128)(2,1)}, u32[]{:S(2)}, u32[]{:S(2)}) %collective-permute-start.1) | collective-permute-done | bytes 688160 | tf_op jit(solution)/shard_map/ppermute | solution.py:99
  27.8 4.1 shard_map.162
  32.0 5.0 all-to-all-start
  39.0 10.7 %collective-permute-done.3.refs_7_.refs_10_ = bf16[128,2688]{1,0:T(8,128)(2,1)} collective-permute-done((bf16[128,2688]{1,0:T(8,128)(2,1)}, bf16[128,2688]{1,0:T(8,128)(2,1)}, u32[]{:S(2)}, u32[]{:S(2)}) %collective-permute-start.3) | collective-permute-done | bytes 688160 | tf_op jit(solution)/shard_map/ppermute | solution.py:99
  52.8 23.3 %collective-permute-done.2.refs_6_.refs_9_ = bf16[128,2688]{1,0:T(8,128)(2,1)S(1)} collective-permute-done((bf16[128,2688]{1,0:T(8,128)(2,1)}, bf16[128,2688]{1,0:T(8,128)(2,1)S(1)}, u32[]{:S(2)}, u32[]{:S(2)}) %collective-permute-start.2) | collective-permute-done | bytes 688160 | tf_op jit(solution)/shard_map/ppermute | solution.py:98
  76.1 9.9 %collective-permute-start.4 = (bf16[128,2688]{1,0:T(8,128)(2,1)S(1)}, bf16[128,2688]{1,0:T(8,128)(2,1)S(1)}, u32[]{:S(2)}, u32[]{:S(2)}) collective-permute-start(bf16[128,2688]{1,0:T(8,128)(2,1)S(1)} %collective-permute-done.2.refs_6_.refs_9_), channel_id=1, source_target_pairs={{0,4},{1,5},{2,0},{3,1},{4,8},{5,9},{6,2},{7,3},{8,12},{9,13},{10,... | collective-permute-start | bytes 2064392 | tf_op jit(solution)/shard_map/ppermute | solution.py:98
  87.1 13.4 %collective-permute-done.4.refs_8_.refs_11_ = bf16[128,2688]{1,0:T(8,128)(2,1)S(1)} collective-permute-done((bf16[128,2688]{1,0:T(8,128)(2,1)S(1)}, bf16[128,2688]{1,0:T(8,128)(2,1)S(1)}, u32[]{:S(2)}, u32[]{:S(2)}) %collective-permute-start.4) | collective-permute-done | bytes 688160 | tf_op jit(solution)/shard_map/ppermute | solution.py:98
  106.1 4.0 collective-permute-done.7.refs_11_.refs_2_.refs_14_
  118.0 8.7 %shard_map.163 = (f32[128,2048]{1,0:T(8,128)}, bf16[128,512]{1,0:T(8,128)(2,1)}, bf16[128,2048]{1,0:T(8,128)(2,1)}, f32[128,128]{1,0:T(8,128)}, f32[8,2048]{1,0:T(8,128)}) custom-call(s32[75]{0:T(128)} %dynamic-slice_bitcast_fusion.1.table_ref.table, bf16[128,2048]{1,0:T(8,128)(2,1)} %bitcast.61, ...), custom_call_target="tpu_custom_call" | custom-call | flops 9900000256 | bytes 29700000 | tf_op jit(solution)/shard_map/pallas_call | solution.py:182
  152.5 3.9 collective-permute-done.27.refs_6_.refs_10_
  160.1 8.4 %collective-permute-done.28.refs_9_.refs_8_.refs_12_ = bf16[128,2048]{1,0:T(8,128)(2,1)} collective-permute-done((bf16[128,2048]{1,0:T(8,128)(2,1)}, bf16[128,2048]{1,0:T(8,128)(2,1)}, u32[]{:S(2)}, u32[]{:S(2)}) %collective-permute-start.28) | collective-permute-done | bytes 524320 | tf_op jit(solution)/shard_map/ppermute | solution.py:98
  178.2 14.2 %shard_map.165 = (bf16[128,2048]{1,0:T(8,128)(2,1)}, bf16[128,2048]{1,0:T(8,128)(2,1)}, f32[16,1,256]{2,1,0:T(1,128)}) custom-call(s32[75]{0:T(128)} %dynamic-slice_bitcast_fusion.1.table_ref.table, f32[128,2048]{1,0:T(8,128)} %get-tuple-element.78.refs_0_, bf16[8,128,512]{2,1,0:T(8,128)(2,1)} %shard_map.164.refs_1_.refs_4_, ...), custom_call_target="tpu_custom_call" | custom-call | flops 15399999488 | bytes 46200000 | tf_op jit(solution)/shard_map/pallas_call | solution.py:977
  193.5 14.2 %shard_map.171 = (bf16[128,2048]{1,0:T(8,128)(2,1)}, bf16[128,2048]{1,0:T(8,128)(2,1)}, f32[16,1,256]{2,1,0:T(1,128)}) custom-call(s32[75]{0:T(128)} %dynamic-slice_bitcast_fusion.1.table_ref.table, f32[128,2048]{1,0:T(8,128)} %get-tuple-element.78.refs_0_, ...), custom_call_target="tpu_custom_call", output_to_operand_aliasing={{0}: (7, {}), {1}: (8, {}), {2}: (9, {})} | custom-call | flops 15399999488 | bytes 46200000 | tf_op jit(solution)/shard_map/pallas_call | solution.py:977
  212.3 8.1 %shard_map.172 = (f32[128,2048]{1,0:T(8,128)}, f32[128,128]{1,0:T(8,128)}, bf16[128,2048]{1,0:T(8,128)(2,1)}) custom-call(s32[75]{0:T(128)} %dynamic-slice_bitcast_fusion.1.table_ref.table, bf16[128,2048]{1,0:T(8,128)(2,1)} %get-tuple-element.83.refs_0_.refs_2_.input_ref, bf16[128,2048]{1,0:T(8,128)(2,1)} %bitcast.62, ...), custom_call_target="tpu_custom_call" | custom-call | flops 8800000000 | bytes 26400000 | tf_op jit(solution)/shard_map/pallas_call | solution.py:182
  225.4 10.2 %collective-permute-done.44.refs_2_ = bf16[128,2048]{1,0:T(8,128)(2,1)S(1)} collective-permute-done((bf16[128,2048]{1,0:T(8,128)(2,1)}, bf16[128,2048]{1,0:T(8,128)(2,1)S(1)}, u32[]{:S(2)}, u32[]{:S(2)}) %collective-permute-start.44) | collective-permute-done | bytes 524320 | tf_op jit(solution)/shard_map/ppermute | solution.py:99
  237.6 6.7 collective-permute-done.59.refs_19_
  249.5 8.6 %collective-permute-done.46.refs_4_ = bf16[128,2048]{1,0:T(8,128)(2,1)S(1)} collective-permute-done((bf16[128,2048]{1,0:T(8,128)(2,1)S(1)}, bf16[128,2048]{1,0:T(8,128)(2,1)S(1)}, u32[]{:S(2)}, u32[]{:S(2)}) %collective-permute-start.46) | collective-permute-done | bytes 524320 | tf_op jit(solution)/shard_map/ppermute | solution.py:99
  259.6 8.3 %collective-permute-done.56.refs_15_ = bf16[128,2048]{1,0:T(8,128)(2,1)S(1)} collective-permute-done((bf16[128,2048]{1,0:T(8,128)(2,1)S(1)}, bf16[128,2048]{1,0:T(8,128)(2,1)S(1)}, u32[]{:S(2)}, u32[]{:S(2)}) %collective-permute-start.56) | collective-permute-done | bytes 524320 | tf_op jit(solution)/shard_map/ppermute | solution.py:99
  270.9 9.5 %collective-permute-done.48.refs_6_ = bf16[128,2048]{1,0:T(8,128)(2,1)S(1)} collective-permute-done((bf16[128,2048]{1,0:T(8,128)(2,1)S(1)}, bf16[128,2048]{1,0:T(8,128)(2,1)S(1)}, u32[]{:S(2)}, u32[]{:S(2)}) %collective-permute-start.48) | collective-permute-done | bytes 524320 | tf_op jit(solution)/shard_map/ppermute | solution.py:99
  286.5 4.1 shard_map.174.refs_22_.down_ref
  293.9 28.6 %shard_map.175 = (bf16[1024,704]{1,0:T(8,128)(2,1)}, bf16[1024,704]{1,0:T(8,128)(2,1)}, bf16[1024,704]{1,0:T(8,128)(2,1)}, bf16[1024,2048]{1,0:T(8,128)(2,1)}, b...) custom-call(s32[75]{0:T(128)} %dynamic-slice_bitcast_fusion.1.table_ref.table, ...), custom_call_target="tpu_custom_call" | custom-call | flops 30799998976 | bytes 92400000 | tf_op jit(solution)/shard_map/pallas_call | solution.py:808
  322.5 7.1 %shard_map.176 = (bf16[1024,704]{1,0:T(8,128)(2,1)}, bf16[1024,704]{1,0:T(8,128)(2,1)}) custom-call(bf16[1024,2048]{1,0:T(8,128)(2,1)} %get-tuple-element.88.input_ref, bf16[1024,704]{1,0:T(8,128)(2,1)} %get-tuple-element.89.refs_0_, bf16[1024,704]{1,0:T(8,128)(2,1)} %get-tuple-element.90.refs_1_), custom_call_target="tpu_custom_call" | custom-call | flops 2310000128 | bytes 6930000 | tf_op jit(solution)/shard_map/pallas_call | solution.py:567
  336.8 6.2 collective-permute-done.66.ccw_ref
  353.6 9.4 %shard_map.177 = (f32[8,2,64,704]{3,2,1,0:T(8,128)}, bf16[8,2,64,704]{3,2,1,0:T(8,128)(2,1)}) custom-call(s32[75]{0:T(128)} %dynamic-slice_bitcast_fusion.1.table_ref.table, bf16[1024,2048]{1,0:T(8,128)(2,1)} %get-tuple-element.88.input_ref, bf16[1024,704]{1,0:T(8,128)(2,1)} %get-tuple-element.89.refs_0_, bf16[1024,704]{1,0:T(8,128)(2,1)} %get-tuple-element.90.refs_1_, ...), custom_call_target="tpu_custom_call" | custom-call | flops 3464999936 | bytes 10395000 | tf_op jit(solution)/shard_map/pallas_call | solution.py:655
  369.5 7.2 %shard_map.178.refs_1_.ahead_ref.back_ref = bf16[1024,2048]{1,0:T(8,128)(2,1)} custom-call(bf16[1024,704]{1,0:T(8,128)(2,1)} %get-tuple-element.87.act_ref, bf16[704,2048]{1,0:T(8,128)(2,1)} %shard_map.174.refs_22_.down_ref, bf16[8,2,64,704]{3,2,1,0:T(8,128)(2,1)} %get-tuple-element.93.refs_0_.refs_1_), custom_call_target="tpu_custom_call" | custom-call | flops 2695000064 | bytes 8085000 | tf_op jit(solution)/shard_map/pallas_call | solution.py:704
  387.7 7.0 %collective-permute-done.71.refs_1_.refs_0_ = bf16[128,2048]{1,0:T(8,128)(2,1)S(1)} collective-permute-done((bf16[128,2048]{1,0:T(8,128)(2,1)}, bf16[128,2048]{1,0:T(8,128)(2,1)S(1)}, u32[]{:S(2)}, u32[]{:S(2)}) %collective-permute-start.71) | collective-permute-done | bytes 524320 | tf_op jit(solution)/shard_map/ppermute | solution.py:121
  397.8 10.2 %shard_map.191 = (f32[128,2048]{1,0:T(8,128)}, bf16[128,2048]{1,0:T(8,128)(2,1)}, bf16[128,2048]{1,0:T(8,128)(2,1)}, f32[8,2048]{1,0:T(8,128)}) custom-call(s32[75]{0:T(128)} %dynamic-slice_bitcast_fusion.1.table_ref.table, bf16[128,2048]{1,0:T(8,128)(2,1)} %slice.127.refs_0_, bf16[128,2048]{1,0:T(8,128)(2,1)} %copy-done.8, bf16[128,2048]{1,0:T(8,128)(2,1)} %copy-done.9, ...), custom_call_target="tpu_custom_call" | custom-call | flops 3849999872 | bytes 11550000 | tf_op jit(solution)/shard_map/pallas_call | solution.py:182
  408.0 4.1 shard_map.193
  415.1 4.3 all-to-all-start.1
  423.3 14.4 %shard_map.192 = (bf16[128,2048]{1,0:T(8,128)(2,1)}, bf16[8,128,512]{2,1,0:T(8,128)(2,1)}, bf16[8,128,512]{2,1,0:T(8,128)(2,1)}) custom-call(s32[75]{0:T(128)} %dynamic-slice_bitcast_fusion.1.table_ref.table, bf16[128,2048]{1,0:T(8,128)(2,1)} %get-tuple-element.107.refs_0_, bf16[128,2048]{1,0:T(8,128)(2,1)} %get-tuple-element.109.refs_1_, ...), custom_call_target="tpu_custom_call" | custom-call | flops 5500000256 | bytes 16500000 | tf_op jit(solution)/shard_map/pallas_call | solution.py:977
  437.6 6.0 shard_map.194
  443.6 9.1 %collective-permute-done.73.cw_ref.refs_12_ = bf16[64,2048]{1,0:T(8,128)(2,1)S(1)} collective-permute-done((bf16[64,2048]{1,0:T(8,128)(2,1)}, bf16[64,2048]{1,0:T(8,128)(2,1)S(1)}, u32[]{:S(2)}, u32[]{:S(2)}) %collective-permute-start.73) | collective-permute-done | bytes 262176 | tf_op jit(solution)/shard_map/ppermute | solution.py:121
  452.7 5.1 all-to-all-done.1.refs_14_.refs_0_
  457.8 14.4 %shard_map.195 = (bf16[128,2048]{1,0:T(8,128)(2,1)}, bf16[8,128,512]{2,1,0:T(8,128)(2,1)}, bf16[8,128,512]{2,1,0:T(8,128)(2,1)}) custom-call(s32[75]{0:T(128)} %dynamic-slice_bitcast_fusion.1.table_ref.table, bf16[128,2048]{1,0:T(8,128)(2,1)} %get-tuple-element.107.refs_0_, ...), custom_call_target="tpu_custom_call", output_to_operand_aliasing={{0}: (10, {}), {1}: (11, {}), {2}: (12, {})} | custom-call | flops 5500000256 | bytes 16500000 | tf_op jit(solution)/shard_map/pallas_call | solution.py:977
  472.2 3.9 shard_map.196.refs_1_
  479.6 6.4 collective-permute-start.75
  487.9 13.0 %collective-permute-done.85.ccw_ref = bf16[64,512]{1,0:T(8,128)(2,1)S(1)} collective-permute-done((bf16[64,512]{1,0:T(8,128)(2,1)S(1)}, bf16[64,512]{1,0:T(8,128)(2,1)S(1)}, u32[]{:S(2)}, u32[]{:S(2)}) %collective-permute-start.85) | collective-permute-done | bytes 65568 | tf_op jit(solution)/shard_map/ppermute | solution.py:122
  515.3 11.9 %collective-permute-done.87.ccw_ref = bf16[128,512]{1,0:T(8,128)(2,1)S(1)} collective-permute-done((bf16[128,512]{1,0:T(8,128)(2,1)S(1)}, bf16[128,512]{1,0:T(8,128)(2,1)S(1)}, u32[]{:S(2)}, u32[]{:S(2)}) %collective-permute-start.87) | collective-permute-done | bytes 131104 | tf_op jit(solution)/shard_map/ppermute | solution.py:122
  531.0 7.1 %shard_map.200.refs_1_.ahead_ref.back_ref = bf16[1536,2048]{1,0:T(8,128)(2,1)} custom-call(bf16[128,2048]{1,0:T(8,128)(2,1)} %get-tuple-element.119.input_ref, bf16[128,2048]{1,0:T(8,128)(2,1)} %get-tuple-element.120.refs_0_.grad_ref, bf16[1024,2048]{1,0:T(8,128)(2,1)} %collective-permute-done.88.got_ref, f32[8,1,64,2048]{3,2,1,0:T(8,128)} %get-tuple-element.124.half_ref, ...), custom_call_target="tpu_custom_call" | custom-call | flops 2200000000 | bytes 6600000 | tf_op jit(solution)/shard_map/pallas_call | solution.py:620
  560.7 9.1 %collective-permute-done.92.refs_1_ = bf16[128,512]{1,0:T(8,128)(2,1)S(1)} collective-permute-done((bf16[128,512]{1,0:T(8,128)(2,1)}, bf16[128,512]{1,0:T(8,128)(2,1)S(1)}, u32[]{:S(2)}, u32[]{:S(2)}) %collective-permute-start.92) | collective-permute-done | bytes 131104 | tf_op jit(solution)/shard_map/ppermute | solution.py:121
  576.8 10.1 %shard_map.218 = (f32[352,2048]{1,0:T(8,128)}, bf16[352,2048]{1,0:T(8,128)(2,1)}) custom-call(s32[75]{0:T(128)} %dynamic-slice_bitcast_fusion.1.table_ref.table, bf16[1024,704]{1,0:T(8,128)(2,1)} %get-tuple-element.87.act_ref, bf16[1024,2048]{1,0:T(8,128)(2,1)} %get-tuple-element.145.cot_ref, bf16[128,2048]{1,0:T(8,128)(2,1)} %copy-done.8, ...), custom_call_target="tpu_custom_call" | custom-call | flops 3849999872 | bytes 11550000 | tf_op jit(solution)/shard_map/pallas_call | solution.py:682
  590.4 11.4 %shard_map.207 = (bf16[128,2048]{1,0:T(8,128)(2,1)}, f32[8,2048]{1,0:T(8,128)}) custom-call(s32[75]{0:T(128)} %dynamic-slice_bitcast_fusion.1.table_ref.table, bf16[128,2048]{1,0:T(8,128)(2,1)} %get-tuple-element.120.refs_0_.grad_ref, bf16[128,512]{1,0:T(8,128)(2,1)} %shard_map.204.refs_1_.refs_0_.refs_2_, bf16[128,2048]{1,0:T(8,128)(2,1)} %bitcast.63, ...), custom_call_target="tpu_custom_call" | custom-call | flops 4427500032 | bytes 13282500 | tf_op jit(solution)/shard_map/pallas_call | solution.py:182
  618.4 10.3 %collective-permute-done.106.ccw_ref = bf16[72,512]{1,0:T(8,128)(2,1)S(1)} collective-permute-done((bf16[72,512]{1,0:T(8,128)(2,1)S(1)}, bf16[72,512]{1,0:T(8,128)(2,1)S(1)}, u32[]{:S(2)}, u32[]{:S(2)}) %collective-permute-start.106) | collective-permute-done | bytes 73760 | tf_op jit(solution)/shard_map/ppermute | solution.py:122
  632.4 4.8 collective-permute-done.107.cw_ref.refs_1_
  638.4 4.1 collective-permute-done.108.ccw_ref.refs_2_
  648.3 5.9 shard_map.217
  667.9 9.4 %collective-permute-done.111 = bf16[144,512]{1,0:T(8,128)(2,1)S(1)} collective-permute-done((bf16[144,512]{1,0:T(8,128)(2,1)}, bf16[144,512]{1,0:T(8,128)(2,1)S(1)}, u32[]{:S(2)}, u32[]{:S(2)}) %collective-permute-start.111) | collective-permute-done | bytes 147488 | tf_op jit(solution)/shard_map/ppermute | solution.py:121
  686.4 11.4 %collective-permute-done.102 = bf16[192,2048]{1,0:T(8,128)(2,1)S(1)} collective-permute-done((bf16[192,2048]{1,0:T(8,128)(2,1)S(1)}, bf16[192,2048]{1,0:T(8,128)(2,1)S(1)}, u32[]{:S(2)}, u32[]{:S(2)}) %collective-permute-start.102) | collective-permute-done | bytes 786464 | tf_op jit(solution)/shard_map/ppermute | solution.py:1087
  (511 shorter events, 257.2 us)
Async XLA Ops:
  7.4 18.8 %collective-permute-start.1 = (bf16[128,2688]{1,0:T(8,128)(2,1)}, bf16[128,2688]{1,0:T(8,128)(2,1)}, u32[]{:S(2)}, u32[]{:S(2)}) collective-permute-start(bf16[128,2688]{1,0:T(8,128)(2,1)} %shard_map.161.refs_3_.refs_6_), channel_id=1, source_target_pairs={{0,2},{1,3},{2,6},{3,7},{4,0},{5,1},{6,10},{7,11},{8,4},{9,5},{10,... | collective-permute-start | bytes 2064392 | tf_op jit(solution)/shard_map/ppermute | solution.py:99
  10.4 26.6 %collective-permute-start = (bf16[128,2688]{1,0:T(8,128)(2,1)}, bf16[128,2688]{1,0:T(8,128)(2,1)}, u32[]{:S(2)}, u32[]{:S(2)}) collective-permute-start(bf16[128,2688]{1,0:T(8,128)(2,1)} %shard_map.161.refs_3_.refs_6_), channel_id=1, source_target_pairs={{0,4},{1,5},{2,0},{3,1},{4,8},{5,9},{6,2},{7,3},{8,12},{9,13},{10,... | collective-permute-start | bytes 2064392 | tf_op jit(solution)/shard_map/ppermute | solution.py:98
  26.2 23.5 %collective-permute-start.3 = (bf16[128,2688]{1,0:T(8,128)(2,1)}, bf16[128,2688]{1,0:T(8,128)(2,1)}, u32[]{:S(2)}, u32[]{:S(2)}) collective-permute-start(bf16[128,2688]{1,0:T(8,128)(2,1)} %collective-permute-done.1.refs_5_.refs_8_), channel_id=1, source_target_pairs={{0,2},{1,3},{2,6},{3,7},{4,0},{5,1},{6,10},{7,11},{8,4},{9,5},{10,... | collective-permute-start | bytes 2064392 | tf_op jit(solution)/shard_map/ppermute | solution.py:99
  32.0 84.9 %all-to-all-start = ((bf16[8,2,64,704]{3,2,1,0:T(8,128)(2,1)}), bf16[8,2,64,704]{3,2,1,0:T(8,128)(2,1)S(1)}, u32[]{:S(2)}, u32[]{:S(2)}) async-start(bf16[8,2,64,704]{3,2,1,0:T(8,128)(2,1)} %shard_map.162), calls=%async_computation | async-start | bytes 3145728 | tf_op jit(solution)/shard_map/all_to_all | solution.py:1099
  37.0 39.2 %collective-permute-start.2 = (bf16[128,2688]{1,0:T(8,128)(2,1)}, bf16[128,2688]{1,0:T(8,128)(2,1)S(1)}, u32[]{:S(2)}, u32[]{:S(2)}) collective-permute-start(bf16[128,2688]{1,0:T(8,128)(2,1)} %collective-permute-done.refs_4_.refs_7_), channel_id=1, source_target_pairs={{0,4},{1,5},{2,0},{3,1},{4,8},{5,9},{6,2},{7,3},{8,12},{9,13},{10,... | collective-permute-start | bytes 2064392 | tf_op jit(solution)/shard_map/ppermute | solution.py:98
  49.7 36.9 %collective-permute-start.5 = (bf16[128,2688]{1,0:T(8,128)(2,1)}, bf16[128,2688]{1,0:T(8,128)(2,1)S(1)}, u32[]{:S(2)}, u32[]{:S(2)}) collective-permute-start(bf16[128,2688]{1,0:T(8,128)(2,1)} %collective-permute-done.3.refs_7_.refs_10_), channel_id=1, source_target_pairs={{0,2},{1,3},{2,6},{3,7},{4,0},{5,1},{6,10},{7,11},{8,4},{9,5},{10,... | collective-permute-start | bytes 2064392 | tf_op jit(solution)/shard_map/ppermute | solution.py:99
  76.1 24.3 %collective-permute-start.4 = (bf16[128,2688]{1,0:T(8,128)(2,1)S(1)}, bf16[128,2688]{1,0:T(8,128)(2,1)S(1)}, u32[]{:S(2)}, u32[]{:S(2)}) collective-permute-start(bf16[128,2688]{1,0:T(8,128)(2,1)S(1)} %collective-permute-done.2.refs_6_.refs_9_), channel_id=1, source_target_pairs={{0,4},{1,5},{2,0},{3,1},{4,8},{5,9},{6,2},{7,3},{8,12},{9,13},{10,... | collective-permute-start | bytes 2064392 | tf_op jit(solution)/shard_map/ppermute | solution.py:98
  86.0 19.1 %collective-permute-start.10 = (bf16[128,2688]{1,0:T(8,128)(2,1)}, bf16[128,2688]{1,0:T(8,128)(2,1)}, u32[]{:S(2)}, u32[]{:S(2)}) collective-permute-start(bf16[128,2688]{1,0:T(8,128)(2,1)} %collective-permute-done.1.refs_5_.refs_8_), channel_id=1, source_target_pairs={{0,1},{1,0},{2,3},{3,2},{4,5},{5,4},{6,7},{7,6},{8,9},{9,8},{10,11... | collective-permute-start | bytes 2064392 | tf_op jit(solution)/shard_map/ppermute | solution.py:89
  86.6 19.2 %collective-permute-start.12 = (bf16[128,2688]{1,0:T(8,128)(2,1)}, bf16[128,2688]{1,0:T(8,128)(2,1)}, u32[]{:S(2)}, u32[]{:S(2)}) collective-permute-start(bf16[128,2688]{1,0:T(8,128)(2,1)} %collective-permute-done.3.refs_7_.refs_10_), channel_id=1, source_target_pairs={{0,1},{1,0},{2,3},{3,2},{4,5},{5,4},{6,7},{7,6},{8,9},{9,8},{10,11... | collective-permute-start | bytes 2064392 | tf_op jit(solution)/shard_map/ppermute | solution.py:89
  114.8 31.6 %collective-permute-start.29 = (bf16[128,2048]{1,0:T(8,128)(2,1)}, bf16[128,2048]{1,0:T(8,128)(2,1)S(1)}, u32[]{:S(2)}, u32[]{:S(2)}) collective-permute-start(bf16[128,2048]{1,0:T(8,128)(2,1)} %shard_map.166.refs_3_.refs_7_), channel_id=1, source_target_pairs={{0,2},{1,3},{2,6},{3,7},{4,0},{5,1},{6,10},{7,11},{8,4},{9,5},{10,... | collective-permute-start | bytes 1572872 | tf_op jit(solution)/shard_map/ppermute | solution.py:99
  116.3 28.7 %collective-permute-start.26 = (bf16[128,2048]{1,0:T(8,128)(2,1)}, bf16[128,2048]{1,0:T(8,128)(2,1)S(1)}, u32[]{:S(2)}, u32[]{:S(2)}) collective-permute-start(bf16[128,2048]{1,0:T(8,128)(2,1)} %shard_map.166.refs_3_.refs_7_), channel_id=1, source_target_pairs={{0,4},{1,5},{2,0},{3,1},{4,8},{5,9},{6,2},{7,3},{8,12},{9,13},{10,... | collective-permute-start | bytes 1572872 | tf_op jit(solution)/shard_map/ppermute | solution.py:98
  152.4 25.3 %collective-permute-start.25 = (bf16[8,128,512]{2,1,0:T(8,128)(2,1)}, bf16[8,128,512]{2,1,0:T(8,128)(2,1)}, u32[]{:S(2)}, u32[]{:S(2)}) collective-permute-start(bf16[8,128,512]{2,1,0:T(8,128)(2,1)} %shard_map.164.refs_1_.refs_4_), channel_id=1, source_target_pairs={{0,1},{1,0},{2,3},{3,2},{4,5},{5,4},{6,7},{7,6},{8,9},{9,8},{10,11... | collective-permute-start | bytes 3145736 | tf_op jit(solution)/shard_map/ppermute | solution.py:89
  172.6 19.8 %collective-permute-start.34 = (bf16[128,2048]{1,0:T(8,128)(2,1)S(1)}, bf16[128,2048]{1,0:T(8,128)(2,1)}, u32[]{:S(2)}, u32[]{:S(2)}) collective-permute-start(bf16[128,2048]{1,0:T(8,128)(2,1)S(1)} %copy-done.11), channel_id=1, source_target_pairs={{0,1},{1,0},{2,3},{3,2},{4,5},{5,4},{6,7},{7,6},{8,9},{9,8},{10,11... | collective-permute-start | bytes 1572872 | tf_op jit(solution)/shard_map/ppermute | solution.py:89
  172.6 19.9 %collective-permute-start.36 = (bf16[128,2048]{1,0:T(8,128)(2,1)S(1)}, bf16[128,2048]{1,0:T(8,128)(2,1)}, u32[]{:S(2)}, u32[]{:S(2)}) collective-permute-start(bf16[128,2048]{1,0:T(8,128)(2,1)S(1)} %collective-permute-done.29.refs_5_.refs_9_), channel_id=1, source_target_pairs={{0,1},{1,0},{2,3},{3,2},{4,5},{5,4},{6,7},{7,6},{8,9},{9,8},{10,11... | collective-permute-start | bytes 1572872 | tf_op jit(solution)/shard_map/ppermute | solution.py:89
  177.7 30.1 %collective-permute-start.38 = (bf16[128,2048]{1,0:T(8,128)(2,1)S(1)}, bf16[128,2048]{1,0:T(8,128)(2,1)}, u32[]{:S(2)}, u32[]{:S(2)}) collective-permute-start(bf16[128,2048]{1,0:T(8,128)(2,1)S(1)} %collective-permute-done.30.refs_7_.refs_11_), channel_id=1, source_target_pairs={{0,1},{1,0},{2,3},{3,2},{4,5},{5,4},{6,7},{7,6},{8,9},{9,8},{10,11... | collective-permute-start | bytes 1572872 | tf_op jit(solution)/shard_map/ppermute | solution.py:89
  207.7 36.5 %collective-permute-start.59 = (bf16[8,2,64,704]{3,2,1,0:T(8,128)(2,1)S(1)}, bf16[8,2,64,704]{3,2,1,0:T(8,128)(2,1)}, u32[]{:S(2)}, u32[]{:S(2)}) collective-permute-start(bf16[8,2,64,704]{3,2,1,0:T(8,128)(2,1)S(1)} %copy-done.17), channel_id=1, source_target_pairs={{0,16},{16,0},{1,17},{17,1},{2,18},{18,2},{3,19},{19,3},{4,20},{20... | collective-permute-start | bytes 4325384 | tf_op jit(solution)/shard_map/ppermute | solution.py:1087
  223.3 23.5 %collective-permute-start.54 = (bf16[128,2048]{1,0:T(8,128)(2,1)S(1)}, bf16[128,2048]{1,0:T(8,128)(2,1)S(1)}, u32[]{:S(2)}, u32[]{:S(2)}) collective-permute-start(bf16[128,2048]{1,0:T(8,128)(2,1)S(1)} %collective-permute-done.52.refs_11_), channel_id=1, source_target_pairs={{0,2},{1,3},{2,6},{3,7},{4,0},{5,1},{6,10},{7,11},{8,4},{9,5},{10,... | collective-permute-start | bytes 1572872 | tf_op jit(solution)/shard_map/ppermute | solution.py:99
  224.6 23.4 %collective-permute-start.53 = (bf16[128,2048]{1,0:T(8,128)(2,1)S(1)}, bf16[128,2048]{1,0:T(8,128)(2,1)S(1)}, u32[]{:S(2)}, u32[]{:S(2)}) collective-permute-start(bf16[128,2048]{1,0:T(8,128)(2,1)S(1)} %collective-permute-done.51.refs_10_), channel_id=1, source_target_pairs={{0,4},{1,5},{2,0},{3,1},{4,8},{5,9},{6,2},{7,3},{8,12},{9,13},{10,... | collective-permute-start | bytes 1572872 | tf_op jit(solution)/shard_map/ppermute | solution.py:98
  235.6 22.5 %collective-permute-start.46 = (bf16[128,2048]{1,0:T(8,128)(2,1)S(1)}, bf16[128,2048]{1,0:T(8,128)(2,1)S(1)}, u32[]{:S(2)}, u32[]{:S(2)}) collective-permute-start(bf16[128,2048]{1,0:T(8,128)(2,1)S(1)} %collective-permute-done.44.refs_2_), channel_id=1, source_target_pairs={{0,2},{1,3},{2,6},{3,7},{4,0},{5,1},{6,10},{7,11},{8,4},{9,5},{10,... | collective-permute-start | bytes 1572872 | tf_op jit(solution)/shard_map/ppermute | solution.py:99
  236.8 22.8 %collective-permute-start.45 = (bf16[128,2048]{1,0:T(8,128)(2,1)S(1)}, bf16[128,2048]{1,0:T(8,128)(2,1)S(1)}, u32[]{:S(2)}, u32[]{:S(2)}) collective-permute-start(bf16[128,2048]{1,0:T(8,128)(2,1)S(1)} %collective-permute-done.43.refs_1_), channel_id=1, source_target_pairs={{0,4},{1,5},{2,0},{3,1},{4,8},{5,9},{6,2},{7,3},{8,12},{9,13},{10,... | collective-permute-start | bytes 1572872 | tf_op jit(solution)/shard_map/ppermute | solution.py:98
  244.3 38.3 %collective-permute-start.62 = (bf16[352,2048]{1,0:T(8,128)(2,1)S(1)}, bf16[352,2048]{1,0:T(8,128)(2,1)S(1)}, u32[]{:S(2)}, u32[]{:S(2)}) collective-permute-start(bf16[352,2048]{1,0:T(8,128)(2,1)S(1)} %copy-done.62), channel_id=1, source_target_pairs={{0,1},{1,0},{2,3},{3,2},{4,5},{5,4},{6,7},{7,6},{8,9},{9,8},{10,11... | collective-permute-start | bytes 4325384 | tf_op jit(solution)/shard_map/ppermute | solution.py:89
  246.8 37.2 %collective-permute-start.60 = (bf16[8,2,64,704]{3,2,1,0:T(8,128)(2,1)S(1)}, bf16[8,2,64,704]{3,2,1,0:T(8,128)(2,1)S(1)}, u32[]{:S(2)}, u32[]{:S(2)}) collective-permute-start(bf16[8,2,64,704]{3,2,1,0:T(8,128)(2,1)S(1)} %copy-done.17), channel_id=1, source_target_pairs={{0,1},{1,0},{2,3},{3,2},{4,5},{5,4},{6,7},{7,6},{8,9},{9,8},{10,11... | collective-permute-start | bytes 4325384 | tf_op jit(solution)/shard_map/ppermute | solution.py:89
  248.0 19.9 %collective-permute-start.56 = (bf16[128,2048]{1,0:T(8,128)(2,1)S(1)}, bf16[128,2048]{1,0:T(8,128)(2,1)S(1)}, u32[]{:S(2)}, u32[]{:S(2)}) collective-permute-start(bf16[128,2048]{1,0:T(8,128)(2,1)S(1)} %collective-permute-done.54.refs_13_), channel_id=1, source_target_pairs={{0,2},{1,3},{2,6},{3,7},{4,0},{5,1},{6,10},{7,11},{8,4},{9,5},{10,... | collective-permute-start | bytes 1572872 | tf_op jit(solution)/shard_map/ppermute | solution.py:99
  259.6 31.0 %collective-permute-start.61 = (bf16[8,2,64,704]{3,2,1,0:T(8,128)(2,1)}, bf16[8,2,64,704]{3,2,1,0:T(8,128)(2,1)}, u32[]{:S(2)}, u32[]{:S(2)}) collective-permute-start(bf16[8,2,64,704]{3,2,1,0:T(8,128)(2,1)} %collective-permute-done.59.refs_19_), channel_id=1, source_target_pairs={{0,1},{1,0},{2,3},{3,2},{4,5},{5,4},{6,7},{7,6},{8,9},{9,8},{10,11... | collective-permute-start | bytes 4325384 | tf_op jit(solution)/shard_map/ppermute | solution.py:89
  333.2 18.8 %collective-permute-start.63 = (bf16[1024,704]{0,1:T(8,128)(2,1)}, bf16[1024,704]{0,1:T(8,128)(2,1)S(1)}, u32[]{:S(2)}, u32[]{:S(2)}) collective-permute-start(bf16[1024,704]{0,1:T(8,128)(2,1)} %copy.58), channel_id=1, source_target_pairs={{0,1},{1,0},{2,3},{3,2},{4,5},{5,4},{6,7},{7,6},{8,9},{9,8},{10,11... | collective-permute-start | bytes 4325384 | tf_op jit(solution)/shard_map/ppermute | solution.py:89
  362.9 34.9 %collective-permute-start.81 = (bf16[8,2,64,704]{3,2,1,0:T(8,128)(2,1)}, bf16[8,2,64,704]{3,2,1,0:T(8,128)(2,1)}, u32[]{:S(2)}, u32[]{:S(2)}) collective-permute-start(bf16[8,2,64,704]{3,2,1,0:T(8,128)(2,1)} %get-tuple-element.93.refs_0_.refs_1_), channel_id=1, source_target_pairs={{0,16},{16,0},{1,17},{17,1},{2,18},{18,2},{3,19},{19,3},{4,20},{20... | collective-permute-start | bytes 4325384 | tf_op jit(solution)/shard_map/ppermute | solution.py:1087
  412.1 25.5 %collective-permute-start.82 = (bf16[1024,2048]{1,0:T(8,128)(2,1)}, bf16[1024,2048]{1,0:T(8,128)(2,1)}, u32[]{:S(2)}, u32[]{:S(2)}) collective-permute-start(bf16[1024,2048]{1,0:T(8,128)(2,1)} %shard_map.193), channel_id=1, source_target_pairs={{0,1},{1,0},{2,3},{3,2},{4,5},{5,4},{6,7},{7,6},{8,9},{9,8},{10,11... | collective-permute-start | bytes 12582920 | tf_op jit(solution)/shard_map/ppermute | solution.py:89
  415.1 42.7 %all-to-all-start.1 = ((bf16[8,2,64,704]{3,2,1,0:T(8,128)(2,1)}), bf16[8,2,64,704]{3,2,1,0:T(8,128)(2,1)}, u32[]{:S(2)}, u32[]{:S(2)}) async-start(bf16[8,2,64,704]{3,2,1,0:T(8,128)(2,1)} %add_convert_fusion), calls=%async_computation.1 | async-start | bytes 3145728 | tf_op jit(solution)/shard_map/all_to_all | solution.py:1146
  421.2 31.4 %collective-permute-start.73 = (bf16[64,2048]{1,0:T(8,128)(2,1)}, bf16[64,2048]{1,0:T(8,128)(2,1)S(1)}, u32[]{:S(2)}, u32[]{:S(2)}) collective-permute-start(bf16[64,2048]{1,0:T(8,128)(2,1)} %shard_map.186), channel_id=1, source_target_pairs={{0,4},{1,5},{2,0},{3,1},{4,8},{5,9},{6,2},{7,3},{8,12},{9,13},{10,... | collective-permute-start | bytes 786440 | tf_op jit(solution)/shard_map/ppermute | solution.py:121
  423.1 29.5 %collective-permute-start.74 = (bf16[64,2048]{1,0:T(8,128)(2,1)}, bf16[64,2048]{1,0:T(8,128)(2,1)S(1)}, u32[]{:S(2)}, u32[]{:S(2)}) collective-permute-start(bf16[64,2048]{1,0:T(8,128)(2,1)} %shard_map.187), channel_id=1, source_target_pairs={{0,2},{1,3},{2,6},{3,7},{4,0},{5,1},{6,10},{7,11},{8,4},{9,5},{10,... | collective-permute-start | bytes 786440 | tf_op jit(solution)/shard_map/ppermute | solution.py:122
  476.1 53.5 %collective-permute-start.88 = (bf16[1024,2048]{1,0:T(8,128)(2,1)}, bf16[1024,2048]{1,0:T(8,128)(2,1)}, u32[]{:S(2)}, u32[]{:S(2)}) collective-permute-start(bf16[1024,2048]{1,0:T(8,128)(2,1)} %shard_map.196.refs_1_), channel_id=1, source_target_pairs={{0,1},{1,0},{2,3},{3,2},{4,5},{5,4},{6,7},{7,6},{8,9},{9,8},{10,11... | collective-permute-start | bytes 12582920 | tf_op jit(solution)/shard_map/ppermute | solution.py:89
  476.6 53.0 %collective-permute-start.89 = (bf16[8,1,64,2048]{3,2,1,0:T(8,128)(2,1)}, bf16[8,1,64,2048]{3,2,1,0:T(8,128)(2,1)S(1)}, u32[]{:S(2)}, u32[]{:S(2)}) collective-permute-start(bf16[8,1,64,2048]{3,2,1,0:T(8,128)(2,1)} %get-tuple-element.116.refs_15_), channel_id=1, source_target_pairs={{0,16},{16,0},{1,17},{17,1},{2,18},{18,2},{3,19},{19,3},{4,20},{20... | collective-permute-start | bytes 6291464 | tf_op jit(solution)/shard_map/ppermute | solution.py:1087
  479.6 29.4 %collective-permute-start.75 = (bf16[128,2048]{1,0:T(8,128)(2,1)}, bf16[128,2048]{1,0:T(8,128)(2,1)S(1)}, u32[]{:S(2)}, u32[]{:S(2)}) collective-permute-start(bf16[128,2048]{1,0:T(8,128)(2,1)} %get-tuple-element.101), channel_id=1, source_target_pairs={{0,4},{1,5},{2,0},{3,1},{4,8},{5,9},{6,2},{7,3},{8,12},{9,13},{10,... | collective-permute-start | bytes 1572872 | tf_op jit(solution)/shard_map/ppermute | solution.py:121
  486.0 23.0 %collective-permute-start.76 = (bf16[128,2048]{1,0:T(8,128)(2,1)}, bf16[128,2048]{1,0:T(8,128)(2,1)}, u32[]{:S(2)}, u32[]{:S(2)}) collective-permute-start(bf16[128,2048]{1,0:T(8,128)(2,1)} %get-tuple-element.102), channel_id=1, source_target_pairs={{0,2},{1,3},{2,6},{3,7},{4,0},{5,1},{6,10},{7,11},{8,4},{9,5},{10,... | collective-permute-start | bytes 1572872 | tf_op jit(solution)/shard_map/ppermute | solution.py:122
  512.4 25.6 %collective-permute-start.77 = (bf16[128,2048]{1,0:T(8,128)(2,1)}, bf16[128,2048]{1,0:T(8,128)(2,1)S(1)}, u32[]{:S(2)}, u32[]{:S(2)}) collective-permute-start(bf16[128,2048]{1,0:T(8,128)(2,1)} %get-tuple-element.103), channel_id=1, source_target_pairs={{0,4},{1,5},{2,0},{3,1},{4,8},{5,9},{6,2},{7,3},{8,12},{9,13},{10,... | collective-permute-start | bytes 1572872 | tf_op jit(solution)/shard_map/ppermute | solution.py:121
  512.7 25.3 %collective-permute-start.78 = (bf16[128,2048]{1,0:T(8,128)(2,1)}, bf16[128,2048]{1,0:T(8,128)(2,1)S(1)}, u32[]{:S(2)}, u32[]{:S(2)}) collective-permute-start(bf16[128,2048]{1,0:T(8,128)(2,1)} %get-tuple-element.104), channel_id=1, source_target_pairs={{0,2},{1,3},{2,6},{3,7},{4,0},{5,1},{6,10},{7,11},{8,4},{9,5},{10,... | collective-permute-start | bytes 1572872 | tf_op jit(solution)/shard_map/ppermute | solution.py:122
  546.9 40.0 %collective-permute-start.79 = (bf16[128,2048]{1,0:T(8,128)(2,1)}, bf16[128,2048]{1,0:T(8,128)(2,1)S(1)}, u32[]{:S(2)}, u32[]{:S(2)}) collective-permute-start(bf16[128,2048]{1,0:T(8,128)(2,1)} %get-tuple-element.105), channel_id=1, source_target_pairs={{0,4},{1,5},{2,0},{3,1},{4,8},{5,9},{6,2},{7,3},{8,12},{9,13},{10,... | collective-permute-start | bytes 1572872 | tf_op jit(solution)/shard_map/ppermute | solution.py:121
  554.9 33.5 %collective-permute-start.80 = (bf16[128,2048]{1,0:T(8,128)(2,1)S(1)}, bf16[128,2048]{1,0:T(8,128)(2,1)S(1)}, u32[]{:S(2)}, u32[]{:S(2)}) collective-permute-start(bf16[128,2048]{1,0:T(8,128)(2,1)S(1)} %copy-done.78), channel_id=1, source_target_pairs={{0,2},{1,3},{2,6},{3,7},{4,0},{5,1},{6,10},{7,11},{8,4},{9,5},{10,... | collective-permute-start | bytes 1572872 | tf_op jit(solution)/shard_map/ppermute | solution.py:122
  559.4 29.8 %collective-permute-start.96 = (bf16[192,2048]{1,0:T(8,128)(2,1)}, bf16[192,2048]{1,0:T(8,128)(2,1)S(1)}, u32[]{:S(2)}, u32[]{:S(2)}) collective-permute-start(bf16[192,2048]{1,0:T(8,128)(2,1)} %get-tuple-element.130), channel_id=1, source_target_pairs={{0,4},{1,5},{2,0},{3,1},{4,8},{5,9},{6,2},{7,3},{8,12},{9,13},{10,... | collective-permute-start | bytes 2359304 | tf_op jit(solution)/shard_map/ppermute | solution.py:121
  569.8 19.4 %collective-permute-start.97 = (bf16[192,2048]{1,0:T(8,128)(2,1)}, bf16[192,2048]{1,0:T(8,128)(2,1)S(1)}, u32[]{:S(2)}, u32[]{:S(2)}) collective-permute-start(bf16[192,2048]{1,0:T(8,128)(2,1)} %get-tuple-element.131), channel_id=1, source_target_pairs={{0,2},{1,3},{2,6},{3,7},{4,0},{5,1},{6,10},{7,11},{8,4},{9,5},{10,... | collective-permute-start | bytes 2359304 | tf_op jit(solution)/shard_map/ppermute | solution.py:122
  576.8 31.2 %collective-permute-start.103 = (bf16[1024,512]{1,0:T(8,128)(2,1)}, bf16[1024,512]{1,0:T(8,128)(2,1)S(1)}, u32[]{:S(2)}, u32[]{:S(2)}) collective-permute-start(bf16[1024,512]{1,0:T(8,128)(2,1)} %shard_map.210), channel_id=1, source_target_pairs={{0,1},{1,0},{2,3},{3,2},{4,5},{5,4},{6,7},{7,6},{8,9},{9,8},{10,11... | collective-permute-start | bytes 3145736 | tf_op jit(solution)/shard_map/ppermute | solution.py:89
  586.9 26.7 %collective-permute-start.115 = (bf16[352,2048]{1,0:T(8,128)(2,1)}, bf16[352,2048]{1,0:T(8,128)(2,1)S(1)}, u32[]{:S(2)}, u32[]{:S(2)}) collective-permute-start(bf16[352,2048]{1,0:T(8,128)(2,1)} %get-tuple-element.147), channel_id=1, source_target_pairs={{0,1},{1,0},{2,3},{3,2},{4,5},{5,4},{6,7},{7,6},{8,9},{9,8},{10,11... | collective-permute-start | bytes 4325384 | tf_op jit(solution)/shard_map/ppermute | solution.py:89
  588.3 59.9 %collective-permute-start.114 = (bf16[8,2,64,704]{3,2,1,0:T(8,128)(2,1)}, bf16[8,2,64,704]{3,2,1,0:T(8,128)(2,1)}, u32[]{:S(2)}, u32[]{:S(2)}) collective-permute-start(bf16[8,2,64,704]{3,2,1,0:T(8,128)(2,1)} %all-to-all-done.1.refs_14_.refs_0_), channel_id=1, source_target_pairs={{0,16},{16,0},{1,17},{17,1},{2,18},{18,2},{3,19},{19,3},{4,20},{20... | collective-permute-start | bytes 4325384 | tf_op jit(solution)/shard_map/ppermute | solution.py:1087
  605.9 39.1 %collective-permute-start.98 = (bf16[192,2048]{1,0:T(8,128)(2,1)}, bf16[192,2048]{1,0:T(8,128)(2,1)S(1)}, u32[]{:S(2)}, u32[]{:S(2)}) collective-permute-start(bf16[192,2048]{1,0:T(8,128)(2,1)} %get-tuple-element.133), channel_id=1, source_target_pairs={{0,4},{1,5},{2,0},{3,1},{4,8},{5,9},{6,2},{7,3},{8,12},{9,13},{10,... | collective-permute-start | bytes 2359304 | tf_op jit(solution)/shard_map/ppermute | solution.py:121
  607.3 37.8 %collective-permute-start.99 = (bf16[192,2048]{1,0:T(8,128)(2,1)}, bf16[192,2048]{1,0:T(8,128)(2,1)S(1)}, u32[]{:S(2)}, u32[]{:S(2)}) collective-permute-start(bf16[192,2048]{1,0:T(8,128)(2,1)} %get-tuple-element.134), channel_id=1, source_target_pairs={{0,2},{1,3},{2,6},{3,7},{4,0},{5,1},{6,10},{7,11},{8,4},{9,5},{10,... | collective-permute-start | bytes 2359304 | tf_op jit(solution)/shard_map/ppermute | solution.py:122
  628.8 38.0 %collective-permute-start.116 = (bf16[352,2048]{1,0:T(8,128)(2,1)}, bf16[352,2048]{1,0:T(8,128)(2,1)S(1)}, u32[]{:S(2)}, u32[]{:S(2)}) collective-permute-start(bf16[352,2048]{1,0:T(8,128)(2,1)} %add_convert_fusion.1), channel_id=1, source_target_pairs={{0,16},{16,0},{1,17},{17,1},{2,18},{18,2},{3,19},{19,3},{4,20},{20... | collective-permute-start | bytes 4325384 | tf_op jit(solution)/shard_map/ppermute | solution.py:1087
  657.4 22.4 %collective-permute-start.100 = (bf16[192,2048]{1,0:T(8,128)(2,1)}, bf16[192,2048]{1,0:T(8,128)(2,1)S(1)}, u32[]{:S(2)}, u32[]{:S(2)}) collective-permute-start(bf16[192,2048]{1,0:T(8,128)(2,1)} %get-tuple-element.135), channel_id=1, source_target_pairs={{0,4},{1,5},{2,0},{3,1},{4,8},{5,9},{6,2},{7,3},{8,12},{9,13},{10,... | collective-permute-start | bytes 2359304 | tf_op jit(solution)/shard_map/ppermute | solution.py:121
  658.0 21.8 %collective-permute-start.101 = (bf16[192,2048]{1,0:T(8,128)(2,1)}, bf16[192,2048]{1,0:T(8,128)(2,1)S(1)}, u32[]{:S(2)}, u32[]{:S(2)}) collective-permute-start(bf16[192,2048]{1,0:T(8,128)(2,1)} %get-tuple-element.136), channel_id=1, source_target_pairs={{0,2},{1,3},{2,6},{3,7},{4,0},{5,1},{6,10},{7,11},{8,4},{9,5},{10,... | collective-permute-start | bytes 2359304 | tf_op jit(solution)/shard_map/ppermute | solution.py:122
  (173 other events, 1722.2 us)

commit v4 on v3

--- a/solution.py
+++ b/solution.py
@@ -102,10 +102,12 @@
         low = lax.ppermute(ccw[h:], "shard", self.back)
         return found + [(self.half, 0, top), (self.half, h, low)]
 
-    def gather_both(self, block, ties=None):
-        own = self.gather(block, ties)
-        other = [(k + self.chips, row, self.swap(piece)) for k, row, piece in own]
-        return own + other, [piece for _, _, piece in own]
+    def gather_shared(self, mine, other, twin, ties=None):
+        own = self.gather(mine, ties)
+        found = [(k, row, 0, piece) for k, row, piece in own]
+        found += [(k, row, 1, twin(piece) if k else other) for k, row, piece in own]
+        found += [(k + self.chips, row, part, self.swap(piece)) for k, row, part, piece in found]
+        return found, [piece for _, _, piece in own]
 
     def scatter(self, parts, ties=None):
         n, m = self.chips, self.half
@@ -213,6 +215,16 @@
     ]
 
 
+def shared_fetches(side, pieces, refs, buffer, sems):
+    copies = []
+    for n, ((k, row, part, _), ref) in enumerate(zip(pieces, refs)):
+        rows, width = ref.shape
+        start = pl.multiple_of((side if part == 0 else 1 - side) * width, LANES)
+        target = buffer.at[k, pl.ds(row, rows), pl.ds(start, width)]
+        copies.append(pltpu.make_async_copy(ref, target, sems.at[n]))
+    return copies
+
+
 def block_at(place):
     return pl.ds(pl.multiple_of(place * LANES, LANES), LANES)
 
@@ -233,19 +245,42 @@
     )
 
 
-def pack_weight(weight, gain_one, gain_two):
+def pack_weight(weight, gain_one, gain_two, side):
     rows, width = weight.shape
-
-    def body(weight_ref, one_ref, two_ref, out_ref):
-        out_ref[:, :width] = weight_ref[...]
+    half = packed_width(width) // 2
+
+    def body(side_ref, weight_ref, one_ref, two_ref, mine_ref, other_ref):
         lane = lax.broadcasted_iota(jnp.int32, (rows, LANES), 1)
         block = jnp.where(lane == 0, one_ref[...], jnp.where(lane == 1, two_ref[...], 0.0))
-        out_ref[:, width:] = block.astype(BF16)
+        first = side_ref[0] == 0
+        tail = width - half
+
+        def put(start, stop, left, right):
+            mine_ref[:, start:stop] = jnp.where(first, left, right)
+            other_ref[:, start:stop] = jnp.where(first, right, left)
+
+        put(0, tail, weight_ref[:, :tail], weight_ref[:, half:])
+        put(tail, tail + LANES, weight_ref[:, tail : tail + LANES], block.astype(BF16))
+        if tail + LANES < half:
+            left = weight_ref[:, tail + LANES : half]
+            put(tail + LANES, half, left, jnp.zeros_like(left))
 
     gains = [g.astype(F32)[:, None] for g in (gain_one, gain_two)]
-    return pl.pallas_call(body, out_shape=shaped((rows, width + LANES), BF16), cost_estimate=takes(3), compiler_params=ROOMY)(
-        weight, *gains
-    )
+    return pl.pallas_call(
+        body,
+        grid_spec=pltpu.PrefetchScalarGridSpec(
+            num_scalar_prefetch=1,
+            grid=(1,),
+            in_specs=[whole(weight.shape)] + [whole((rows, 1))] * 2,
+            out_specs=[whole((rows, half))] * 2,
+        ),
+        out_shape=[shaped((rows, half), BF16)] * 2,
+        cost_estimate=takes(3), compiler_params=ROOMY,
+    )(side.astype(jnp.int32)[None], weight, *gains)
+
+
+def packed_width(width):
+    return -(-(width + LANES) // (2 * LANES)) * 2 * LANES
 
 
 def project(ring, hidden, cosine, sine, pieces, width, others):
@@ -258,7 +293,7 @@
         hidden_ref, cos_ref, sin_ref = ins
         q_ref, kv_ref, input_ref, factor_ref, gain_ref = outs
         buffer, sems = scratch
-        copies = fetches(pieces, refs, buffer, sems)
+        copies = shared_fetches(table[ring.side_at], pieces, refs, buffer, sems)
         for copy in copies:
             copy.start()
         values = hidden_ref[...].astype(F32)
@@ -298,9 +333,9 @@
             shaped((rows, LANES), F32),
             shaped((8, model), F32),
         ],
-        [piece for _, _, piece in pieces],
+        [piece for *_, piece in pieces],
         [
-            pltpu.VMEM((size, rows, width + LANES), BF16),
+            pltpu.VMEM((size, rows, packed_width(width)), BF16),
             pltpu.SemaphoreType.DMA((len(pieces),)),
         ],
         others,
@@ -337,7 +372,7 @@
         att_ref, hidden_ref, gain_ref = ins
         residual_ref, factor_ref, input_ref = outs
         buffer, sems = scratch
-        copies = fetches(pieces, refs, buffer, sems)
+        copies = shared_fetches(table[ring.side_at], pieces, refs, buffer, sems)
         for copy in copies:
             copy.start()
         for copy in copies:
@@ -362,7 +397,7 @@
         ring.table,
         [attended, hidden, gains],
         [shaped((rows, model), F32), shaped((rows, LANES), F32), shaped((rows, model), BF16)],
-        [piece for _, _, piece in pieces],
+        [piece for *_, piece in pieces],
         [
             pltpu.VMEM((size, rows, model), BF16),
             pltpu.SemaphoreType.DMA((len(pieces),)),
@@ -380,7 +415,7 @@
         own_ref, cw_ref, ccw_ref, residual_ref, factor_ref, gain_ref, cot_ref = ins
         grad_res_ref, half_ref, att_ref, term_ref = outs
         buffer, sems, total = scratch
-        copies = fetches(pieces, refs, buffer, sems)
+        copies = shared_fetches(table[ring.side_at], pieces, refs, buffer, sems)
         for copy in copies:
             copy.start()
         factor = factor_ref[...]
@@ -422,7 +457,7 @@
             shaped((rows, model), BF16),
             shaped((8, model), F32),
         ],
-        [piece for _, _, piece in pieces],
+        [piece for *_, piece in pieces],
         [
             pltpu.VMEM((size, rows, model), BF16),
             pltpu.SemaphoreType.DMA((len(pieces),)),
@@ -468,14 +503,14 @@
         gq_ref, gkv_ref, hidden_ref, factor_ref, gain_ref, grad_res_ref = ins
         grad_ref, term_ref = outs
         buffer, sems, total = scratch
-        copies = fetches(pieces, refs, buffer, sems)
+        copies = shared_fetches(table[ring.side_at], pieces, refs, buffer, sems)
         for copy in copies:
             copy.start()
         for copy in copies:
             copy.wait()
         queries, keys = gq_ref[...], gkv_ref[...]
         for k in range(0, size, 2):
-            weights = buffer[k : k + 2].reshape(2 * rows, width + LANES)
+            weights = buffer[k : k + 2].reshape(2 * rows, packed_width(width))
             total[:, k * LANES : (k + 2) * LANES] = dot(
                 queries, weights[:, :qsize], LAST
             ) + dot(keys, weights[:, qsize:width], LAST)
@@ -501,9 +536,9 @@
         ring.table,
         [grad_queries, grad_kv, hidden, factor, gains, grad_residual],
         [shaped((rows, model), BF16), shaped((8, model), F32)],
-        [piece for _, _, piece in pieces],
+        [piece for *_, piece in pieces],
         [
-            pltpu.VMEM((size, rows, width + LANES), BF16),
+            pltpu.VMEM((size, rows, packed_width(width)), BF16),
             pltpu.SemaphoreType.DMA((len(pieces),)),
             pltpu.VMEM((rows, model), F32),
         ],
@@ -849,11 +884,14 @@
             target[...] = other_ref[place - chips]
 
 
-def allowed_pairs(first_ref, reach, keys, rows):
+def write_bias(first_ref, bias, rows):
+    keys = bias.shape[0]
     key = lax.broadcasted_iota(jnp.int32, (keys, rows), 0)
     token = lax.broadcasted_iota(jnp.int32, (keys, rows), 1)
-    allowed = (key >= first_ref[...]) & (key <= token + reach)
-    return jnp.concatenate([allowed, allowed], 1)
+    allowed = (key >= first_ref[...]) & (key <= token + (keys - rows))
+    values = jnp.where(allowed, 0.0, -jnp.inf)
+    bias[:, :rows] = values
+    bias[:, rows:] = values
 
 
 def stacked(block, low_side):
@@ -867,28 +905,29 @@
 
 
 def attend_kernel(
-    ring, table, proj_ref, own_ref, other_ref, first_ref, cos_ref, sin_ref, q_ref, out_ref, log_ref, window
+    ring, table, proj_ref, own_ref, other_ref, first_ref, cos_ref, sin_ref, q_ref, out_ref, log_ref, window, turned, bias
 ):
     rows = proj_ref.shape[0]
-    keys = window.shape[0]
 
     @pl.when(pl.program_id(1) == 0)
     def _():
         load_window(table, ring.window, own_ref, other_ref, window, rows)
+        turned[...] = jnp.transpose(window[...].astype(F32)).astype(BF16)
+
+    @pl.when((pl.program_id(0) == 0) & (pl.program_id(1) == 0))
+    def _():
+        write_bias(first_ref, bias, rows)
 
     block = proj_ref[...]
     block = block * cos_ref[...] + rotated(block) * sin_ref[...]
     q_ref[...] = block.astype(BF16)
-    queries = stacked(block, True)
-    score = dot(window[...], queries, LAST) * SCALE
-    allowed = allowed_pairs(first_ref, keys - rows, keys, rows)
-    score = jnp.where(allowed, score, -jnp.inf)
+    queries = stacked(block * SCALE, True)
+    score = dot(window[...], queries, LAST) + bias[...]
     top = jnp.max(score, 0, keepdims=True)
     expon = jnp.exp(score - top)
     total = jnp.sum(expon, 0, keepdims=True)
     log_ref[0] = top + jnp.log(total)
-    probs = (expon * (1.0 / total)).astype(BF16)
-    out = dot(probs, window[...], FIRST)
+    out = jnp.transpose(dot(turned[...], expon.astype(BF16)) * (1.0 / total))
     one, two = out[:rows], out[rows:]
     out_ref[...] = jnp.where(lane_low(one.shape), pltpu.roll(one, HEAD_DIM, 1), two).astype(BF16)
 
@@ -909,7 +948,9 @@
     gown_ref,
     gother_ref,
     window,
+    turned,
     total,
+    bias,
 ):
     rows = q_ref.shape[0]
     keys = window.shape[0]
@@ -919,10 +960,15 @@
     @pl.when(step == 0)
     def _():
         load_window(table, ring.window, own_ref, other_ref, window, rows)
+        turned[...] = jnp.transpose(window[...].astype(F32)).astype(BF16)
         total[...] = jnp.zeros_like(total)
 
+    @pl.when((pl.program_id(0) == 0) & (step == 0))
+    def _():
+        write_bias(first_ref, bias, rows)
+
     grad = grad_ref[...].astype(F32)
-    queries = stacked(q_ref[...].astype(F32), True)
+    queries = stacked(q_ref[...].astype(F32) * SCALE, True)
     grads = stacked(grad, False)
     product = jnp.transpose(grad * att_ref[...].astype(F32))
     delta = jnp.concatenate(
@@ -932,13 +978,12 @@
         ],
         1,
     )
-    score = dot(window[...], queries, LAST) * SCALE
-    allowed = allowed_pairs(first_ref, keys - rows, keys, rows)
-    probs = jnp.where(allowed, jnp.exp(score - log_ref[0]), 0.0)
+    score = dot(window[...], queries, LAST) + bias[...]
+    probs = jnp.exp(score - log_ref[0])
     grad_probs = dot(window[...], grads, LAST)
-    grad_scores = (probs * (grad_probs - delta) * SCALE).astype(BF16)
+    grad_scores = (probs * (grad_probs - delta)).astype(BF16)
     total[...] += dot(grad_scores, queries) + dot(probs.astype(BF16), grads)
-    grad_queries = dot(grad_scores, window[...], FIRST)
+    grad_queries = jnp.transpose(dot(turned[...], grad_scores) * SCALE)
     one, two = grad_queries[:rows], grad_queries[rows:]
     block = jnp.where(lane_low(one.shape), one, pltpu.roll(two, HEAD_DIM, 1))
     gq_ref[...] = (block * cos_ref[...] - rotated(block) * sin_ref[...]).astype(BF16)
@@ -1015,7 +1060,11 @@
             (shaped((rows, pairs * LANES), BF16), near_block),
             (shaped((pairs, 1, 2 * rows), F32), log_block),
         ],
-        [pltpu.VMEM((keys, LANES), BF16)],
+        [
+            pltpu.VMEM((keys, LANES), BF16),
+            pltpu.VMEM((LANES, keys), BF16),
+            pltpu.VMEM((keys, 2 * rows), F32),
+        ],
         before,
         others,
         14,
@@ -1047,7 +1096,12 @@
             (shaped(own.shape, BF16), kv_block),
             (shaped(own.shape, BF16), kv_block),
         ],
-        [pltpu.VMEM((keys, LANES), BF16), pltpu.VMEM((keys, LANES), F32)],
+        [
+            pltpu.VMEM((keys, LANES), BF16),
+            pltpu.VMEM((LANES, keys), BF16),
+            pltpu.VMEM((keys, LANES), F32),
+            pltpu.VMEM((keys, 2 * rows), F32),
+        ],
         before,
         others,
         5,
@@ -1096,12 +1150,12 @@
         return mine.astype(F32) + twin(mine).astype(F32)
 
     mine = cut_columns(ring, gate_up_weight, wide)
+
+    packed = pack_weight(qkv_weight, attn_gain, ffn_gain, side)
+    qkv_pieces, qkv_marks = ring.gather_shared(*packed, twin)
     mine = lax.all_to_all(
-        mine, "shard", 0, 0, axis_index_groups=ring.core_groups, tiled=True
-    )
-
-    packed = pack_weight(qkv_weight, attn_gain, ffn_gain)
-    qkv_pieces, qkv_marks = ring.gather_both(packed)
+        after(mine, *qkv_marks[-2:]), "shard", 0, 0, axis_index_groups=ring.core_groups, tiled=True
+    )
 
     offset = ring.index * tok
     local_seg = lax.dynamic_slice_in_dim(seg_row, offset, tok)
@@ -1115,19 +1169,26 @@
     first = (starts - offset + (blocks - 1) * tok)[None, :]
 
     proj, kv_local, input_one, factor_one, gains = project(
-        ring, hidden, cosine, sine, qkv_pieces, width, (mine,)
-    )
-    kv_own = stack_blocks(ring, ring.gather(kv_local), ())
+        ring, hidden, cosine, sine, qkv_pieces, width, ()
+    )
+    kv_own = stack_blocks(ring, ring.gather(kv_local), (mine,))
     kv_other = ring.swap(kv_own)
-    out_pieces, out_marks = ring.gather_both(
-        after(out_weight, *qkv_marks[-2:]), {2: (kv_local,), 3: (kv_own,)}
-    )
-    theirs = twin(mine)
-    cots = ring.gather(after(cot_local, *out_marks[-2:]))
     tables = (kv_own, kv_other, first, cosine, sine)
     keys = blocks * tok
     kept = attend(ring, groups[0], (), keys, proj, *tables)
-    kept = attend(ring, groups[1], tuple(out_marks[5:7]), keys, proj, *tables, kept)
+    out_halves = [
+        lax.dynamic_slice_in_dim(out_weight, place * (model // 2), model // 2, 1)
+        for place in (side, 1 - side)
+    ]
+    out_pieces, out_marks = ring.gather_shared(
+        after(out_halves[0], *qkv_marks[-2:]),
+        out_halves[1],
+        twin,
+        {2: (kv_local,), 3: (kv_own,), 4: (kept[0],)},
+    )
+    theirs = twin(mine)
+    cots = ring.gather(after(cot_local, *out_marks[-2:]))
+    kept = attend(ring, groups[1], (), keys, proj, *tables, kept)
     queries, attended, logs = kept
     residual, factor_two, input_two = project_out(ring, attended, hidden, gains, out_pieces, ())
 

time: 710 us -> 696 us (0.980)
  waiting for transfers between devices: 259 us -> 246 us
    ppermute x7 -> x23, waiting for transfers between devices: 20.4 us -> 70.5 us  [twin(): return lax.ppermute(value, 'rep', twin_map)]
    ppermute x15, waiting for transfers between devices: 50.4 us -> 4.94 us  [gather(): cw = lax.ppermute(cw, 'shard', self.ahead)]
    ppermute x7 -> x23, starting transfers between devices: 6.17 us -> 25.4 us  [twin(): return lax.ppermute(value, 'rep', twin_map)]
    ppermute x15, waiting for transfers between devices: 75.2 us -> 64.9 us  [gather(): ccw = lax.ppermute(ccw, 'shard', self.back)]
    ppermute x15, starting transfers between devices: 22.2 us -> 12.6 us  [gather(): cw = lax.ppermute(cw, 'shard', self.ahead)]
    ppermute x15, starting transfers between devices: 24.2 us -> 16.5 us  [gather(): ccw = lax.ppermute(ccw, 'shard', self.back)]
    unnamed x211 -> x274, local copies, waits for them, and re-layouts: 28.7 us -> 26.6 us
  transfers between devices with their start and end apart: 119 -> 153, of which waited for: 45 -> 49; matrix products, arithmetic and copies ran while one was open for 6% -> 6% of each run, Pallas kernels for 24% -> 24%
where the time goes in v4:
time: 696 us; the launch traced here: 687 us
  waiting for transfers between devices  246 us (35%)
  Pallas kernels  237 us (34%)
  starting transfers between devices  130 us (19%)
  local copies, waits for them, and re-layouts  48.8 us (7%)
  other arithmetic  22.3 us (3%)
    ppermute x23, waiting for transfers between devices, twin(): return lax.ppermute(value, 'rep', twin_map)  70.5 us
    ppermute x15, waiting for transfers between devices, gather(): ccw = lax.ppermute(ccw, 'shard', self.back)  64.9 us
    pallas_call x4, Pallas kernels, attention_call(): pl.pallas_call(body, grid_spec=pltpu.PrefetchScalarGridSpec(num_scalar_pr...  52.9 us
    pallas_call x7, Pallas kernels, call(): pl.pallas_call(body, grid_spec=pltpu.PrefetchScalarGridSpec(num_scalar_pr...  52 us
    ppermute x20, waiting for transfers between devices, scatter(): ccw = lax.ppermute(ccw, 'shard', self.back)  49 us
    ppermute x20, waiting for transfers between devices, scatter(): cw = lax.ppermute(cw, 'shard', self.ahead)  46.7 us
    pallas_call x15, Pallas kernels, add_step(): pl.pallas_call(body, grid=(1,), in_specs=[pl.BlockSpec((rows, width), lam...  35.5 us
    pallas_call x1, Pallas kernels, feed_forward(): pl.pallas_call(body, grid_spec=pltpu.PrefetchScalarGridSpec(num_scalar_pr...  28.6 us
  transfers between devices with their start and end apart: 153, of which 49 were waited for; matrix products, arithmetic and copies ran while one was open for 6% of the time, Pallas kernels for 24%

profile of v4, /device:TPU:0, one launch (start us, length us, event | category | flops | bytes accessed | tf_op | source)
XLA Modules:
  0.0 687.0 jit_solution(13470688459726100914)
XLA Ops:
  9.0 8.2 %collective-permute-done.1.refs_5_.refs_8_ = bf16[128,1408]{1,0:T(8,128)(2,1)S(1)} collective-permute-done((bf16[128,1408]{1,0:T(8,128)(2,1)}, bf16[128,1408]{1,0:T(8,128)(2,1)S(1)}, u32[]{:S(2)}, u32[]{:S(2)}) %collective-permute-start.1) | collective-permute-done | bytes 360480 | tf_op jit(solution)/shard_map/ppermute | solution.py:99
  21.6 6.8 collective-permute-done.9.refs_14_.refs_17_
  36.6 6.8 collective-permute-done.11.refs_16_.refs_19_
  57.0 4.1 shard_map.163.refs_0_
  61.2 6.1 all-to-all-start
  69.1 6.8 collective-permute-done.15.refs_20_.refs_23_
  85.9 9.1 %shard_map.162 = (f32[128,2048]{1,0:T(8,128)}, bf16[128,512]{1,0:T(8,128)(2,1)}, bf16[128,2048]{1,0:T(8,128)(2,1)}, f32[128,128]{1,0:T(8,128)}, f32[8,2048]{1,0:T(8,128)}) custom-call(s32[75]{0:T(128)} %fusion.9.table_ref.table, bf16[128,2048]{1,0:T(8,128)(2,1)} %bitcast.58, f32[128,128]{1,0:T(8,128)} %get-tuple-element.169.refs_1_.refs_4_.refs_7_.refs_3_, ...), custom_call_target="tpu_custom_call" | custom-call | flops 9900000256 | bytes 29700000 | tf_op jit(solution)/shard_map/pallas_call | solution.py:184
  99.9 7.5 %collective-permute-done.35.refs_2_ = bf16[128,512]{1,0:T(8,128)(2,1)S(1)} collective-permute-done((bf16[128,512]{1,0:T(8,128)(2,1)}, bf16[128,512]{1,0:T(8,128)(2,1)S(1)}, u32[]{:S(2)}, u32[]{:S(2)}) %collective-permute-start.35) | collective-permute-done | bytes 131104 | tf_op jit(solution)/shard_map/ppermute | solution.py:99
  109.4 6.4 collective-permute-done.37.refs_4_
  148.9 4.3 collective-permute-done.53.refs_15_.refs_19_
  153.3 5.2 collective-permute-done.54.refs_16_.refs_20_
  168.2 5.5 collective-permute-done.57.refs_19_.refs_23_
  176.5 12.8 %shard_map.166 = (bf16[128,2048]{1,0:T(8,128)(2,1)}, bf16[128,2048]{1,0:T(8,128)(2,1)}, f32[16,1,256]{2,1,0:T(1,128)}) custom-call(s32[75]{0:T(128)} %fusion.9.table_ref.table, f32[128,2048]{1,0:T(8,128)} %get-tuple-element.82.refs_0_, bf16[8,128,512]{2,1,0:T(8,128)(2,1)} %shard_map.165.refs_1_.refs_4_, ...), custom_call_target="tpu_custom_call" | custom-call | flops 15399999488 | bytes 46200000 | tf_op jit(solution)/shard_map/pallas_call | solution.py:1022
  193.7 12.7 %shard_map.167 = (bf16[128,2048]{1,0:T(8,128)(2,1)}, bf16[128,2048]{1,0:T(8,128)(2,1)}, f32[16,1,256]{2,1,0:T(1,128)}) custom-call(s32[75]{0:T(128)} %fusion.9.table_ref.table, f32[128,2048]{1,0:T(8,128)} %get-tuple-element.82.refs_0_, bf16[8,128,512]{2,1,0:T(8,128)(2,1)} %shard_map.165.refs_1_.refs_4_, ...), custom_call_target="tpu_custom_call", output_to_operand_aliasing={{0}: (7, {}), {1}: (8, {}), {2}: (9, {})} | custom-call | flops 15399999488 | bytes 46200000 | tf_op jit(solution)/shard_map/pallas_call | solution.py:1022
  209.3 8.2 %shard_map.173 = (f32[128,2048]{1,0:T(8,128)}, f32[128,128]{1,0:T(8,128)}, bf16[128,2048]{1,0:T(8,128)(2,1)}) custom-call(s32[75]{0:T(128)} %fusion.9.table_ref.table, bf16[128,2048]{1,0:T(8,128)(2,1)} %get-tuple-element.87.refs_0_.refs_2_.input_ref, bf16[128,2048]{1,0:T(8,128)(2,1)} %bitcast.59, f32[8,2048]{1,0:T(8,128)} %get-tuple-element.88.refs_2_.refs_5_.refs_4_, ...), custom_call_target="tpu_custom_call" | custom-call | flops 8800000000 | bytes 26400000 | tf_op jit(solution)/shard_map/pallas_call | solution.py:184
  226.0 6.7 collective-permute-done.78.refs_2_
  233.5 10.4 %collective-permute-done.90.refs_15_ = bf16[128,2048]{1,0:T(8,128)(2,1)S(1)} collective-permute-done((bf16[128,2048]{1,0:T(8,128)(2,1)S(1)}, bf16[128,2048]{1,0:T(8,128)(2,1)S(1)}, u32[]{:S(2)}, u32[]{:S(2)}) %collective-permute-start.90) | collective-permute-done | bytes 524320 | tf_op jit(solution)/shard_map/ppermute | solution.py:99
  244.2 10.0 %collective-permute-done.80.refs_4_ = bf16[128,2048]{1,0:T(8,128)(2,1)S(1)} collective-permute-done((bf16[128,2048]{1,0:T(8,128)(2,1)S(1)}, bf16[128,2048]{1,0:T(8,128)(2,1)S(1)}, u32[]{:S(2)}, u32[]{:S(2)}) %collective-permute-start.80) | collective-permute-done | bytes 524320 | tf_op jit(solution)/shard_map/ppermute | solution.py:99
  256.3 10.8 %collective-permute-done.82.refs_6_ = bf16[128,2048]{1,0:T(8,128)(2,1)S(1)} collective-permute-done((bf16[128,2048]{1,0:T(8,128)(2,1)S(1)}, bf16[128,2048]{1,0:T(8,128)(2,1)S(1)}, u32[]{:S(2)}, u32[]{:S(2)}) %collective-permute-start.82) | collective-permute-done | bytes 524320 | tf_op jit(solution)/shard_map/ppermute | solution.py:99
  272.7 4.1 shard_map.175.refs_22_.down_ref
  280.5 28.6 %shard_map.176 = (bf16[1024,704]{1,0:T(8,128)(2,1)}, bf16[1024,704]{1,0:T(8,128)(2,1)}, bf16[1024,704]{1,0:T(8,128)(2,1)}, bf16[1024,2048]{1,0:T(8,128)(2,1)}, b...) custom-call(s32[75]{0:T(128)} %fusion.9.table_ref.table, bf16[128,2048]{1,0:T(8,128)(2,1)} %get-tuple-element.90.refs_0_, ...), custom_call_target="tpu_custom_call" | custom-call | flops 30799998976 | bytes 92400000 | tf_op jit(solution)/shard_map/pallas_call | solution.py:843
  309.1 7.1 %shard_map.177 = (bf16[1024,704]{1,0:T(8,128)(2,1)}, bf16[1024,704]{1,0:T(8,128)(2,1)}) custom-call(bf16[1024,2048]{1,0:T(8,128)(2,1)} %get-tuple-element.92.input_ref, bf16[1024,704]{1,0:T(8,128)(2,1)} %get-tuple-element.93.refs_0_, bf16[1024,704]{1,0:T(8,128)(2,1)} %get-tuple-element.94.refs_1_), custom_call_target="tpu_custom_call" | custom-call | flops 2310000128 | bytes 6930000 | tf_op jit(solution)/shard_map/pallas_call | solution.py:602
  323.3 6.2 collective-permute-done.100.ccw_ref
  339.6 9.3 %shard_map.178 = (f32[8,2,64,704]{3,2,1,0:T(8,128)}, bf16[8,2,64,704]{3,2,1,0:T(8,128)(2,1)}) custom-call(s32[75]{0:T(128)} %fusion.9.table_ref.table, bf16[1024,2048]{1,0:T(8,128)(2,1)} %get-tuple-element.92.input_ref, bf16[1024,704]{1,0:T(8,128)(2,1)} %get-tuple-element.93.refs_0_, bf16[1024,704]{1,0:T(8,128)(2,1)} %get-tuple-element.94.refs_1_, ...), custom_call_target="tpu_custom_call" | custom-call | flops 3464999936 | bytes 10395000 | tf_op jit(solution)/shard_map/pallas_call | solution.py:690
  354.7 7.2 %shard_map.179.refs_1_.ahead_ref.back_ref = bf16[1024,2048]{1,0:T(8,128)(2,1)} custom-call(bf16[1024,704]{1,0:T(8,128)(2,1)} %get-tuple-element.91.act_ref, bf16[704,2048]{1,0:T(8,128)(2,1)} %shard_map.175.refs_22_.down_ref, bf16[8,2,64,704]{3,2,1,0:T(8,128)(2,1)} %get-tuple-element.97.refs_0_.refs_1_), custom_call_target="tpu_custom_call" | custom-call | flops 2695000064 | bytes 8085000 | tf_op jit(solution)/shard_map/pallas_call | solution.py:739
  373.4 7.4 %collective-permute-done.105.refs_1_.refs_0_ = bf16[128,2048]{1,0:T(8,128)(2,1)S(1)} collective-permute-done((bf16[128,2048]{1,0:T(8,128)(2,1)}, bf16[128,2048]{1,0:T(8,128)(2,1)S(1)}, u32[]{:S(2)}, u32[]{:S(2)}) %collective-permute-start.105) | collective-permute-done | bytes 524320 | tf_op jit(solution)/shard_map/ppermute | solution.py:123
  384.1 10.4 %shard_map.192 = (f32[128,2048]{1,0:T(8,128)}, bf16[128,2048]{1,0:T(8,128)(2,1)}, bf16[128,2048]{1,0:T(8,128)(2,1)}, f32[8,2048]{1,0:T(8,128)}) custom-call(s32[75]{0:T(128)} %fusion.9.table_ref.table, bf16[128,2048]{1,0:T(8,128)(2,1)} %slice.127.refs_0_, bf16[128,2048]{1,0:T(8,128)(2,1)} %copy-done.12, bf16[128,2048]{1,0:T(8,128)(2,1)} %copy-done.13, ...), custom_call_target="tpu_custom_call" | custom-call | flops 3849999872 | bytes 11550000 | tf_op jit(solution)/shard_map/pallas_call | solution.py:184
  394.5 4.1 shard_map.194
  401.6 4.3 all-to-all-start.1
  409.8 13.7 %shard_map.193 = (bf16[128,2048]{1,0:T(8,128)(2,1)}, bf16[8,128,512]{2,1,0:T(8,128)(2,1)}, bf16[8,128,512]{2,1,0:T(8,128)(2,1)}) custom-call(s32[75]{0:T(128)} %fusion.9.table_ref.table, bf16[128,2048]{1,0:T(8,128)(2,1)} %get-tuple-element.111.refs_0_, bf16[128,2048]{1,0:T(8,128)(2,1)} %get-tuple-element.113.refs_1_, ...), custom_call_target="tpu_custom_call" | custom-call | flops 5500000256 | bytes 16500000 | tf_op jit(solution)/shard_map/pallas_call | solution.py:1022
  423.5 5.9 shard_map.195
  429.5 9.7 %collective-permute-done.107.cw_ref.refs_12_ = bf16[64,2048]{1,0:T(8,128)(2,1)S(1)} collective-permute-done((bf16[64,2048]{1,0:T(8,128)(2,1)}, bf16[64,2048]{1,0:T(8,128)(2,1)S(1)}, u32[]{:S(2)}, u32[]{:S(2)}) %collective-permute-start.107) | collective-permute-done | bytes 262176 | tf_op jit(solution)/shard_map/ppermute | solution.py:123
  439.2 5.1 all-to-all-done.1.refs_14_.refs_0_
  444.3 13.7 %shard_map.196 = (bf16[128,2048]{1,0:T(8,128)(2,1)}, bf16[8,128,512]{2,1,0:T(8,128)(2,1)}, bf16[8,128,512]{2,1,0:T(8,128)(2,1)}) custom-call(s32[75]{0:T(128)} %fusion.9.table_ref.table, bf16[128,2048]{1,0:T(8,128)(2,1)} %get-tuple-element.111.refs_0_, ...), custom_call_target="tpu_custom_call", output_to_operand_aliasing={{0}: (10, {}), {1}: (11, {}), {2}: (12, {})} | custom-call | flops 5500000256 | bytes 16500000 | tf_op jit(solution)/shard_map/pallas_call | solution.py:1022
  458.0 4.0 shard_map.197.refs_1_
  465.3 6.4 collective-permute-start.109
  473.7 13.1 %collective-permute-done.119.ccw_ref = bf16[64,512]{1,0:T(8,128)(2,1)S(1)} collective-permute-done((bf16[64,512]{1,0:T(8,128)(2,1)S(1)}, bf16[64,512]{1,0:T(8,128)(2,1)S(1)}, u32[]{:S(2)}, u32[]{:S(2)}) %collective-permute-start.119) | collective-permute-done | bytes 65568 | tf_op jit(solution)/shard_map/ppermute | solution.py:124
  500.9 12.2 %collective-permute-done.121.ccw_ref = bf16[128,512]{1,0:T(8,128)(2,1)S(1)} collective-permute-done((bf16[128,512]{1,0:T(8,128)(2,1)S(1)}, bf16[128,512]{1,0:T(8,128)(2,1)S(1)}, u32[]{:S(2)}, u32[]{:S(2)}) %collective-permute-start.121) | collective-permute-done | bytes 131104 | tf_op jit(solution)/shard_map/ppermute | solution.py:124
  516.9 7.0 %shard_map.201.refs_1_.ahead_ref.back_ref = bf16[1536,2048]{1,0:T(8,128)(2,1)} custom-call(bf16[128,2048]{1,0:T(8,128)(2,1)} %get-tuple-element.123.input_ref, bf16[128,2048]{1,0:T(8,128)(2,1)} %get-tuple-element.124.refs_0_.grad_ref, bf16[1024,2048]{1,0:T(8,128)(2,1)} %collective-permute-done.122.got_ref, f32[8,1,64,2048]{3,2,1,0:T(8,128)} %get-tuple-element.128.half_ref, ...), custom_call_target="tpu_custom_call" | custom-call | flops 2200000000 | bytes 6600000 | tf_op jit(solution)/shard_map/pallas_call | solution.py:655
  546.7 9.2 %collective-permute-done.126.refs_1_ = bf16[128,512]{1,0:T(8,128)(2,1)S(1)} collective-permute-done((bf16[128,512]{1,0:T(8,128)(2,1)}, bf16[128,512]{1,0:T(8,128)(2,1)S(1)}, u32[]{:S(2)}, u32[]{:S(2)}) %collective-permute-start.126) | collective-permute-done | bytes 131104 | tf_op jit(solution)/shard_map/ppermute | solution.py:123
  562.9 10.1 %shard_map.219 = (f32[352,2048]{1,0:T(8,128)}, bf16[352,2048]{1,0:T(8,128)(2,1)}) custom-call(s32[75]{0:T(128)} %fusion.9.table_ref.table, bf16[1024,704]{1,0:T(8,128)(2,1)} %get-tuple-element.91.act_ref, bf16[1024,2048]{1,0:T(8,128)(2,1)} %get-tuple-element.149.cot_ref, bf16[128,2048]{1,0:T(8,128)(2,1)} %copy-done.12, bf16[128,2048]{1,0:T(8,128)(2,1)} %copy-done.13), custom_call_target="tpu_custom_call" | custom-call | flops 3849999872 | bytes 11550000 | tf_op jit(solution)/shard_map/pallas_call | solution.py:717
  576.5 11.7 %shard_map.208 = (bf16[128,2048]{1,0:T(8,128)(2,1)}, f32[8,2048]{1,0:T(8,128)}) custom-call(s32[75]{0:T(128)} %fusion.9.table_ref.table, bf16[128,2048]{1,0:T(8,128)(2,1)} %get-tuple-element.124.refs_0_.grad_ref, bf16[128,512]{1,0:T(8,128)(2,1)} %shard_map.205.refs_1_.refs_0_.refs_2_, bf16[128,2048]{1,0:T(8,128)(2,1)} %bitcast.60, ...), custom_call_target="tpu_custom_call" | custom-call | flops 4427500032 | bytes 13282500 | tf_op jit(solution)/shard_map/pallas_call | solution.py:184
  603.9 11.2 %collective-permute-done.140.ccw_ref = bf16[72,512]{1,0:T(8,128)(2,1)S(1)} collective-permute-done((bf16[72,512]{1,0:T(8,128)(2,1)S(1)}, bf16[72,512]{1,0:T(8,128)(2,1)S(1)}, u32[]{:S(2)}, u32[]{:S(2)}) %collective-permute-start.140) | collective-permute-done | bytes 73760 | tf_op jit(solution)/shard_map/ppermute | solution.py:124
  618.8 4.8 collective-permute-done.141.cw_ref.refs_1_
  624.8 4.1 collective-permute-done.142.ccw_ref.refs_2_
  634.7 5.9 shard_map.218
  654.2 9.4 %collective-permute-done.145 = bf16[144,512]{1,0:T(8,128)(2,1)S(1)} collective-permute-done((bf16[144,512]{1,0:T(8,128)(2,1)}, bf16[144,512]{1,0:T(8,128)(2,1)S(1)}, u32[]{:S(2)}, u32[]{:S(2)}) %collective-permute-start.145) | collective-permute-done | bytes 147488 | tf_op jit(solution)/shard_map/ppermute | solution.py:123
  672.7 11.4 %collective-permute-done.136 = bf16[192,2048]{1,0:T(8,128)(2,1)S(1)} collective-permute-done((bf16[192,2048]{1,0:T(8,128)(2,1)S(1)}, bf16[192,2048]{1,0:T(8,128)(2,1)S(1)}, u32[]{:S(2)}, u32[]{:S(2)}) %collective-permute-start.136) | collective-permute-done | bytes 786464 | tf_op jit(solution)/shard_map/ppermute | solution.py:1141
  (644 shorter events, 278.6 us)
Async XLA Ops:
  51.1 24.9 %collective-permute-start.22 = (bf16[128,1408]{1,0:T(8,128)(2,1)S(1)}, bf16[128,1408]{1,0:T(8,128)(2,1)}, u32[]{:S(2)}, u32[]{:S(2)}) collective-permute-start(bf16[128,1408]{1,0:T(8,128)(2,1)S(1)} %collective-permute-done.5.refs_9_.refs_12_), channel_id=1, source_target_pairs={{0,1},{1,0},{2,3},{3,2},{4,5},{5,4},{6,7},{7,6},{8,9},{9,8},{10,11... | collective-permute-start | bytes 1081352 | tf_op jit(solution)/shard_map/ppermute | solution.py:89
  54.4 22.1 %collective-permute-start.13 = (bf16[128,1408]{1,0:T(8,128)(2,1)S(1)}, bf16[128,1408]{1,0:T(8,128)(2,1)}, u32[]{:S(2)}, u32[]{:S(2)}) collective-permute-start(bf16[128,1408]{1,0:T(8,128)(2,1)S(1)} %collective-permute-done.5.refs_9_.refs_12_), channel_id=1, source_target_pairs={{0,16},{16,0},{1,17},{17,1},{2,18},{18,2},{3,19},{19,3},{4,20},{20... | collective-permute-start | bytes 1081352 | tf_op jit(solution)/shard_map/ppermute | solution.py:1141
  56.1 22.1 %collective-permute-start.12 = (bf16[128,1408]{1,0:T(8,128)(2,1)S(1)}, bf16[128,1408]{1,0:T(8,128)(2,1)}, u32[]{:S(2)}, u32[]{:S(2)}) collective-permute-start(bf16[128,1408]{1,0:T(8,128)(2,1)S(1)} %collective-permute-done.4.refs_8_.refs_11_), channel_id=1, source_target_pairs={{0,16},{16,0},{1,17},{17,1},{2,18},{18,2},{3,19},{19,3},{4,20},{20... | collective-permute-start | bytes 1081352 | tf_op jit(solution)/shard_map/ppermute | solution.py:1141
  56.4 21.7 %collective-permute-start.28 = (bf16[128,1408]{1,0:T(8,128)(2,1)}, bf16[128,1408]{1,0:T(8,128)(2,1)}, u32[]{:S(2)}, u32[]{:S(2)}) collective-permute-start(bf16[128,1408]{1,0:T(8,128)(2,1)} %collective-permute-done.10.refs_15_.refs_18_), channel_id=1, source_target_pairs={{0,1},{1,0},{2,3},{3,2},{4,5},{5,4},{6,7},{7,6},{8,9},{9,8},{10,11... | collective-permute-start | bytes 1081352 | tf_op jit(solution)/shard_map/ppermute | solution.py:89
  61.2 75.4 %all-to-all-start = ((bf16[8,2,64,704]{3,2,1,0:T(8,128)(2,1)}), bf16[8,2,64,704]{3,2,1,0:T(8,128)(2,1)S(1)}, u32[]{:S(2)}, u32[]{:S(2)}) async-start(bf16[8,2,64,704]{3,2,1,0:T(8,128)(2,1)} %shard_map.164), calls=%async_computation | async-start | bytes 3145728 | tf_op jit(solution)/shard_map/all_to_all | solution.py:1156
  97.8 20.0 %collective-permute-start.44 = (bf16[128,1024]{1,0:T(8,128)(2,1)}, bf16[128,1024]{1,0:T(8,128)(2,1)S(1)}, u32[]{:S(2)}, u32[]{:S(2)}) collective-permute-start(bf16[128,1024]{1,0:T(8,128)(2,1)} %shard_map.168.refs_3_.refs_7_), channel_id=1, source_target_pairs={{0,2},{1,3},{2,6},{3,7},{4,0},{5,1},{6,10},{7,11},{8,4},{9,5},{10,... | collective-permute-start | bytes 786440 | tf_op jit(solution)/shard_map/ppermute | solution.py:99
  99.5 18.8 %collective-permute-start.43 = (bf16[128,1024]{1,0:T(8,128)(2,1)}, bf16[128,1024]{1,0:T(8,128)(2,1)S(1)}, u32[]{:S(2)}, u32[]{:S(2)}) collective-permute-start(bf16[128,1024]{1,0:T(8,128)(2,1)} %shard_map.168.refs_3_.refs_7_), channel_id=1, source_target_pairs={{0,4},{1,5},{2,0},{3,1},{4,8},{5,9},{6,2},{7,3},{8,12},{9,13},{10,... | collective-permute-start | bytes 786440 | tf_op jit(solution)/shard_map/ppermute | solution.py:98
  140.1 35.9 %collective-permute-start.42 = (bf16[8,128,512]{2,1,0:T(8,128)(2,1)}, bf16[8,128,512]{2,1,0:T(8,128)(2,1)}, u32[]{:S(2)}, u32[]{:S(2)}) collective-permute-start(bf16[8,128,512]{2,1,0:T(8,128)(2,1)} %shard_map.165.refs_1_.refs_4_), channel_id=1, source_target_pairs={{0,1},{1,0},{2,3},{3,2},{4,5},{5,4},{6,7},{7,6},{8,9},{9,8},{10,11... | collective-permute-start | bytes 3145736 | tf_op jit(solution)/shard_map/ppermute | solution.py:89
  173.6 17.4 %collective-permute-start.65 = (bf16[128,1024]{1,0:T(8,128)(2,1)S(1)}, bf16[128,1024]{1,0:T(8,128)(2,1)S(1)}, u32[]{:S(2)}, u32[]{:S(2)}) collective-permute-start(bf16[128,1024]{1,0:T(8,128)(2,1)S(1)} %collective-permute-done.48.refs_9_.refs_13_), channel_id=1, source_target_pairs={{0,1},{1,0},{2,3},{3,2},{4,5},{5,4},{6,7},{7,6},{8,9},{9,8},{10,11... | collective-permute-start | bytes 786440 | tf_op jit(solution)/shard_map/ppermute | solution.py:89
  173.6 18.0 %collective-permute-start.56 = (bf16[128,1024]{1,0:T(8,128)(2,1)S(1)}, bf16[128,1024]{1,0:T(8,128)(2,1)S(1)}, u32[]{:S(2)}, u32[]{:S(2)}) collective-permute-start(bf16[128,1024]{1,0:T(8,128)(2,1)S(1)} %collective-permute-done.48.refs_9_.refs_13_), channel_id=1, source_target_pairs={{0,16},{16,0},{1,17},{17,1},{2,18},{18,2},{3,19},{19,3},{4,20},{20... | collective-permute-start | bytes 786440 | tf_op jit(solution)/shard_map/ppermute | solution.py:1141
  176.0 17.2 %collective-permute-start.75 = (bf16[64,1024]{1,0:T(8,128)(2,1)S(1)}, bf16[64,1024]{1,0:T(8,128)(2,1)S(1)}, u32[]{:S(2)}, u32[]{:S(2)}) collective-permute-start(bf16[64,1024]{1,0:T(8,128)(2,1)S(1)} %collective-permute-done.57.refs_19_.refs_23_), channel_id=1, source_target_pairs={{0,1},{1,0},{2,3},{3,2},{4,5},{5,4},{6,7},{7,6},{8,9},{9,8},{10,11... | collective-permute-start | bytes 393224 | tf_op jit(solution)/shard_map/ppermute | solution.py:89
  176.0 17.2 %collective-permute-start.76 = (bf16[64,1024]{1,0:T(8,128)(2,1)S(1)}, bf16[64,1024]{1,0:T(8,128)(2,1)S(1)}, u32[]{:S(2)}, u32[]{:S(2)}) collective-permute-start(bf16[64,1024]{1,0:T(8,128)(2,1)S(1)} %collective-permute-done.58.refs_20_.refs_24_), channel_id=1, source_target_pairs={{0,1},{1,0},{2,3},{3,2},{4,5},{5,4},{6,7},{7,6},{8,9},{9,8},{10,11... | collective-permute-start | bytes 393224 | tf_op jit(solution)/shard_map/ppermute | solution.py:89
  189.4 36.6 %collective-permute-start.93 = (bf16[8,2,64,704]{3,2,1,0:T(8,128)(2,1)S(1)}, bf16[8,2,64,704]{3,2,1,0:T(8,128)(2,1)}, u32[]{:S(2)}, u32[]{:S(2)}) collective-permute-start(bf16[8,2,64,704]{3,2,1,0:T(8,128)(2,1)S(1)} %copy-done.22), channel_id=1, source_target_pairs={{0,16},{16,0},{1,17},{17,1},{2,18},{18,2},{3,19},{19,3},{4,20},{20... | collective-permute-start | bytes 4325384 | tf_op jit(solution)/shard_map/ppermute | solution.py:1141
  220.8 23.1 %collective-permute-start.90 = (bf16[128,2048]{1,0:T(8,128)(2,1)S(1)}, bf16[128,2048]{1,0:T(8,128)(2,1)S(1)}, u32[]{:S(2)}, u32[]{:S(2)}) collective-permute-start(bf16[128,2048]{1,0:T(8,128)(2,1)S(1)} %collective-permute-done.88.refs_13_), channel_id=1, source_target_pairs={{0,2},{1,3},{2,6},{3,7},{4,0},{5,1},{6,10},{7,11},{8,4},{9,5},{10,... | collective-permute-start | bytes 1572872 | tf_op jit(solution)/shard_map/ppermute | solution.py:99
  221.4 22.7 %collective-permute-start.89 = (bf16[128,2048]{1,0:T(8,128)(2,1)S(1)}, bf16[128,2048]{1,0:T(8,128)(2,1)S(1)}, u32[]{:S(2)}, u32[]{:S(2)}) collective-permute-start(bf16[128,2048]{1,0:T(8,128)(2,1)S(1)} %collective-permute-done.87.refs_12_), channel_id=1, source_target_pairs={{0,4},{1,5},{2,0},{3,1},{4,8},{5,9},{6,2},{7,3},{8,12},{9,13},{10,... | collective-permute-start | bytes 1572872 | tf_op jit(solution)/shard_map/ppermute | solution.py:98
  226.0 43.2 %collective-permute-start.96 = (bf16[352,2048]{1,0:T(8,128)(2,1)S(1)}, bf16[352,2048]{1,0:T(8,128)(2,1)S(1)}, u32[]{:S(2)}, u32[]{:S(2)}) collective-permute-start(bf16[352,2048]{1,0:T(8,128)(2,1)S(1)} %copy-done.82), channel_id=1, source_target_pairs={{0,1},{1,0},{2,3},{3,2},{4,5},{5,4},{6,7},{7,6},{8,9},{9,8},{10,11... | collective-permute-start | bytes 4325384 | tf_op jit(solution)/shard_map/ppermute | solution.py:89
  232.7 37.2 %collective-permute-start.94 = (bf16[8,2,64,704]{3,2,1,0:T(8,128)(2,1)S(1)}, bf16[8,2,64,704]{3,2,1,0:T(8,128)(2,1)S(1)}, u32[]{:S(2)}, u32[]{:S(2)}) collective-permute-start(bf16[8,2,64,704]{3,2,1,0:T(8,128)(2,1)S(1)} %copy-done.22), channel_id=1, source_target_pairs={{0,1},{1,0},{2,3},{3,2},{4,5},{5,4},{6,7},{7,6},{8,9},{9,8},{10,11... | collective-permute-start | bytes 4325384 | tf_op jit(solution)/shard_map/ppermute | solution.py:89
  233.3 20.8 %collective-permute-start.80 = (bf16[128,2048]{1,0:T(8,128)(2,1)S(1)}, bf16[128,2048]{1,0:T(8,128)(2,1)S(1)}, u32[]{:S(2)}, u32[]{:S(2)}) collective-permute-start(bf16[128,2048]{1,0:T(8,128)(2,1)S(1)} %collective-permute-done.78.refs_2_), channel_id=1, source_target_pairs={{0,2},{1,3},{2,6},{3,7},{4,0},{5,1},{6,10},{7,11},{8,4},{9,5},{10,... | collective-permute-start | bytes 1572872 | tf_op jit(solution)/shard_map/ppermute | solution.py:99
  244.1 35.6 %collective-permute-start.95 = (bf16[8,2,64,704]{3,2,1,0:T(8,128)(2,1)}, bf16[8,2,64,704]{3,2,1,0:T(8,128)(2,1)}, u32[]{:S(2)}, u32[]{:S(2)}) collective-permute-start(bf16[8,2,64,704]{3,2,1,0:T(8,128)(2,1)} %collective-permute-done.93.refs_19_), channel_id=1, source_target_pairs={{0,1},{1,0},{2,3},{3,2},{4,5},{5,4},{6,7},{7,6},{8,9},{9,8},{10,11... | collective-permute-start | bytes 4325384 | tf_op jit(solution)/shard_map/ppermute | solution.py:89
  318.1 17.3 %collective-permute-start.98 = (bf16[1024,704]{0,1:T(8,128)(2,1)S(1)}, bf16[1024,704]{0,1:T(8,128)(2,1)}, u32[]{:S(2)}, u32[]{:S(2)}) collective-permute-start(bf16[1024,704]{0,1:T(8,128)(2,1)S(1)} %copy.60), channel_id=1, source_target_pairs={{0,1},{1,0},{2,3},{3,2},{4,5},{5,4},{6,7},{7,6},{8,9},{9,8},{10,11... | collective-permute-start | bytes 4325384 | tf_op jit(solution)/shard_map/ppermute | solution.py:89
  319.7 18.3 %collective-permute-start.97 = (bf16[1024,704]{0,1:T(8,128)(2,1)}, bf16[1024,704]{0,1:T(8,128)(2,1)S(1)}, u32[]{:S(2)}, u32[]{:S(2)}) collective-permute-start(bf16[1024,704]{0,1:T(8,128)(2,1)} %copy.59), channel_id=1, source_target_pairs={{0,1},{1,0},{2,3},{3,2},{4,5},{5,4},{6,7},{7,6},{8,9},{9,8},{10,11... | collective-permute-start | bytes 4325384 | tf_op jit(solution)/shard_map/ppermute | solution.py:89
  348.9 35.2 %collective-permute-start.115 = (bf16[8,2,64,704]{3,2,1,0:T(8,128)(2,1)}, bf16[8,2,64,704]{3,2,1,0:T(8,128)(2,1)}, u32[]{:S(2)}, u32[]{:S(2)}) collective-permute-start(bf16[8,2,64,704]{3,2,1,0:T(8,128)(2,1)} %get-tuple-element.97.refs_0_.refs_1_), channel_id=1, source_target_pairs={{0,16},{16,0},{1,17},{17,1},{2,18},{18,2},{3,19},{19,3},{4,20},{20... | collective-permute-start | bytes 4325384 | tf_op jit(solution)/shard_map/ppermute | solution.py:1141
  398.6 24.9 %collective-permute-start.116 = (bf16[1024,2048]{1,0:T(8,128)(2,1)}, bf16[1024,2048]{1,0:T(8,128)(2,1)}, u32[]{:S(2)}, u32[]{:S(2)}) collective-permute-start(bf16[1024,2048]{1,0:T(8,128)(2,1)} %shard_map.194), channel_id=1, source_target_pairs={{0,1},{1,0},{2,3},{3,2},{4,5},{5,4},{6,7},{7,6},{8,9},{9,8},{10,11... | collective-permute-start | bytes 12582920 | tf_op jit(solution)/shard_map/ppermute | solution.py:89
  401.6 42.7 %all-to-all-start.1 = ((bf16[8,2,64,704]{3,2,1,0:T(8,128)(2,1)}), bf16[8,2,64,704]{3,2,1,0:T(8,128)(2,1)}, u32[]{:S(2)}, u32[]{:S(2)}) async-start(bf16[8,2,64,704]{3,2,1,0:T(8,128)(2,1)} %add_convert_fusion), calls=%async_computation.1 | async-start | bytes 3145728 | tf_op jit(solution)/shard_map/all_to_all | solution.py:1207
  407.7 31.4 %collective-permute-start.107 = (bf16[64,2048]{1,0:T(8,128)(2,1)}, bf16[64,2048]{1,0:T(8,128)(2,1)S(1)}, u32[]{:S(2)}, u32[]{:S(2)}) collective-permute-start(bf16[64,2048]{1,0:T(8,128)(2,1)} %shard_map.187), channel_id=1, source_target_pairs={{0,4},{1,5},{2,0},{3,1},{4,8},{5,9},{6,2},{7,3},{8,12},{9,13},{10,... | collective-permute-start | bytes 786440 | tf_op jit(solution)/shard_map/ppermute | solution.py:123
  409.6 29.5 %collective-permute-start.108 = (bf16[64,2048]{1,0:T(8,128)(2,1)}, bf16[64,2048]{1,0:T(8,128)(2,1)S(1)}, u32[]{:S(2)}, u32[]{:S(2)}) collective-permute-start(bf16[64,2048]{1,0:T(8,128)(2,1)} %shard_map.188), channel_id=1, source_target_pairs={{0,2},{1,3},{2,6},{3,7},{4,0},{5,1},{6,10},{7,11},{8,4},{9,5},{10,... | collective-permute-start | bytes 786440 | tf_op jit(solution)/shard_map/ppermute | solution.py:124
  462.0 53.6 %collective-permute-start.122 = (bf16[1024,2048]{1,0:T(8,128)(2,1)}, bf16[1024,2048]{1,0:T(8,128)(2,1)}, u32[]{:S(2)}, u32[]{:S(2)}) collective-permute-start(bf16[1024,2048]{1,0:T(8,128)(2,1)} %shard_map.197.refs_1_), channel_id=1, source_target_pairs={{0,1},{1,0},{2,3},{3,2},{4,5},{5,4},{6,7},{7,6},{8,9},{9,8},{10,11... | collective-permute-start | bytes 12582920 | tf_op jit(solution)/shard_map/ppermute | solution.py:89
  462.5 53.1 %collective-permute-start.123 = (bf16[8,1,64,2048]{3,2,1,0:T(8,128)(2,1)}, bf16[8,1,64,2048]{3,2,1,0:T(8,128)(2,1)S(1)}, u32[]{:S(2)}, u32[]{:S(2)}) collective-permute-start(bf16[8,1,64,2048]{3,2,1,0:T(8,128)(2,1)} %get-tuple-element.120.refs_15_), channel_id=1, source_target_pairs={{0,16},{16,0},{1,17},{17,1},{2,18},{18,2},{3,19},{19,3},{4,20},{20... | collective-permute-start | bytes 6291464 | tf_op jit(solution)/shard_map/ppermute | solution.py:1141
  465.3 29.5 %collective-permute-start.109 = (bf16[128,2048]{1,0:T(8,128)(2,1)}, bf16[128,2048]{1,0:T(8,128)(2,1)S(1)}, u32[]{:S(2)}, u32[]{:S(2)}) collective-permute-start(bf16[128,2048]{1,0:T(8,128)(2,1)} %get-tuple-element.105), channel_id=1, source_target_pairs={{0,4},{1,5},{2,0},{3,1},{4,8},{5,9},{6,2},{7,3},{8,12},{9,13},{10,... | collective-permute-start | bytes 1572872 | tf_op jit(solution)/shard_map/ppermute | solution.py:123
  471.7 23.1 %collective-permute-start.110 = (bf16[128,2048]{1,0:T(8,128)(2,1)}, bf16[128,2048]{1,0:T(8,128)(2,1)}, u32[]{:S(2)}, u32[]{:S(2)}) collective-permute-start(bf16[128,2048]{1,0:T(8,128)(2,1)} %get-tuple-element.106), channel_id=1, source_target_pairs={{0,2},{1,3},{2,6},{3,7},{4,0},{5,1},{6,10},{7,11},{8,4},{9,5},{10,... | collective-permute-start | bytes 1572872 | tf_op jit(solution)/shard_map/ppermute | solution.py:124
  498.2 25.7 %collective-permute-start.111 = (bf16[128,2048]{1,0:T(8,128)(2,1)}, bf16[128,2048]{1,0:T(8,128)(2,1)S(1)}, u32[]{:S(2)}, u32[]{:S(2)}) collective-permute-start(bf16[128,2048]{1,0:T(8,128)(2,1)} %get-tuple-element.107), channel_id=1, source_target_pairs={{0,4},{1,5},{2,0},{3,1},{4,8},{5,9},{6,2},{7,3},{8,12},{9,13},{10,... | collective-permute-start | bytes 1572872 | tf_op jit(solution)/shard_map/ppermute | solution.py:123
  498.5 25.4 %collective-permute-start.112 = (bf16[128,2048]{1,0:T(8,128)(2,1)}, bf16[128,2048]{1,0:T(8,128)(2,1)S(1)}, u32[]{:S(2)}, u32[]{:S(2)}) collective-permute-start(bf16[128,2048]{1,0:T(8,128)(2,1)} %get-tuple-element.108), channel_id=1, source_target_pairs={{0,2},{1,3},{2,6},{3,7},{4,0},{5,1},{6,10},{7,11},{8,4},{9,5},{10,... | collective-permute-start | bytes 1572872 | tf_op jit(solution)/shard_map/ppermute | solution.py:124
  533.0 40.0 %collective-permute-start.113 = (bf16[128,2048]{1,0:T(8,128)(2,1)}, bf16[128,2048]{1,0:T(8,128)(2,1)S(1)}, u32[]{:S(2)}, u32[]{:S(2)}) collective-permute-start(bf16[128,2048]{1,0:T(8,128)(2,1)} %get-tuple-element.109), channel_id=1, source_target_pairs={{0,4},{1,5},{2,0},{3,1},{4,8},{5,9},{6,2},{7,3},{8,12},{9,13},{10,... | collective-permute-start | bytes 1572872 | tf_op jit(solution)/shard_map/ppermute | solution.py:123
  537.3 18.6 %collective-permute-start.126 = (bf16[128,512]{1,0:T(8,128)(2,1)}, bf16[128,512]{1,0:T(8,128)(2,1)S(1)}, u32[]{:S(2)}, u32[]{:S(2)}) collective-permute-start(bf16[128,512]{1,0:T(8,128)(2,1)} %get-tuple-element.130), channel_id=1, source_target_pairs={{0,4},{1,5},{2,0},{3,1},{4,8},{5,9},{6,2},{7,3},{8,12},{9,13},{10,... | collective-permute-start | bytes 393224 | tf_op jit(solution)/shard_map/ppermute | solution.py:123
  538.8 18.5 %collective-permute-start.127 = (bf16[128,512]{1,0:T(8,128)(2,1)}, bf16[128,512]{1,0:T(8,128)(2,1)S(1)}, u32[]{:S(2)}, u32[]{:S(2)}) collective-permute-start(bf16[128,512]{1,0:T(8,128)(2,1)} %get-tuple-element.131), channel_id=1, source_target_pairs={{0,2},{1,3},{2,6},{3,7},{4,0},{5,1},{6,10},{7,11},{8,4},{9,5},{10,... | collective-permute-start | bytes 393224 | tf_op jit(solution)/shard_map/ppermute | solution.py:124
  540.9 33.5 %collective-permute-start.114 = (bf16[128,2048]{1,0:T(8,128)(2,1)S(1)}, bf16[128,2048]{1,0:T(8,128)(2,1)S(1)}, u32[]{:S(2)}, u32[]{:S(2)}) collective-permute-start(bf16[128,2048]{1,0:T(8,128)(2,1)S(1)} %copy-done.92), channel_id=1, source_target_pairs={{0,2},{1,3},{2,6},{3,7},{4,0},{5,1},{6,10},{7,11},{8,4},{9,5},{10,... | collective-permute-start | bytes 1572872 | tf_op jit(solution)/shard_map/ppermute | solution.py:124
  545.5 29.8 %collective-permute-start.130 = (bf16[192,2048]{1,0:T(8,128)(2,1)}, bf16[192,2048]{1,0:T(8,128)(2,1)S(1)}, u32[]{:S(2)}, u32[]{:S(2)}) collective-permute-start(bf16[192,2048]{1,0:T(8,128)(2,1)} %get-tuple-element.134), channel_id=1, source_target_pairs={{0,4},{1,5},{2,0},{3,1},{4,8},{5,9},{6,2},{7,3},{8,12},{9,13},{10,... | collective-permute-start | bytes 2359304 | tf_op jit(solution)/shard_map/ppermute | solution.py:123
  555.9 19.4 %collective-permute-start.131 = (bf16[192,2048]{1,0:T(8,128)(2,1)}, bf16[192,2048]{1,0:T(8,128)(2,1)S(1)}, u32[]{:S(2)}, u32[]{:S(2)}) collective-permute-start(bf16[192,2048]{1,0:T(8,128)(2,1)} %get-tuple-element.135), channel_id=1, source_target_pairs={{0,2},{1,3},{2,6},{3,7},{4,0},{5,1},{6,10},{7,11},{8,4},{9,5},{10,... | collective-permute-start | bytes 2359304 | tf_op jit(solution)/shard_map/ppermute | solution.py:124
  562.9 31.5 %collective-permute-start.137 = (bf16[1024,512]{1,0:T(8,128)(2,1)}, bf16[1024,512]{1,0:T(8,128)(2,1)}, u32[]{:S(2)}, u32[]{:S(2)}) collective-permute-start(bf16[1024,512]{1,0:T(8,128)(2,1)} %shard_map.211), channel_id=1, source_target_pairs={{0,1},{1,0},{2,3},{3,2},{4,5},{5,4},{6,7},{7,6},{8,9},{9,8},{10,11... | collective-permute-start | bytes 3145736 | tf_op jit(solution)/shard_map/ppermute | solution.py:89
  573.0 26.0 %collective-permute-start.149 = (bf16[352,2048]{1,0:T(8,128)(2,1)}, bf16[352,2048]{1,0:T(8,128)(2,1)S(1)}, u32[]{:S(2)}, u32[]{:S(2)}) collective-permute-start(bf16[352,2048]{1,0:T(8,128)(2,1)} %get-tuple-element.151), channel_id=1, source_target_pairs={{0,1},{1,0},{2,3},{3,2},{4,5},{5,4},{6,7},{7,6},{8,9},{9,8},{10,11... | collective-permute-start | bytes 4325384 | tf_op jit(solution)/shard_map/ppermute | solution.py:89
  574.5 60.2 %collective-permute-start.148 = (bf16[8,2,64,704]{3,2,1,0:T(8,128)(2,1)}, bf16[8,2,64,704]{3,2,1,0:T(8,128)(2,1)}, u32[]{:S(2)}, u32[]{:S(2)}) collective-permute-start(bf16[8,2,64,704]{3,2,1,0:T(8,128)(2,1)} %all-to-all-done.1.refs_14_.refs_0_), channel_id=1, source_target_pairs={{0,16},{16,0},{1,17},{17,1},{2,18},{18,2},{3,19},{19,3},{4,20},{20... | collective-permute-start | bytes 4325384 | tf_op jit(solution)/shard_map/ppermute | solution.py:1141
  592.3 39.2 %collective-permute-start.132 = (bf16[192,2048]{1,0:T(8,128)(2,1)}, bf16[192,2048]{1,0:T(8,128)(2,1)S(1)}, u32[]{:S(2)}, u32[]{:S(2)}) collective-permute-start(bf16[192,2048]{1,0:T(8,128)(2,1)} %get-tuple-element.137), channel_id=1, source_target_pairs={{0,4},{1,5},{2,0},{3,1},{4,8},{5,9},{6,2},{7,3},{8,12},{9,13},{10,... | collective-permute-start | bytes 2359304 | tf_op jit(solution)/shard_map/ppermute | solution.py:123
  593.7 37.8 %collective-permute-start.133 = (bf16[192,2048]{1,0:T(8,128)(2,1)}, bf16[192,2048]{1,0:T(8,128)(2,1)S(1)}, u32[]{:S(2)}, u32[]{:S(2)}) collective-permute-start(bf16[192,2048]{1,0:T(8,128)(2,1)} %get-tuple-element.138), channel_id=1, source_target_pairs={{0,2},{1,3},{2,6},{3,7},{4,0},{5,1},{6,10},{7,11},{8,4},{9,5},{10,... | collective-permute-start | bytes 2359304 | tf_op jit(solution)/shard_map/ppermute | solution.py:124
  598.4 16.7 %collective-permute-start.140 = (bf16[72,512]{1,0:T(8,128)(2,1)S(1)}, bf16[72,512]{1,0:T(8,128)(2,1)S(1)}, u32[]{:S(2)}, u32[]{:S(2)}) collective-permute-start(bf16[72,512]{1,0:T(8,128)(2,1)S(1)} %get-tuple-element.160), channel_id=1, source_target_pairs={{0,2},{1,3},{2,6},{3,7},{4,0},{5,1},{6,10},{7,11},{8,4},{9,5},{10,... | collective-permute-start | bytes 221192 | tf_op jit(solution)/shard_map/ppermute | solution.py:124
  599.1 16.6 %collective-permute-start.139 = (bf16[72,512]{1,0:T(8,128)(2,1)S(1)}, bf16[72,512]{1,0:T(8,128)(2,1)S(1)}, u32[]{:S(2)}, u32[]{:S(2)}) collective-permute-start(bf16[72,512]{1,0:T(8,128)(2,1)S(1)} %get-tuple-element.161), channel_id=1, source_target_pairs={{0,4},{1,5},{2,0},{3,1},{4,8},{5,9},{6,2},{7,3},{8,12},{9,13},{10,... | collective-permute-start | bytes 221192 | tf_op jit(solution)/shard_map/ppermute | solution.py:123
  615.1 38.0 %collective-permute-start.150 = (bf16[352,2048]{1,0:T(8,128)(2,1)}, bf16[352,2048]{1,0:T(8,128)(2,1)S(1)}, u32[]{:S(2)}, u32[]{:S(2)}) collective-permute-start(bf16[352,2048]{1,0:T(8,128)(2,1)} %add_convert_fusion.1), channel_id=1, source_target_pairs={{0,16},{16,0},{1,17},{17,1},{2,18},{18,2},{3,19},{19,3},{4,20},{20... | collective-permute-start | bytes 4325384 | tf_op jit(solution)/shard_map/ppermute | solution.py:1141
  643.7 22.4 %collective-permute-start.134 = (bf16[192,2048]{1,0:T(8,128)(2,1)}, bf16[192,2048]{1,0:T(8,128)(2,1)S(1)}, u32[]{:S(2)}, u32[]{:S(2)}) collective-permute-start(bf16[192,2048]{1,0:T(8,128)(2,1)} %get-tuple-element.139), channel_id=1, source_target_pairs={{0,4},{1,5},{2,0},{3,1},{4,8},{5,9},{6,2},{7,3},{8,12},{9,13},{10,... | collective-permute-start | bytes 2359304 | tf_op jit(solution)/shard_map/ppermute | solution.py:123
  644.3 21.8 %collective-permute-start.135 = (bf16[192,2048]{1,0:T(8,128)(2,1)}, bf16[192,2048]{1,0:T(8,128)(2,1)S(1)}, u32[]{:S(2)}, u32[]{:S(2)}) collective-permute-start(bf16[192,2048]{1,0:T(8,128)(2,1)} %get-tuple-element.140), channel_id=1, source_target_pairs={{0,2},{1,3},{2,6},{3,7},{4,0},{5,1},{6,10},{7,11},{8,4},{9,5},{10,... | collective-permute-start | bytes 2359304 | tf_op jit(solution)/shard_map/ppermute | solution.py:124
  (239 other events, 2475.8 us)

commit v5 on v4

--- a/solution.py
+++ b/solution.py
@@ -151,7 +151,7 @@
         ],
         out_specs=[whole((rows, width))] * 2,
         out_shape=[shaped((rows, width), BF16)] * 2,
-        cost_estimate=takes(0.875), compiler_params=ROOMY,
+        cost_estimate=takes(2.5), compiler_params=ROOMY,
     )(parts, parts, cw, ccw)
 
 
@@ -779,8 +779,9 @@
     chips = ring.chips
     tok, model = twos[0][2].shape
     _, _, half, wide = weights[0].shape
-    steps = chips // 2
-    chunk = 2 * tok
+    each = chips // 2
+    steps = chips // each
+    chunk = each * tok
     count = len(twos)
 
     def body(table, *refs):
@@ -814,11 +815,11 @@
             @pl.when(step == at)
             def _():
                 for (slot, _, _), block in zip(twos + cots, blocks):
-                    if slot // 2 == at:
+                    if slot // each == at:
                         block.wait()
 
-        two = two_buf[pl.ds(step * 2, 2)].reshape(chunk, model)
-        cot = cot_buf[pl.ds(step * 2, 2)].reshape(chunk, model)
+        two = two_buf[pl.ds(step * each, each)].reshape(chunk, model)
+        cot = cot_buf[pl.ds(step * each, each)].reshape(chunk, model)
         two_out[...] = two
         cot_out[...] = cot
         gate_weight = weight_buf[0].reshape(model, wide)
@@ -1153,8 +1154,15 @@
 
     packed = pack_weight(qkv_weight, attn_gain, ffn_gain, side)
     qkv_pieces, qkv_marks = ring.gather_shared(*packed, twin)
+    out_halves = [
+        lax.dynamic_slice_in_dim(out_weight, place * (model // 2), model // 2, 1)
+        for place in (side, 1 - side)
+    ]
+    out_pieces, out_marks = ring.gather_shared(
+        after(out_halves[0], *qkv_marks[-2:]), out_halves[1], twin
+    )
     mine = lax.all_to_all(
-        after(mine, *qkv_marks[-2:]), "shard", 0, 0, axis_index_groups=ring.core_groups, tiled=True
+        after(mine, *out_marks[-2:]), "shard", 0, 0, axis_index_groups=ring.core_groups, tiled=True
     )
 
     offset = ring.index * tok
@@ -1169,28 +1177,18 @@
     first = (starts - offset + (blocks - 1) * tok)[None, :]
 
     proj, kv_local, input_one, factor_one, gains = project(
-        ring, hidden, cosine, sine, qkv_pieces, width, ()
-    )
-    kv_own = stack_blocks(ring, ring.gather(kv_local), (mine,))
+        ring, hidden, cosine, sine, qkv_pieces, width, tuple(out_marks[5:7])
+    )
+    kv_own = stack_blocks(ring, ring.gather(kv_local), ())
     kv_other = ring.swap(kv_own)
     tables = (kv_own, kv_other, first, cosine, sine)
     keys = blocks * tok
     kept = attend(ring, groups[0], (), keys, proj, *tables)
-    out_halves = [
-        lax.dynamic_slice_in_dim(out_weight, place * (model // 2), model // 2, 1)
-        for place in (side, 1 - side)
-    ]
-    out_pieces, out_marks = ring.gather_shared(
-        after(out_halves[0], *qkv_marks[-2:]),
-        out_halves[1],
-        twin,
-        {2: (kv_local,), 3: (kv_own,), 4: (kept[0],)},
-    )
     theirs = twin(mine)
-    cots = ring.gather(after(cot_local, *out_marks[-2:]))
+    cots = ring.gather(after(cot_local, mine))
     kept = attend(ring, groups[1], (), keys, proj, *tables, kept)
     queries, attended, logs = kept
-    residual, factor_two, input_two = project_out(ring, attended, hidden, gains, out_pieces, ())
+    residual, factor_two, input_two = project_out(ring, attended, hidden, gains, out_pieces, tuple(p for *_, p in cots[1:3]))
 
     twos = ring.gather(input_two)
     weights = (mine, theirs, ring.swap(mine), ring.swap(theirs))

time: 696 us -> 680 us (0.977)
  waiting for transfers between devices: 246 us -> 227 us
  starting transfers between devices: 130 us -> 142 us
    ppermute x20, waiting for transfers between devices: 49 us -> 9.72 us  [scatter(): ccw = lax.ppermute(ccw, 'shard', self.back)]
    ppermute x20, waiting for transfers between devices: 46.7 us -> 65.1 us  [scatter(): cw = lax.ppermute(cw, 'shard', self.ahead)]
    ppermute x23, waiting for transfers between devices: 70.5 us -> 85.7 us  [twin(): return lax.ppermute(value, 'rep', twin_map)]
    ppermute x15, waiting for transfers between devices: 64.9 us -> 52.2 us  [gather(): ccw = lax.ppermute(ccw, 'shard', self.back)]
    ppermute x15, starting transfers between devices: 16.5 us -> 24.2 us  [gather(): ccw = lax.ppermute(ccw, 'shard', self.back)]
    unnamed x274 -> x280, local copies, waits for them, and re-layouts: 26.6 us -> 20.9 us
  transfers between devices with their start and end apart: 153 -> 153, of which waited for: 49 -> 53; matrix products, arithmetic and copies ran while one was open for 6% -> 5% of each run, Pallas kernels for 24% -> 24%
where the time goes in v5:
time: 680 us; the launch traced here: 672 us
  Pallas kernels  238 us (35%)
  waiting for transfers between devices  227 us (33%)
  starting transfers between devices  142 us (21%)
  local copies, waits for them, and re-layouts  43.7 us (6%)
  other arithmetic  19.7 us (3%)
    ppermute x23, waiting for transfers between devices, twin(): return lax.ppermute(value, 'rep', twin_map)  85.7 us
    ppermute x20, waiting for transfers between devices, scatter(): cw = lax.ppermute(cw, 'shard', self.ahead)  65.1 us
    pallas_call x4, Pallas kernels, attention_call(): pl.pallas_call(body, grid_spec=pltpu.PrefetchScalarGridSpec(num_scalar_pr...  53 us
    ppermute x15, waiting for transfers between devices, gather(): ccw = lax.ppermute(ccw, 'shard', self.back)  52.2 us
    pallas_call x7, Pallas kernels, call(): pl.pallas_call(body, grid_spec=pltpu.PrefetchScalarGridSpec(num_scalar_pr...  52.1 us
    pallas_call x15, Pallas kernels, add_step(): pl.pallas_call(body, grid=(1,), in_specs=[pl.BlockSpec((rows, width), lam...  35.5 us
    ppermute x20, starting transfers between devices, scatter(): cw = lax.ppermute(cw, 'shard', self.ahead)  28.7 us
    pallas_call x1, Pallas kernels, feed_forward(): pl.pallas_call(body, grid_spec=pltpu.PrefetchScalarGridSpec(num_scalar_pr...  28.6 us
  transfers between devices with their start and end apart: 153, of which 53 were waited for; matrix products, arithmetic and copies ran while one was open for 5% of the time, Pallas kernels for 24%

profile of v5, /device:TPU:0, one launch (start us, length us, event | category | flops | bytes accessed | tf_op | source)
XLA Modules:
  0.0 671.9 jit_solution(16604246782002428212)
XLA Ops:
  9.1 8.2 %collective-permute-done.1.refs_5_.refs_8_ = bf16[128,1408]{1,0:T(8,128)(2,1)S(1)} collective-permute-done((bf16[128,1408]{1,0:T(8,128)(2,1)}, bf16[128,1408]{1,0:T(8,128)(2,1)S(1)}, u32[]{:S(2)}, u32[]{:S(2)}) %collective-permute-start.1) | collective-permute-done | bytes 360480 | tf_op jit(solution)/shard_map/ppermute | solution.py:99
  21.7 6.8 %collective-permute-done.9.refs_14_.refs_17_ = bf16[128,1408]{1,0:T(8,128)(2,1)S(1)} collective-permute-done((bf16[128,1408]{1,0:T(8,128)(2,1)S(1)}, bf16[128,1408]{1,0:T(8,128)(2,1)S(1)}, u32[]{:S(2)}, u32[]{:S(2)}) %collective-permute-start.9) | collective-permute-done | bytes 360480 | tf_op jit(solution)/shard_map/ppermute | solution.py:1142
  30.7 5.5 collective-permute-done.8.refs_13_.refs_16_
  38.8 4.8 collective-permute-done.11.refs_16_.refs_19_
  49.4 4.3 collective-permute-done.10.refs_15_.refs_18_
  59.7 7.2 %collective-permute-done.15.refs_20_.refs_23_ = bf16[64,1408]{1,0:T(8,128)(2,1)} collective-permute-done((bf16[64,1408]{1,0:T(8,128)(2,1)S(1)}, bf16[64,1408]{1,0:T(8,128)(2,1)}, u32[]{:S(2)}, u32[]{:S(2)}) %collective-permute-start.15) | collective-permute-done | bytes 180256 | tf_op jit(solution)/shard_map/ppermute | solution.py:1142
  75.8 7.5 %collective-permute-done.14.refs_19_.refs_22_ = bf16[64,1408]{1,0:T(8,128)(2,1)S(1)} collective-permute-done((bf16[64,1408]{1,0:T(8,128)(2,1)}, bf16[64,1408]{1,0:T(8,128)(2,1)S(1)}, u32[]{:S(2)}, u32[]{:S(2)}) %collective-permute-start.14) | collective-permute-done | bytes 180256 | tf_op jit(solution)/shard_map/ppermute | solution.py:1142
  88.9 4.0 collective-permute-done.39.refs_40_.refs_9_.refs_13_
  93.7 9.0 %shard_map.163 = (f32[128,2048]{1,0:T(8,128)}, bf16[128,512]{1,0:T(8,128)(2,1)}, bf16[128,2048]{1,0:T(8,128)(2,1)}, f32[128,128]{1,0:T(8,128)}, f32[8,2048]{1,0:T(8,128)}) custom-call(s32[75]{0:T(128)} %fusion.9.table_ref.table, bf16[128,2048]{1,0:T(8,128)(2,1)} %bitcast.58, f32[128,128]{1,0:T(8,128)} %get-tuple-element.169.refs_1_.refs_4_.refs_7_.refs_3_, ...), custom_call_target="tpu_custom_call" | custom-call | flops 9900000256 | bytes 29700000 | tf_op jit(solution)/shard_map/pallas_call | solution.py:184
  121.2 4.1 shard_map.167.refs_0_
  126.1 6.7 all-to-all-start
  137.8 4.4 collective-permute-done.52.refs_14_.refs_18_
  144.2 3.6 collective-permute-done.51.refs_13_.refs_17_
  170.0 12.7 %shard_map.165 = (bf16[128,2048]{1,0:T(8,128)(2,1)}, bf16[128,2048]{1,0:T(8,128)(2,1)}, f32[16,1,256]{2,1,0:T(1,128)}) custom-call(s32[75]{0:T(128)} %fusion.9.table_ref.table, f32[128,2048]{1,0:T(8,128)} %get-tuple-element.82.refs_0_, bf16[8,128,512]{2,1,0:T(8,128)(2,1)} %shard_map.164.refs_1_.refs_4_, bf16[8,128,512]{2,1,0:T(8,128)(2,1)} %copy-done.77, ...), custom_call_target="tpu_custom_call" | custom-call | flops 15399999488 | bytes 46200000 | tf_op jit(solution)/shard_map/pallas_call | solution.py:1023
  186.6 12.8 %shard_map.166 = (bf16[128,2048]{1,0:T(8,128)(2,1)}, bf16[128,2048]{1,0:T(8,128)(2,1)}, f32[16,1,256]{2,1,0:T(1,128)}) custom-call(s32[75]{0:T(128)} %fusion.9.table_ref.table, f32[128,2048]{1,0:T(8,128)} %get-tuple-element.82.refs_0_, bf16[8,128,512]{2,1,0:T(8,128)(2,1)} %shard_map.164.refs_1_.refs_4_, ...), custom_call_target="tpu_custom_call", output_to_operand_aliasing={{0}: (7, {}), {1}: (8, {}), {2}: (9, {})} | custom-call | flops 15399999488 | bytes 46200000 | tf_op jit(solution)/shard_map/pallas_call | solution.py:1023
  203.1 8.2 %shard_map.170 = (f32[128,2048]{1,0:T(8,128)}, f32[128,128]{1,0:T(8,128)}, bf16[128,2048]{1,0:T(8,128)(2,1)}) custom-call(s32[75]{0:T(128)} %fusion.9.table_ref.table, bf16[128,2048]{1,0:T(8,128)(2,1)} %get-tuple-element.87.refs_0_.refs_2_.input_ref, bf16[128,2048]{1,0:T(8,128)(2,1)} %bitcast.59, f32[8,2048]{1,0:T(8,128)} %get-tuple-element.88.refs_2_.refs_5_.refs_4_, ...), custom_call_target="tpu_custom_call" | custom-call | flops 8800000000 | bytes 26400000 | tf_op jit(solution)/shard_map/pallas_call | solution.py:184
  216.1 10.3 %collective-permute-done.80.refs_2_ = bf16[128,2048]{1,0:T(8,128)(2,1)S(1)} collective-permute-done((bf16[128,2048]{1,0:T(8,128)(2,1)}, bf16[128,2048]{1,0:T(8,128)(2,1)S(1)}, u32[]{:S(2)}, u32[]{:S(2)}) %collective-permute-start.80) | collective-permute-done | bytes 524320 | tf_op jit(solution)/shard_map/ppermute | solution.py:99
  228.3 7.9 %collective-permute-done.93.refs_19_ = bf16[8,2,64,704]{3,2,1,0:T(8,128)(2,1)} collective-permute-done((bf16[8,2,64,704]{3,2,1,0:T(8,128)(2,1)S(1)}, bf16[8,2,64,704]{3,2,1,0:T(8,128)(2,1)}, u32[]{:S(2)}, u32[]{:S(2)}) %collective-permute-start.93) | collective-permute-done | bytes 1441824 | tf_op jit(solution)/shard_map/ppermute | solution.py:1142
  238.2 11.1 %collective-permute-done.82.refs_4_ = bf16[128,2048]{1,0:T(8,128)(2,1)S(1)} collective-permute-done((bf16[128,2048]{1,0:T(8,128)(2,1)S(1)}, bf16[128,2048]{1,0:T(8,128)(2,1)S(1)}, u32[]{:S(2)}, u32[]{:S(2)}) %collective-permute-start.82) | collective-permute-done | bytes 524320 | tf_op jit(solution)/shard_map/ppermute | solution.py:99
  251.5 10.1 %collective-permute-done.84.refs_6_ = bf16[128,2048]{1,0:T(8,128)(2,1)S(1)} collective-permute-done((bf16[128,2048]{1,0:T(8,128)(2,1)S(1)}, bf16[128,2048]{1,0:T(8,128)(2,1)S(1)}, u32[]{:S(2)}, u32[]{:S(2)}) %collective-permute-start.84) | collective-permute-done | bytes 524320 | tf_op jit(solution)/shard_map/ppermute | solution.py:99
  267.3 4.1 shard_map.171.refs_22_.down_ref
  274.8 28.6 %shard_map.172 = (bf16[1024,704]{1,0:T(8,128)(2,1)}, bf16[1024,704]{1,0:T(8,128)(2,1)}, bf16[1024,704]{1,0:T(8,128)(2,1)}, bf16[1024,2048]{1,0:T(8,128)(2,1)}, b...) custom-call(s32[75]{0:T(128)} %fusion.9.table_ref.table, bf16[128,2048]{1,0:T(8,128)(2,1)} %get-tuple-element.90.refs_0_, ...), custom_call_target="tpu_custom_call" | custom-call | flops 30799998976 | bytes 92400000 | tf_op jit(solution)/shard_map/pallas_call | solution.py:844
  303.4 7.1 %shard_map.173 = (bf16[1024,704]{1,0:T(8,128)(2,1)}, bf16[1024,704]{1,0:T(8,128)(2,1)}) custom-call(bf16[1024,2048]{1,0:T(8,128)(2,1)} %get-tuple-element.92.input_ref, bf16[1024,704]{1,0:T(8,128)(2,1)} %get-tuple-element.93.refs_0_, bf16[1024,704]{1,0:T(8,128)(2,1)} %get-tuple-element.94.refs_1_), custom_call_target="tpu_custom_call" | custom-call | flops 2310000128 | bytes 6930000 | tf_op jit(solution)/shard_map/pallas_call | solution.py:602
  317.7 6.2 collective-permute-done.100.ccw_ref
  333.9 9.3 %shard_map.174 = (f32[8,2,64,704]{3,2,1,0:T(8,128)}, bf16[8,2,64,704]{3,2,1,0:T(8,128)(2,1)}) custom-call(s32[75]{0:T(128)} %fusion.9.table_ref.table, bf16[1024,2048]{1,0:T(8,128)(2,1)} %get-tuple-element.92.input_ref, bf16[1024,704]{1,0:T(8,128)(2,1)} %get-tuple-element.93.refs_0_, bf16[1024,704]{1,0:T(8,128)(2,1)} %get-tuple-element.94.refs_1_, ...), custom_call_target="tpu_custom_call" | custom-call | flops 3464999936 | bytes 10395000 | tf_op jit(solution)/shard_map/pallas_call | solution.py:690
  350.0 7.2 %shard_map.175.refs_1_.ahead_ref.back_ref = bf16[1024,2048]{1,0:T(8,128)(2,1)} custom-call(bf16[1024,704]{1,0:T(8,128)(2,1)} %get-tuple-element.91.act_ref, bf16[704,2048]{1,0:T(8,128)(2,1)} %shard_map.171.refs_22_.down_ref, bf16[8,2,64,704]{3,2,1,0:T(8,128)(2,1)} %get-tuple-element.97.refs_0_.refs_1_), custom_call_target="tpu_custom_call" | custom-call | flops 2695000064 | bytes 8085000 | tf_op jit(solution)/shard_map/pallas_call | solution.py:739
  368.1 7.5 %collective-permute-done.105.refs_1_.refs_0_ = bf16[128,2048]{1,0:T(8,128)(2,1)S(1)} collective-permute-done((bf16[128,2048]{1,0:T(8,128)(2,1)}, bf16[128,2048]{1,0:T(8,128)(2,1)S(1)}, u32[]{:S(2)}, u32[]{:S(2)}) %collective-permute-start.105) | collective-permute-done | bytes 524320 | tf_op jit(solution)/shard_map/ppermute | solution.py:123
  379.5 10.4 %shard_map.188 = (f32[128,2048]{1,0:T(8,128)}, bf16[128,2048]{1,0:T(8,128)(2,1)}, bf16[128,2048]{1,0:T(8,128)(2,1)}, f32[8,2048]{1,0:T(8,128)}) custom-call(s32[75]{0:T(128)} %fusion.9.table_ref.table, bf16[128,2048]{1,0:T(8,128)(2,1)} %slice.127.refs_0_, bf16[128,2048]{1,0:T(8,128)(2,1)} %copy-done.13, bf16[128,2048]{1,0:T(8,128)(2,1)} %copy-done.14, ...), custom_call_target="tpu_custom_call" | custom-call | flops 3849999872 | bytes 11550000 | tf_op jit(solution)/shard_map/pallas_call | solution.py:184
  389.9 4.1 shard_map.190
  395.5 4.7 all-to-all-start.1
  404.2 13.7 %shard_map.189 = (bf16[128,2048]{1,0:T(8,128)(2,1)}, bf16[8,128,512]{2,1,0:T(8,128)(2,1)}, bf16[8,128,512]{2,1,0:T(8,128)(2,1)}) custom-call(s32[75]{0:T(128)} %fusion.9.table_ref.table, bf16[128,2048]{1,0:T(8,128)(2,1)} %get-tuple-element.111.refs_0_, bf16[128,2048]{1,0:T(8,128)(2,1)} %get-tuple-element.113.refs_1_, ...), custom_call_target="tpu_custom_call" | custom-call | flops 5500000256 | bytes 16500000 | tf_op jit(solution)/shard_map/pallas_call | solution.py:1023
  417.9 6.0 shard_map.191
  423.9 9.5 %collective-permute-done.107.cw_ref.refs_12_ = bf16[64,2048]{1,0:T(8,128)(2,1)S(1)} collective-permute-done((bf16[64,2048]{1,0:T(8,128)(2,1)}, bf16[64,2048]{1,0:T(8,128)(2,1)S(1)}, u32[]{:S(2)}, u32[]{:S(2)}) %collective-permute-start.107) | collective-permute-done | bytes 262176 | tf_op jit(solution)/shard_map/ppermute | solution.py:123
  433.4 5.3 all-to-all-done.1.refs_14_.refs_0_
  438.7 13.8 %shard_map.192 = (bf16[128,2048]{1,0:T(8,128)(2,1)}, bf16[8,128,512]{2,1,0:T(8,128)(2,1)}, bf16[8,128,512]{2,1,0:T(8,128)(2,1)}) custom-call(s32[75]{0:T(128)} %fusion.9.table_ref.table, bf16[128,2048]{1,0:T(8,128)(2,1)} %get-tuple-element.111.refs_0_, ...), custom_call_target="tpu_custom_call", output_to_operand_aliasing={{0}: (10, {}), {1}: (11, {}), {2}: (12, {})} | custom-call | flops 5500000256 | bytes 16500000 | tf_op jit(solution)/shard_map/pallas_call | solution.py:1023
  452.5 3.9 shard_map.193.refs_1_
  457.5 10.1 %shard_map.215 = (f32[352,2048]{1,0:T(8,128)}, bf16[352,2048]{1,0:T(8,128)(2,1)}) custom-call(s32[75]{0:T(128)} %fusion.9.table_ref.table, bf16[1024,704]{1,0:T(8,128)(2,1)} %get-tuple-element.91.act_ref, bf16[1024,2048]{1,0:T(8,128)(2,1)} %get-tuple-element.149.cot_ref, bf16[128,2048]{1,0:T(8,128)(2,1)} %copy-done.13, bf16[128,2048]{1,0:T(8,128)(2,1)} %copy-done.14), custom_call_target="tpu_custom_call" | custom-call | flops 3849999872 | bytes 11550000 | tf_op jit(solution)/shard_map/pallas_call | solution.py:717
  470.1 6.1 collective-permute-start.109
  477.4 10.9 %collective-permute-done.109.cw_ref = bf16[128,2048]{1,0:T(8,128)(2,1)S(1)} collective-permute-done((bf16[128,2048]{1,0:T(8,128)(2,1)}, bf16[128,2048]{1,0:T(8,128)(2,1)S(1)}, u32[]{:S(2)}, u32[]{:S(2)}) %collective-permute-start.109) | collective-permute-done | bytes 524320 | tf_op jit(solution)/shard_map/ppermute | solution.py:123
  500.1 4.6 collective-permute-done.123.half_got_ref
  504.7 6.1 collective-permute-start.120
  510.8 7.0 %shard_map.197.refs_1_.ahead_ref.back_ref = bf16[1536,2048]{1,0:T(8,128)(2,1)} custom-call(bf16[128,2048]{1,0:T(8,128)(2,1)} %get-tuple-element.123.input_ref, bf16[128,2048]{1,0:T(8,128)(2,1)} %get-tuple-element.124.refs_0_.grad_ref, bf16[1024,2048]{1,0:T(8,128)(2,1)} %collective-permute-done.122.got_ref, f32[8,1,64,2048]{3,2,1,0:T(8,128)} %get-tuple-element.128.half_ref, ...), custom_call_target="tpu_custom_call" | custom-call | flops 2200000000 | bytes 6600000 | tf_op jit(solution)/shard_map/pallas_call | solution.py:655
  544.0 12.0 %collective-permute-done.126.refs_1_ = bf16[128,512]{1,0:T(8,128)(2,1)S(1)} collective-permute-done((bf16[128,512]{1,0:T(8,128)(2,1)}, bf16[128,512]{1,0:T(8,128)(2,1)S(1)}, u32[]{:S(2)}, u32[]{:S(2)}) %collective-permute-start.126) | collective-permute-done | bytes 131104 | tf_op jit(solution)/shard_map/ppermute | solution.py:123
  567.5 11.9 %shard_map.204 = (bf16[128,2048]{1,0:T(8,128)(2,1)}, f32[8,2048]{1,0:T(8,128)}) custom-call(s32[75]{0:T(128)} %fusion.9.table_ref.table, bf16[128,2048]{1,0:T(8,128)(2,1)} %get-tuple-element.124.refs_0_.grad_ref, bf16[128,512]{1,0:T(8,128)(2,1)} %shard_map.201.refs_1_.refs_0_.refs_2_, bf16[128,2048]{1,0:T(8,128)(2,1)} %bitcast.60, ...), custom_call_target="tpu_custom_call" | custom-call | flops 4427500032 | bytes 13282500 | tf_op jit(solution)/shard_map/pallas_call | solution.py:184
  604.6 5.9 shard_map.214
  610.5 5.6 collective-permute-done.141.cw_ref.refs_1_
  636.6 11.0 %collective-permute-done.145 = bf16[144,512]{1,0:T(8,128)(2,1)S(1)} collective-permute-done((bf16[144,512]{1,0:T(8,128)(2,1)}, bf16[144,512]{1,0:T(8,128)(2,1)S(1)}, u32[]{:S(2)}, u32[]{:S(2)}) %collective-permute-start.145) | collective-permute-done | bytes 147488 | tf_op jit(solution)/shard_map/ppermute | solution.py:123
  656.3 13.0 %collective-permute-done.136 = bf16[192,2048]{1,0:T(8,128)(2,1)S(1)} collective-permute-done((bf16[192,2048]{1,0:T(8,128)(2,1)S(1)}, bf16[192,2048]{1,0:T(8,128)(2,1)S(1)}, u32[]{:S(2)}, u32[]{:S(2)}) %collective-permute-start.136) | collective-permute-done | bytes 786464 | tf_op jit(solution)/shard_map/ppermute | solution.py:1142
  (646 shorter events, 274.9 us)
Async XLA Ops:
  20.5 15.7 %collective-permute-start.8 = (bf16[128,1408]{1,0:T(8,128)(2,1)S(1)}, bf16[128,1408]{1,0:T(8,128)(2,1)S(1)}, u32[]{:S(2)}, u32[]{:S(2)}) collective-permute-start(bf16[128,1408]{1,0:T(8,128)(2,1)S(1)} %collective-permute-done.refs_4_.refs_7_), channel_id=1, source_target_pairs={{0,16},{16,0},{1,17},{17,1},{2,18},{18,2},{3,19},{19,3},{4,20},{20... | collective-permute-start | bytes 1081352 | tf_op jit(solution)/shard_map/ppermute | solution.py:1142
  21.2 16.7 %collective-permute-start.2 = (bf16[128,1408]{1,0:T(8,128)(2,1)S(1)}, bf16[128,1408]{1,0:T(8,128)(2,1)S(1)}, u32[]{:S(2)}, u32[]{:S(2)}) collective-permute-start(bf16[128,1408]{1,0:T(8,128)(2,1)S(1)} %collective-permute-done.refs_4_.refs_7_), channel_id=1, source_target_pairs={{0,4},{1,5},{2,0},{3,1},{4,8},{5,9},{6,2},{7,3},{8,12},{9,13},{10,... | collective-permute-start | bytes 1081352 | tf_op jit(solution)/shard_map/ppermute | solution.py:98
  49.4 19.2 %collective-permute-start.22 = (bf16[128,1408]{1,0:T(8,128)(2,1)S(1)}, bf16[128,1408]{1,0:T(8,128)(2,1)}, u32[]{:S(2)}, u32[]{:S(2)}) collective-permute-start(bf16[128,1408]{1,0:T(8,128)(2,1)S(1)} %collective-permute-done.5.refs_9_.refs_12_), channel_id=1, source_target_pairs={{0,1},{1,0},{2,3},{3,2},{4,5},{5,4},{6,7},{7,6},{8,9},{9,8},{10,11... | collective-permute-start | bytes 1081352 | tf_op jit(solution)/shard_map/ppermute | solution.py:89
  115.0 21.6 %collective-permute-start.68 = (bf16[128,1024]{1,0:T(8,128)(2,1)}, bf16[128,1024]{1,0:T(8,128)(2,1)}, u32[]{:S(2)}, u32[]{:S(2)}) collective-permute-start(bf16[128,1024]{1,0:T(8,128)(2,1)} %get-tuple-element.164.refs_12_.refs_16_), channel_id=1, source_target_pairs={{0,1},{1,0},{2,3},{3,2},{4,5},{5,4},{6,7},{7,6},{8,9},{9,8},{10,11... | collective-permute-start | bytes 786440 | tf_op jit(solution)/shard_map/ppermute | solution.py:89
  125.4 16.8 %collective-permute-start.61 = (bf16[128,1024]{1,0:T(8,128)(2,1)}, bf16[128,1024]{1,0:T(8,128)(2,1)}, u32[]{:S(2)}, u32[]{:S(2)}) collective-permute-start(bf16[128,1024]{1,0:T(8,128)(2,1)} %collective-permute-done.37.refs_5_.refs_9_), channel_id=1, source_target_pairs={{0,1},{1,0},{2,3},{3,2},{4,5},{5,4},{6,7},{7,6},{8,9},{9,8},{10,11... | collective-permute-start | bytes 786440 | tf_op jit(solution)/shard_map/ppermute | solution.py:89
  126.1 56.6 %all-to-all-start = ((bf16[8,2,64,704]{3,2,1,0:T(8,128)(2,1)}), bf16[8,2,64,704]{3,2,1,0:T(8,128)(2,1)S(1)}, u32[]{:S(2)}, u32[]{:S(2)}) async-start(bf16[8,2,64,704]{3,2,1,0:T(8,128)(2,1)} %shard_map.168), calls=%async_computation | async-start | bytes 3145728 | tf_op jit(solution)/shard_map/all_to_all | solution.py:1164
  136.6 32.3 %collective-permute-start.48 = (bf16[8,128,512]{2,1,0:T(8,128)(2,1)}, bf16[8,128,512]{2,1,0:T(8,128)(2,1)S(1)}, u32[]{:S(2)}, u32[]{:S(2)}) collective-permute-start(bf16[8,128,512]{2,1,0:T(8,128)(2,1)} %shard_map.164.refs_1_.refs_4_), channel_id=1, source_target_pairs={{0,1},{1,0},{2,3},{3,2},{4,5},{5,4},{6,7},{7,6},{8,9},{9,8},{10,11... | collective-permute-start | bytes 3145736 | tf_op jit(solution)/shard_map/ppermute | solution.py:89
  164.7 19.2 %collective-permute-start.55 = (bf16[128,1024]{1,0:T(8,128)(2,1)S(1)}, bf16[128,1024]{1,0:T(8,128)(2,1)}, u32[]{:S(2)}, u32[]{:S(2)}) collective-permute-start(bf16[128,1024]{1,0:T(8,128)(2,1)S(1)} %copy-done.70), channel_id=1, source_target_pairs={{0,16},{16,0},{1,17},{17,1},{2,18},{18,2},{3,19},{19,3},{4,20},{20... | collective-permute-start | bytes 786440 | tf_op jit(solution)/shard_map/ppermute | solution.py:1142
  166.2 17.7 %collective-permute-start.67 = (bf16[64,1024]{1,0:T(8,128)(2,1)S(1)}, bf16[64,1024]{1,0:T(8,128)(2,1)S(1)}, u32[]{:S(2)}, u32[]{:S(2)}) collective-permute-start(bf16[64,1024]{1,0:T(8,128)(2,1)S(1)} %copy-done.64), channel_id=1, source_target_pairs={{0,1},{1,0},{2,3},{3,2},{4,5},{5,4},{6,7},{7,6},{8,9},{9,8},{10,11... | collective-permute-start | bytes 393224 | tf_op jit(solution)/shard_map/ppermute | solution.py:89
  166.2 18.3 %collective-permute-start.66 = (bf16[64,1024]{1,0:T(8,128)(2,1)S(1)}, bf16[64,1024]{1,0:T(8,128)(2,1)S(1)}, u32[]{:S(2)}, u32[]{:S(2)}) collective-permute-start(bf16[64,1024]{1,0:T(8,128)(2,1)S(1)} %copy-done.66), channel_id=1, source_target_pairs={{0,1},{1,0},{2,3},{3,2},{4,5},{5,4},{6,7},{7,6},{8,9},{9,8},{10,11... | collective-permute-start | bytes 393224 | tf_op jit(solution)/shard_map/ppermute | solution.py:89
  167.5 16.9 %collective-permute-start.57 = (bf16[64,1024]{1,0:T(8,128)(2,1)S(1)}, bf16[64,1024]{1,0:T(8,128)(2,1)S(1)}, u32[]{:S(2)}, u32[]{:S(2)}) collective-permute-start(bf16[64,1024]{1,0:T(8,128)(2,1)S(1)} %copy-done.66), channel_id=1, source_target_pairs={{0,16},{16,0},{1,17},{17,1},{2,18},{18,2},{3,19},{19,3},{4,20},{20... | collective-permute-start | bytes 393224 | tf_op jit(solution)/shard_map/ppermute | solution.py:1142
  169.0 17.6 %collective-permute-start.76 = (bf16[64,1024]{1,0:T(8,128)(2,1)S(1)}, bf16[64,1024]{1,0:T(8,128)(2,1)S(1)}, u32[]{:S(2)}, u32[]{:S(2)}) collective-permute-start(bf16[64,1024]{1,0:T(8,128)(2,1)S(1)} %collective-permute-done.58.refs_20_.refs_24_), channel_id=1, source_target_pairs={{0,1},{1,0},{2,3},{3,2},{4,5},{5,4},{6,7},{7,6},{8,9},{9,8},{10,11... | collective-permute-start | bytes 393224 | tf_op jit(solution)/shard_map/ppermute | solution.py:89
  183.9 18.3 %collective-permute-start.74 = (bf16[128,1024]{1,0:T(8,128)(2,1)S(1)}, bf16[128,1024]{1,0:T(8,128)(2,1)S(1)}, u32[]{:S(2)}, u32[]{:S(2)}) collective-permute-start(bf16[128,1024]{1,0:T(8,128)(2,1)S(1)} %copy-done.106), channel_id=1, source_target_pairs={{0,1},{1,0},{2,3},{3,2},{4,5},{5,4},{6,7},{7,6},{8,9},{9,8},{10,11... | collective-permute-start | bytes 786440 | tf_op jit(solution)/shard_map/ppermute | solution.py:89
  183.9 18.3 %collective-permute-start.73 = (bf16[128,1024]{1,0:T(8,128)(2,1)}, bf16[128,1024]{1,0:T(8,128)(2,1)S(1)}, u32[]{:S(2)}, u32[]{:S(2)}) collective-permute-start(bf16[128,1024]{1,0:T(8,128)(2,1)} %collective-permute-done.55.refs_17_.refs_21_), channel_id=1, source_target_pairs={{0,1},{1,0},{2,3},{3,2},{4,5},{5,4},{6,7},{7,6},{8,9},{9,8},{10,11... | collective-permute-start | bytes 786440 | tf_op jit(solution)/shard_map/ppermute | solution.py:89
  199.5 36.6 %collective-permute-start.93 = (bf16[8,2,64,704]{3,2,1,0:T(8,128)(2,1)S(1)}, bf16[8,2,64,704]{3,2,1,0:T(8,128)(2,1)}, u32[]{:S(2)}, u32[]{:S(2)}) collective-permute-start(bf16[8,2,64,704]{3,2,1,0:T(8,128)(2,1)S(1)} %copy-done.3), channel_id=1, source_target_pairs={{0,16},{16,0},{1,17},{17,1},{2,18},{18,2},{3,19},{19,3},{4,20},{20... | collective-permute-start | bytes 4325384 | tf_op jit(solution)/shard_map/ppermute | solution.py:1142
  214.1 23.7 %collective-permute-start.90 = (bf16[128,2048]{1,0:T(8,128)(2,1)S(1)}, bf16[128,2048]{1,0:T(8,128)(2,1)S(1)}, u32[]{:S(2)}, u32[]{:S(2)}) collective-permute-start(bf16[128,2048]{1,0:T(8,128)(2,1)S(1)} %collective-permute-done.88.refs_13_), channel_id=1, source_target_pairs={{0,2},{1,3},{2,6},{3,7},{4,0},{5,1},{6,10},{7,11},{8,4},{9,5},{10,... | collective-permute-start | bytes 1572872 | tf_op jit(solution)/shard_map/ppermute | solution.py:99
  215.9 22.3 %collective-permute-start.89 = (bf16[128,2048]{1,0:T(8,128)(2,1)S(1)}, bf16[128,2048]{1,0:T(8,128)(2,1)S(1)}, u32[]{:S(2)}, u32[]{:S(2)}) collective-permute-start(bf16[128,2048]{1,0:T(8,128)(2,1)S(1)} %collective-permute-done.87.refs_12_), channel_id=1, source_target_pairs={{0,4},{1,5},{2,0},{3,1},{4,8},{5,9},{6,2},{7,3},{8,12},{9,13},{10,... | collective-permute-start | bytes 1572872 | tf_op jit(solution)/shard_map/ppermute | solution.py:98
  226.5 37.2 %collective-permute-start.96 = (bf16[352,2048]{1,0:T(8,128)(2,1)S(1)}, bf16[352,2048]{1,0:T(8,128)(2,1)S(1)}, u32[]{:S(2)}, u32[]{:S(2)}) collective-permute-start(bf16[352,2048]{1,0:T(8,128)(2,1)S(1)} %copy-done.75), channel_id=1, source_target_pairs={{0,1},{1,0},{2,3},{3,2},{4,5},{5,4},{6,7},{7,6},{8,9},{9,8},{10,11... | collective-permute-start | bytes 4325384 | tf_op jit(solution)/shard_map/ppermute | solution.py:89
  228.3 36.7 %collective-permute-start.94 = (bf16[8,2,64,704]{3,2,1,0:T(8,128)(2,1)S(1)}, bf16[8,2,64,704]{3,2,1,0:T(8,128)(2,1)S(1)}, u32[]{:S(2)}, u32[]{:S(2)}) collective-permute-start(bf16[8,2,64,704]{3,2,1,0:T(8,128)(2,1)S(1)} %copy-done.3), channel_id=1, source_target_pairs={{0,1},{1,0},{2,3},{3,2},{4,5},{5,4},{6,7},{7,6},{8,9},{9,8},{10,11... | collective-permute-start | bytes 4325384 | tf_op jit(solution)/shard_map/ppermute | solution.py:89
  238.2 35.9 %collective-permute-start.95 = (bf16[8,2,64,704]{3,2,1,0:T(8,128)(2,1)}, bf16[8,2,64,704]{3,2,1,0:T(8,128)(2,1)}, u32[]{:S(2)}, u32[]{:S(2)}) collective-permute-start(bf16[8,2,64,704]{3,2,1,0:T(8,128)(2,1)} %collective-permute-done.93.refs_19_), channel_id=1, source_target_pairs={{0,1},{1,0},{2,3},{3,2},{4,5},{5,4},{6,7},{7,6},{8,9},{9,8},{10,11... | collective-permute-start | bytes 4325384 | tf_op jit(solution)/shard_map/ppermute | solution.py:89
  312.4 17.4 %collective-permute-start.98 = (bf16[1024,704]{0,1:T(8,128)(2,1)S(1)}, bf16[1024,704]{0,1:T(8,128)(2,1)}, u32[]{:S(2)}, u32[]{:S(2)}) collective-permute-start(bf16[1024,704]{0,1:T(8,128)(2,1)S(1)} %copy.56), channel_id=1, source_target_pairs={{0,1},{1,0},{2,3},{3,2},{4,5},{5,4},{6,7},{7,6},{8,9},{9,8},{10,11... | collective-permute-start | bytes 4325384 | tf_op jit(solution)/shard_map/ppermute | solution.py:89
  314.1 18.3 %collective-permute-start.97 = (bf16[1024,704]{0,1:T(8,128)(2,1)}, bf16[1024,704]{0,1:T(8,128)(2,1)S(1)}, u32[]{:S(2)}, u32[]{:S(2)}) collective-permute-start(bf16[1024,704]{0,1:T(8,128)(2,1)} %copy.55), channel_id=1, source_target_pairs={{0,1},{1,0},{2,3},{3,2},{4,5},{5,4},{6,7},{7,6},{8,9},{9,8},{10,11... | collective-permute-start | bytes 4325384 | tf_op jit(solution)/shard_map/ppermute | solution.py:89
  327.7 16.0 %collective-permute-start.101 = (bf16[128,2048]{1,0:T(8,128)(2,1)}, bf16[128,2048]{1,0:T(8,128)(2,1)S(1)}, u32[]{:S(2)}, u32[]{:S(2)}) collective-permute-start(bf16[128,2048]{1,0:T(8,128)(2,1)} %get-tuple-element.99), channel_id=1, source_target_pairs={{0,4},{1,5},{2,0},{3,1},{4,8},{5,9},{6,2},{7,3},{8,12},{9,13},{10,... | collective-permute-start | bytes 1572872 | tf_op jit(solution)/shard_map/ppermute | solution.py:123
  343.2 35.1 %collective-permute-start.115 = (bf16[8,2,64,704]{3,2,1,0:T(8,128)(2,1)}, bf16[8,2,64,704]{3,2,1,0:T(8,128)(2,1)S(1)}, u32[]{:S(2)}, u32[]{:S(2)}) collective-permute-start(bf16[8,2,64,704]{3,2,1,0:T(8,128)(2,1)} %get-tuple-element.97.refs_0_.refs_1_), channel_id=1, source_target_pairs={{0,16},{16,0},{1,17},{17,1},{2,18},{18,2},{3,19},{19,3},{4,20},{20... | collective-permute-start | bytes 4325384 | tf_op jit(solution)/shard_map/ppermute | solution.py:1142
  393.9 24.0 %collective-permute-start.116 = (bf16[1024,2048]{1,0:T(8,128)(2,1)}, bf16[1024,2048]{1,0:T(8,128)(2,1)}, u32[]{:S(2)}, u32[]{:S(2)}) collective-permute-start(bf16[1024,2048]{1,0:T(8,128)(2,1)} %shard_map.190), channel_id=1, source_target_pairs={{0,1},{1,0},{2,3},{3,2},{4,5},{5,4},{6,7},{7,6},{8,9},{9,8},{10,11... | collective-permute-start | bytes 12582920 | tf_op jit(solution)/shard_map/ppermute | solution.py:89
  395.5 43.2 %all-to-all-start.1 = ((bf16[8,2,64,704]{3,2,1,0:T(8,128)(2,1)}), bf16[8,2,64,704]{3,2,1,0:T(8,128)(2,1)}, u32[]{:S(2)}, u32[]{:S(2)}) async-start(bf16[8,2,64,704]{3,2,1,0:T(8,128)(2,1)} %add_convert_fusion), calls=%async_computation.1 | async-start | bytes 3145728 | tf_op jit(solution)/shard_map/all_to_all | solution.py:1205
  402.1 31.2 %collective-permute-start.107 = (bf16[64,2048]{1,0:T(8,128)(2,1)}, bf16[64,2048]{1,0:T(8,128)(2,1)S(1)}, u32[]{:S(2)}, u32[]{:S(2)}) collective-permute-start(bf16[64,2048]{1,0:T(8,128)(2,1)} %shard_map.183), channel_id=1, source_target_pairs={{0,4},{1,5},{2,0},{3,1},{4,8},{5,9},{6,2},{7,3},{8,12},{9,13},{10,... | collective-permute-start | bytes 786440 | tf_op jit(solution)/shard_map/ppermute | solution.py:123
  404.2 29.2 %collective-permute-start.108 = (bf16[64,2048]{1,0:T(8,128)(2,1)}, bf16[64,2048]{1,0:T(8,128)(2,1)S(1)}, u32[]{:S(2)}, u32[]{:S(2)}) collective-permute-start(bf16[64,2048]{1,0:T(8,128)(2,1)} %shard_map.184), channel_id=1, source_target_pairs={{0,2},{1,3},{2,6},{3,7},{4,0},{5,1},{6,10},{7,11},{8,4},{9,5},{10,... | collective-permute-start | bytes 786440 | tf_op jit(solution)/shard_map/ppermute | solution.py:124
  456.4 54.3 %collective-permute-start.122 = (bf16[1024,2048]{1,0:T(8,128)(2,1)}, bf16[1024,2048]{1,0:T(8,128)(2,1)}, u32[]{:S(2)}, u32[]{:S(2)}) collective-permute-start(bf16[1024,2048]{1,0:T(8,128)(2,1)} %shard_map.193.refs_1_), channel_id=1, source_target_pairs={{0,1},{1,0},{2,3},{3,2},{4,5},{5,4},{6,7},{7,6},{8,9},{9,8},{10,11... | collective-permute-start | bytes 12582920 | tf_op jit(solution)/shard_map/ppermute | solution.py:89
  456.4 20.6 %collective-permute-start.117 = (bf16[8,128,512]{2,1,0:T(8,128)(2,1)}, bf16[8,128,512]{2,1,0:T(8,128)(2,1)S(1)}, u32[]{:S(2)}, u32[]{:S(2)}) collective-permute-start(bf16[8,128,512]{2,1,0:T(8,128)(2,1)} %shard_map.194), channel_id=1, source_target_pairs={{0,1},{1,0},{2,3},{3,2},{4,5},{5,4},{6,7},{7,6},{8,9},{9,8},{10,11... | collective-permute-start | bytes 3145736 | tf_op jit(solution)/shard_map/ppermute | solution.py:89
  457.0 47.7 %collective-permute-start.123 = (bf16[8,1,64,2048]{3,2,1,0:T(8,128)(2,1)}, bf16[8,1,64,2048]{3,2,1,0:T(8,128)(2,1)S(1)}, u32[]{:S(2)}, u32[]{:S(2)}) collective-permute-start(bf16[8,1,64,2048]{3,2,1,0:T(8,128)(2,1)} %get-tuple-element.120.refs_15_), channel_id=1, source_target_pairs={{0,16},{16,0},{1,17},{17,1},{2,18},{18,2},{3,19},{19,3},{4,20},{20... | collective-permute-start | bytes 6291464 | tf_op jit(solution)/shard_map/ppermute | solution.py:1142
  467.6 113.0 %collective-permute-start.149 = (bf16[352,2048]{1,0:T(8,128)(2,1)}, bf16[352,2048]{1,0:T(8,128)(2,1)}, u32[]{:S(2)}, u32[]{:S(2)}) collective-permute-start(bf16[352,2048]{1,0:T(8,128)(2,1)} %get-tuple-element.151), channel_id=1, source_target_pairs={{0,1},{1,0},{2,3},{3,2},{4,5},{5,4},{6,7},{7,6},{8,9},{9,8},{10,11... | collective-permute-start | bytes 4325384 | tf_op jit(solution)/shard_map/ppermute | solution.py:89
  470.1 18.2 %collective-permute-start.109 = (bf16[128,2048]{1,0:T(8,128)(2,1)}, bf16[128,2048]{1,0:T(8,128)(2,1)S(1)}, u32[]{:S(2)}, u32[]{:S(2)}) collective-permute-start(bf16[128,2048]{1,0:T(8,128)(2,1)} %get-tuple-element.105), channel_id=1, source_target_pairs={{0,4},{1,5},{2,0},{3,1},{4,8},{5,9},{6,2},{7,3},{8,12},{9,13},{10,... | collective-permute-start | bytes 1572872 | tf_op jit(solution)/shard_map/ppermute | solution.py:123
  496.3 22.7 %collective-permute-start.111 = (bf16[128,2048]{1,0:T(8,128)(2,1)}, bf16[128,2048]{1,0:T(8,128)(2,1)S(1)}, u32[]{:S(2)}, u32[]{:S(2)}) collective-permute-start(bf16[128,2048]{1,0:T(8,128)(2,1)} %get-tuple-element.107), channel_id=1, source_target_pairs={{0,4},{1,5},{2,0},{3,1},{4,8},{5,9},{6,2},{7,3},{8,12},{9,13},{10,... | collective-permute-start | bytes 1572872 | tf_op jit(solution)/shard_map/ppermute | solution.py:123
  496.6 24.0 %collective-permute-start.112 = (bf16[128,2048]{1,0:T(8,128)(2,1)}, bf16[128,2048]{1,0:T(8,128)(2,1)S(1)}, u32[]{:S(2)}, u32[]{:S(2)}) collective-permute-start(bf16[128,2048]{1,0:T(8,128)(2,1)} %get-tuple-element.108), channel_id=1, source_target_pairs={{0,2},{1,3},{2,6},{3,7},{4,0},{5,1},{6,10},{7,11},{8,4},{9,5},{10,... | collective-permute-start | bytes 1572872 | tf_op jit(solution)/shard_map/ppermute | solution.py:124
  504.7 19.3 %collective-permute-start.120 = (bf16[128,512]{1,0:T(8,128)(2,1)}, bf16[128,512]{1,0:T(8,128)(2,1)S(1)}, u32[]{:S(2)}, u32[]{:S(2)}) collective-permute-start(bf16[128,512]{1,0:T(8,128)(2,1)} %get-tuple-element.125), channel_id=1, source_target_pairs={{0,4},{1,5},{2,0},{3,1},{4,8},{5,9},{6,2},{7,3},{8,12},{9,13},{10,... | collective-permute-start | bytes 393224 | tf_op jit(solution)/shard_map/ppermute | solution.py:123
  535.3 30.9 %collective-permute-start.130 = (bf16[192,2048]{1,0:T(8,128)(2,1)}, bf16[192,2048]{1,0:T(8,128)(2,1)S(1)}, u32[]{:S(2)}, u32[]{:S(2)}) collective-permute-start(bf16[192,2048]{1,0:T(8,128)(2,1)} %get-tuple-element.134), channel_id=1, source_target_pairs={{0,4},{1,5},{2,0},{3,1},{4,8},{5,9},{6,2},{7,3},{8,12},{9,13},{10,... | collective-permute-start | bytes 2359304 | tf_op jit(solution)/shard_map/ppermute | solution.py:123
  535.4 30.8 %collective-permute-start.131 = (bf16[192,2048]{1,0:T(8,128)(2,1)}, bf16[192,2048]{1,0:T(8,128)(2,1)S(1)}, u32[]{:S(2)}, u32[]{:S(2)}) collective-permute-start(bf16[192,2048]{1,0:T(8,128)(2,1)} %get-tuple-element.135), channel_id=1, source_target_pairs={{0,2},{1,3},{2,6},{3,7},{4,0},{5,1},{6,10},{7,11},{8,4},{9,5},{10,... | collective-permute-start | bytes 2359304 | tf_op jit(solution)/shard_map/ppermute | solution.py:124
  565.3 37.6 %collective-permute-start.148 = (bf16[8,2,64,704]{3,2,1,0:T(8,128)(2,1)}, bf16[8,2,64,704]{3,2,1,0:T(8,128)(2,1)}, u32[]{:S(2)}, u32[]{:S(2)}) collective-permute-start(bf16[8,2,64,704]{3,2,1,0:T(8,128)(2,1)} %all-to-all-done.1.refs_14_.refs_0_), channel_id=1, source_target_pairs={{0,16},{16,0},{1,17},{17,1},{2,18},{18,2},{3,19},{19,3},{4,20},{20... | collective-permute-start | bytes 4325384 | tf_op jit(solution)/shard_map/ppermute | solution.py:1142
  566.2 18.6 %collective-permute-start.137 = (bf16[1024,512]{1,0:T(8,128)(2,1)}, bf16[1024,512]{1,0:T(8,128)(2,1)}, u32[]{:S(2)}, u32[]{:S(2)}) collective-permute-start(bf16[1024,512]{1,0:T(8,128)(2,1)} %shard_map.207), channel_id=1, source_target_pairs={{0,1},{1,0},{2,3},{3,2},{4,5},{5,4},{6,7},{7,6},{8,9},{9,8},{10,11... | collective-permute-start | bytes 3145736 | tf_op jit(solution)/shard_map/ppermute | solution.py:89
  583.5 52.0 %collective-permute-start.150 = (bf16[352,2048]{1,0:T(8,128)(2,1)}, bf16[352,2048]{1,0:T(8,128)(2,1)S(1)}, u32[]{:S(2)}, u32[]{:S(2)}) collective-permute-start(bf16[352,2048]{1,0:T(8,128)(2,1)} %add_convert_fusion.1), channel_id=1, source_target_pairs={{0,16},{16,0},{1,17},{17,1},{2,18},{18,2},{3,19},{19,3},{4,20},{20... | collective-permute-start | bytes 4325384 | tf_op jit(solution)/shard_map/ppermute | solution.py:1142
  594.0 25.5 %collective-permute-start.132 = (bf16[192,2048]{1,0:T(8,128)(2,1)}, bf16[192,2048]{1,0:T(8,128)(2,1)S(1)}, u32[]{:S(2)}, u32[]{:S(2)}) collective-permute-start(bf16[192,2048]{1,0:T(8,128)(2,1)} %get-tuple-element.137), channel_id=1, source_target_pairs={{0,4},{1,5},{2,0},{3,1},{4,8},{5,9},{6,2},{7,3},{8,12},{9,13},{10,... | collective-permute-start | bytes 2359304 | tf_op jit(solution)/shard_map/ppermute | solution.py:123
  595.1 24.4 %collective-permute-start.133 = (bf16[192,2048]{1,0:T(8,128)(2,1)}, bf16[192,2048]{1,0:T(8,128)(2,1)S(1)}, u32[]{:S(2)}, u32[]{:S(2)}) collective-permute-start(bf16[192,2048]{1,0:T(8,128)(2,1)} %get-tuple-element.138), channel_id=1, source_target_pairs={{0,2},{1,3},{2,6},{3,7},{4,0},{5,1},{6,10},{7,11},{8,4},{9,5},{10,... | collective-permute-start | bytes 2359304 | tf_op jit(solution)/shard_map/ppermute | solution.py:124
  598.5 17.7 %collective-permute-start.141 = (bf16[144,512]{1,0:T(8,128)(2,1)}, bf16[144,512]{1,0:T(8,128)(2,1)S(1)}, u32[]{:S(2)}, u32[]{:S(2)}) collective-permute-start(bf16[144,512]{1,0:T(8,128)(2,1)} %get-tuple-element.143), channel_id=1, source_target_pairs={{0,4},{1,5},{2,0},{3,1},{4,8},{5,9},{6,2},{7,3},{8,12},{9,13},{10,... | collective-permute-start | bytes 442376 | tf_op jit(solution)/shard_map/ppermute | solution.py:123
  625.9 23.7 %collective-permute-start.134 = (bf16[192,2048]{1,0:T(8,128)(2,1)}, bf16[192,2048]{1,0:T(8,128)(2,1)S(1)}, u32[]{:S(2)}, u32[]{:S(2)}) collective-permute-start(bf16[192,2048]{1,0:T(8,128)(2,1)} %get-tuple-element.139), channel_id=1, source_target_pairs={{0,4},{1,5},{2,0},{3,1},{4,8},{5,9},{6,2},{7,3},{8,12},{9,13},{10,... | collective-permute-start | bytes 2359304 | tf_op jit(solution)/shard_map/ppermute | solution.py:123
  627.5 22.1 %collective-permute-start.135 = (bf16[192,2048]{1,0:T(8,128)(2,1)}, bf16[192,2048]{1,0:T(8,128)(2,1)S(1)}, u32[]{:S(2)}, u32[]{:S(2)}) collective-permute-start(bf16[192,2048]{1,0:T(8,128)(2,1)} %get-tuple-element.140), channel_id=1, source_target_pairs={{0,2},{1,3},{2,6},{3,7},{4,0},{5,1},{6,10},{7,11},{8,4},{9,5},{10,... | collective-permute-start | bytes 2359304 | tf_op jit(solution)/shard_map/ppermute | solution.py:124
  631.4 16.2 %collective-permute-start.145 = (bf16[144,512]{1,0:T(8,128)(2,1)}, bf16[144,512]{1,0:T(8,128)(2,1)S(1)}, u32[]{:S(2)}, u32[]{:S(2)}) collective-permute-start(bf16[144,512]{1,0:T(8,128)(2,1)} %get-tuple-element.147), channel_id=1, source_target_pairs={{0,4},{1,5},{2,0},{3,1},{4,8},{5,9},{6,2},{7,3},{8,12},{9,13},{10,... | collective-permute-start | bytes 442376 | tf_op jit(solution)/shard_map/ppermute | solution.py:123
  651.1 18.2 %collective-permute-start.136 = (bf16[192,2048]{1,0:T(8,128)(2,1)S(1)}, bf16[192,2048]{1,0:T(8,128)(2,1)S(1)}, u32[]{:S(2)}, u32[]{:S(2)}) collective-permute-start(bf16[192,2048]{1,0:T(8,128)(2,1)S(1)} %add_convert_fusion.3), channel_id=1, source_target_pairs={{0,16},{16,0},{1,17},{17,1},{2,18},{18,2},{3,19},{19,3},{4,20},{20... | collective-permute-start | bytes 2359304 | tf_op jit(solution)/shard_map/ppermute | solution.py:1142
  (244 other events, 2711.6 us)

commit v6 on v5

--- a/solution.py
+++ b/solution.py
@@ -1266,10 +1266,10 @@
     gain_terms = jnp.concatenate([gain_one_term[:1], gain_two_term[:1]], 0)
     gain_terms = gain_terms[:, :middle] + ring.swap(gain_terms[:, middle:])
     below = gain_terms.reshape(2, chips, rows).transpose(1, 0, 2).reshape(chips, 1, 2 * rows)
-    below = jnp.pad(below, ((0, 0), (0, 15), (0, kv_term.shape[1] - 2 * rows))).astype(BF16)
+    below = jnp.pad(below, ((0, 0), (0, 31), (0, kv_term.shape[1] - 2 * rows))).astype(BF16)
     parts = jnp.concatenate([kv_term.reshape(chips, rows, -1), below], 1)
     kv_sum, last_marks = ring.scatter(
-        parts.reshape(chips * (rows + 16), -1),
+        parts.reshape(chips * (rows + 32), -1),
         lambda step, _: {3: merged_marks[2]}.get(step),
     )
     kv_sum = over_reps(summed(kv_sum))

time: 680 us -> 682 us (level)
  no operation moved by 1% of the time
where the time goes in v6:
time: 682 us; the launch traced here: 673 us
  Pallas kernels  238 us (35%)
  waiting for transfers between devices  228 us (33%)
  starting transfers between devices  142 us (21%)
  local copies, waits for them, and re-layouts  43.7 us (6%)
  other arithmetic  19.7 us (3%)
    ppermute x23, waiting for transfers between devices, twin(): return lax.ppermute(value, 'rep', twin_map)  86 us
    ppermute x20, waiting for transfers between devices, scatter(): cw = lax.ppermute(cw, 'shard', self.ahead)  65.9 us
    pallas_call x4, Pallas kernels, attention_call(): pl.pallas_call(body, grid_spec=pltpu.PrefetchScalarGridSpec(num_scalar_pr...  53 us
    ppermute x15, waiting for transfers between devices, gather(): ccw = lax.ppermute(ccw, 'shard', self.back)  52.2 us
    pallas_call x7, Pallas kernels, call(): pl.pallas_call(body, grid_spec=pltpu.PrefetchScalarGridSpec(num_scalar_pr...  52.1 us
    pallas_call x15, Pallas kernels, add_step(): pl.pallas_call(body, grid=(1,), in_specs=[pl.BlockSpec((rows, width), lam...  35.6 us
    pallas_call x1, Pallas kernels, feed_forward(): pl.pallas_call(body, grid_spec=pltpu.PrefetchScalarGridSpec(num_scalar_pr...  28.6 us
    ppermute x20, starting transfers between devices, scatter(): cw = lax.ppermute(cw, 'shard', self.ahead)  28.4 us
  transfers between devices with their start and end apart: 153, of which 53 were waited for; matrix products, arithmetic and copies ran while one was open for 5% of the time, Pallas kernels for 24%

profile of v6, /device:TPU:0, one launch (start us, length us, event | category | flops | bytes accessed | tf_op | source)
XLA Modules:
  0.0 673.2 jit_solution(15059622031841859426)
XLA Ops:
  9.1 8.2 %collective-permute-done.1.refs_5_.refs_8_ = bf16[128,1408]{1,0:T(8,128)(2,1)S(1)} collective-permute-done((bf16[128,1408]{1,0:T(8,128)(2,1)}, bf16[128,1408]{1,0:T(8,128)(2,1)S(1)}, u32[]{:S(2)}, u32[]{:S(2)}) %collective-permute-start.1) | collective-permute-done | bytes 360480 | tf_op jit(solution)/shard_map/ppermute | solution.py:99
  21.7 6.8 %collective-permute-done.9.refs_14_.refs_17_ = bf16[128,1408]{1,0:T(8,128)(2,1)S(1)} collective-permute-done((bf16[128,1408]{1,0:T(8,128)(2,1)S(1)}, bf16[128,1408]{1,0:T(8,128)(2,1)S(1)}, u32[]{:S(2)}, u32[]{:S(2)}) %collective-permute-start.9) | collective-permute-done | bytes 360480 | tf_op jit(solution)/shard_map/ppermute | solution.py:1142
  30.7 5.5 collective-permute-done.8.refs_13_.refs_16_
  38.8 4.8 collective-permute-done.11.refs_16_.refs_19_
  49.4 4.3 collective-permute-done.10.refs_15_.refs_18_
  59.7 7.2 %collective-permute-done.15.refs_20_.refs_23_ = bf16[64,1408]{1,0:T(8,128)(2,1)} collective-permute-done((bf16[64,1408]{1,0:T(8,128)(2,1)S(1)}, bf16[64,1408]{1,0:T(8,128)(2,1)}, u32[]{:S(2)}, u32[]{:S(2)}) %collective-permute-start.15) | collective-permute-done | bytes 180256 | tf_op jit(solution)/shard_map/ppermute | solution.py:1142
  75.8 7.5 %collective-permute-done.14.refs_19_.refs_22_ = bf16[64,1408]{1,0:T(8,128)(2,1)S(1)} collective-permute-done((bf16[64,1408]{1,0:T(8,128)(2,1)}, bf16[64,1408]{1,0:T(8,128)(2,1)S(1)}, u32[]{:S(2)}, u32[]{:S(2)}) %collective-permute-start.14) | collective-permute-done | bytes 180256 | tf_op jit(solution)/shard_map/ppermute | solution.py:1142
  88.9 4.0 collective-permute-done.39.refs_40_.refs_9_.refs_13_
  93.7 9.0 %shard_map.163 = (f32[128,2048]{1,0:T(8,128)}, bf16[128,512]{1,0:T(8,128)(2,1)}, bf16[128,2048]{1,0:T(8,128)(2,1)}, f32[128,128]{1,0:T(8,128)}, f32[8,2048]{1,0:T(8,128)}) custom-call(s32[75]{0:T(128)} %fusion.9.table_ref.table, bf16[128,2048]{1,0:T(8,128)(2,1)} %bitcast.58, f32[128,128]{1,0:T(8,128)} %get-tuple-element.169.refs_1_.refs_4_.refs_7_.refs_3_, ...), custom_call_target="tpu_custom_call" | custom-call | flops 9900000256 | bytes 29700000 | tf_op jit(solution)/shard_map/pallas_call | solution.py:184
  121.2 4.1 shard_map.167.refs_0_
  126.1 6.7 all-to-all-start
  137.8 4.4 collective-permute-done.52.refs_14_.refs_18_
  144.2 3.6 collective-permute-done.51.refs_13_.refs_17_
  170.0 12.7 %shard_map.165 = (bf16[128,2048]{1,0:T(8,128)(2,1)}, bf16[128,2048]{1,0:T(8,128)(2,1)}, f32[16,1,256]{2,1,0:T(1,128)}) custom-call(s32[75]{0:T(128)} %fusion.9.table_ref.table, f32[128,2048]{1,0:T(8,128)} %get-tuple-element.82.refs_0_, bf16[8,128,512]{2,1,0:T(8,128)(2,1)} %shard_map.164.refs_1_.refs_4_, bf16[8,128,512]{2,1,0:T(8,128)(2,1)} %copy-done.77, ...), custom_call_target="tpu_custom_call" | custom-call | flops 15399999488 | bytes 46200000 | tf_op jit(solution)/shard_map/pallas_call | solution.py:1023
  186.6 12.8 %shard_map.166 = (bf16[128,2048]{1,0:T(8,128)(2,1)}, bf16[128,2048]{1,0:T(8,128)(2,1)}, f32[16,1,256]{2,1,0:T(1,128)}) custom-call(s32[75]{0:T(128)} %fusion.9.table_ref.table, f32[128,2048]{1,0:T(8,128)} %get-tuple-element.82.refs_0_, bf16[8,128,512]{2,1,0:T(8,128)(2,1)} %shard_map.164.refs_1_.refs_4_, ...), custom_call_target="tpu_custom_call", output_to_operand_aliasing={{0}: (7, {}), {1}: (8, {}), {2}: (9, {})} | custom-call | flops 15399999488 | bytes 46200000 | tf_op jit(solution)/shard_map/pallas_call | solution.py:1023
  203.1 8.2 %shard_map.170 = (f32[128,2048]{1,0:T(8,128)}, f32[128,128]{1,0:T(8,128)}, bf16[128,2048]{1,0:T(8,128)(2,1)}) custom-call(s32[75]{0:T(128)} %fusion.9.table_ref.table, bf16[128,2048]{1,0:T(8,128)(2,1)} %get-tuple-element.87.refs_0_.refs_2_.input_ref, bf16[128,2048]{1,0:T(8,128)(2,1)} %bitcast.59, f32[8,2048]{1,0:T(8,128)} %get-tuple-element.88.refs_2_.refs_5_.refs_4_, ...), custom_call_target="tpu_custom_call" | custom-call | flops 8800000000 | bytes 26400000 | tf_op jit(solution)/shard_map/pallas_call | solution.py:184
  216.1 10.3 %collective-permute-done.80.refs_2_ = bf16[128,2048]{1,0:T(8,128)(2,1)S(1)} collective-permute-done((bf16[128,2048]{1,0:T(8,128)(2,1)}, bf16[128,2048]{1,0:T(8,128)(2,1)S(1)}, u32[]{:S(2)}, u32[]{:S(2)}) %collective-permute-start.80) | collective-permute-done | bytes 524320 | tf_op jit(solution)/shard_map/ppermute | solution.py:99
  228.3 7.9 %collective-permute-done.93.refs_19_ = bf16[8,2,64,704]{3,2,1,0:T(8,128)(2,1)} collective-permute-done((bf16[8,2,64,704]{3,2,1,0:T(8,128)(2,1)S(1)}, bf16[8,2,64,704]{3,2,1,0:T(8,128)(2,1)}, u32[]{:S(2)}, u32[]{:S(2)}) %collective-permute-start.93) | collective-permute-done | bytes 1441824 | tf_op jit(solution)/shard_map/ppermute | solution.py:1142
  238.2 11.1 %collective-permute-done.82.refs_4_ = bf16[128,2048]{1,0:T(8,128)(2,1)S(1)} collective-permute-done((bf16[128,2048]{1,0:T(8,128)(2,1)S(1)}, bf16[128,2048]{1,0:T(8,128)(2,1)S(1)}, u32[]{:S(2)}, u32[]{:S(2)}) %collective-permute-start.82) | collective-permute-done | bytes 524320 | tf_op jit(solution)/shard_map/ppermute | solution.py:99
  251.5 10.1 %collective-permute-done.84.refs_6_ = bf16[128,2048]{1,0:T(8,128)(2,1)S(1)} collective-permute-done((bf16[128,2048]{1,0:T(8,128)(2,1)S(1)}, bf16[128,2048]{1,0:T(8,128)(2,1)S(1)}, u32[]{:S(2)}, u32[]{:S(2)}) %collective-permute-start.84) | collective-permute-done | bytes 524320 | tf_op jit(solution)/shard_map/ppermute | solution.py:99
  267.3 4.1 shard_map.171.refs_22_.down_ref
  274.8 28.6 %shard_map.172 = (bf16[1024,704]{1,0:T(8,128)(2,1)}, bf16[1024,704]{1,0:T(8,128)(2,1)}, bf16[1024,704]{1,0:T(8,128)(2,1)}, bf16[1024,2048]{1,0:T(8,128)(2,1)}, b...) custom-call(s32[75]{0:T(128)} %fusion.9.table_ref.table, bf16[128,2048]{1,0:T(8,128)(2,1)} %get-tuple-element.90.refs_0_, ...), custom_call_target="tpu_custom_call" | custom-call | flops 30799998976 | bytes 92400000 | tf_op jit(solution)/shard_map/pallas_call | solution.py:844
  303.4 7.1 %shard_map.173 = (bf16[1024,704]{1,0:T(8,128)(2,1)}, bf16[1024,704]{1,0:T(8,128)(2,1)}) custom-call(bf16[1024,2048]{1,0:T(8,128)(2,1)} %get-tuple-element.92.input_ref, bf16[1024,704]{1,0:T(8,128)(2,1)} %get-tuple-element.93.refs_0_, bf16[1024,704]{1,0:T(8,128)(2,1)} %get-tuple-element.94.refs_1_), custom_call_target="tpu_custom_call" | custom-call | flops 2310000128 | bytes 6930000 | tf_op jit(solution)/shard_map/pallas_call | solution.py:602
  317.7 6.2 collective-permute-done.100.ccw_ref
  333.9 9.3 %shard_map.174 = (f32[8,2,64,704]{3,2,1,0:T(8,128)}, bf16[8,2,64,704]{3,2,1,0:T(8,128)(2,1)}) custom-call(s32[75]{0:T(128)} %fusion.9.table_ref.table, bf16[1024,2048]{1,0:T(8,128)(2,1)} %get-tuple-element.92.input_ref, bf16[1024,704]{1,0:T(8,128)(2,1)} %get-tuple-element.93.refs_0_, bf16[1024,704]{1,0:T(8,128)(2,1)} %get-tuple-element.94.refs_1_, ...), custom_call_target="tpu_custom_call" | custom-call | flops 3464999936 | bytes 10395000 | tf_op jit(solution)/shard_map/pallas_call | solution.py:690
  350.0 7.2 %shard_map.175.refs_1_.ahead_ref.back_ref = bf16[1024,2048]{1,0:T(8,128)(2,1)} custom-call(bf16[1024,704]{1,0:T(8,128)(2,1)} %get-tuple-element.91.act_ref, bf16[704,2048]{1,0:T(8,128)(2,1)} %shard_map.171.refs_22_.down_ref, bf16[8,2,64,704]{3,2,1,0:T(8,128)(2,1)} %get-tuple-element.97.refs_0_.refs_1_), custom_call_target="tpu_custom_call" | custom-call | flops 2695000064 | bytes 8085000 | tf_op jit(solution)/shard_map/pallas_call | solution.py:739
  368.1 7.5 %collective-permute-done.105.refs_1_.refs_0_ = bf16[128,2048]{1,0:T(8,128)(2,1)S(1)} collective-permute-done((bf16[128,2048]{1,0:T(8,128)(2,1)}, bf16[128,2048]{1,0:T(8,128)(2,1)S(1)}, u32[]{:S(2)}, u32[]{:S(2)}) %collective-permute-start.105) | collective-permute-done | bytes 524320 | tf_op jit(solution)/shard_map/ppermute | solution.py:123
  379.5 10.4 %shard_map.188 = (f32[128,2048]{1,0:T(8,128)}, bf16[128,2048]{1,0:T(8,128)(2,1)}, bf16[128,2048]{1,0:T(8,128)(2,1)}, f32[8,2048]{1,0:T(8,128)}) custom-call(s32[75]{0:T(128)} %fusion.9.table_ref.table, bf16[128,2048]{1,0:T(8,128)(2,1)} %slice.127.refs_0_, bf16[128,2048]{1,0:T(8,128)(2,1)} %copy-done.13, bf16[128,2048]{1,0:T(8,128)(2,1)} %copy-done.14, ...), custom_call_target="tpu_custom_call" | custom-call | flops 3849999872 | bytes 11550000 | tf_op jit(solution)/shard_map/pallas_call | solution.py:184
  389.9 4.1 shard_map.190
  395.5 4.7 all-to-all-start.1
  404.2 13.7 %shard_map.189 = (bf16[128,2048]{1,0:T(8,128)(2,1)}, bf16[8,128,512]{2,1,0:T(8,128)(2,1)}, bf16[8,128,512]{2,1,0:T(8,128)(2,1)}) custom-call(s32[75]{0:T(128)} %fusion.9.table_ref.table, bf16[128,2048]{1,0:T(8,128)(2,1)} %get-tuple-element.111.refs_0_, bf16[128,2048]{1,0:T(8,128)(2,1)} %get-tuple-element.113.refs_1_, ...), custom_call_target="tpu_custom_call" | custom-call | flops 5500000256 | bytes 16500000 | tf_op jit(solution)/shard_map/pallas_call | solution.py:1023
  417.9 6.0 shard_map.191
  423.9 9.5 %collective-permute-done.107.cw_ref.refs_12_ = bf16[64,2048]{1,0:T(8,128)(2,1)S(1)} collective-permute-done((bf16[64,2048]{1,0:T(8,128)(2,1)}, bf16[64,2048]{1,0:T(8,128)(2,1)S(1)}, u32[]{:S(2)}, u32[]{:S(2)}) %collective-permute-start.107) | collective-permute-done | bytes 262176 | tf_op jit(solution)/shard_map/ppermute | solution.py:123
  433.4 5.3 all-to-all-done.1.refs_14_.refs_0_
  438.7 13.8 %shard_map.192 = (bf16[128,2048]{1,0:T(8,128)(2,1)}, bf16[8,128,512]{2,1,0:T(8,128)(2,1)}, bf16[8,128,512]{2,1,0:T(8,128)(2,1)}) custom-call(s32[75]{0:T(128)} %fusion.9.table_ref.table, bf16[128,2048]{1,0:T(8,128)(2,1)} %get-tuple-element.111.refs_0_, ...), custom_call_target="tpu_custom_call", output_to_operand_aliasing={{0}: (10, {}), {1}: (11, {}), {2}: (12, {})} | custom-call | flops 5500000256 | bytes 16500000 | tf_op jit(solution)/shard_map/pallas_call | solution.py:1023
  452.5 3.9 shard_map.193.refs_1_
  457.5 10.1 %shard_map.215 = (f32[352,2048]{1,0:T(8,128)}, bf16[352,2048]{1,0:T(8,128)(2,1)}) custom-call(s32[75]{0:T(128)} %fusion.9.table_ref.table, bf16[1024,704]{1,0:T(8,128)(2,1)} %get-tuple-element.91.act_ref, bf16[1024,2048]{1,0:T(8,128)(2,1)} %get-tuple-element.149.cot_ref, bf16[128,2048]{1,0:T(8,128)(2,1)} %copy-done.13, bf16[128,2048]{1,0:T(8,128)(2,1)} %copy-done.14), custom_call_target="tpu_custom_call" | custom-call | flops 3849999872 | bytes 11550000 | tf_op jit(solution)/shard_map/pallas_call | solution.py:717
  470.1 6.1 collective-permute-start.109
  477.4 10.9 %collective-permute-done.109.cw_ref = bf16[128,2048]{1,0:T(8,128)(2,1)S(1)} collective-permute-done((bf16[128,2048]{1,0:T(8,128)(2,1)}, bf16[128,2048]{1,0:T(8,128)(2,1)S(1)}, u32[]{:S(2)}, u32[]{:S(2)}) %collective-permute-start.109) | collective-permute-done | bytes 524320 | tf_op jit(solution)/shard_map/ppermute | solution.py:123
  500.1 4.6 collective-permute-done.123.half_got_ref
  504.7 6.1 collective-permute-start.120
  510.8 7.0 %shard_map.197.refs_1_.ahead_ref.back_ref = bf16[1536,2048]{1,0:T(8,128)(2,1)} custom-call(bf16[128,2048]{1,0:T(8,128)(2,1)} %get-tuple-element.123.input_ref, bf16[128,2048]{1,0:T(8,128)(2,1)} %get-tuple-element.124.refs_0_.grad_ref, bf16[1024,2048]{1,0:T(8,128)(2,1)} %collective-permute-done.122.got_ref, f32[8,1,64,2048]{3,2,1,0:T(8,128)} %get-tuple-element.128.half_ref, ...), custom_call_target="tpu_custom_call" | custom-call | flops 2200000000 | bytes 6600000 | tf_op jit(solution)/shard_map/pallas_call | solution.py:655
  544.0 12.0 %collective-permute-done.126.refs_1_ = bf16[128,512]{1,0:T(8,128)(2,1)S(1)} collective-permute-done((bf16[128,512]{1,0:T(8,128)(2,1)}, bf16[128,512]{1,0:T(8,128)(2,1)S(1)}, u32[]{:S(2)}, u32[]{:S(2)}) %collective-permute-start.126) | collective-permute-done | bytes 131104 | tf_op jit(solution)/shard_map/ppermute | solution.py:123
  567.5 11.9 %shard_map.204 = (bf16[128,2048]{1,0:T(8,128)(2,1)}, f32[8,2048]{1,0:T(8,128)}) custom-call(s32[75]{0:T(128)} %fusion.9.table_ref.table, bf16[128,2048]{1,0:T(8,128)(2,1)} %get-tuple-element.124.refs_0_.grad_ref, bf16[128,512]{1,0:T(8,128)(2,1)} %shard_map.201.refs_1_.refs_0_.refs_2_, bf16[128,2048]{1,0:T(8,128)(2,1)} %bitcast.60, ...), custom_call_target="tpu_custom_call" | custom-call | flops 4427500032 | bytes 13282500 | tf_op jit(solution)/shard_map/pallas_call | solution.py:184
  604.6 5.9 shard_map.214
  610.5 6.0 collective-permute-done.141.cw_ref.refs_1_
  637.4 11.1 %collective-permute-done.145 = bf16[160,512]{1,0:T(8,128)(2,1)S(1)} collective-permute-done((bf16[160,512]{1,0:T(8,128)(2,1)}, bf16[160,512]{1,0:T(8,128)(2,1)S(1)}, u32[]{:S(2)}, u32[]{:S(2)}) %collective-permute-start.145) | collective-permute-done | bytes 163872 | tf_op jit(solution)/shard_map/ppermute | solution.py:123
  657.3 13.3 %collective-permute-done.136 = bf16[192,2048]{1,0:T(8,128)(2,1)S(1)} collective-permute-done((bf16[192,2048]{1,0:T(8,128)(2,1)S(1)}, bf16[192,2048]{1,0:T(8,128)(2,1)S(1)}, u32[]{:S(2)}, u32[]{:S(2)}) %collective-permute-start.136) | collective-permute-done | bytes 786464 | tf_op jit(solution)/shard_map/ppermute | solution.py:1142
  (646 shorter events, 275.4 us)
Async XLA Ops:
  20.5 15.7 %collective-permute-start.8 = (bf16[128,1408]{1,0:T(8,128)(2,1)S(1)}, bf16[128,1408]{1,0:T(8,128)(2,1)S(1)}, u32[]{:S(2)}, u32[]{:S(2)}) collective-permute-start(bf16[128,1408]{1,0:T(8,128)(2,1)S(1)} %collective-permute-done.refs_4_.refs_7_), channel_id=1, source_target_pairs={{0,16},{16,0},{1,17},{17,1},{2,18},{18,2},{3,19},{19,3},{4,20},{20... | collective-permute-start | bytes 1081352 | tf_op jit(solution)/shard_map/ppermute | solution.py:1142
  21.2 16.7 %collective-permute-start.2 = (bf16[128,1408]{1,0:T(8,128)(2,1)S(1)}, bf16[128,1408]{1,0:T(8,128)(2,1)S(1)}, u32[]{:S(2)}, u32[]{:S(2)}) collective-permute-start(bf16[128,1408]{1,0:T(8,128)(2,1)S(1)} %collective-permute-done.refs_4_.refs_7_), channel_id=1, source_target_pairs={{0,4},{1,5},{2,0},{3,1},{4,8},{5,9},{6,2},{7,3},{8,12},{9,13},{10,... | collective-permute-start | bytes 1081352 | tf_op jit(solution)/shard_map/ppermute | solution.py:98
  49.4 19.2 %collective-permute-start.22 = (bf16[128,1408]{1,0:T(8,128)(2,1)S(1)}, bf16[128,1408]{1,0:T(8,128)(2,1)}, u32[]{:S(2)}, u32[]{:S(2)}) collective-permute-start(bf16[128,1408]{1,0:T(8,128)(2,1)S(1)} %collective-permute-done.5.refs_9_.refs_12_), channel_id=1, source_target_pairs={{0,1},{1,0},{2,3},{3,2},{4,5},{5,4},{6,7},{7,6},{8,9},{9,8},{10,11... | collective-permute-start | bytes 1081352 | tf_op jit(solution)/shard_map/ppermute | solution.py:89
  115.0 21.6 %collective-permute-start.68 = (bf16[128,1024]{1,0:T(8,128)(2,1)}, bf16[128,1024]{1,0:T(8,128)(2,1)}, u32[]{:S(2)}, u32[]{:S(2)}) collective-permute-start(bf16[128,1024]{1,0:T(8,128)(2,1)} %get-tuple-element.164.refs_12_.refs_16_), channel_id=1, source_target_pairs={{0,1},{1,0},{2,3},{3,2},{4,5},{5,4},{6,7},{7,6},{8,9},{9,8},{10,11... | collective-permute-start | bytes 786440 | tf_op jit(solution)/shard_map/ppermute | solution.py:89
  125.4 16.8 %collective-permute-start.61 = (bf16[128,1024]{1,0:T(8,128)(2,1)}, bf16[128,1024]{1,0:T(8,128)(2,1)}, u32[]{:S(2)}, u32[]{:S(2)}) collective-permute-start(bf16[128,1024]{1,0:T(8,128)(2,1)} %collective-permute-done.37.refs_5_.refs_9_), channel_id=1, source_target_pairs={{0,1},{1,0},{2,3},{3,2},{4,5},{5,4},{6,7},{7,6},{8,9},{9,8},{10,11... | collective-permute-start | bytes 786440 | tf_op jit(solution)/shard_map/ppermute | solution.py:89
  126.1 56.6 %all-to-all-start = ((bf16[8,2,64,704]{3,2,1,0:T(8,128)(2,1)}), bf16[8,2,64,704]{3,2,1,0:T(8,128)(2,1)S(1)}, u32[]{:S(2)}, u32[]{:S(2)}) async-start(bf16[8,2,64,704]{3,2,1,0:T(8,128)(2,1)} %shard_map.168), calls=%async_computation | async-start | bytes 3145728 | tf_op jit(solution)/shard_map/all_to_all | solution.py:1164
  136.6 32.3 %collective-permute-start.48 = (bf16[8,128,512]{2,1,0:T(8,128)(2,1)}, bf16[8,128,512]{2,1,0:T(8,128)(2,1)S(1)}, u32[]{:S(2)}, u32[]{:S(2)}) collective-permute-start(bf16[8,128,512]{2,1,0:T(8,128)(2,1)} %shard_map.164.refs_1_.refs_4_), channel_id=1, source_target_pairs={{0,1},{1,0},{2,3},{3,2},{4,5},{5,4},{6,7},{7,6},{8,9},{9,8},{10,11... | collective-permute-start | bytes 3145736 | tf_op jit(solution)/shard_map/ppermute | solution.py:89
  164.7 19.2 %collective-permute-start.55 = (bf16[128,1024]{1,0:T(8,128)(2,1)S(1)}, bf16[128,1024]{1,0:T(8,128)(2,1)}, u32[]{:S(2)}, u32[]{:S(2)}) collective-permute-start(bf16[128,1024]{1,0:T(8,128)(2,1)S(1)} %copy-done.70), channel_id=1, source_target_pairs={{0,16},{16,0},{1,17},{17,1},{2,18},{18,2},{3,19},{19,3},{4,20},{20... | collective-permute-start | bytes 786440 | tf_op jit(solution)/shard_map/ppermute | solution.py:1142
  166.2 17.7 %collective-permute-start.67 = (bf16[64,1024]{1,0:T(8,128)(2,1)S(1)}, bf16[64,1024]{1,0:T(8,128)(2,1)S(1)}, u32[]{:S(2)}, u32[]{:S(2)}) collective-permute-start(bf16[64,1024]{1,0:T(8,128)(2,1)S(1)} %copy-done.64), channel_id=1, source_target_pairs={{0,1},{1,0},{2,3},{3,2},{4,5},{5,4},{6,7},{7,6},{8,9},{9,8},{10,11... | collective-permute-start | bytes 393224 | tf_op jit(solution)/shard_map/ppermute | solution.py:89
  166.2 18.3 %collective-permute-start.66 = (bf16[64,1024]{1,0:T(8,128)(2,1)S(1)}, bf16[64,1024]{1,0:T(8,128)(2,1)S(1)}, u32[]{:S(2)}, u32[]{:S(2)}) collective-permute-start(bf16[64,1024]{1,0:T(8,128)(2,1)S(1)} %copy-done.66), channel_id=1, source_target_pairs={{0,1},{1,0},{2,3},{3,2},{4,5},{5,4},{6,7},{7,6},{8,9},{9,8},{10,11... | collective-permute-start | bytes 393224 | tf_op jit(solution)/shard_map/ppermute | solution.py:89
  167.5 16.9 %collective-permute-start.57 = (bf16[64,1024]{1,0:T(8,128)(2,1)S(1)}, bf16[64,1024]{1,0:T(8,128)(2,1)S(1)}, u32[]{:S(2)}, u32[]{:S(2)}) collective-permute-start(bf16[64,1024]{1,0:T(8,128)(2,1)S(1)} %copy-done.66), channel_id=1, source_target_pairs={{0,16},{16,0},{1,17},{17,1},{2,18},{18,2},{3,19},{19,3},{4,20},{20... | collective-permute-start | bytes 393224 | tf_op jit(solution)/shard_map/ppermute | solution.py:1142
  169.0 17.6 %collective-permute-start.76 = (bf16[64,1024]{1,0:T(8,128)(2,1)S(1)}, bf16[64,1024]{1,0:T(8,128)(2,1)S(1)}, u32[]{:S(2)}, u32[]{:S(2)}) collective-permute-start(bf16[64,1024]{1,0:T(8,128)(2,1)S(1)} %collective-permute-done.58.refs_20_.refs_24_), channel_id=1, source_target_pairs={{0,1},{1,0},{2,3},{3,2},{4,5},{5,4},{6,7},{7,6},{8,9},{9,8},{10,11... | collective-permute-start | bytes 393224 | tf_op jit(solution)/shard_map/ppermute | solution.py:89
  183.9 18.3 %collective-permute-start.74 = (bf16[128,1024]{1,0:T(8,128)(2,1)S(1)}, bf16[128,1024]{1,0:T(8,128)(2,1)S(1)}, u32[]{:S(2)}, u32[]{:S(2)}) collective-permute-start(bf16[128,1024]{1,0:T(8,128)(2,1)S(1)} %copy-done.106), channel_id=1, source_target_pairs={{0,1},{1,0},{2,3},{3,2},{4,5},{5,4},{6,7},{7,6},{8,9},{9,8},{10,11... | collective-permute-start | bytes 786440 | tf_op jit(solution)/shard_map/ppermute | solution.py:89
  183.9 18.3 %collective-permute-start.73 = (bf16[128,1024]{1,0:T(8,128)(2,1)}, bf16[128,1024]{1,0:T(8,128)(2,1)S(1)}, u32[]{:S(2)}, u32[]{:S(2)}) collective-permute-start(bf16[128,1024]{1,0:T(8,128)(2,1)} %collective-permute-done.55.refs_17_.refs_21_), channel_id=1, source_target_pairs={{0,1},{1,0},{2,3},{3,2},{4,5},{5,4},{6,7},{7,6},{8,9},{9,8},{10,11... | collective-permute-start | bytes 786440 | tf_op jit(solution)/shard_map/ppermute | solution.py:89
  199.5 36.6 %collective-permute-start.93 = (bf16[8,2,64,704]{3,2,1,0:T(8,128)(2,1)S(1)}, bf16[8,2,64,704]{3,2,1,0:T(8,128)(2,1)}, u32[]{:S(2)}, u32[]{:S(2)}) collective-permute-start(bf16[8,2,64,704]{3,2,1,0:T(8,128)(2,1)S(1)} %copy-done.3), channel_id=1, source_target_pairs={{0,16},{16,0},{1,17},{17,1},{2,18},{18,2},{3,19},{19,3},{4,20},{20... | collective-permute-start | bytes 4325384 | tf_op jit(solution)/shard_map/ppermute | solution.py:1142
  214.1 23.7 %collective-permute-start.90 = (bf16[128,2048]{1,0:T(8,128)(2,1)S(1)}, bf16[128,2048]{1,0:T(8,128)(2,1)S(1)}, u32[]{:S(2)}, u32[]{:S(2)}) collective-permute-start(bf16[128,2048]{1,0:T(8,128)(2,1)S(1)} %collective-permute-done.88.refs_13_), channel_id=1, source_target_pairs={{0,2},{1,3},{2,6},{3,7},{4,0},{5,1},{6,10},{7,11},{8,4},{9,5},{10,... | collective-permute-start | bytes 1572872 | tf_op jit(solution)/shard_map/ppermute | solution.py:99
  215.9 22.3 %collective-permute-start.89 = (bf16[128,2048]{1,0:T(8,128)(2,1)S(1)}, bf16[128,2048]{1,0:T(8,128)(2,1)S(1)}, u32[]{:S(2)}, u32[]{:S(2)}) collective-permute-start(bf16[128,2048]{1,0:T(8,128)(2,1)S(1)} %collective-permute-done.87.refs_12_), channel_id=1, source_target_pairs={{0,4},{1,5},{2,0},{3,1},{4,8},{5,9},{6,2},{7,3},{8,12},{9,13},{10,... | collective-permute-start | bytes 1572872 | tf_op jit(solution)/shard_map/ppermute | solution.py:98
  226.5 37.2 %collective-permute-start.96 = (bf16[352,2048]{1,0:T(8,128)(2,1)S(1)}, bf16[352,2048]{1,0:T(8,128)(2,1)S(1)}, u32[]{:S(2)}, u32[]{:S(2)}) collective-permute-start(bf16[352,2048]{1,0:T(8,128)(2,1)S(1)} %copy-done.75), channel_id=1, source_target_pairs={{0,1},{1,0},{2,3},{3,2},{4,5},{5,4},{6,7},{7,6},{8,9},{9,8},{10,11... | collective-permute-start | bytes 4325384 | tf_op jit(solution)/shard_map/ppermute | solution.py:89
  228.3 36.7 %collective-permute-start.94 = (bf16[8,2,64,704]{3,2,1,0:T(8,128)(2,1)S(1)}, bf16[8,2,64,704]{3,2,1,0:T(8,128)(2,1)S(1)}, u32[]{:S(2)}, u32[]{:S(2)}) collective-permute-start(bf16[8,2,64,704]{3,2,1,0:T(8,128)(2,1)S(1)} %copy-done.3), channel_id=1, source_target_pairs={{0,1},{1,0},{2,3},{3,2},{4,5},{5,4},{6,7},{7,6},{8,9},{9,8},{10,11... | collective-permute-start | bytes 4325384 | tf_op jit(solution)/shard_map/ppermute | solution.py:89
  238.2 35.9 %collective-permute-start.95 = (bf16[8,2,64,704]{3,2,1,0:T(8,128)(2,1)}, bf16[8,2,64,704]{3,2,1,0:T(8,128)(2,1)}, u32[]{:S(2)}, u32[]{:S(2)}) collective-permute-start(bf16[8,2,64,704]{3,2,1,0:T(8,128)(2,1)} %collective-permute-done.93.refs_19_), channel_id=1, source_target_pairs={{0,1},{1,0},{2,3},{3,2},{4,5},{5,4},{6,7},{7,6},{8,9},{9,8},{10,11... | collective-permute-start | bytes 4325384 | tf_op jit(solution)/shard_map/ppermute | solution.py:89
  312.4 17.4 %collective-permute-start.98 = (bf16[1024,704]{0,1:T(8,128)(2,1)S(1)}, bf16[1024,704]{0,1:T(8,128)(2,1)}, u32[]{:S(2)}, u32[]{:S(2)}) collective-permute-start(bf16[1024,704]{0,1:T(8,128)(2,1)S(1)} %copy.56), channel_id=1, source_target_pairs={{0,1},{1,0},{2,3},{3,2},{4,5},{5,4},{6,7},{7,6},{8,9},{9,8},{10,11... | collective-permute-start | bytes 4325384 | tf_op jit(solution)/shard_map/ppermute | solution.py:89
  314.1 18.3 %collective-permute-start.97 = (bf16[1024,704]{0,1:T(8,128)(2,1)}, bf16[1024,704]{0,1:T(8,128)(2,1)S(1)}, u32[]{:S(2)}, u32[]{:S(2)}) collective-permute-start(bf16[1024,704]{0,1:T(8,128)(2,1)} %copy.55), channel_id=1, source_target_pairs={{0,1},{1,0},{2,3},{3,2},{4,5},{5,4},{6,7},{7,6},{8,9},{9,8},{10,11... | collective-permute-start | bytes 4325384 | tf_op jit(solution)/shard_map/ppermute | solution.py:89
  327.7 16.0 %collective-permute-start.101 = (bf16[128,2048]{1,0:T(8,128)(2,1)}, bf16[128,2048]{1,0:T(8,128)(2,1)S(1)}, u32[]{:S(2)}, u32[]{:S(2)}) collective-permute-start(bf16[128,2048]{1,0:T(8,128)(2,1)} %get-tuple-element.99), channel_id=1, source_target_pairs={{0,4},{1,5},{2,0},{3,1},{4,8},{5,9},{6,2},{7,3},{8,12},{9,13},{10,... | collective-permute-start | bytes 1572872 | tf_op jit(solution)/shard_map/ppermute | solution.py:123
  343.2 35.1 %collective-permute-start.115 = (bf16[8,2,64,704]{3,2,1,0:T(8,128)(2,1)}, bf16[8,2,64,704]{3,2,1,0:T(8,128)(2,1)S(1)}, u32[]{:S(2)}, u32[]{:S(2)}) collective-permute-start(bf16[8,2,64,704]{3,2,1,0:T(8,128)(2,1)} %get-tuple-element.97.refs_0_.refs_1_), channel_id=1, source_target_pairs={{0,16},{16,0},{1,17},{17,1},{2,18},{18,2},{3,19},{19,3},{4,20},{20... | collective-permute-start | bytes 4325384 | tf_op jit(solution)/shard_map/ppermute | solution.py:1142
  393.9 24.0 %collective-permute-start.116 = (bf16[1024,2048]{1,0:T(8,128)(2,1)}, bf16[1024,2048]{1,0:T(8,128)(2,1)}, u32[]{:S(2)}, u32[]{:S(2)}) collective-permute-start(bf16[1024,2048]{1,0:T(8,128)(2,1)} %shard_map.190), channel_id=1, source_target_pairs={{0,1},{1,0},{2,3},{3,2},{4,5},{5,4},{6,7},{7,6},{8,9},{9,8},{10,11... | collective-permute-start | bytes 12582920 | tf_op jit(solution)/shard_map/ppermute | solution.py:89
  395.5 43.2 %all-to-all-start.1 = ((bf16[8,2,64,704]{3,2,1,0:T(8,128)(2,1)}), bf16[8,2,64,704]{3,2,1,0:T(8,128)(2,1)}, u32[]{:S(2)}, u32[]{:S(2)}) async-start(bf16[8,2,64,704]{3,2,1,0:T(8,128)(2,1)} %add_convert_fusion), calls=%async_computation.1 | async-start | bytes 3145728 | tf_op jit(solution)/shard_map/all_to_all | solution.py:1205
  402.1 31.2 %collective-permute-start.107 = (bf16[64,2048]{1,0:T(8,128)(2,1)}, bf16[64,2048]{1,0:T(8,128)(2,1)S(1)}, u32[]{:S(2)}, u32[]{:S(2)}) collective-permute-start(bf16[64,2048]{1,0:T(8,128)(2,1)} %shard_map.183), channel_id=1, source_target_pairs={{0,4},{1,5},{2,0},{3,1},{4,8},{5,9},{6,2},{7,3},{8,12},{9,13},{10,... | collective-permute-start | bytes 786440 | tf_op jit(solution)/shard_map/ppermute | solution.py:123
  404.2 29.2 %collective-permute-start.108 = (bf16[64,2048]{1,0:T(8,128)(2,1)}, bf16[64,2048]{1,0:T(8,128)(2,1)S(1)}, u32[]{:S(2)}, u32[]{:S(2)}) collective-permute-start(bf16[64,2048]{1,0:T(8,128)(2,1)} %shard_map.184), channel_id=1, source_target_pairs={{0,2},{1,3},{2,6},{3,7},{4,0},{5,1},{6,10},{7,11},{8,4},{9,5},{10,... | collective-permute-start | bytes 786440 | tf_op jit(solution)/shard_map/ppermute | solution.py:124
  456.4 54.3 %collective-permute-start.122 = (bf16[1024,2048]{1,0:T(8,128)(2,1)}, bf16[1024,2048]{1,0:T(8,128)(2,1)}, u32[]{:S(2)}, u32[]{:S(2)}) collective-permute-start(bf16[1024,2048]{1,0:T(8,128)(2,1)} %shard_map.193.refs_1_), channel_id=1, source_target_pairs={{0,1},{1,0},{2,3},{3,2},{4,5},{5,4},{6,7},{7,6},{8,9},{9,8},{10,11... | collective-permute-start | bytes 12582920 | tf_op jit(solution)/shard_map/ppermute | solution.py:89
  456.4 20.6 %collective-permute-start.117 = (bf16[8,128,512]{2,1,0:T(8,128)(2,1)}, bf16[8,128,512]{2,1,0:T(8,128)(2,1)S(1)}, u32[]{:S(2)}, u32[]{:S(2)}) collective-permute-start(bf16[8,128,512]{2,1,0:T(8,128)(2,1)} %shard_map.194), channel_id=1, source_target_pairs={{0,1},{1,0},{2,3},{3,2},{4,5},{5,4},{6,7},{7,6},{8,9},{9,8},{10,11... | collective-permute-start | bytes 3145736 | tf_op jit(solution)/shard_map/ppermute | solution.py:89
  457.0 47.7 %collective-permute-start.123 = (bf16[8,1,64,2048]{3,2,1,0:T(8,128)(2,1)}, bf16[8,1,64,2048]{3,2,1,0:T(8,128)(2,1)S(1)}, u32[]{:S(2)}, u32[]{:S(2)}) collective-permute-start(bf16[8,1,64,2048]{3,2,1,0:T(8,128)(2,1)} %get-tuple-element.120.refs_15_), channel_id=1, source_target_pairs={{0,16},{16,0},{1,17},{17,1},{2,18},{18,2},{3,19},{19,3},{4,20},{20... | collective-permute-start | bytes 6291464 | tf_op jit(solution)/shard_map/ppermute | solution.py:1142
  467.6 113.0 %collective-permute-start.149 = (bf16[352,2048]{1,0:T(8,128)(2,1)}, bf16[352,2048]{1,0:T(8,128)(2,1)}, u32[]{:S(2)}, u32[]{:S(2)}) collective-permute-start(bf16[352,2048]{1,0:T(8,128)(2,1)} %get-tuple-element.151), channel_id=1, source_target_pairs={{0,1},{1,0},{2,3},{3,2},{4,5},{5,4},{6,7},{7,6},{8,9},{9,8},{10,11... | collective-permute-start | bytes 4325384 | tf_op jit(solution)/shard_map/ppermute | solution.py:89
  470.1 18.2 %collective-permute-start.109 = (bf16[128,2048]{1,0:T(8,128)(2,1)}, bf16[128,2048]{1,0:T(8,128)(2,1)S(1)}, u32[]{:S(2)}, u32[]{:S(2)}) collective-permute-start(bf16[128,2048]{1,0:T(8,128)(2,1)} %get-tuple-element.105), channel_id=1, source_target_pairs={{0,4},{1,5},{2,0},{3,1},{4,8},{5,9},{6,2},{7,3},{8,12},{9,13},{10,... | collective-permute-start | bytes 1572872 | tf_op jit(solution)/shard_map/ppermute | solution.py:123
  496.3 22.7 %collective-permute-start.111 = (bf16[128,2048]{1,0:T(8,128)(2,1)}, bf16[128,2048]{1,0:T(8,128)(2,1)S(1)}, u32[]{:S(2)}, u32[]{:S(2)}) collective-permute-start(bf16[128,2048]{1,0:T(8,128)(2,1)} %get-tuple-element.107), channel_id=1, source_target_pairs={{0,4},{1,5},{2,0},{3,1},{4,8},{5,9},{6,2},{7,3},{8,12},{9,13},{10,... | collective-permute-start | bytes 1572872 | tf_op jit(solution)/shard_map/ppermute | solution.py:123
  496.6 24.0 %collective-permute-start.112 = (bf16[128,2048]{1,0:T(8,128)(2,1)}, bf16[128,2048]{1,0:T(8,128)(2,1)S(1)}, u32[]{:S(2)}, u32[]{:S(2)}) collective-permute-start(bf16[128,2048]{1,0:T(8,128)(2,1)} %get-tuple-element.108), channel_id=1, source_target_pairs={{0,2},{1,3},{2,6},{3,7},{4,0},{5,1},{6,10},{7,11},{8,4},{9,5},{10,... | collective-permute-start | bytes 1572872 | tf_op jit(solution)/shard_map/ppermute | solution.py:124
  504.7 19.3 %collective-permute-start.120 = (bf16[128,512]{1,0:T(8,128)(2,1)}, bf16[128,512]{1,0:T(8,128)(2,1)S(1)}, u32[]{:S(2)}, u32[]{:S(2)}) collective-permute-start(bf16[128,512]{1,0:T(8,128)(2,1)} %get-tuple-element.125), channel_id=1, source_target_pairs={{0,4},{1,5},{2,0},{3,1},{4,8},{5,9},{6,2},{7,3},{8,12},{9,13},{10,... | collective-permute-start | bytes 393224 | tf_op jit(solution)/shard_map/ppermute | solution.py:123
  535.3 30.9 %collective-permute-start.130 = (bf16[192,2048]{1,0:T(8,128)(2,1)}, bf16[192,2048]{1,0:T(8,128)(2,1)S(1)}, u32[]{:S(2)}, u32[]{:S(2)}) collective-permute-start(bf16[192,2048]{1,0:T(8,128)(2,1)} %get-tuple-element.134), channel_id=1, source_target_pairs={{0,4},{1,5},{2,0},{3,1},{4,8},{5,9},{6,2},{7,3},{8,12},{9,13},{10,... | collective-permute-start | bytes 2359304 | tf_op jit(solution)/shard_map/ppermute | solution.py:123
  535.4 30.8 %collective-permute-start.131 = (bf16[192,2048]{1,0:T(8,128)(2,1)}, bf16[192,2048]{1,0:T(8,128)(2,1)S(1)}, u32[]{:S(2)}, u32[]{:S(2)}) collective-permute-start(bf16[192,2048]{1,0:T(8,128)(2,1)} %get-tuple-element.135), channel_id=1, source_target_pairs={{0,2},{1,3},{2,6},{3,7},{4,0},{5,1},{6,10},{7,11},{8,4},{9,5},{10,... | collective-permute-start | bytes 2359304 | tf_op jit(solution)/shard_map/ppermute | solution.py:124
  565.3 37.6 %collective-permute-start.148 = (bf16[8,2,64,704]{3,2,1,0:T(8,128)(2,1)}, bf16[8,2,64,704]{3,2,1,0:T(8,128)(2,1)}, u32[]{:S(2)}, u32[]{:S(2)}) collective-permute-start(bf16[8,2,64,704]{3,2,1,0:T(8,128)(2,1)} %all-to-all-done.1.refs_14_.refs_0_), channel_id=1, source_target_pairs={{0,16},{16,0},{1,17},{17,1},{2,18},{18,2},{3,19},{19,3},{4,20},{20... | collective-permute-start | bytes 4325384 | tf_op jit(solution)/shard_map/ppermute | solution.py:1142
  566.2 18.6 %collective-permute-start.137 = (bf16[1024,512]{1,0:T(8,128)(2,1)}, bf16[1024,512]{1,0:T(8,128)(2,1)}, u32[]{:S(2)}, u32[]{:S(2)}) collective-permute-start(bf16[1024,512]{1,0:T(8,128)(2,1)} %shard_map.207), channel_id=1, source_target_pairs={{0,1},{1,0},{2,3},{3,2},{4,5},{5,4},{6,7},{7,6},{8,9},{9,8},{10,11... | collective-permute-start | bytes 3145736 | tf_op jit(solution)/shard_map/ppermute | solution.py:89
  583.5 52.8 %collective-permute-start.150 = (bf16[352,2048]{1,0:T(8,128)(2,1)}, bf16[352,2048]{1,0:T(8,128)(2,1)S(1)}, u32[]{:S(2)}, u32[]{:S(2)}) collective-permute-start(bf16[352,2048]{1,0:T(8,128)(2,1)} %add_convert_fusion.1), channel_id=1, source_target_pairs={{0,16},{16,0},{1,17},{17,1},{2,18},{18,2},{3,19},{19,3},{4,20},{20... | collective-permute-start | bytes 4325384 | tf_op jit(solution)/shard_map/ppermute | solution.py:1142
  594.0 25.9 %collective-permute-start.132 = (bf16[192,2048]{1,0:T(8,128)(2,1)}, bf16[192,2048]{1,0:T(8,128)(2,1)S(1)}, u32[]{:S(2)}, u32[]{:S(2)}) collective-permute-start(bf16[192,2048]{1,0:T(8,128)(2,1)} %get-tuple-element.137), channel_id=1, source_target_pairs={{0,4},{1,5},{2,0},{3,1},{4,8},{5,9},{6,2},{7,3},{8,12},{9,13},{10,... | collective-permute-start | bytes 2359304 | tf_op jit(solution)/shard_map/ppermute | solution.py:123
  595.2 24.8 %collective-permute-start.133 = (bf16[192,2048]{1,0:T(8,128)(2,1)}, bf16[192,2048]{1,0:T(8,128)(2,1)S(1)}, u32[]{:S(2)}, u32[]{:S(2)}) collective-permute-start(bf16[192,2048]{1,0:T(8,128)(2,1)} %get-tuple-element.138), channel_id=1, source_target_pairs={{0,2},{1,3},{2,6},{3,7},{4,0},{5,1},{6,10},{7,11},{8,4},{9,5},{10,... | collective-permute-start | bytes 2359304 | tf_op jit(solution)/shard_map/ppermute | solution.py:124
  598.6 18.0 %collective-permute-start.141 = (bf16[160,512]{1,0:T(8,128)(2,1)}, bf16[160,512]{1,0:T(8,128)(2,1)S(1)}, u32[]{:S(2)}, u32[]{:S(2)}) collective-permute-start(bf16[160,512]{1,0:T(8,128)(2,1)} %get-tuple-element.143), channel_id=1, source_target_pairs={{0,4},{1,5},{2,0},{3,1},{4,8},{5,9},{6,2},{7,3},{8,12},{9,13},{10,... | collective-permute-start | bytes 491528 | tf_op jit(solution)/shard_map/ppermute | solution.py:123
  626.3 24.0 %collective-permute-start.134 = (bf16[192,2048]{1,0:T(8,128)(2,1)}, bf16[192,2048]{1,0:T(8,128)(2,1)S(1)}, u32[]{:S(2)}, u32[]{:S(2)}) collective-permute-start(bf16[192,2048]{1,0:T(8,128)(2,1)} %get-tuple-element.139), channel_id=1, source_target_pairs={{0,4},{1,5},{2,0},{3,1},{4,8},{5,9},{6,2},{7,3},{8,12},{9,13},{10,... | collective-permute-start | bytes 2359304 | tf_op jit(solution)/shard_map/ppermute | solution.py:123
  627.9 22.5 %collective-permute-start.135 = (bf16[192,2048]{1,0:T(8,128)(2,1)}, bf16[192,2048]{1,0:T(8,128)(2,1)S(1)}, u32[]{:S(2)}, u32[]{:S(2)}) collective-permute-start(bf16[192,2048]{1,0:T(8,128)(2,1)} %get-tuple-element.140), channel_id=1, source_target_pairs={{0,2},{1,3},{2,6},{3,7},{4,0},{5,1},{6,10},{7,11},{8,4},{9,5},{10,... | collective-permute-start | bytes 2359304 | tf_op jit(solution)/shard_map/ppermute | solution.py:124
  632.2 16.3 %collective-permute-start.145 = (bf16[160,512]{1,0:T(8,128)(2,1)}, bf16[160,512]{1,0:T(8,128)(2,1)S(1)}, u32[]{:S(2)}, u32[]{:S(2)}) collective-permute-start(bf16[160,512]{1,0:T(8,128)(2,1)} %get-tuple-element.147), channel_id=1, source_target_pairs={{0,4},{1,5},{2,0},{3,1},{4,8},{5,9},{6,2},{7,3},{8,12},{9,13},{10,... | collective-permute-start | bytes 491528 | tf_op jit(solution)/shard_map/ppermute | solution.py:123
  651.9 18.7 %collective-permute-start.136 = (bf16[192,2048]{1,0:T(8,128)(2,1)S(1)}, bf16[192,2048]{1,0:T(8,128)(2,1)S(1)}, u32[]{:S(2)}, u32[]{:S(2)}) collective-permute-start(bf16[192,2048]{1,0:T(8,128)(2,1)S(1)} %add_convert_fusion.3), channel_id=1, source_target_pairs={{0,16},{16,0},{1,17},{17,1},{2,18},{18,2},{3,19},{19,3},{4,20},{20... | collective-permute-start | bytes 2359304 | tf_op jit(solution)/shard_map/ppermute | solution.py:1142
  (244 other events, 2714.4 us)

commit v7 on v6

--- a/solution.py
+++ b/solution.py
@@ -416,8 +416,8 @@
         grad_res_ref, half_ref, att_ref, term_ref = outs
         buffer, sems, total = scratch
         copies = shared_fetches(table[ring.side_at], pieces, refs, buffer, sems)
-        for copy in copies:
-            copy.start()
+        for n in sorted(range(len(copies)), key=lambda n: pieces[n][0]):
+            copies[n].start()
         factor = factor_ref[...]
         mean = jnp.zeros((rows, 1), F32)
         for d in range(size):
@@ -440,10 +440,11 @@
             back = cot_ref[:, columns(d)].astype(F32) + factor * (grad - normed * mean)
             grad_res_ref[:, columns(d)] = back
             half_ref[:, columns(d)] = back.astype(BF16)
-        for copy in copies:
-            copy.wait()
         halves = half_ref[...]
         for k in range(0, size, 2):
+            for piece, copy in zip(pieces, copies):
+                if piece[0] // 2 == k // 2:
+                    copy.wait()
             weights = buffer[k : k + 2].reshape(2 * rows, model)
             att_ref[:, k * LANES : (k + 2) * LANES] = dot(halves, weights, LAST).astype(BF16)
 
@@ -504,12 +505,13 @@
         grad_ref, term_ref = outs
         buffer, sems, total = scratch
         copies = shared_fetches(table[ring.side_at], pieces, refs, buffer, sems)
-        for copy in copies:
-            copy.start()
-        for copy in copies:
-            copy.wait()
+        for n in sorted(range(len(copies)), key=lambda n: pieces[n][0]):
+            copies[n].start()
         queries, keys = gq_ref[...], gkv_ref[...]
         for k in range(0, size, 2):
+            for piece, copy in zip(pieces, copies):
+                if piece[0] // 2 == k // 2:
+                    copy.wait()
             weights = buffer[k : k + 2].reshape(2 * rows, packed_width(width))
             total[:, k * LANES : (k + 2) * LANES] = dot(
                 queries, weights[:, :qsize], LAST

time: 682 us -> 683 us (level)
  no operation moved by 1% of the time
where the time goes in v7:
time: 683 us; the launch traced here: 674 us
  Pallas kernels  239 us (35%)
  waiting for transfers between devices  228 us (33%)
  starting transfers between devices  142 us (21%)
  local copies, waits for them, and re-layouts  43.7 us (6%)
  other arithmetic  19.7 us (3%)
    ppermute x23, waiting for transfers between devices, twin(): return lax.ppermute(value, 'rep', twin_map)  85.6 us
    ppermute x20, waiting for transfers between devices, scatter(): cw = lax.ppermute(cw, 'shard', self.ahead)  66.2 us
    pallas_call x7, Pallas kernels, call(): pl.pallas_call(body, grid_spec=pltpu.PrefetchScalarGridSpec(num_scalar_pr...  53.1 us
    pallas_call x4, Pallas kernels, attention_call(): pl.pallas_call(body, grid_spec=pltpu.PrefetchScalarGridSpec(num_scalar_pr...  53 us
    ppermute x15, waiting for transfers between devices, gather(): ccw = lax.ppermute(ccw, 'shard', self.back)  52.2 us
    pallas_call x15, Pallas kernels, add_step(): pl.pallas_call(body, grid=(1,), in_specs=[pl.BlockSpec((rows, width), lam...  35.6 us
    pallas_call x1, Pallas kernels, feed_forward(): pl.pallas_call(body, grid_spec=pltpu.PrefetchScalarGridSpec(num_scalar_pr...  28.6 us
    ppermute x20, starting transfers between devices, scatter(): cw = lax.ppermute(cw, 'shard', self.ahead)  28.1 us
  transfers between devices with their start and end apart: 153, of which 53 were waited for; matrix products, arithmetic and copies ran while one was open for 5% of the time, Pallas kernels for 24%

profile of v7, /device:TPU:0, one launch (start us, length us, event | category | flops | bytes accessed | tf_op | source)
XLA Modules:
  0.0 674.4 jit_solution(3387834970871782182)
XLA Ops:
  9.1 8.2 %collective-permute-done.1.refs_5_.refs_8_ = bf16[128,1408]{1,0:T(8,128)(2,1)S(1)} collective-permute-done((bf16[128,1408]{1,0:T(8,128)(2,1)}, bf16[128,1408]{1,0:T(8,128)(2,1)S(1)}, u32[]{:S(2)}, u32[]{:S(2)}) %collective-permute-start.1) | collective-permute-done | bytes 360480 | tf_op jit(solution)/shard_map/ppermute | solution.py:99
  21.7 6.8 %collective-permute-done.9.refs_14_.refs_17_ = bf16[128,1408]{1,0:T(8,128)(2,1)S(1)} collective-permute-done((bf16[128,1408]{1,0:T(8,128)(2,1)S(1)}, bf16[128,1408]{1,0:T(8,128)(2,1)S(1)}, u32[]{:S(2)}, u32[]{:S(2)}) %collective-permute-start.9) | collective-permute-done | bytes 360480 | tf_op jit(solution)/shard_map/ppermute | solution.py:1144
  30.7 5.5 collective-permute-done.8.refs_13_.refs_16_
  38.8 4.8 collective-permute-done.11.refs_16_.refs_19_
  49.4 4.3 collective-permute-done.10.refs_15_.refs_18_
  59.7 7.2 %collective-permute-done.15.refs_20_.refs_23_ = bf16[64,1408]{1,0:T(8,128)(2,1)} collective-permute-done((bf16[64,1408]{1,0:T(8,128)(2,1)S(1)}, bf16[64,1408]{1,0:T(8,128)(2,1)}, u32[]{:S(2)}, u32[]{:S(2)}) %collective-permute-start.15) | collective-permute-done | bytes 180256 | tf_op jit(solution)/shard_map/ppermute | solution.py:1144
  75.8 7.5 %collective-permute-done.14.refs_19_.refs_22_ = bf16[64,1408]{1,0:T(8,128)(2,1)S(1)} collective-permute-done((bf16[64,1408]{1,0:T(8,128)(2,1)}, bf16[64,1408]{1,0:T(8,128)(2,1)S(1)}, u32[]{:S(2)}, u32[]{:S(2)}) %collective-permute-start.14) | collective-permute-done | bytes 180256 | tf_op jit(solution)/shard_map/ppermute | solution.py:1144
  88.9 4.0 collective-permute-done.39.refs_40_.refs_9_.refs_13_
  93.7 9.0 %shard_map.163 = (f32[128,2048]{1,0:T(8,128)}, bf16[128,512]{1,0:T(8,128)(2,1)}, bf16[128,2048]{1,0:T(8,128)(2,1)}, f32[128,128]{1,0:T(8,128)}, f32[8,2048]{1,0:T(8,128)}) custom-call(s32[75]{0:T(128)} %fusion.9.table_ref.table, bf16[128,2048]{1,0:T(8,128)(2,1)} %bitcast.58, f32[128,128]{1,0:T(8,128)} %get-tuple-element.169.refs_1_.refs_4_.refs_7_.refs_3_, ...), custom_call_target="tpu_custom_call" | custom-call | flops 9900000256 | bytes 29700000 | tf_op jit(solution)/shard_map/pallas_call | solution.py:184
  121.2 4.1 shard_map.167.refs_0_
  126.1 6.7 all-to-all-start
  137.8 4.4 collective-permute-done.52.refs_14_.refs_18_
  144.2 3.6 collective-permute-done.51.refs_13_.refs_17_
  170.0 12.7 %shard_map.165 = (bf16[128,2048]{1,0:T(8,128)(2,1)}, bf16[128,2048]{1,0:T(8,128)(2,1)}, f32[16,1,256]{2,1,0:T(1,128)}) custom-call(s32[75]{0:T(128)} %fusion.9.table_ref.table, f32[128,2048]{1,0:T(8,128)} %get-tuple-element.82.refs_0_, bf16[8,128,512]{2,1,0:T(8,128)(2,1)} %shard_map.164.refs_1_.refs_4_, bf16[8,128,512]{2,1,0:T(8,128)(2,1)} %copy-done.77, ...), custom_call_target="tpu_custom_call" | custom-call | flops 15399999488 | bytes 46200000 | tf_op jit(solution)/shard_map/pallas_call | solution.py:1025
  186.6 12.8 %shard_map.166 = (bf16[128,2048]{1,0:T(8,128)(2,1)}, bf16[128,2048]{1,0:T(8,128)(2,1)}, f32[16,1,256]{2,1,0:T(1,128)}) custom-call(s32[75]{0:T(128)} %fusion.9.table_ref.table, f32[128,2048]{1,0:T(8,128)} %get-tuple-element.82.refs_0_, bf16[8,128,512]{2,1,0:T(8,128)(2,1)} %shard_map.164.refs_1_.refs_4_, ...), custom_call_target="tpu_custom_call", output_to_operand_aliasing={{0}: (7, {}), {1}: (8, {}), {2}: (9, {})} | custom-call | flops 15399999488 | bytes 46200000 | tf_op jit(solution)/shard_map/pallas_call | solution.py:1025
  203.1 8.2 %shard_map.170 = (f32[128,2048]{1,0:T(8,128)}, f32[128,128]{1,0:T(8,128)}, bf16[128,2048]{1,0:T(8,128)(2,1)}) custom-call(s32[75]{0:T(128)} %fusion.9.table_ref.table, bf16[128,2048]{1,0:T(8,128)(2,1)} %get-tuple-element.87.refs_0_.refs_2_.input_ref, bf16[128,2048]{1,0:T(8,128)(2,1)} %bitcast.59, f32[8,2048]{1,0:T(8,128)} %get-tuple-element.88.refs_2_.refs_5_.refs_4_, ...), custom_call_target="tpu_custom_call" | custom-call | flops 8800000000 | bytes 26400000 | tf_op jit(solution)/shard_map/pallas_call | solution.py:184
  216.1 10.3 %collective-permute-done.80.refs_2_ = bf16[128,2048]{1,0:T(8,128)(2,1)S(1)} collective-permute-done((bf16[128,2048]{1,0:T(8,128)(2,1)}, bf16[128,2048]{1,0:T(8,128)(2,1)S(1)}, u32[]{:S(2)}, u32[]{:S(2)}) %collective-permute-start.80) | collective-permute-done | bytes 524320 | tf_op jit(solution)/shard_map/ppermute | solution.py:99
  228.3 7.9 %collective-permute-done.93.refs_19_ = bf16[8,2,64,704]{3,2,1,0:T(8,128)(2,1)} collective-permute-done((bf16[8,2,64,704]{3,2,1,0:T(8,128)(2,1)S(1)}, bf16[8,2,64,704]{3,2,1,0:T(8,128)(2,1)}, u32[]{:S(2)}, u32[]{:S(2)}) %collective-permute-start.93) | collective-permute-done | bytes 1441824 | tf_op jit(solution)/shard_map/ppermute | solution.py:1144
  238.2 11.1 %collective-permute-done.82.refs_4_ = bf16[128,2048]{1,0:T(8,128)(2,1)S(1)} collective-permute-done((bf16[128,2048]{1,0:T(8,128)(2,1)S(1)}, bf16[128,2048]{1,0:T(8,128)(2,1)S(1)}, u32[]{:S(2)}, u32[]{:S(2)}) %collective-permute-start.82) | collective-permute-done | bytes 524320 | tf_op jit(solution)/shard_map/ppermute | solution.py:99
  251.5 10.1 %collective-permute-done.84.refs_6_ = bf16[128,2048]{1,0:T(8,128)(2,1)S(1)} collective-permute-done((bf16[128,2048]{1,0:T(8,128)(2,1)S(1)}, bf16[128,2048]{1,0:T(8,128)(2,1)S(1)}, u32[]{:S(2)}, u32[]{:S(2)}) %collective-permute-start.84) | collective-permute-done | bytes 524320 | tf_op jit(solution)/shard_map/ppermute | solution.py:99
  267.3 4.1 shard_map.171.refs_22_.down_ref
  274.8 28.6 %shard_map.172 = (bf16[1024,704]{1,0:T(8,128)(2,1)}, bf16[1024,704]{1,0:T(8,128)(2,1)}, bf16[1024,704]{1,0:T(8,128)(2,1)}, bf16[1024,2048]{1,0:T(8,128)(2,1)}, b...) custom-call(s32[75]{0:T(128)} %fusion.9.table_ref.table, bf16[128,2048]{1,0:T(8,128)(2,1)} %get-tuple-element.90.refs_0_, ...), custom_call_target="tpu_custom_call" | custom-call | flops 30799998976 | bytes 92400000 | tf_op jit(solution)/shard_map/pallas_call | solution.py:846
  303.4 7.1 %shard_map.173 = (bf16[1024,704]{1,0:T(8,128)(2,1)}, bf16[1024,704]{1,0:T(8,128)(2,1)}) custom-call(bf16[1024,2048]{1,0:T(8,128)(2,1)} %get-tuple-element.92.input_ref, bf16[1024,704]{1,0:T(8,128)(2,1)} %get-tuple-element.93.refs_0_, bf16[1024,704]{1,0:T(8,128)(2,1)} %get-tuple-element.94.refs_1_), custom_call_target="tpu_custom_call" | custom-call | flops 2310000128 | bytes 6930000 | tf_op jit(solution)/shard_map/pallas_call | solution.py:604
  317.7 6.2 collective-permute-done.100.ccw_ref
  333.9 9.3 %shard_map.174 = (f32[8,2,64,704]{3,2,1,0:T(8,128)}, bf16[8,2,64,704]{3,2,1,0:T(8,128)(2,1)}) custom-call(s32[75]{0:T(128)} %fusion.9.table_ref.table, bf16[1024,2048]{1,0:T(8,128)(2,1)} %get-tuple-element.92.input_ref, bf16[1024,704]{1,0:T(8,128)(2,1)} %get-tuple-element.93.refs_0_, bf16[1024,704]{1,0:T(8,128)(2,1)} %get-tuple-element.94.refs_1_, ...), custom_call_target="tpu_custom_call" | custom-call | flops 3464999936 | bytes 10395000 | tf_op jit(solution)/shard_map/pallas_call | solution.py:692
  350.0 7.2 %shard_map.175.refs_1_.ahead_ref.back_ref = bf16[1024,2048]{1,0:T(8,128)(2,1)} custom-call(bf16[1024,704]{1,0:T(8,128)(2,1)} %get-tuple-element.91.act_ref, bf16[704,2048]{1,0:T(8,128)(2,1)} %shard_map.171.refs_22_.down_ref, bf16[8,2,64,704]{3,2,1,0:T(8,128)(2,1)} %get-tuple-element.97.refs_0_.refs_1_), custom_call_target="tpu_custom_call" | custom-call | flops 2695000064 | bytes 8085000 | tf_op jit(solution)/shard_map/pallas_call | solution.py:741
  368.1 7.5 %collective-permute-done.105.refs_1_.refs_0_ = bf16[128,2048]{1,0:T(8,128)(2,1)S(1)} collective-permute-done((bf16[128,2048]{1,0:T(8,128)(2,1)}, bf16[128,2048]{1,0:T(8,128)(2,1)S(1)}, u32[]{:S(2)}, u32[]{:S(2)}) %collective-permute-start.105) | collective-permute-done | bytes 524320 | tf_op jit(solution)/shard_map/ppermute | solution.py:123
  379.5 11.1 %shard_map.188 = (f32[128,2048]{1,0:T(8,128)}, bf16[128,2048]{1,0:T(8,128)(2,1)}, bf16[128,2048]{1,0:T(8,128)(2,1)}, f32[8,2048]{1,0:T(8,128)}) custom-call(s32[75]{0:T(128)} %fusion.9.table_ref.table, bf16[128,2048]{1,0:T(8,128)(2,1)} %slice.127.refs_0_, bf16[128,2048]{1,0:T(8,128)(2,1)} %copy-done.13, bf16[128,2048]{1,0:T(8,128)(2,1)} %copy-done.14, ...), custom_call_target="tpu_custom_call" | custom-call | flops 3849999872 | bytes 11550000 | tf_op jit(solution)/shard_map/pallas_call | solution.py:184
  390.6 4.1 shard_map.190
  396.2 4.7 all-to-all-start.1
  404.9 13.7 %shard_map.189 = (bf16[128,2048]{1,0:T(8,128)(2,1)}, bf16[8,128,512]{2,1,0:T(8,128)(2,1)}, bf16[8,128,512]{2,1,0:T(8,128)(2,1)}) custom-call(s32[75]{0:T(128)} %fusion.9.table_ref.table, bf16[128,2048]{1,0:T(8,128)(2,1)} %get-tuple-element.111.refs_0_, bf16[128,2048]{1,0:T(8,128)(2,1)} %get-tuple-element.113.refs_1_, ...), custom_call_target="tpu_custom_call" | custom-call | flops 5500000256 | bytes 16500000 | tf_op jit(solution)/shard_map/pallas_call | solution.py:1025
  418.6 6.0 shard_map.191
  424.6 9.5 %collective-permute-done.107.cw_ref.refs_12_ = bf16[64,2048]{1,0:T(8,128)(2,1)S(1)} collective-permute-done((bf16[64,2048]{1,0:T(8,128)(2,1)}, bf16[64,2048]{1,0:T(8,128)(2,1)S(1)}, u32[]{:S(2)}, u32[]{:S(2)}) %collective-permute-start.107) | collective-permute-done | bytes 262176 | tf_op jit(solution)/shard_map/ppermute | solution.py:123
  434.1 5.3 all-to-all-done.1.refs_14_.refs_0_
  439.4 13.8 %shard_map.192 = (bf16[128,2048]{1,0:T(8,128)(2,1)}, bf16[8,128,512]{2,1,0:T(8,128)(2,1)}, bf16[8,128,512]{2,1,0:T(8,128)(2,1)}) custom-call(s32[75]{0:T(128)} %fusion.9.table_ref.table, bf16[128,2048]{1,0:T(8,128)(2,1)} %get-tuple-element.111.refs_0_, ...), custom_call_target="tpu_custom_call", output_to_operand_aliasing={{0}: (10, {}), {1}: (11, {}), {2}: (12, {})} | custom-call | flops 5500000256 | bytes 16500000 | tf_op jit(solution)/shard_map/pallas_call | solution.py:1025
  453.2 3.9 shard_map.193.refs_1_
  458.2 10.1 %shard_map.215 = (f32[352,2048]{1,0:T(8,128)}, bf16[352,2048]{1,0:T(8,128)(2,1)}) custom-call(s32[75]{0:T(128)} %fusion.9.table_ref.table, bf16[1024,704]{1,0:T(8,128)(2,1)} %get-tuple-element.91.act_ref, bf16[1024,2048]{1,0:T(8,128)(2,1)} %get-tuple-element.149.cot_ref, bf16[128,2048]{1,0:T(8,128)(2,1)} %copy-done.13, bf16[128,2048]{1,0:T(8,128)(2,1)} %copy-done.14), custom_call_target="tpu_custom_call" | custom-call | flops 3849999872 | bytes 11550000 | tf_op jit(solution)/shard_map/pallas_call | solution.py:719
  470.8 6.1 collective-permute-start.109
  478.2 10.7 %collective-permute-done.109.cw_ref = bf16[128,2048]{1,0:T(8,128)(2,1)S(1)} collective-permute-done((bf16[128,2048]{1,0:T(8,128)(2,1)}, bf16[128,2048]{1,0:T(8,128)(2,1)S(1)}, u32[]{:S(2)}, u32[]{:S(2)}) %collective-permute-start.109) | collective-permute-done | bytes 524320 | tf_op jit(solution)/shard_map/ppermute | solution.py:123
  500.8 4.6 collective-permute-done.123.half_got_ref
  505.4 6.1 collective-permute-start.120
  511.5 7.0 %shard_map.197.refs_1_.ahead_ref.back_ref = bf16[1536,2048]{1,0:T(8,128)(2,1)} custom-call(bf16[128,2048]{1,0:T(8,128)(2,1)} %get-tuple-element.123.input_ref, bf16[128,2048]{1,0:T(8,128)(2,1)} %get-tuple-element.124.refs_0_.grad_ref, bf16[1024,2048]{1,0:T(8,128)(2,1)} %collective-permute-done.122.got_ref, f32[8,1,64,2048]{3,2,1,0:T(8,128)} %get-tuple-element.128.half_ref, ...), custom_call_target="tpu_custom_call" | custom-call | flops 2200000000 | bytes 6600000 | tf_op jit(solution)/shard_map/pallas_call | solution.py:657
  544.7 12.0 %collective-permute-done.126.refs_1_ = bf16[128,512]{1,0:T(8,128)(2,1)S(1)} collective-permute-done((bf16[128,512]{1,0:T(8,128)(2,1)}, bf16[128,512]{1,0:T(8,128)(2,1)S(1)}, u32[]{:S(2)}, u32[]{:S(2)}) %collective-permute-start.126) | collective-permute-done | bytes 131104 | tf_op jit(solution)/shard_map/ppermute | solution.py:123
  568.2 12.2 %shard_map.204 = (bf16[128,2048]{1,0:T(8,128)(2,1)}, f32[8,2048]{1,0:T(8,128)}) custom-call(s32[75]{0:T(128)} %fusion.9.table_ref.table, bf16[128,2048]{1,0:T(8,128)(2,1)} %get-tuple-element.124.refs_0_.grad_ref, bf16[128,512]{1,0:T(8,128)(2,1)} %shard_map.201.refs_1_.refs_0_.refs_2_, bf16[128,2048]{1,0:T(8,128)(2,1)} %bitcast.60, ...), custom_call_target="tpu_custom_call" | custom-call | flops 4427500032 | bytes 13282500 | tf_op jit(solution)/shard_map/pallas_call | solution.py:184
  605.3 5.9 shard_map.214
  611.3 6.4 collective-permute-done.141.cw_ref.refs_1_
  638.6 11.1 %collective-permute-done.145 = bf16[160,512]{1,0:T(8,128)(2,1)S(1)} collective-permute-done((bf16[160,512]{1,0:T(8,128)(2,1)}, bf16[160,512]{1,0:T(8,128)(2,1)S(1)}, u32[]{:S(2)}, u32[]{:S(2)}) %collective-permute-start.145) | collective-permute-done | bytes 163872 | tf_op jit(solution)/shard_map/ppermute | solution.py:123
  658.4 13.3 %collective-permute-done.136 = bf16[192,2048]{1,0:T(8,128)(2,1)S(1)} collective-permute-done((bf16[192,2048]{1,0:T(8,128)(2,1)S(1)}, bf16[192,2048]{1,0:T(8,128)(2,1)S(1)}, u32[]{:S(2)}, u32[]{:S(2)}) %collective-permute-start.136) | collective-permute-done | bytes 786464 | tf_op jit(solution)/shard_map/ppermute | solution.py:1144
  (646 shorter events, 275.2 us)
Async XLA Ops:
  20.5 15.7 %collective-permute-start.8 = (bf16[128,1408]{1,0:T(8,128)(2,1)S(1)}, bf16[128,1408]{1,0:T(8,128)(2,1)S(1)}, u32[]{:S(2)}, u32[]{:S(2)}) collective-permute-start(bf16[128,1408]{1,0:T(8,128)(2,1)S(1)} %collective-permute-done.refs_4_.refs_7_), channel_id=1, source_target_pairs={{0,16},{16,0},{1,17},{17,1},{2,18},{18,2},{3,19},{19,3},{4,20},{20... | collective-permute-start | bytes 1081352 | tf_op jit(solution)/shard_map/ppermute | solution.py:1144
  21.2 16.7 %collective-permute-start.2 = (bf16[128,1408]{1,0:T(8,128)(2,1)S(1)}, bf16[128,1408]{1,0:T(8,128)(2,1)S(1)}, u32[]{:S(2)}, u32[]{:S(2)}) collective-permute-start(bf16[128,1408]{1,0:T(8,128)(2,1)S(1)} %collective-permute-done.refs_4_.refs_7_), channel_id=1, source_target_pairs={{0,4},{1,5},{2,0},{3,1},{4,8},{5,9},{6,2},{7,3},{8,12},{9,13},{10,... | collective-permute-start | bytes 1081352 | tf_op jit(solution)/shard_map/ppermute | solution.py:98
  49.4 19.2 %collective-permute-start.22 = (bf16[128,1408]{1,0:T(8,128)(2,1)S(1)}, bf16[128,1408]{1,0:T(8,128)(2,1)}, u32[]{:S(2)}, u32[]{:S(2)}) collective-permute-start(bf16[128,1408]{1,0:T(8,128)(2,1)S(1)} %collective-permute-done.5.refs_9_.refs_12_), channel_id=1, source_target_pairs={{0,1},{1,0},{2,3},{3,2},{4,5},{5,4},{6,7},{7,6},{8,9},{9,8},{10,11... | collective-permute-start | bytes 1081352 | tf_op jit(solution)/shard_map/ppermute | solution.py:89
  115.0 21.6 %collective-permute-start.68 = (bf16[128,1024]{1,0:T(8,128)(2,1)}, bf16[128,1024]{1,0:T(8,128)(2,1)}, u32[]{:S(2)}, u32[]{:S(2)}) collective-permute-start(bf16[128,1024]{1,0:T(8,128)(2,1)} %get-tuple-element.164.refs_12_.refs_16_), channel_id=1, source_target_pairs={{0,1},{1,0},{2,3},{3,2},{4,5},{5,4},{6,7},{7,6},{8,9},{9,8},{10,11... | collective-permute-start | bytes 786440 | tf_op jit(solution)/shard_map/ppermute | solution.py:89
  125.4 16.8 %collective-permute-start.61 = (bf16[128,1024]{1,0:T(8,128)(2,1)}, bf16[128,1024]{1,0:T(8,128)(2,1)}, u32[]{:S(2)}, u32[]{:S(2)}) collective-permute-start(bf16[128,1024]{1,0:T(8,128)(2,1)} %collective-permute-done.37.refs_5_.refs_9_), channel_id=1, source_target_pairs={{0,1},{1,0},{2,3},{3,2},{4,5},{5,4},{6,7},{7,6},{8,9},{9,8},{10,11... | collective-permute-start | bytes 786440 | tf_op jit(solution)/shard_map/ppermute | solution.py:89
  126.1 56.6 %all-to-all-start = ((bf16[8,2,64,704]{3,2,1,0:T(8,128)(2,1)}), bf16[8,2,64,704]{3,2,1,0:T(8,128)(2,1)S(1)}, u32[]{:S(2)}, u32[]{:S(2)}) async-start(bf16[8,2,64,704]{3,2,1,0:T(8,128)(2,1)} %shard_map.168), calls=%async_computation | async-start | bytes 3145728 | tf_op jit(solution)/shard_map/all_to_all | solution.py:1166
  136.6 32.3 %collective-permute-start.48 = (bf16[8,128,512]{2,1,0:T(8,128)(2,1)}, bf16[8,128,512]{2,1,0:T(8,128)(2,1)S(1)}, u32[]{:S(2)}, u32[]{:S(2)}) collective-permute-start(bf16[8,128,512]{2,1,0:T(8,128)(2,1)} %shard_map.164.refs_1_.refs_4_), channel_id=1, source_target_pairs={{0,1},{1,0},{2,3},{3,2},{4,5},{5,4},{6,7},{7,6},{8,9},{9,8},{10,11... | collective-permute-start | bytes 3145736 | tf_op jit(solution)/shard_map/ppermute | solution.py:89
  164.7 19.2 %collective-permute-start.55 = (bf16[128,1024]{1,0:T(8,128)(2,1)S(1)}, bf16[128,1024]{1,0:T(8,128)(2,1)}, u32[]{:S(2)}, u32[]{:S(2)}) collective-permute-start(bf16[128,1024]{1,0:T(8,128)(2,1)S(1)} %copy-done.70), channel_id=1, source_target_pairs={{0,16},{16,0},{1,17},{17,1},{2,18},{18,2},{3,19},{19,3},{4,20},{20... | collective-permute-start | bytes 786440 | tf_op jit(solution)/shard_map/ppermute | solution.py:1144
  166.2 17.7 %collective-permute-start.67 = (bf16[64,1024]{1,0:T(8,128)(2,1)S(1)}, bf16[64,1024]{1,0:T(8,128)(2,1)S(1)}, u32[]{:S(2)}, u32[]{:S(2)}) collective-permute-start(bf16[64,1024]{1,0:T(8,128)(2,1)S(1)} %copy-done.64), channel_id=1, source_target_pairs={{0,1},{1,0},{2,3},{3,2},{4,5},{5,4},{6,7},{7,6},{8,9},{9,8},{10,11... | collective-permute-start | bytes 393224 | tf_op jit(solution)/shard_map/ppermute | solution.py:89
  166.2 18.3 %collective-permute-start.66 = (bf16[64,1024]{1,0:T(8,128)(2,1)S(1)}, bf16[64,1024]{1,0:T(8,128)(2,1)S(1)}, u32[]{:S(2)}, u32[]{:S(2)}) collective-permute-start(bf16[64,1024]{1,0:T(8,128)(2,1)S(1)} %copy-done.66), channel_id=1, source_target_pairs={{0,1},{1,0},{2,3},{3,2},{4,5},{5,4},{6,7},{7,6},{8,9},{9,8},{10,11... | collective-permute-start | bytes 393224 | tf_op jit(solution)/shard_map/ppermute | solution.py:89
  167.5 16.9 %collective-permute-start.57 = (bf16[64,1024]{1,0:T(8,128)(2,1)S(1)}, bf16[64,1024]{1,0:T(8,128)(2,1)S(1)}, u32[]{:S(2)}, u32[]{:S(2)}) collective-permute-start(bf16[64,1024]{1,0:T(8,128)(2,1)S(1)} %copy-done.66), channel_id=1, source_target_pairs={{0,16},{16,0},{1,17},{17,1},{2,18},{18,2},{3,19},{19,3},{4,20},{20... | collective-permute-start | bytes 393224 | tf_op jit(solution)/shard_map/ppermute | solution.py:1144
  169.0 17.6 %collective-permute-start.76 = (bf16[64,1024]{1,0:T(8,128)(2,1)S(1)}, bf16[64,1024]{1,0:T(8,128)(2,1)S(1)}, u32[]{:S(2)}, u32[]{:S(2)}) collective-permute-start(bf16[64,1024]{1,0:T(8,128)(2,1)S(1)} %collective-permute-done.58.refs_20_.refs_24_), channel_id=1, source_target_pairs={{0,1},{1,0},{2,3},{3,2},{4,5},{5,4},{6,7},{7,6},{8,9},{9,8},{10,11... | collective-permute-start | bytes 393224 | tf_op jit(solution)/shard_map/ppermute | solution.py:89
  183.9 18.3 %collective-permute-start.74 = (bf16[128,1024]{1,0:T(8,128)(2,1)S(1)}, bf16[128,1024]{1,0:T(8,128)(2,1)S(1)}, u32[]{:S(2)}, u32[]{:S(2)}) collective-permute-start(bf16[128,1024]{1,0:T(8,128)(2,1)S(1)} %copy-done.106), channel_id=1, source_target_pairs={{0,1},{1,0},{2,3},{3,2},{4,5},{5,4},{6,7},{7,6},{8,9},{9,8},{10,11... | collective-permute-start | bytes 786440 | tf_op jit(solution)/shard_map/ppermute | solution.py:89
  183.9 18.3 %collective-permute-start.73 = (bf16[128,1024]{1,0:T(8,128)(2,1)}, bf16[128,1024]{1,0:T(8,128)(2,1)S(1)}, u32[]{:S(2)}, u32[]{:S(2)}) collective-permute-start(bf16[128,1024]{1,0:T(8,128)(2,1)} %collective-permute-done.55.refs_17_.refs_21_), channel_id=1, source_target_pairs={{0,1},{1,0},{2,3},{3,2},{4,5},{5,4},{6,7},{7,6},{8,9},{9,8},{10,11... | collective-permute-start | bytes 786440 | tf_op jit(solution)/shard_map/ppermute | solution.py:89
  199.5 36.6 %collective-permute-start.93 = (bf16[8,2,64,704]{3,2,1,0:T(8,128)(2,1)S(1)}, bf16[8,2,64,704]{3,2,1,0:T(8,128)(2,1)}, u32[]{:S(2)}, u32[]{:S(2)}) collective-permute-start(bf16[8,2,64,704]{3,2,1,0:T(8,128)(2,1)S(1)} %copy-done.3), channel_id=1, source_target_pairs={{0,16},{16,0},{1,17},{17,1},{2,18},{18,2},{3,19},{19,3},{4,20},{20... | collective-permute-start | bytes 4325384 | tf_op jit(solution)/shard_map/ppermute | solution.py:1144
  214.1 23.7 %collective-permute-start.90 = (bf16[128,2048]{1,0:T(8,128)(2,1)S(1)}, bf16[128,2048]{1,0:T(8,128)(2,1)S(1)}, u32[]{:S(2)}, u32[]{:S(2)}) collective-permute-start(bf16[128,2048]{1,0:T(8,128)(2,1)S(1)} %collective-permute-done.88.refs_13_), channel_id=1, source_target_pairs={{0,2},{1,3},{2,6},{3,7},{4,0},{5,1},{6,10},{7,11},{8,4},{9,5},{10,... | collective-permute-start | bytes 1572872 | tf_op jit(solution)/shard_map/ppermute | solution.py:99
  215.9 22.3 %collective-permute-start.89 = (bf16[128,2048]{1,0:T(8,128)(2,1)S(1)}, bf16[128,2048]{1,0:T(8,128)(2,1)S(1)}, u32[]{:S(2)}, u32[]{:S(2)}) collective-permute-start(bf16[128,2048]{1,0:T(8,128)(2,1)S(1)} %collective-permute-done.87.refs_12_), channel_id=1, source_target_pairs={{0,4},{1,5},{2,0},{3,1},{4,8},{5,9},{6,2},{7,3},{8,12},{9,13},{10,... | collective-permute-start | bytes 1572872 | tf_op jit(solution)/shard_map/ppermute | solution.py:98
  226.5 37.2 %collective-permute-start.96 = (bf16[352,2048]{1,0:T(8,128)(2,1)S(1)}, bf16[352,2048]{1,0:T(8,128)(2,1)S(1)}, u32[]{:S(2)}, u32[]{:S(2)}) collective-permute-start(bf16[352,2048]{1,0:T(8,128)(2,1)S(1)} %copy-done.75), channel_id=1, source_target_pairs={{0,1},{1,0},{2,3},{3,2},{4,5},{5,4},{6,7},{7,6},{8,9},{9,8},{10,11... | collective-permute-start | bytes 4325384 | tf_op jit(solution)/shard_map/ppermute | solution.py:89
  228.3 36.7 %collective-permute-start.94 = (bf16[8,2,64,704]{3,2,1,0:T(8,128)(2,1)S(1)}, bf16[8,2,64,704]{3,2,1,0:T(8,128)(2,1)S(1)}, u32[]{:S(2)}, u32[]{:S(2)}) collective-permute-start(bf16[8,2,64,704]{3,2,1,0:T(8,128)(2,1)S(1)} %copy-done.3), channel_id=1, source_target_pairs={{0,1},{1,0},{2,3},{3,2},{4,5},{5,4},{6,7},{7,6},{8,9},{9,8},{10,11... | collective-permute-start | bytes 4325384 | tf_op jit(solution)/shard_map/ppermute | solution.py:89
  238.2 35.9 %collective-permute-start.95 = (bf16[8,2,64,704]{3,2,1,0:T(8,128)(2,1)}, bf16[8,2,64,704]{3,2,1,0:T(8,128)(2,1)}, u32[]{:S(2)}, u32[]{:S(2)}) collective-permute-start(bf16[8,2,64,704]{3,2,1,0:T(8,128)(2,1)} %collective-permute-done.93.refs_19_), channel_id=1, source_target_pairs={{0,1},{1,0},{2,3},{3,2},{4,5},{5,4},{6,7},{7,6},{8,9},{9,8},{10,11... | collective-permute-start | bytes 4325384 | tf_op jit(solution)/shard_map/ppermute | solution.py:89
  312.4 17.4 %collective-permute-start.98 = (bf16[1024,704]{0,1:T(8,128)(2,1)S(1)}, bf16[1024,704]{0,1:T(8,128)(2,1)}, u32[]{:S(2)}, u32[]{:S(2)}) collective-permute-start(bf16[1024,704]{0,1:T(8,128)(2,1)S(1)} %copy.56), channel_id=1, source_target_pairs={{0,1},{1,0},{2,3},{3,2},{4,5},{5,4},{6,7},{7,6},{8,9},{9,8},{10,11... | collective-permute-start | bytes 4325384 | tf_op jit(solution)/shard_map/ppermute | solution.py:89
  314.1 18.3 %collective-permute-start.97 = (bf16[1024,704]{0,1:T(8,128)(2,1)}, bf16[1024,704]{0,1:T(8,128)(2,1)S(1)}, u32[]{:S(2)}, u32[]{:S(2)}) collective-permute-start(bf16[1024,704]{0,1:T(8,128)(2,1)} %copy.55), channel_id=1, source_target_pairs={{0,1},{1,0},{2,3},{3,2},{4,5},{5,4},{6,7},{7,6},{8,9},{9,8},{10,11... | collective-permute-start | bytes 4325384 | tf_op jit(solution)/shard_map/ppermute | solution.py:89
  327.7 16.0 %collective-permute-start.101 = (bf16[128,2048]{1,0:T(8,128)(2,1)}, bf16[128,2048]{1,0:T(8,128)(2,1)S(1)}, u32[]{:S(2)}, u32[]{:S(2)}) collective-permute-start(bf16[128,2048]{1,0:T(8,128)(2,1)} %get-tuple-element.99), channel_id=1, source_target_pairs={{0,4},{1,5},{2,0},{3,1},{4,8},{5,9},{6,2},{7,3},{8,12},{9,13},{10,... | collective-permute-start | bytes 1572872 | tf_op jit(solution)/shard_map/ppermute | solution.py:123
  343.2 35.1 %collective-permute-start.115 = (bf16[8,2,64,704]{3,2,1,0:T(8,128)(2,1)}, bf16[8,2,64,704]{3,2,1,0:T(8,128)(2,1)S(1)}, u32[]{:S(2)}, u32[]{:S(2)}) collective-permute-start(bf16[8,2,64,704]{3,2,1,0:T(8,128)(2,1)} %get-tuple-element.97.refs_0_.refs_1_), channel_id=1, source_target_pairs={{0,16},{16,0},{1,17},{17,1},{2,18},{18,2},{3,19},{19,3},{4,20},{20... | collective-permute-start | bytes 4325384 | tf_op jit(solution)/shard_map/ppermute | solution.py:1144
  394.7 24.0 %collective-permute-start.116 = (bf16[1024,2048]{1,0:T(8,128)(2,1)}, bf16[1024,2048]{1,0:T(8,128)(2,1)}, u32[]{:S(2)}, u32[]{:S(2)}) collective-permute-start(bf16[1024,2048]{1,0:T(8,128)(2,1)} %shard_map.190), channel_id=1, source_target_pairs={{0,1},{1,0},{2,3},{3,2},{4,5},{5,4},{6,7},{7,6},{8,9},{9,8},{10,11... | collective-permute-start | bytes 12582920 | tf_op jit(solution)/shard_map/ppermute | solution.py:89
  396.2 43.2 %all-to-all-start.1 = ((bf16[8,2,64,704]{3,2,1,0:T(8,128)(2,1)}), bf16[8,2,64,704]{3,2,1,0:T(8,128)(2,1)}, u32[]{:S(2)}, u32[]{:S(2)}) async-start(bf16[8,2,64,704]{3,2,1,0:T(8,128)(2,1)} %add_convert_fusion), calls=%async_computation.1 | async-start | bytes 3145728 | tf_op jit(solution)/shard_map/all_to_all | solution.py:1207
  402.8 31.2 %collective-permute-start.107 = (bf16[64,2048]{1,0:T(8,128)(2,1)}, bf16[64,2048]{1,0:T(8,128)(2,1)S(1)}, u32[]{:S(2)}, u32[]{:S(2)}) collective-permute-start(bf16[64,2048]{1,0:T(8,128)(2,1)} %shard_map.183), channel_id=1, source_target_pairs={{0,4},{1,5},{2,0},{3,1},{4,8},{5,9},{6,2},{7,3},{8,12},{9,13},{10,... | collective-permute-start | bytes 786440 | tf_op jit(solution)/shard_map/ppermute | solution.py:123
  404.9 29.2 %collective-permute-start.108 = (bf16[64,2048]{1,0:T(8,128)(2,1)}, bf16[64,2048]{1,0:T(8,128)(2,1)S(1)}, u32[]{:S(2)}, u32[]{:S(2)}) collective-permute-start(bf16[64,2048]{1,0:T(8,128)(2,1)} %shard_map.184), channel_id=1, source_target_pairs={{0,2},{1,3},{2,6},{3,7},{4,0},{5,1},{6,10},{7,11},{8,4},{9,5},{10,... | collective-permute-start | bytes 786440 | tf_op jit(solution)/shard_map/ppermute | solution.py:124
  457.1 54.3 %collective-permute-start.122 = (bf16[1024,2048]{1,0:T(8,128)(2,1)}, bf16[1024,2048]{1,0:T(8,128)(2,1)}, u32[]{:S(2)}, u32[]{:S(2)}) collective-permute-start(bf16[1024,2048]{1,0:T(8,128)(2,1)} %shard_map.193.refs_1_), channel_id=1, source_target_pairs={{0,1},{1,0},{2,3},{3,2},{4,5},{5,4},{6,7},{7,6},{8,9},{9,8},{10,11... | collective-permute-start | bytes 12582920 | tf_op jit(solution)/shard_map/ppermute | solution.py:89
  457.2 20.6 %collective-permute-start.117 = (bf16[8,128,512]{2,1,0:T(8,128)(2,1)}, bf16[8,128,512]{2,1,0:T(8,128)(2,1)S(1)}, u32[]{:S(2)}, u32[]{:S(2)}) collective-permute-start(bf16[8,128,512]{2,1,0:T(8,128)(2,1)} %shard_map.194), channel_id=1, source_target_pairs={{0,1},{1,0},{2,3},{3,2},{4,5},{5,4},{6,7},{7,6},{8,9},{9,8},{10,11... | collective-permute-start | bytes 3145736 | tf_op jit(solution)/shard_map/ppermute | solution.py:89
  457.7 47.7 %collective-permute-start.123 = (bf16[8,1,64,2048]{3,2,1,0:T(8,128)(2,1)}, bf16[8,1,64,2048]{3,2,1,0:T(8,128)(2,1)S(1)}, u32[]{:S(2)}, u32[]{:S(2)}) collective-permute-start(bf16[8,1,64,2048]{3,2,1,0:T(8,128)(2,1)} %get-tuple-element.120.refs_15_), channel_id=1, source_target_pairs={{0,16},{16,0},{1,17},{17,1},{2,18},{18,2},{3,19},{19,3},{4,20},{20... | collective-permute-start | bytes 6291464 | tf_op jit(solution)/shard_map/ppermute | solution.py:1144
  468.3 113.4 %collective-permute-start.149 = (bf16[352,2048]{1,0:T(8,128)(2,1)}, bf16[352,2048]{1,0:T(8,128)(2,1)}, u32[]{:S(2)}, u32[]{:S(2)}) collective-permute-start(bf16[352,2048]{1,0:T(8,128)(2,1)} %get-tuple-element.151), channel_id=1, source_target_pairs={{0,1},{1,0},{2,3},{3,2},{4,5},{5,4},{6,7},{7,6},{8,9},{9,8},{10,11... | collective-permute-start | bytes 4325384 | tf_op jit(solution)/shard_map/ppermute | solution.py:89
  470.8 18.2 %collective-permute-start.109 = (bf16[128,2048]{1,0:T(8,128)(2,1)}, bf16[128,2048]{1,0:T(8,128)(2,1)S(1)}, u32[]{:S(2)}, u32[]{:S(2)}) collective-permute-start(bf16[128,2048]{1,0:T(8,128)(2,1)} %get-tuple-element.105), channel_id=1, source_target_pairs={{0,4},{1,5},{2,0},{3,1},{4,8},{5,9},{6,2},{7,3},{8,12},{9,13},{10,... | collective-permute-start | bytes 1572872 | tf_op jit(solution)/shard_map/ppermute | solution.py:123
  497.0 22.7 %collective-permute-start.111 = (bf16[128,2048]{1,0:T(8,128)(2,1)}, bf16[128,2048]{1,0:T(8,128)(2,1)S(1)}, u32[]{:S(2)}, u32[]{:S(2)}) collective-permute-start(bf16[128,2048]{1,0:T(8,128)(2,1)} %get-tuple-element.107), channel_id=1, source_target_pairs={{0,4},{1,5},{2,0},{3,1},{4,8},{5,9},{6,2},{7,3},{8,12},{9,13},{10,... | collective-permute-start | bytes 1572872 | tf_op jit(solution)/shard_map/ppermute | solution.py:123
  497.3 24.0 %collective-permute-start.112 = (bf16[128,2048]{1,0:T(8,128)(2,1)}, bf16[128,2048]{1,0:T(8,128)(2,1)S(1)}, u32[]{:S(2)}, u32[]{:S(2)}) collective-permute-start(bf16[128,2048]{1,0:T(8,128)(2,1)} %get-tuple-element.108), channel_id=1, source_target_pairs={{0,2},{1,3},{2,6},{3,7},{4,0},{5,1},{6,10},{7,11},{8,4},{9,5},{10,... | collective-permute-start | bytes 1572872 | tf_op jit(solution)/shard_map/ppermute | solution.py:124
  505.4 19.3 %collective-permute-start.120 = (bf16[128,512]{1,0:T(8,128)(2,1)}, bf16[128,512]{1,0:T(8,128)(2,1)S(1)}, u32[]{:S(2)}, u32[]{:S(2)}) collective-permute-start(bf16[128,512]{1,0:T(8,128)(2,1)} %get-tuple-element.125), channel_id=1, source_target_pairs={{0,4},{1,5},{2,0},{3,1},{4,8},{5,9},{6,2},{7,3},{8,12},{9,13},{10,... | collective-permute-start | bytes 393224 | tf_op jit(solution)/shard_map/ppermute | solution.py:123
  536.0 30.9 %collective-permute-start.130 = (bf16[192,2048]{1,0:T(8,128)(2,1)}, bf16[192,2048]{1,0:T(8,128)(2,1)S(1)}, u32[]{:S(2)}, u32[]{:S(2)}) collective-permute-start(bf16[192,2048]{1,0:T(8,128)(2,1)} %get-tuple-element.134), channel_id=1, source_target_pairs={{0,4},{1,5},{2,0},{3,1},{4,8},{5,9},{6,2},{7,3},{8,12},{9,13},{10,... | collective-permute-start | bytes 2359304 | tf_op jit(solution)/shard_map/ppermute | solution.py:123
  536.1 30.8 %collective-permute-start.131 = (bf16[192,2048]{1,0:T(8,128)(2,1)}, bf16[192,2048]{1,0:T(8,128)(2,1)S(1)}, u32[]{:S(2)}, u32[]{:S(2)}) collective-permute-start(bf16[192,2048]{1,0:T(8,128)(2,1)} %get-tuple-element.135), channel_id=1, source_target_pairs={{0,2},{1,3},{2,6},{3,7},{4,0},{5,1},{6,10},{7,11},{8,4},{9,5},{10,... | collective-permute-start | bytes 2359304 | tf_op jit(solution)/shard_map/ppermute | solution.py:124
  566.0 37.6 %collective-permute-start.148 = (bf16[8,2,64,704]{3,2,1,0:T(8,128)(2,1)}, bf16[8,2,64,704]{3,2,1,0:T(8,128)(2,1)}, u32[]{:S(2)}, u32[]{:S(2)}) collective-permute-start(bf16[8,2,64,704]{3,2,1,0:T(8,128)(2,1)} %all-to-all-done.1.refs_14_.refs_0_), channel_id=1, source_target_pairs={{0,16},{16,0},{1,17},{17,1},{2,18},{18,2},{3,19},{19,3},{4,20},{20... | collective-permute-start | bytes 4325384 | tf_op jit(solution)/shard_map/ppermute | solution.py:1144
  566.9 19.0 %collective-permute-start.137 = (bf16[1024,512]{1,0:T(8,128)(2,1)}, bf16[1024,512]{1,0:T(8,128)(2,1)}, u32[]{:S(2)}, u32[]{:S(2)}) collective-permute-start(bf16[1024,512]{1,0:T(8,128)(2,1)} %shard_map.207), channel_id=1, source_target_pairs={{0,1},{1,0},{2,3},{3,2},{4,5},{5,4},{6,7},{7,6},{8,9},{9,8},{10,11... | collective-permute-start | bytes 3145736 | tf_op jit(solution)/shard_map/ppermute | solution.py:89
  584.6 52.9 %collective-permute-start.150 = (bf16[352,2048]{1,0:T(8,128)(2,1)}, bf16[352,2048]{1,0:T(8,128)(2,1)S(1)}, u32[]{:S(2)}, u32[]{:S(2)}) collective-permute-start(bf16[352,2048]{1,0:T(8,128)(2,1)} %add_convert_fusion.1), channel_id=1, source_target_pairs={{0,16},{16,0},{1,17},{17,1},{2,18},{18,2},{3,19},{19,3},{4,20},{20... | collective-permute-start | bytes 4325384 | tf_op jit(solution)/shard_map/ppermute | solution.py:1144
  595.1 25.9 %collective-permute-start.132 = (bf16[192,2048]{1,0:T(8,128)(2,1)}, bf16[192,2048]{1,0:T(8,128)(2,1)S(1)}, u32[]{:S(2)}, u32[]{:S(2)}) collective-permute-start(bf16[192,2048]{1,0:T(8,128)(2,1)} %get-tuple-element.137), channel_id=1, source_target_pairs={{0,4},{1,5},{2,0},{3,1},{4,8},{5,9},{6,2},{7,3},{8,12},{9,13},{10,... | collective-permute-start | bytes 2359304 | tf_op jit(solution)/shard_map/ppermute | solution.py:123
  596.3 24.8 %collective-permute-start.133 = (bf16[192,2048]{1,0:T(8,128)(2,1)}, bf16[192,2048]{1,0:T(8,128)(2,1)S(1)}, u32[]{:S(2)}, u32[]{:S(2)}) collective-permute-start(bf16[192,2048]{1,0:T(8,128)(2,1)} %get-tuple-element.138), channel_id=1, source_target_pairs={{0,2},{1,3},{2,6},{3,7},{4,0},{5,1},{6,10},{7,11},{8,4},{9,5},{10,... | collective-permute-start | bytes 2359304 | tf_op jit(solution)/shard_map/ppermute | solution.py:124
  599.6 18.0 %collective-permute-start.141 = (bf16[160,512]{1,0:T(8,128)(2,1)}, bf16[160,512]{1,0:T(8,128)(2,1)S(1)}, u32[]{:S(2)}, u32[]{:S(2)}) collective-permute-start(bf16[160,512]{1,0:T(8,128)(2,1)} %get-tuple-element.143), channel_id=1, source_target_pairs={{0,4},{1,5},{2,0},{3,1},{4,8},{5,9},{6,2},{7,3},{8,12},{9,13},{10,... | collective-permute-start | bytes 491528 | tf_op jit(solution)/shard_map/ppermute | solution.py:123
  627.4 24.0 %collective-permute-start.134 = (bf16[192,2048]{1,0:T(8,128)(2,1)}, bf16[192,2048]{1,0:T(8,128)(2,1)S(1)}, u32[]{:S(2)}, u32[]{:S(2)}) collective-permute-start(bf16[192,2048]{1,0:T(8,128)(2,1)} %get-tuple-element.139), channel_id=1, source_target_pairs={{0,4},{1,5},{2,0},{3,1},{4,8},{5,9},{6,2},{7,3},{8,12},{9,13},{10,... | collective-permute-start | bytes 2359304 | tf_op jit(solution)/shard_map/ppermute | solution.py:123
  629.0 22.4 %collective-permute-start.135 = (bf16[192,2048]{1,0:T(8,128)(2,1)}, bf16[192,2048]{1,0:T(8,128)(2,1)S(1)}, u32[]{:S(2)}, u32[]{:S(2)}) collective-permute-start(bf16[192,2048]{1,0:T(8,128)(2,1)} %get-tuple-element.140), channel_id=1, source_target_pairs={{0,2},{1,3},{2,6},{3,7},{4,0},{5,1},{6,10},{7,11},{8,4},{9,5},{10,... | collective-permute-start | bytes 2359304 | tf_op jit(solution)/shard_map/ppermute | solution.py:124
  633.3 16.3 %collective-permute-start.145 = (bf16[160,512]{1,0:T(8,128)(2,1)}, bf16[160,512]{1,0:T(8,128)(2,1)S(1)}, u32[]{:S(2)}, u32[]{:S(2)}) collective-permute-start(bf16[160,512]{1,0:T(8,128)(2,1)} %get-tuple-element.147), channel_id=1, source_target_pairs={{0,4},{1,5},{2,0},{3,1},{4,8},{5,9},{6,2},{7,3},{8,12},{9,13},{10,... | collective-permute-start | bytes 491528 | tf_op jit(solution)/shard_map/ppermute | solution.py:123
  653.0 18.8 %collective-permute-start.136 = (bf16[192,2048]{1,0:T(8,128)(2,1)S(1)}, bf16[192,2048]{1,0:T(8,128)(2,1)S(1)}, u32[]{:S(2)}, u32[]{:S(2)}) collective-permute-start(bf16[192,2048]{1,0:T(8,128)(2,1)S(1)} %add_convert_fusion.3), channel_id=1, source_target_pairs={{0,16},{16,0},{1,17},{17,1},{2,18},{18,2},{3,19},{19,3},{4,20},{20... | collective-permute-start | bytes 2359304 | tf_op jit(solution)/shard_map/ppermute | solution.py:1144
  (244 other events, 2715.2 us)
